TPU v7x, 32 devices: a whole 2x2x4 slice. The times are simulated.
32 devices in a mesh: dp: 8 (over z, x), mp: 4 (over y, core).
Axes of the slice: x: 2, y: 2, z: 4, core: 2. Of those that a mesh axis runs over, the one named last changes fastest.
Arguments:
- tokens: bfloat16 [8192, 512], P('dp'), may hold values from -6 to 6
- ln1_gain: float32 [512], replicated, may hold values from 0.5 to 1.5
- ln1_bias: float32 [512], replicated, may hold values from -4 to 4
- w_qkv: bfloat16 [3, 512, 512], P(None, None, 'mp'), may hold values from -0.25 to 0.25
- w_out: bfloat16 [512, 512], P('mp'), may hold values from -2 to 2
- b_out: float32 [512], replicated, may hold values from -4 to 4
- ln2_gain: float32 [512], replicated, may hold values from 0.5 to 1.5
- ln2_bias: float32 [512], replicated, may hold values from -4 to 4
- w_up: bfloat16 [512, 2048], P(None, 'mp'), may hold values from -0.25 to 0.25
- b_up: float32 [2048], P('mp'), may hold values from -6 to 6
- w_down: bfloat16 [2048, 512], P('mp'), may hold values from -0.25 to 0.25
- b_down: float32 [512], replicated, may hold values from -4 to 4
- cotangent: bfloat16 [8192, 512], P('dp'), may hold values from -6 to 6
Outputs:
- output: bfloat16 [8192, 512], P('dp')
- grad_tokens: bfloat16 [8192, 512], P('dp')
- grad_ln1_gain: float32 [512], replicated
- grad_ln1_bias: float32 [512], replicated
- grad_w_qkv: float32 [3, 512, 512], P(None, None, 'mp')
- grad_w_out: float32 [512, 512], P('mp')
- grad_b_out: float32 [512], replicated
- grad_ln2_gain: float32 [512], replicated
- grad_ln2_bias: float32 [512], replicated
- grad_w_up: float32 [512, 2048], P(None, 'mp')
- grad_b_up: float32 [2048], P('mp')
- grad_w_down: float32 [2048, 512], P('mp')
- grad_b_down: float32 [512], replicated
All inputs are finite; a program needn't handle non-finite values.
Results may differ from a plain program's by a relative error of at most 0.012.
Values may be sent and summed in bfloat16 or wider, within the bound.
No kernel may reach another device: no remote copies, remote signals or barrier semaphores. Data moves between devices by JAX's collectives and lax.ppermute only.
A program may use at most 64 MiB of HBM per device.

v0:
```python
import math

import jax
import jax.numpy as jnp
from jax import lax
from jax.sharding import PartitionSpec as P

HEAD_DIM = 64
SPAN = 128
LENGTH = 4096


EPSILON = 1e-05


def layer_norm(values, gain, offset):
    center = values - jnp.mean(values, axis=-1, keepdims=True)
    spread = jnp.mean(center * center, axis=-1, keepdims=True)
    return center * lax.rsqrt(spread + EPSILON) * gain + offset


def per_device(
    tokens,
    ln1_gain,
    ln1_bias,
    w_qkv,
    w_out,
    b_out,
    ln2_gain,
    ln2_bias,
    w_up,
    b_up,
    w_down,
    b_down,
    cotangent,
):
    f32 = jnp.float32
    bf16 = jnp.bfloat16
    inputs = tokens.astype(f32)
    rows = inputs.shape[0]
    width = w_qkv.shape[2]
    heads = width // HEAD_DIM
    blocks = rows // SPAN
    scale = HEAD_DIM ** (-0.5)

    def heads_first(array):
        return array.reshape(blocks, SPAN, heads, HEAD_DIM).transpose(2, 0, 1, 3)

    def heads_last(array):
        return array.transpose(1, 2, 0, 3).reshape(rows, width)

    first_full, first_pull = jax.vjp(layer_norm, inputs, ln1_gain, ln1_bias)
    first = first_full.astype(bf16)
    projected = jnp.einsum("td,sde->ste", first, w_qkv, preferred_element_type=f32).astype(bf16)
    query_heads = heads_first(projected[0])
    key_heads = heads_first(projected[1])
    value_heads = heads_first(projected[2])
    key_summary = jnp.mean(key_heads.astype(f32), axis=2).transpose(1, 0, 2).astype(bf16)
    value_summary = jnp.mean(value_heads.astype(f32), axis=2).transpose(1, 0, 2).astype(bf16)
    gathered_keys, gathered_values = (
        lax.all_gather(key_summary, "dp", axis=0, tiled=True),
        lax.all_gather(value_summary, "dp", axis=0, tiled=True),
    )
    seq_blocks = LENGTH // SPAN
    first_block = lax.axis_index("dp") * blocks
    seq_start = first_block // seq_blocks * seq_blocks
    all_keys = lax.dynamic_slice_in_dim(gathered_keys, seq_start, seq_blocks, 0)
    all_values = lax.dynamic_slice_in_dim(gathered_values, seq_start, seq_blocks, 0)
    query_block = first_block + jnp.arange(blocks, dtype=jnp.int32)
    summary_block = seq_start + jnp.arange(seq_blocks, dtype=jnp.int32)
    allowed = summary_block[None, :] < query_block[:, None]
    causal = jnp.arange(SPAN)[:, None] >= jnp.arange(SPAN)[None, :]
    local = (
        jnp.einsum("hbqd,hbkd->hbqk", query_heads, key_heads, preferred_element_type=f32) * scale
    )
    local = jnp.where(causal[None, None], local, -1e30)
    summary = jnp.einsum(
        "hbqd,ghd->hbqg", query_heads, all_keys, preferred_element_type=f32
    ) * scale + math.log(SPAN)
    summary = jnp.where(allowed[None, :, None, :], summary, -1e30)
    scores = jnp.concatenate([local, summary], axis=-1)
    highest = jnp.max(scores, axis=-1, keepdims=True)
    weights = jnp.exp(scores - highest)
    probs = weights / jnp.sum(weights, axis=-1, keepdims=True)
    probs_low = probs.astype(bf16)
    attended = jnp.einsum(
        "hbqk,hbkd->hbqd", probs_low[..., :SPAN], value_heads, preferred_element_type=f32
    )
    attended = attended + jnp.einsum(
        "hbqg,ghd->hbqd", probs_low[..., SPAN:], all_values, preferred_element_type=f32
    )
    attended = heads_last(attended.astype(bf16))
    attention_terms = jnp.dot(attended, w_out, preferred_element_type=f32)
    mid = inputs + lax.psum(attention_terms, "mp") + b_out
    second_full, second_pull = jax.vjp(layer_norm, mid, ln2_gain, ln2_bias)
    second = second_full.astype(bf16)
    upper = jnp.dot(second, w_up, preferred_element_type=f32) + b_up
    active_full, gelu_pull = jax.vjp(jax.nn.gelu, upper)
    active = active_full.astype(bf16)
    feedforward_terms = jnp.dot(active, w_down, preferred_element_type=f32)
    feedforward = lax.psum(feedforward_terms, "mp")
    output = (mid + feedforward + b_down).astype(bf16)
    grad_out = cotangent.astype(f32)
    grad_w_down = jnp.einsum("tf,td->fd", active, cotangent, preferred_element_type=f32)
    grad_b_down = jnp.sum(grad_out, axis=0)
    grad_active = jnp.einsum("td,fd->tf", cotangent, w_down, preferred_element_type=f32)
    grad_upper = gelu_pull(grad_active)[0].astype(bf16)
    grad_w_up = jnp.einsum("td,tf->df", second, grad_upper, preferred_element_type=f32)
    grad_b_up = jnp.sum(grad_upper.astype(f32), axis=0)
    grad_second = lax.psum(
        jnp.einsum("tf,df->td", grad_upper, w_up, preferred_element_type=f32), "mp"
    )
    grad_mid_norm, grad_ln2_gain, grad_ln2_bias = second_pull(grad_second)
    grad_mid = grad_out + grad_mid_norm
    grad_attention = grad_mid.astype(bf16)
    grad_w_out = jnp.einsum("tc,td->cd", attended, grad_attention, preferred_element_type=f32)
    grad_b_out = jnp.sum(grad_mid, axis=0)
    grad_attended = heads_first(
        jnp.einsum("td,cd->tc", grad_attention, w_out, preferred_element_type=f32).astype(bf16)
    )
    grad_probs = jnp.concatenate(
        [
            jnp.einsum("hbqd,hbkd->hbqk", grad_attended, value_heads, preferred_element_type=f32),
            jnp.einsum("hbqd,ghd->hbqg", grad_attended, all_values, preferred_element_type=f32),
        ],
        axis=-1,
    )
    centered = jnp.sum(probs * grad_probs, axis=-1, keepdims=True)
    grad_scores = (probs * (grad_probs - centered)).astype(bf16)
    grad_local = grad_scores[..., :SPAN]
    grad_remote = grad_scores[..., SPAN:]
    grad_query = (
        jnp.einsum("hbqk,hbkd->hbqd", grad_local, key_heads, preferred_element_type=f32)
        + jnp.einsum("hbqg,ghd->hbqd", grad_remote, all_keys, preferred_element_type=f32)
    ) * scale
    grad_keys = (
        jnp.einsum("hbqk,hbqd->hbkd", grad_local, query_heads, preferred_element_type=f32) * scale
    )
    grad_values = jnp.einsum(
        "hbqk,hbqd->hbkd", probs_low[..., :SPAN], grad_attended, preferred_element_type=f32
    )
    grad_key_summary = (
        jnp.einsum("hbqg,hbqd->ghd", grad_remote, query_heads, preferred_element_type=f32) * scale
    )
    grad_value_summary = jnp.einsum(
        "hbqg,hbqd->ghd", probs_low[..., SPAN:], grad_attended, preferred_element_type=f32
    )
    empty = jnp.zeros(gathered_keys.shape, f32)
    placed_keys = lax.dynamic_update_slice_in_dim(empty, grad_key_summary, seq_start, 0)
    placed_values = lax.dynamic_update_slice_in_dim(empty, grad_value_summary, seq_start, 0)
    own_keys, own_values = (
        lax.psum_scatter(placed_keys, "dp", scatter_dimension=0, tiled=True),
        lax.psum_scatter(placed_values, "dp", scatter_dimension=0, tiled=True),
    )
    grad_keys = grad_keys + own_keys.transpose(1, 0, 2)[:, :, None, :] / SPAN
    grad_values = grad_values + own_values.transpose(1, 0, 2)[:, :, None, :] / SPAN
    grad_qkv = jnp.stack(
        [
            heads_last(grad_query.astype(bf16)),
            heads_last(grad_keys.astype(bf16)),
            heads_last(grad_values.astype(bf16)),
        ]
    )
    grad_w_qkv = jnp.einsum("td,ste->sde", first, grad_qkv, preferred_element_type=f32)
    grad_first = lax.psum(
        jnp.einsum("ste,sde->td", grad_qkv, w_qkv, preferred_element_type=f32), "mp"
    )
    grad_in_norm, grad_ln1_gain, grad_ln1_bias = first_pull(grad_first)
    grad_tokens = (grad_mid + grad_in_norm).astype(bf16)
    (
        grad_ln1_gain,
        grad_ln1_bias,
        grad_w_qkv,
        grad_w_out,
        grad_b_out,
        grad_ln2_gain,
        grad_ln2_bias,
        grad_w_up,
        grad_b_up,
        grad_w_down,
        grad_b_down,
    ) = lax.psum(
        (
            grad_ln1_gain,
            grad_ln1_bias,
            grad_w_qkv,
            grad_w_out,
            grad_b_out,
            grad_ln2_gain,
            grad_ln2_bias,
            grad_w_up,
            grad_b_up,
            grad_w_down,
            grad_b_down,
        ),
        "dp",
    )
    return (
        output,
        grad_tokens,
        grad_ln1_gain,
        grad_ln1_bias,
        grad_w_qkv,
        grad_w_out,
        grad_b_out,
        grad_ln2_gain,
        grad_ln2_bias,
        grad_w_up,
        grad_b_up,
        grad_w_down,
        grad_b_down,
    )


def solution(mesh):
    return jax.shard_map(
        per_device,
        mesh=mesh,
        in_specs=(
            P("dp", None),
            P(),
            P(),
            P(None, None, "mp"),
            P("mp", None),
            P(),
            P(),
            P(),
            P(None, "mp"),
            P("mp"),
            P("mp", None),
            P(),
            P("dp", None),
        ),
        out_specs=(
            P("dp", None),
            P("dp", None),
            P(),
            P(),
            P(None, None, "mp"),
            P("mp", None),
            P(),
            P(),
            P(),
            P(None, "mp"),
            P("mp"),
            P("mp", None),
            P(),
        ),
        check_vma=False,
    )
```

profile of v0, /device:TPU:0, one launch (start us, length us, event | category | flops | bytes accessed | tf_op | source)
XLA Modules:
  0.0 554.7 jit_solution(17324848607552887038)
XLA Ops:
  7.4 1.5 convert_reduce_fusion
  8.9 1.7 fusion.17
  10.7 0.8 fusion.25
  12.4 27.8 %all_gather.7 = bf16[64,2,64]{2,0,1:T(8,128)(2,1)S(1)} all-gather(bf16[8,2,64]{2,0,1:T(8,128)(2,1)S(1)} %fusion.89), channel_id=1, replica_groups=mesh['dp'=8,'mp'=4] {'dp'}, dimensions={0}, use_global_device_ids=true | all-gather | bytes 18432 | tf_op jit(solution)/shard_map/all_gather | solution.py:62
  41.1 26.0 %all_gather.6 = bf16[64,2,64]{2,0,1:T(8,128)(2,1)S(1)} all-gather(bf16[8,2,64]{2,0,1:T(8,128)(2,1)S(1)} %fusion.88), channel_id=1, replica_groups=mesh['dp'=8,'mp'=4] {'dp'}, dimensions={0}, use_global_device_ids=true | all-gather | bytes 18432 | tf_op jit(solution)/shard_map/all_gather | solution.py:61
  67.3 0.4 copy.37
  69.8 1.8 fusion.58
  71.6 49.4 %all-reduce.8.cloned.1.call-done = f32[1024,512]{1,0:T(8,128)} async-done(((f32[1024,512]{1,0:T(8,128)}), f32[1024,512]{1,0:T(8,128)}) %all-reduce.8.cloned.1.call-update) | async-done | bytes 2097168 | tf_op jit(solution)/shard_map/psum | solution.py:94
  121.0 2.2 fusion.104
  123.3 0.4 multiply_reduce_fusion.2
  123.7 0.6 copy-done.41
  124.3 0.6 copy-done.35
  125.3 0.7 fusion.109
  126.0 0.9 copy-done.8
  126.9 3.6 convert_reduce_fusion.2
  130.6 1.0 copy-done.24
  131.6 2.1 fusion.111
  133.9 3.2 fusion.110
  137.1 48.1 %all-reduce.10.cloned.1.call-done = f32[1024,512]{1,0:T(8,128)} async-done(((f32[1024,512]{1,0:T(8,128)}), f32[1024,512]{1,0:T(8,128)}) %all-reduce.10.cloned.1.call-update) | async-done | bytes 2097168 | tf_op jit(solution)/shard_map/psum | solution.py:110
  185.3 3.1 multiply_reduce_fusion
  188.5 0.8 fusion.103
  189.3 1.3 copy-done.4
  190.7 1.2 convolution_convert_fusion.1
  191.9 1.8 copy.44
  193.7 1.0 copy.82
  194.7 1.6 fusion.73
  196.3 1.3 fusion.60
  197.7 1.1 fusion.39
  198.8 0.6 copy-done.31
  199.5 3.1 fusion.23
  202.6 1.1 fusion.50
  203.9 1.4 fusion.38
  205.3 1.1 copy.75
  206.4 1.3 reshape.167
  207.8 0.7 constant_dynamic-update-slice_fusion.2
  208.6 44.8 %reduce-scatter.5.cloned.1.call-done = f32[8,2,64]{2,0,1:T(8,128)} async-done(((f32[64,2,64]{2,0,1:T(8,128)}), f32[8,2,64]{2,0,1:T(8,128)}) %reduce-scatter.5.cloned.1.call-update) | async-done | bytes 4112 | tf_op jit(solution)/shard_map/reduce_scatter | solution.py:153
  253.3 0.7 broadcast_multiply_fusion
  254.0 1.5 fusion.32
  255.5 1.1 copy.77
  256.6 1.3 reshape.169
  258.0 51.7 %reduce-scatter.3.cloned.1.call-done = f32[8,2,64]{2,0,1:T(8,128)} async-done(((f32[64,2,64]{2,0,1:T(8,128)}), f32[8,2,64]{2,0,1:T(8,128)}) %reduce-scatter.3.cloned.1.call-update) | async-done | bytes 4112 | tf_op jit(solution)/shard_map/reduce_scatter | solution.py:152
  309.6 0.7 broadcast_multiply_fusion.1
  310.3 2.2 fusion.31
  312.6 1.3 copy.76
  313.8 1.0 reshape.168
  314.8 1.7 constant_dynamic-update-slice_fusion.1
  316.5 0.7 constant_dynamic-update-slice_fusion
  317.2 3.3 convolution_bitcast_fusion
  320.6 3.4 fusion.112
  324.0 1.7 fusion.113
  325.7 0.7 copy-done.5
  326.4 1.2 fusion.46
  327.9 1.8 convolution_bitcast_fusion.1
  329.7 75.7 %all-reduce.14.cloned.1.call-done = (f32[1024,512]{1,0:T(8,128)}, f32[1024,512]{1,0:T(8,128)}) async-done(((f32[1024,512]{1,0:T(8,128)}, f32[1024,512]{1,0:T(8,128)}), (f32[1024,512]{1,0:T(8,128)}, f32[1024,512]{1,0:T(8,128)})) %all-reduce.14.cloned.1.call-update) | async-done | bytes 4194320 | tf_op jit(solution)/shard_map/psum | solution.py:101
  405.4 2.7 fusion.101
  408.3 1.2 fusion.9
  410.0 2.1 convert_reduce_fusion.1
  412.1 39.9 %all-reduce = (f32[512]{0:T(512)}, f32[512]{0:T(512)}, f32[512]{0:T(512)}, f32[512]{0:T(512)}, f32[512]{0:T(512)}, /*index=5*/f32[512]{0:T(512)}, f32[512]{0:T(512)}) all-reduce(f32[512]{0:T(512)S(1)} %get-tuple-element.41, f32[512]{0:T(512)S(1)} %get-tuple-element.44, ...), channel_id=1, replica_groups=mesh['dp'=8,'mp'=4] {'dp'}, use_global_device_ids=true, to_apply=%region_21.22 | all-reduce | flops 3584 | bytes 28672 | tf_op jit(solution)/shard_map/psum | solution.py:182
  452.0 3.1 add_convert_fusion.1
  455.1 86.7 %all-reduce.12.cloned.1.call-done = (f32[3,512,128]{1,2,0:T(8,128)}, f32[128,512]{1,0:T(8,128)}, f32[512,512]{1,0:T(8,128)}, f32[512,512]{1,0:T(8,128)}) async-done(((f32[3,512,128]{1,2,0:T(8,128)}, f32[128,512]{1,0:T(8,128)}, f32[512,512]{1,0:T(8,128)}, f32[512,512]{1,0:T(8,128)}), (f32[3,512,128]{1,2,0:T(8,128)}, f32[128,512]{1,0:T(8,128)}, f32[512,512]{1,0:T(8,128)}, ...) | async-done | bytes 3145744 | tf_op jit(solution)/shard_map/psum | solution.py:182
  541.8 2.4 copy.59
  544.2 1.7 copy.111
  545.9 1.0 copy.112
  546.8 1.0 copy.113
  (155 shorter events, 6.3 us)
Async XLA Ops:
  7.2 118.8 %copy-start = (bf16[512,512]{1,0:T(8,128)(2,1)S(1)}, bf16[512,512]{1,0:T(8,128)(2,1)}, u32[]{:S(2)}) copy-start(bf16[512,512]{1,0:T(8,128)(2,1)} %param.23) | copy-start | bytes 1572868
  7.2 3.4 copy-start.1
  7.2 3.4 copy-start.47
  7.2 3.4 copy-start.29
  7.2 3.4 copy-start.56
  7.2 113.8 %all-reduce.8.cloned.1.call-start = ((), (), s32[]{:S(2)}) async-start(), calls=%async_computation.2 | async-start | bytes 4194304 | tf_op jit(solution)/shard_map/psum | solution.py:94
  10.6 0.8 copy-start.39
  10.7 0.8 copy-start.37
  40.2 29.0 %copy-start.34 = (bf16[64,2,64]{2,0,1:T(8,128)(2,1)}, bf16[64,2,64]{2,0,1:T(8,128)(2,1)S(1)}, u32[]{:S(2)}) copy-start(bf16[64,2,64]{2,0,1:T(8,128)(2,1)S(1)} %all_gather.7) | copy-start | bytes 49156
  67.1 1.6 copy-start.32
  68.2 1.0 copy-start.12
  68.4 0.8 copy-start.18
  68.7 0.9 copy-start.43
  68.7 1.1 copy-start.28
  68.9 2.6 copy-start.15
  69.7 1.8 copy-start.16
  69.8 51.3 %copy-start.51 = (f32[512]{0:T(512)S(1)}, f32[512]{0:T(512)}, u32[]{:S(2)}) copy-start(f32[512]{0:T(512)} %param.18) | copy-start | bytes 6148
  71.6 113.7 %all-reduce.10.cloned.1.call-start = ((), (), s32[]{:S(2)}) async-start(), calls=%async_computation.3 | async-start | bytes 4194304 | tf_op jit(solution)/shard_map/psum | solution.py:110
  123.2 1.7 copy-start.45
  123.2 1.6 copy-start.52
  123.7 0.6 copy-start.41
  124.3 1.0 copy-start.21
  124.3 0.6 copy-start.35
  125.3 5.3 copy-start.14
  125.3 1.6 copy-start.8
  125.3 1.6 copy-start.55
  130.6 1.0 copy-start.24
  133.6 119.7 %reduce-scatter.5.cloned.1.call-start = ((), (), s32[]{:S(2)}) async-start(), calls=%async_computation.5 | async-start | bytes 73728 | tf_op jit(solution)/shard_map/reduce_scatter | solution.py:153
  185.3 3.2 copy-start.42
  185.3 3.2 copy-start.13
  185.3 3.2 copy-start.36
  185.3 3.2 copy-start.46
  188.4 2.2 copy-start.9
  189.3 1.4 copy-start.4
  191.9 7.6 %copy-start.44 = (f32[2,8,128]{2,1,0:T(8,128)S(1)}, f32[2,8,128]{2,1,0:T(8,128)}, u32[]{:S(2)}) copy-start(f32[2,8,128]{2,1,0:T(8,128)} %copy-done.43) | copy-start | bytes 24580
  194.7 3.0 copy-start.19
  198.8 0.6 copy-start.31
  199.4 4.5 copy-start.33
  199.4 110.2 %reduce-scatter.3.cloned.1.call-start = ((), (), s32[]{:S(2)}) async-start(), calls=%async_computation.4 | async-start | bytes 73728 | tf_op jit(solution)/shard_map/reduce_scatter | solution.py:152
  202.6 1.1 copy-start.27
  203.7 50.3 %copy-start.20 = (bf16[16,8,8,128]{3,2,1,0:T(8,128)(2,1)S(1)}, bf16[16,8,8,128]{3,2,1,0:T(8,128)(2,1)}, u32[]{:S(2)}) copy-start(bf16[16,8,8,128]{3,2,1,0:T(8,128)(2,1)} %copy-done.19) | copy-start | bytes 786436
  203.9 4.6 copy-start.30
  208.5 196.9 %all-reduce.14.cloned.1.call-start = ((), (), s32[]{:S(2)}) async-start(), calls=%async_computation.7 | async-start | bytes 8388608 | tf_op jit(solution)/shard_map/psum | solution.py:101
  320.5 221.2 %all-reduce.12.cloned.1.call-start = ((), (), s32[]{:S(2)}) async-start(), calls=%async_computation.6 | async-start | bytes 6291456 | tf_op jit(solution)/shard_map/psum | solution.py:182
  320.6 3.4 copy-start.10
  320.6 3.4 copy-start.23
  324.0 2.4 copy-start.5
  324.0 2.4 copy-start.17
  326.4 1.2 copy-start.2
  326.4 1.5 copy-start.22
  326.4 1.5 copy-start.38
  326.4 1.5 copy-start.48
  326.4 1.5 copy-start.57
  329.7 78.4 %copy-start.40 = (f32[1024]{0:T(1024)S(1)}, f32[1024]{0:T(1024)}, u32[]{:S(2)}) copy-start(f32[1024]{0:T(1024)} %copy-done.39) | copy-start | bytes 12292
  405.4 2.7 copy-start.3
  405.4 2.9 copy-start.7
  408.1 1.6 copy-start.6
  408.1 1.9 copy-start.11
  410.0 2.1 copy-start.49
  410.0 2.1 copy-start.50
  410.0 2.1 copy-start.54
  410.0 42.0 %copy-start.53 = (f32[512]{0:T(512)S(1)}, f32[512]{0:T(512)}, u32[]{:S(2)}) copy-start(f32[512]{0:T(512)} %param.24) | copy-start | bytes 6148
  541.8 4.1 copy-start.26
  541.8 5.1 copy-start.25
Sparse Core Ops, SparseCore 0:
  71.7 49.2 all-reduce.7
  133.8 51.4 all-reduce.9
  199.6 53.7 reduce-scatter.4
  256.9 52.7 reduce-scatter.2
  320.7 84.7 all-reduce.13
  410.8 130.9 all-reduce.11
where the time goes:
time: 556 us; the launch traced here: 555 us
  waiting for transfers between devices  356 us (64%)
  blocking collectives  93.7 us (17%)
  matrix products  36.3 us (7%)
  local copies, waits for them, and re-layouts  28.1 us (5%)
  other arithmetic  24.8 us (4%)
  between operations  14.9 us (3%)
    psum x1, waiting for transfers between devices, per_device(): lax.psum((grad_ln1_gain, grad_ln1_bias, grad_w_qkv, grad_w_out, grad_b_ou...  86.7 us
    psum x1, waiting for transfers between devices, per_device(): feedforward = lax.psum(feedforward_terms, 'mp')  75.7 us
    reduce_scatter x1, waiting for transfers between devices, per_device(): lax.psum_scatter(placed_keys, 'dp', scatter_dimension=0, tiled=True)  51.7 us
    psum x1, waiting for transfers between devices, per_device(): mid = inputs + lax.psum(attention_terms, 'mp') + b_out  49.4 us
    psum x1, waiting for transfers between devices, per_device(): lax.psum(jnp.einsum('tf,df->td', grad_upper, w_up, preferred_element_type...  48.1 us
    reduce_scatter x1, waiting for transfers between devices, per_device(): lax.psum_scatter(placed_values, 'dp', scatter_dimension=0, tiled=True)  44.8 us
    psum x1, blocking collectives, per_device(): lax.psum((grad_ln1_gain, grad_ln1_bias, grad_w_qkv, grad_w_out, grad_b_ou...  39.9 us
    all_gather x1, blocking collectives, per_device(): lax.all_gather(value_summary, 'dp', axis=0, tiled=True)  27.8 us
  transfers between devices with their start and end apart: 6, of which 6 were waited for; matrix products, arithmetic and copies ran while one was open for 6% of the time, Pallas kernels for 0%

commit v1 on v0

v1 whole, which is shorter than its diff:
```python
import math

import jax
import jax.numpy as jnp
from jax import lax
from jax.sharding import PartitionSpec as P

HEAD_DIM = 64
SPAN = 128
LENGTH = 4096
EPSILON = 1e-05

f32 = jnp.float32
bf16 = jnp.bfloat16


def layer_norm(values, gain, offset):
    center = values - jnp.mean(values, axis=-1, keepdims=True)
    spread = jnp.mean(center * center, axis=-1, keepdims=True)
    return center * lax.rsqrt(spread + EPSILON) * gain + offset


def masks_of(count):
    return [1 << i for i in range(count.bit_length() - 1)]


def build(n_dp, n_mp):
    def swap(x, axis, mask):
        n = n_dp if axis == "dp" else n_mp
        return lax.ppermute(x, axis, [(i, i ^ mask) for i in range(n)])

    def gather_slots(x, axis, masks):
        slots = {0: x}
        for m in masks:
            slots.update({j ^ m: swap(s, axis, m) for j, s in list(slots.items())})
        return slots

    def pick(x, index, rows):
        return lax.dynamic_slice_in_dim(x, index * rows, rows, 0)

    def join(own, other, bit):
        return jnp.where(
            bit == 0, jnp.concatenate([own, other]), jnp.concatenate([other, own])
        )

    core_masks = masks_of(n_mp)[:1]
    far_masks = masks_of(n_mp)[1:]
    dp_masks = masks_of(n_dp)

    def reduce_half(x):
        c = lax.axis_index("mp") & 1
        half = x.shape[0] // 2
        got = swap(pick(x, 1 - c, half).astype(bf16), "mp", 1)
        x = pick(x, c, half) + got.astype(f32)
        for m in far_masks:
            low = x.astype(bf16)
            x = low.astype(f32) + swap(low, "mp", m).astype(f32)
        return x

    def both_halves(x):
        c = lax.axis_index("mp") & 1
        return join(x, swap(x, "mp", 1), c)

    def reduce_dp(x, masks):
        d = lax.axis_index("dp")
        for m in masks:
            bit = jnp.where((d & m) == 0, 0, 1)
            half = x.shape[0] // 2
            got = swap(pick(x, 1 - bit, half), "dp", m)
            x = (pick(x, bit, half).astype(f32) + got.astype(f32)).astype(bf16)
        for m in reversed(masks):
            bit = jnp.where((d & m) == 0, 0, 1)
            x = join(x, swap(x, "dp", m), bit)
        return x.astype(f32)

    def per_device(
        tokens,
        ln1_gain,
        ln1_bias,
        w_qkv,
        w_out,
        b_out,
        ln2_gain,
        ln2_bias,
        w_up,
        b_up,
        w_down,
        b_down,
        cotangent,
    ):
        inputs = tokens.astype(f32)
        rows = inputs.shape[0]
        width = w_qkv.shape[2]
        heads = width // HEAD_DIM
        blocks = rows // SPAN
        scale = HEAD_DIM ** (-0.5)
        group = LENGTH // rows
        seq_masks = masks_of(group)
        place = lax.axis_index("dp") % group
        core = lax.axis_index("mp") & 1

        def heads_first(array):
            return array.reshape(blocks, SPAN, heads, HEAD_DIM).transpose(2, 0, 1, 3)

        def heads_last(array):
            return array.transpose(1, 2, 0, 3).reshape(rows, width)

        out_slots = gather_slots(w_out, "mp", far_masks + core_masks)

        first_full, first_pull = jax.vjp(layer_norm, inputs, ln1_gain, ln1_bias)
        first = first_full.astype(bf16)
        projected = jnp.einsum("td,sde->ste", first, w_qkv, preferred_element_type=f32).astype(bf16)
        query_heads = heads_first(projected[0])
        key_heads = heads_first(projected[1])
        value_heads = heads_first(projected[2])
        own_summary = jnp.mean(
            jnp.stack([key_heads, value_heads]).astype(f32), axis=3
        ).astype(bf16)
        summary = own_summary[None]
        for m in seq_masks:
            summary = jnp.concatenate([summary, swap(summary, "dp", m)])
        all_keys = summary[:, 0].transpose(1, 0, 2, 3).reshape(heads, group * blocks, HEAD_DIM)
        all_values = summary[:, 1].transpose(1, 0, 2, 3).reshape(heads, group * blocks, HEAD_DIM)
        slot_place = place ^ jnp.arange(group)
        summary_block = (slot_place[:, None] * blocks + jnp.arange(blocks)[None, :]).reshape(-1)
        query_block = place * blocks + jnp.arange(blocks)
        allowed = summary_block[None, :] < query_block[:, None]
        causal = jnp.arange(SPAN)[:, None] >= jnp.arange(SPAN)[None, :]
        local = (
            jnp.einsum("hbqd,hbkd->hbqk", query_heads, key_heads, preferred_element_type=f32)
            * scale
        )
        local = jnp.where(causal[None, None], local, -1e30)
        remote = jnp.einsum(
            "hbqd,hgd->hbqg", query_heads, all_keys, preferred_element_type=f32
        ) * scale + math.log(SPAN)
        remote = jnp.where(allowed[None, :, None, :], remote, -1e30)
        scores = jnp.concatenate([local, remote], axis=-1)
        highest = jnp.max(scores, axis=-1, keepdims=True)
        weights = jnp.exp(scores - highest)
        probs = weights / jnp.sum(weights, axis=-1, keepdims=True)
        probs_low = probs.astype(bf16)
        attended = jnp.einsum(
            "hbqk,hbkd->hbqd", probs_low[..., :SPAN], value_heads, preferred_element_type=f32
        )
        attended = attended + jnp.einsum(
            "hbqg,hgd->hbqd", probs_low[..., SPAN:], all_values, preferred_element_type=f32
        )
        attended = heads_last(attended.astype(bf16))
        att_slots = gather_slots(attended, "mp", far_masks + core_masks)
        me = lax.axis_index("mp")
        terms = jnp.stack(
            [jnp.dot(att_slots[j], out_slots[j], preferred_element_type=f32) for j in range(n_mp)]
        )
        mid = inputs + b_out
        for i in range(n_mp):
            mid = mid + lax.dynamic_index_in_dim(terms, me ^ i, 0, keepdims=False)
        second_full, second_pull = jax.vjp(layer_norm, mid, ln2_gain, ln2_bias)
        second = second_full.astype(bf16)
        upper = jnp.dot(second, w_up, preferred_element_type=f32) + b_up
        active_full, gelu_pull = jax.vjp(jax.nn.gelu, upper)
        active = active_full.astype(bf16)
        grad_active = jnp.einsum("td,fd->tf", cotangent, w_down, preferred_element_type=f32)
        grad_upper = gelu_pull(grad_active)[0].astype(bf16)
        grad_second = both_halves(
            reduce_half(
                jnp.einsum("tf,df->td", grad_upper, w_up, preferred_element_type=f32)
            ).astype(bf16)
        ).astype(f32)

        feedforward = reduce_half(jnp.dot(active, w_down, preferred_element_type=f32))
        output = both_halves((pick(mid, core, rows // 2) + feedforward + b_down).astype(bf16))

        grad_out = cotangent.astype(f32)
        grad_w_down = jnp.einsum("tf,td->fd", active, cotangent, preferred_element_type=f32)
        grad_b_down = jnp.sum(grad_out, axis=0)
        grad_w_up = jnp.einsum("td,tf->df", second, grad_upper, preferred_element_type=f32)
        grad_b_up = jnp.sum(grad_upper.astype(f32), axis=0)

        grad_mid_norm, grad_ln2_gain, grad_ln2_bias = second_pull(grad_second)
        grad_mid = grad_out + grad_mid_norm
        grad_attention = grad_mid.astype(bf16)
        grad_w_out = jnp.einsum("tc,td->cd", attended, grad_attention, preferred_element_type=f32)
        grad_b_out = jnp.sum(grad_mid, axis=0)
        grad_attended = heads_first(
            jnp.einsum("td,cd->tc", grad_attention, w_out, preferred_element_type=f32).astype(bf16)
        )
        grad_probs = jnp.concatenate(
            [
                jnp.einsum(
                    "hbqd,hbkd->hbqk", grad_attended, value_heads, preferred_element_type=f32
                ),
                jnp.einsum("hbqd,hgd->hbqg", grad_attended, all_values, preferred_element_type=f32),
            ],
            axis=-1,
        )
        centered = jnp.sum(probs * grad_probs, axis=-1, keepdims=True)
        grad_scores = (probs * (grad_probs - centered)).astype(bf16)
        grad_local = grad_scores[..., :SPAN]
        grad_remote = grad_scores[..., SPAN:]
        grad_query = (
            jnp.einsum("hbqk,hbkd->hbqd", grad_local, key_heads, preferred_element_type=f32)
            + jnp.einsum("hbqg,hgd->hbqd", grad_remote, all_keys, preferred_element_type=f32)
        ) * scale
        grad_keys = (
            jnp.einsum("hbqk,hbqd->hbkd", grad_local, query_heads, preferred_element_type=f32)
            * scale
        )
        grad_values = jnp.einsum(
            "hbqk,hbqd->hbkd", probs_low[..., :SPAN], grad_attended, preferred_element_type=f32
        )
        grad_key_summary = (
            jnp.einsum("hbqg,hbqd->hgd", grad_remote, query_heads, preferred_element_type=f32)
            * scale
        )
        grad_value_summary = jnp.einsum(
            "hbqg,hbqd->hgd", probs_low[..., SPAN:], grad_attended, preferred_element_type=f32
        )
        partial = (
            jnp.stack([grad_key_summary, grad_value_summary])
            .reshape(2, heads, group, blocks, HEAD_DIM)
            .transpose(2, 0, 1, 3, 4)
        )
        for m in reversed(seq_masks):
            partial = partial[:m] + swap(partial[m:], "dp", m)
        own = partial[0] / SPAN
        grad_keys = grad_keys + own[0][:, :, None, :]
        grad_values = grad_values + own[1][:, :, None, :]
        grad_qkv = jnp.stack(
            [
                heads_last(grad_query.astype(bf16)),
                heads_last(grad_keys.astype(bf16)),
                heads_last(grad_values.astype(bf16)),
            ]
        )
        grad_w_qkv = jnp.einsum("td,ste->sde", first, grad_qkv, preferred_element_type=f32)
        grad_first_part = jnp.einsum("ste,sde->td", grad_qkv, w_qkv, preferred_element_type=f32)
        ln1_part = first_pull(grad_first_part)[1:]
        grad_first = reduce_half(grad_first_part)

        def pull_rows(x, g):
            return jax.vjp(layer_norm, x, ln1_gain, ln1_bias)[1](g)[0]

        grad_in_norm = pull_rows(pick(inputs, core, rows // 2), grad_first)
        grad_tokens = both_halves((pick(grad_mid, core, rows // 2) + grad_in_norm).astype(bf16))

        share = jnp.stack(ln1_part)
        for m in core_masks + far_masks:
            share = share + swap(share, "mp", m)
        vectors = jnp.concatenate(
            [
                jnp.stack([grad_b_out, grad_ln2_gain, grad_ln2_bias, grad_b_down]),
                jnp.pad(grad_b_up, (0, grad_b_down.shape[0] - grad_b_up.shape[0]))[None],
                share,
                jnp.zeros_like(grad_b_down)[None],
            ]
        )
        for m in dp_masks:
            vectors = vectors + swap(vectors, "dp", m)
        feed = reduce_dp(
            jnp.concatenate([grad_w_down.reshape(-1, 512), grad_w_up.reshape(-1, 512)]).astype(bf16), dp_masks
        )
        size = grad_w_down.size // 512
        grad_w_down = feed[:size].reshape(grad_w_down.shape)
        grad_w_up = feed[size:].reshape(grad_w_up.shape)
        rest = reduce_dp(
            jnp.concatenate([grad_w_qkv.reshape(-1, width), grad_w_out.reshape(-1, width)]).astype(bf16),
            dp_masks,
        )
        size = grad_w_qkv.size // width
        return (
            output,
            grad_tokens,
            vectors[5],
            vectors[6],
            rest[:size].reshape(grad_w_qkv.shape),
            rest[size:].reshape(grad_w_out.shape),
            vectors[0],
            vectors[1],
            vectors[2],
            grad_w_up,
            vectors[4, : grad_b_up.shape[0]],
            grad_w_down,
            vectors[3],
        )

    return per_device


def solution(mesh):
    return jax.shard_map(
        build(mesh.shape["dp"], mesh.shape["mp"]),
        mesh=mesh,
        in_specs=(
            P("dp", None),
            P(),
            P(),
            P(None, None, "mp"),
            P("mp", None),
            P(),
            P(),
            P(),
            P(None, "mp"),
            P("mp"),
            P("mp", None),
            P(),
            P("dp", None),
        ),
        out_specs=(
            P("dp", None),
            P("dp", None),
            P(),
            P(),
            P(None, None, "mp"),
            P("mp", None),
            P(),
            P(),
            P(),
            P(None, "mp"),
            P("mp"),
            P("mp", None),
            P(),
        ),
        check_vma=False,
    )
```

time: 556 us -> 171 us (0.31)
  waiting for transfers between devices: 356 us -> 46 us
  blocking collectives: 93.7 us -> 0 us
  starting transfers between devices: 0.43 us -> 36.9 us
  between operations: 14.9 us -> 1.76 us
  matrix products: 36.3 us -> 25.4 us
  other arithmetic: 24.8 us -> 32 us
    psum x4 -> x0, waiting for transfers between devices: 260 us -> none  [the longest x1 86.7 us: per_device(): lax.psum((grad_ln1_gain, grad_ln1_bias, grad_w_qkv, grad_w_out, grad_b_ou...]
    reduce_scatter x2 -> x0, waiting for transfers between devices: 96.5 us -> none  [the longest x1 51.7 us: per_device(): lax.psum_scatter(placed_keys, 'dp', scatter_dimension=0, tiled=True)]
    all_gather x2 -> x0, blocking collectives: 53.8 us -> none  [the longest x1 27.8 us: per_device(): lax.all_gather(value_summary, 'dp', axis=0, tiled=True)]
    ppermute x0 -> x36, waiting for transfers between devices: none -> 46 us  [swap(): return lax.ppermute(x, axis, [(i, i ^ mask) for i in range(n)])]
    psum x1 -> x0, blocking collectives: 39.9 us -> none  [per_device(): lax.psum((grad_ln1_gain, grad_ln1_bias, grad_w_qkv, grad_w_out, grad_b_ou...]
    ppermute x0 -> x36, starting transfers between devices: none -> 36.9 us  [swap(): return lax.ppermute(x, axis, [(i, i ^ mask) for i in range(n)])]
    unnamed x123 -> x100, local copies, waits for them, and re-layouts: 16.4 us -> 9.04 us
  transfers between devices with their start and end apart: 6 -> 36, of which waited for: 6 -> 18; matrix products, arithmetic and copies ran while one was open for 6% -> 37% of each run, Pallas kernels for 0% -> 0%
where the time goes in v1:
time: 171 us; the launch traced here: 170 us
  waiting for transfers between devices  46 us (27%)
  starting transfers between devices  36.9 us (22%)
  other arithmetic  32 us (19%)
  local copies, waits for them, and re-layouts  27.9 us (16%)
  matrix products  25.4 us (15%)
  between operations  1.76 us (1%)
    ppermute x36, waiting for transfers between devices, swap(): return lax.ppermute(x, axis, [(i, i ^ mask) for i in range(n)])  46 us
    ppermute x36, starting transfers between devices, swap(): return lax.ppermute(x, axis, [(i, i ^ mask) for i in range(n)])  36.9 us
    unnamed x100, local copies, waits for them, and re-layouts  9.04 us
    another operation x7, local copies, waits for them, and re-layouts, per_device(): jnp.stack([heads_last(grad_query.astype(bf16)), heads_last(grad_keys.asty...  6.88 us
    select_n x6, other arithmetic, join(): jnp.where(bit == 0, jnp.concatenate([own, other]), jnp.concatenate([other...  5.08 us
    reduce_sum x4, other arithmetic, layer_norm(): center = values - jnp.mean(values, axis=-1, keepdims=True)  4.04 us
    dot_general x1, matrix products, per_device(): jnp.einsum('ste,sde->td', grad_qkv, w_qkv, preferred_element_type=f32)  3.85 us
    dot_general x4, matrix products, per_device(): jnp.dot(att_slots[j], out_slots[j], preferred_element_type=f32)  3.62 us
  transfers between devices with their start and end apart: 36, of which 18 were waited for; matrix products, arithmetic and copies ran while one was open for 37% of the time, Pallas kernels for 0%

profile of v1, /device:TPU:0, one launch (start us, length us, event | category | flops | bytes accessed | tf_op | source)
XLA Modules:
  0.0 170.0 jit_solution(11490271613072114584)
XLA Ops:
  0.7 1.6 convert_reduce_fusion.3
  2.3 1.7 multiply_reduce_fusion.2
  7.1 3.0 %collective-permute-start = (bf16[1,2,2,8,64]{4,3,0,2,1:T(8,128)(2,1)S(1)}, bf16[1,2,2,8,64]{4,3,0,2,1:T(8,128)(2,1)S(1)}, u32[]{:S(2)}, u32[]{:S(2)}) collective-permute-start(bf16[1,2,2,8,64]{4,3,0,2,1:T(8,128)(2,1)S(1)} %fusion.76), channel_id=1, source_target_pairs={{0,4},{4,0},{8,12},{12,8},{16,20},{20,16},{24,28},{28,24},{1,5},{5... | collective-permute-start | bytes 12296 | tf_op jit(solution)/shard_map/ppermute | solution.py:30
  11.8 2.2 %collective-permute-start.1 = (bf16[2,2,2,8,64]{4,3,0,2,1:T(8,128)(2,1)S(1)}, bf16[2,2,2,8,64]{4,3,0,2,1:T(8,128)(2,1)S(1)}, u32[]{:S(2)}, u32[]{:S(2)}) collective-permute-start(bf16[2,2,2,8,64]{4,3,0,2,1:T(8,128)(2,1)S(1)} %pad_maximum_fusion.5), channel_id=1, source_target_pairs={{0,8},{4,12},{8,0},{12,4},{16,24},{20,28},{24,16},{28,20},{1,9},{5... | collective-permute-start | bytes 24584 | tf_op jit(solution)/shard_map/ppermute | solution.py:30
  14.0 1.6 collective-permute-done.1
  17.4 2.0 %collective-permute-start.4 = (bf16[1024,128]{0,1:T(8,128)(2,1)S(1)}, bf16[1024,128]{0,1:T(8,128)(2,1)S(1)}, u32[]{:S(2)}, u32[]{:S(2)}) collective-permute-start(bf16[1024,128]{0,1:T(8,128)(2,1)S(1)} %bitcast.196), channel_id=1, source_target_pairs={{0,2},{1,3},{2,0},{3,1},{4,6},{5,7},{6,4},{7,5},{8,10},{9,11},{10,... | collective-permute-start | bytes 786440 | tf_op jit(solution)/shard_map/ppermute | solution.py:30
  19.6 1.7 convert_element_type.196
  21.2 1.4 dynamic-slice_reduce_fusion
  23.6 3.0 %collective-permute-done.5 = bf16[128,512]{1,0:T(8,128)(2,1)} collective-permute-done((bf16[128,512]{1,0:T(8,128)(2,1)S(1)}, bf16[128,512]{1,0:T(8,128)(2,1)}, u32[]{:S(2)}, u32[]{:S(2)}) %collective-permute-start.5) | collective-permute-done | bytes 131104 | tf_op jit(solution)/shard_map/ppermute | solution.py:30
  27.1 1.4 convolution_bitcast_fusion.2
  28.5 1.4 convolution_bitcast_fusion.3
  30.3 1.1 pad_maximum_fusion
  34.4 1.1 convolution_convert_fusion.2
  35.5 2.6 %convert_reduce_fusion.2 = (f32[512]{0:T(512)}, bf16[1024,512]{1,0:T(8,128)(2,1)S(1)}) fusion(f32[1024,512]{1,0:T(8,128)S(1)} %fusion.83, f32[512]{0:T(512)S(1)} %copy-done.45, bf16[1024,512]{1,0:T(8,128)(2,1)S(1)} %copy-done.20, bf16[512,512]{1,0:T(8,128)(2,1)S(1)} %copy-done), kind=kOutput, calls=%fused_computation.26 | convolution fusion | flops 548929024 | bytes 4722688 | tf_op jit(solution)/shard_map/td,fd->tf/dot_general | solution.py:163
  38.1 1.1 convolution_convert_fusion.1
  40.0 1.6 collective-permute-start.30
  43.1 10.8 %collective-permute-done.30 = bf16[512,512]{1,0:T(8,128)(2,1)S(1)} collective-permute-done((bf16[512,512]{1,0:T(8,128)(2,1)S(1)}, bf16[512,512]{1,0:T(8,128)(2,1)S(1)}, u32[]{:S(2)}, u32[]{:S(2)}) %collective-permute-start.30) | collective-permute-done | bytes 524320 | tf_op jit(solution)/shard_map/ppermute | solution.py:30
  54.8 1.6 collective-permute-start.31
  56.7 1.6 collective-permute-start.12
  59.4 2.9 %collective-permute-done.31 = bf16[256,512]{1,0:T(8,128)(2,1)S(1)} collective-permute-done((bf16[256,512]{1,0:T(8,128)(2,1)S(1)}, bf16[256,512]{1,0:T(8,128)(2,1)S(1)}, u32[]{:S(2)}, u32[]{:S(2)}) %collective-permute-start.31) | collective-permute-done | bytes 262176 | tf_op jit(solution)/shard_map/ppermute | solution.py:30
  62.4 2.6 %collective-permute-start.32 = (bf16[128,512]{1,0:T(8,128)(2,1)S(1)}, bf16[128,512]{1,0:T(8,128)(2,1)S(1)}, u32[]{:S(2)}, u32[]{:S(2)}) collective-permute-start(bf16[128,512]{1,0:T(8,128)(2,1)S(1)} %constant_dynamic-slice_fusion), channel_id=1, source_target_pairs={{0,16},{4,20},{8,24},{12,28},{16,0},{20,4},{24,8},{28,12},{1,17},{... | collective-permute-start | bytes 393224 | tf_op jit(solution)/shard_map/ppermute | solution.py:30
  65.0 4.4 %collective-permute-done.12 = bf16[512,512]{1,0:T(8,128)(2,1)S(1)} collective-permute-done((bf16[512,512]{1,0:T(8,128)(2,1)S(1)}, bf16[512,512]{1,0:T(8,128)(2,1)S(1)}, u32[]{:S(2)}, u32[]{:S(2)}) %collective-permute-start.12) | collective-permute-done | bytes 524320 | tf_op jit(solution)/shard_map/ppermute | solution.py:30
  69.8 2.6 %collective-permute-start.33 = (bf16[128,512]{1,0:T(8,128)(2,1)S(1)}, bf16[128,512]{1,0:T(8,128)(2,1)S(1)}, u32[]{:S(2)}, u32[]{:S(2)}) collective-permute-start(bf16[128,512]{1,0:T(8,128)(2,1)S(1)} %add_convert_fusion.13), channel_id=1, source_target_pairs={{0,16},{4,20},{8,24},{12,28},{16,0},{20,4},{24,8},{28,12},{1,17},{... | collective-permute-start | bytes 393224 | tf_op jit(solution)/shard_map/ppermute | solution.py:30
  73.4 1.5 collective-permute-start.9
  74.8 4.4 %collective-permute-done.33 = bf16[128,512]{1,0:T(8,128)(2,1)S(1)} collective-permute-done((bf16[128,512]{1,0:T(8,128)(2,1)S(1)}, bf16[128,512]{1,0:T(8,128)(2,1)S(1)}, u32[]{:S(2)}, u32[]{:S(2)}) %collective-permute-start.33) | collective-permute-done | bytes 131104 | tf_op jit(solution)/shard_map/ppermute | solution.py:30
  80.8 2.7 %fusion.11 = (f32[512]{0:T(512)}, f32[1024]{0:T(1024)S(1)}, f32[512]{0:T(512)}) fusion(f32[1024,512]{1,0:T(8,128)S(1)} %get-tuple-element.27, f32[1024]{0:T(1024)S(1)} %fusion.77, f32[1024]{0:T(1024)S(1)} %broadcast_multiply_fusion, bf16[512,512]{1,0:T(8,128)(2,1)S(1)} %add_convert_fusion.5, bf16[512,512]{1,0:T(8,128)(2,1)S(1)} %collective-permute-done.13, ...), kind=kLoop, calls=%fused_computation.20 | loop fusion | flops 11008000 | bytes 3168257 | tf_op jit(solution)/shard_map/transpose(jvp())/reduce_sum | solution.py:20
  83.6 2.8 %fusion.87 = (f32[512]{0:T(512)}, f32[1024,512]{1,0:T(8,128)S(1)}, f32[512]{0:T(512)}) fusion(f32[1024]{0:T(1024)S(1)} %negate_multiply_fusion, f32[1024]{0:T(1024)S(1)} %multiply_multiply_fusion.2, f32[1024,512]{1,0:T(8,128)S(1)} %get-tuple-element.27, f32[1024]{0:T(1024)S(1)} %broadcast_multiply_fusion, f32[1024]{0:T(1024)S(1)} %fusion.77, ...), kind=kLoop, calls=%fused_computation.194 | loop fusion | flops 11009024 | bytes 6313985 | tf_op jit(solution)/shard_map/reduce_sum | solution.py:184
  86.4 1.3 copy-done.2
  87.7 1.1 convolution_convert_fusion.4
  88.8 1.8 %copy.45 = bf16[1024,128]{0,1:T(8,128)(2,1)} copy(bf16[1024,128]{1,0:T(8,128)(2,1)} %convolution_convert_fusion.4) | data formatting | bytes 524288 | tf_op jit(solution)/shard_map/convert_element_type | solution.py:186
  90.7 1.1 copy.86
  92.5 1.1 convolution_bitcast_fusion.6
  96.4 2.0 %collective-permute-start.14 = (f32[2,2,2,8,64]{4,3,2,1,0:T(8,128)}, f32[2,2,2,8,64]{4,3,2,1,0:T(8,128)S(1)}, u32[]{:S(2)}, u32[]{:S(2)}) collective-permute-start(f32[2,2,2,8,64]{4,3,2,1,0:T(8,128)} %slice.118), channel_id=1, source_target_pairs={{0,8},{4,12},{8,0},{12,4},{16,24},{20,28},{24,16},{28,20},{1,9},{5... | collective-permute-start | bytes 49160 | tf_op jit(solution)/shard_map/ppermute | solution.py:30
  98.4 1.0 fusion.27
  99.4 2.0 %copy.78 = bf16[8,128,2,64]{3,2,1,0:T(2,128)(2,1)} copy(bf16[8,128,2,64]{1,3,0,2:T(8,128)(2,1)} %fusion.27) | data formatting | bytes 524288 | tf_op jit(solution)/shard_map/stack;reshape | solution.py:229
  101.4 2.0 %reshape.255 = bf16[1,1024,128]{2,1,0:T(8,128)(2,1)} reshape(bf16[8,128,2,64]{3,2,1,0:T(2,128)(2,1)} %copy.78) | data formatting | bytes 524288 | tf_op jit(solution)/shard_map/stack;reshape | solution.py:229
  104.0 1.5 collective-permute-start.15
  105.5 1.7 constant_dynamic-update-slice_fusion.2
  108.7 1.2 add_convert_fusion.11
  109.9 1.3 copy.81
  111.4 1.5 add_convert_fusion.12
  115.1 3.9 %multiply_reduce_fusion = (f32[512]{0:T(512)S(1)}, f32[512]{0:T(512)S(1)}, f32[1024,512]{1,0:T(8,128)}) fusion(bf16[1024,512]{1,0:T(8,128)(2,1)} %param.13, f32[1024]{0:T(1024)} %copy-done.38, f32[1024]{0:T(1024)S(1)} %copy-done.31, bf16[3,1024,128]{2,1,0:T(8,128)(2,1)} %constant_dynamic-update-slice_fusion, bf16[3,512,128]{2,1,0:T(8,128)(2,1)} %param.16), kind=kOutput, calls=%fused_computation.25 | convolution fusion | flops 405797888 | bytes 4337664 | tf_op jit(solution)/shard_map/ste,sde->td/dot_general | solution.py:237
  119.0 1.7 fusion.21
  120.7 1.3 copy.62
  122.1 1.4 fusion.47
  123.5 1.5 collective-permute-start.24
  125.0 1.6 collective-permute-start.20
  126.6 1.4 add_convert_fusion.7
  129.4 3.3 %collective-permute-done.24 = bf16[1024,128]{1,0:T(8,128)(2,1)} collective-permute-done((bf16[1024,128]{1,0:T(8,128)(2,1)}, bf16[1024,128]{1,0:T(8,128)(2,1)}, u32[]{:S(2)}, u32[]{:S(2)}) %collective-permute-start.24) | collective-permute-done | bytes 262176 | tf_op jit(solution)/shard_map/ppermute | solution.py:30
  132.7 1.6 add_convert_fusion.10
  134.4 1.4 maximum_select_fusion.5
  135.8 1.6 collective-permute-start.35
  137.4 2.1 %collective-permute-start.22 = (f32[8,512]{1,0:T(8,128)S(1)}, f32[8,512]{1,0:T(8,128)S(1)}, u32[]{:S(2)}, u32[]{:S(2)}) collective-permute-start(f32[8,512]{1,0:T(8,128)S(1)} %add.352), channel_id=1, source_target_pairs={{0,8},{4,12},{8,0},{12,4},{16,24},{20,28},{24,16},{28,20},{1,9},{5... | collective-permute-start | bytes 49160 | tf_op jit(solution)/shard_map/ppermute | solution.py:30
  139.4 1.3 dynamic-slice_convert_fusion
  141.2 3.1 %collective-permute-start.23 = (f32[8,512]{1,0:T(8,128)S(1)}, f32[8,512]{1,0:T(8,128)S(1)}, u32[]{:S(2)}, u32[]{:S(2)}) collective-permute-start(f32[8,512]{1,0:T(8,128)S(1)} %add.353), channel_id=1, source_target_pairs={{0,16},{4,20},{8,24},{12,28},{16,0},{20,4},{24,8},{28,12},{1,17},{... | collective-permute-start | bytes 49160 | tf_op jit(solution)/shard_map/ppermute | solution.py:30
  144.5 1.4 maximum_select_fusion
  146.2 3.6 %collective-permute-done.26 = bf16[256,128]{1,0:T(8,128)(2,1)S(1)} collective-permute-done((bf16[256,128]{1,0:T(8,128)(2,1)S(1)}, bf16[256,128]{1,0:T(8,128)(2,1)S(1)}, u32[]{:S(2)}, u32[]{:S(2)}) %collective-permute-start.26) | collective-permute-done | bytes 65568 | tf_op jit(solution)/shard_map/ppermute | solution.py:30
  150.1 1.6 collective-permute-start.17
  152.3 2.9 %collective-permute-done.27 = bf16[256,128]{1,0:T(8,128)(2,1)S(1)} collective-permute-done((bf16[256,128]{1,0:T(8,128)(2,1)S(1)}, bf16[256,128]{1,0:T(8,128)(2,1)S(1)}, u32[]{:S(2)}, u32[]{:S(2)}) %collective-permute-start.27) | collective-permute-done | bytes 65568 | tf_op jit(solution)/shard_map/ppermute | solution.py:30
  155.6 4.6 %collective-permute-done.28 = bf16[512,128]{1,0:T(8,128)(2,1)S(1)} collective-permute-done((bf16[512,128]{1,0:T(8,128)(2,1)S(1)}, bf16[512,128]{1,0:T(8,128)(2,1)S(1)}, u32[]{:S(2)}, u32[]{:S(2)}) %collective-permute-start.28) | collective-permute-done | bytes 131104 | tf_op jit(solution)/shard_map/ppermute | solution.py:30
  160.9 1.2 collective-permute-done.17
  163.1 1.0 copy-done.4
  164.4 1.5 fusion.90
  168.6 1.4 maximum_select_fusion.2
  (236 shorter events, 35.0 us)
Async XLA Ops:
  0.6 34.9 %copy-start = (bf16[512,512]{1,0:T(8,128)(2,1)S(1)}, bf16[512,512]{1,0:T(8,128)(2,1)}, u32[]{:S(2)}) copy-start(bf16[512,512]{1,0:T(8,128)(2,1)} %param.23) | copy-start | bytes 1572868
  0.7 3.9 %copy-start.5 = (bf16[1024,512]{1,0:T(8,128)(2,1)S(1)}, bf16[1024,512]{1,0:T(8,128)(2,1)}, u32[]{:S(2)}) copy-start(bf16[1024,512]{1,0:T(8,128)(2,1)} %param.13) | copy-start | bytes 3145732
  0.7 3.9 %copy-start.32 = (f32[512]{0:T(512)S(1)}, f32[512]{0:T(512)}, u32[]{:S(2)}) copy-start(f32[512]{0:T(512)} %param.14) | copy-start | bytes 6148
  0.7 3.9 %copy-start.46 = (f32[512]{0:T(512)S(1)}, f32[512]{0:T(512)}, u32[]{:S(2)}) copy-start(f32[512]{0:T(512)} %param.15) | copy-start | bytes 6148
  0.7 3.9 %copy-start.43 = (bf16[3,512,128]{2,1,0:T(8,128)(2,1)S(1)}, bf16[3,512,128]{2,1,0:T(8,128)(2,1)}, u32[]{:S(2)}) copy-start(bf16[3,512,128]{2,1,0:T(8,128)(2,1)} %param.16) | copy-start | bytes 1179652
  6.8 9.6 %copy-start.11 = (bf16[8,128,2,64]{1,3,0,2:T(8,128)(2,1)}, bf16[8,128,2,64]{1,3,0,2:T(8,128)(2,1)S(1)}, u32[]{:S(2)}) copy-start(bf16[8,128,2,64]{1,3,0,2:T(8,128)(2,1)S(1)} %copy.42) | copy-start | bytes 786436
  7.1 4.6 %collective-permute-start = (bf16[1,2,2,8,64]{4,3,0,2,1:T(8,128)(2,1)S(1)}, bf16[1,2,2,8,64]{4,3,0,2,1:T(8,128)(2,1)S(1)}, u32[]{:S(2)}, u32[]{:S(2)}) collective-permute-start(bf16[1,2,2,8,64]{4,3,0,2,1:T(8,128)(2,1)S(1)} %fusion.76), channel_id=1, source_target_pairs={{0,4},{4,0},{8,12},{12,8},{16,20},{20,16},{24,28},{28,24},{1,5},{5... | collective-permute-start | bytes 12296 | tf_op jit(solution)/shard_map/ppermute | solution.py:30
  11.3 5.4 %copy-start.9 = (f32[2,8,128,128]{2,3,1,0:T(8,128)}, f32[2,8,128,128]{2,3,1,0:T(8,128)S(1)}, u32[]{:S(2)}) copy-start(f32[2,8,128,128]{2,3,1,0:T(8,128)S(1)} %get-tuple-element.46) | copy-start | bytes 3145732
  11.8 3.9 %collective-permute-start.1 = (bf16[2,2,2,8,64]{4,3,0,2,1:T(8,128)(2,1)S(1)}, bf16[2,2,2,8,64]{4,3,0,2,1:T(8,128)(2,1)S(1)}, u32[]{:S(2)}, u32[]{:S(2)}) collective-permute-start(bf16[2,2,2,8,64]{4,3,0,2,1:T(8,128)(2,1)S(1)} %pad_maximum_fusion.5), channel_id=1, source_target_pairs={{0,8},{4,12},{8,0},{12,4},{16,24},{20,28},{24,16},{28,20},{1,9},{5... | collective-permute-start | bytes 24584 | tf_op jit(solution)/shard_map/ppermute | solution.py:30
  17.4 9.1 %collective-permute-start.4 = (bf16[1024,128]{0,1:T(8,128)(2,1)S(1)}, bf16[1024,128]{0,1:T(8,128)(2,1)S(1)}, u32[]{:S(2)}, u32[]{:S(2)}) collective-permute-start(bf16[1024,128]{0,1:T(8,128)(2,1)S(1)} %bitcast.196), channel_id=1, source_target_pairs={{0,2},{1,3},{2,0},{3,1},{4,6},{5,7},{6,4},{7,5},{8,10},{9,11},{10,... | collective-permute-start | bytes 786440 | tf_op jit(solution)/shard_map/ppermute | solution.py:30
  19.5 7.1 %collective-permute-start.5 = (bf16[128,512]{1,0:T(8,128)(2,1)S(1)}, bf16[128,512]{1,0:T(8,128)(2,1)}, u32[]{:S(2)}, u32[]{:S(2)}) collective-permute-start(bf16[128,512]{1,0:T(8,128)(2,1)S(1)} %copy-done.23), channel_id=1, source_target_pairs={{0,2},{1,3},{2,0},{3,1},{4,6},{5,7},{6,4},{7,5},{8,10},{9,11},{10,... | collective-permute-start | bytes 393224 | tf_op jit(solution)/shard_map/ppermute | solution.py:30
  19.6 8.9 %collective-permute-start.3 = (bf16[128,512]{1,0:T(8,128)(2,1)S(1)}, bf16[128,512]{1,0:T(8,128)(2,1)}, u32[]{:S(2)}, u32[]{:S(2)}) collective-permute-start(bf16[128,512]{1,0:T(8,128)(2,1)S(1)} %copy-done.23), channel_id=1, source_target_pairs={{0,1},{1,0},{2,3},{3,2},{4,5},{5,4},{6,7},{7,6},{8,9},{9,8},{10,11... | collective-permute-start | bytes 393224 | tf_op jit(solution)/shard_map/ppermute | solution.py:30
  22.6 5.9 %collective-permute-start.2 = (bf16[1024,128]{0,1:T(8,128)(2,1)S(1)}, bf16[1024,128]{0,1:T(8,128)(2,1)S(1)}, u32[]{:S(2)}, u32[]{:S(2)}) collective-permute-start(bf16[1024,128]{0,1:T(8,128)(2,1)S(1)} %bitcast.197), channel_id=1, source_target_pairs={{0,1},{1,0},{2,3},{3,2},{4,5},{5,4},{6,7},{7,6},{8,9},{9,8},{10,11... | collective-permute-start | bytes 786440 | tf_op jit(solution)/shard_map/ppermute | solution.py:30
  26.6 3.3 %collective-permute-start.7 = (bf16[128,512]{1,0:T(8,128)(2,1)}, bf16[128,512]{1,0:T(8,128)(2,1)S(1)}, u32[]{:S(2)}, u32[]{:S(2)}) collective-permute-start(bf16[128,512]{1,0:T(8,128)(2,1)} %collective-permute-done.5), channel_id=1, source_target_pairs={{0,1},{1,0},{2,3},{3,2},{4,5},{5,4},{6,7},{7,6},{8,9},{9,8},{10,11... | collective-permute-start | bytes 393224 | tf_op jit(solution)/shard_map/ppermute | solution.py:30
  26.6 3.3 %collective-permute-start.6 = (bf16[1024,128]{0,1:T(8,128)(2,1)S(1)}, bf16[1024,128]{0,1:T(8,128)(2,1)S(1)}, u32[]{:S(2)}, u32[]{:S(2)}) collective-permute-start(bf16[1024,128]{0,1:T(8,128)(2,1)S(1)} %collective-permute-done.4), channel_id=1, source_target_pairs={{0,1},{1,0},{2,3},{3,2},{4,5},{5,4},{6,7},{7,6},{8,9},{9,8},{10,11... | collective-permute-start | bytes 786440 | tf_op jit(solution)/shard_map/ppermute | solution.py:30
  40.0 13.9 %collective-permute-start.30 = (bf16[512,512]{1,0:T(8,128)(2,1)S(1)}, bf16[512,512]{1,0:T(8,128)(2,1)S(1)}, u32[]{:S(2)}, u32[]{:S(2)}) collective-permute-start(bf16[512,512]{1,0:T(8,128)(2,1)S(1)} %fusion.34), channel_id=1, source_target_pairs={{0,4},{4,0},{8,12},{12,8},{16,20},{20,16},{24,28},{28,24},{1,5},{5... | collective-permute-start | bytes 1572872 | tf_op jit(solution)/shard_map/ppermute | solution.py:30
  42.4 14.0 %collective-permute-start.11 = (bf16[512,512]{1,0:T(8,128)(2,1)S(1)}, bf16[512,512]{1,0:T(8,128)(2,1)S(1)}, u32[]{:S(2)}, u32[]{:S(2)}) collective-permute-start(bf16[512,512]{1,0:T(8,128)(2,1)S(1)} %dynamic-slice_convert_fusion.1), channel_id=1, source_target_pairs={{0,1},{1,0},{2,3},{3,2},{4,5},{5,4},{6,7},{7,6},{8,9},{9,8},{10,11... | collective-permute-start | bytes 1572872 | tf_op jit(solution)/shard_map/ppermute | solution.py:30
  54.8 7.4 %collective-permute-start.31 = (bf16[256,512]{1,0:T(8,128)(2,1)S(1)}, bf16[256,512]{1,0:T(8,128)(2,1)S(1)}, u32[]{:S(2)}, u32[]{:S(2)}) collective-permute-start(bf16[256,512]{1,0:T(8,128)(2,1)S(1)} %constant_dynamic-slice_fusion.1), channel_id=1, source_target_pairs={{0,8},{4,12},{8,0},{12,4},{16,24},{20,28},{24,16},{28,20},{1,9},{5... | collective-permute-start | bytes 786440 | tf_op jit(solution)/shard_map/ppermute | solution.py:30
  56.7 12.7 %collective-permute-start.12 = (bf16[512,512]{1,0:T(8,128)(2,1)S(1)}, bf16[512,512]{1,0:T(8,128)(2,1)S(1)}, u32[]{:S(2)}, u32[]{:S(2)}) collective-permute-start(bf16[512,512]{1,0:T(8,128)(2,1)S(1)} %add_convert_fusion.6), channel_id=1, source_target_pairs={{0,2},{1,3},{2,0},{3,1},{4,6},{5,7},{6,4},{7,5},{8,10},{9,11},{10,... | collective-permute-start | bytes 1572872 | tf_op jit(solution)/shard_map/ppermute | solution.py:30
  59.3 13.1 %collective-permute-start.8 = (bf16[512,512]{1,0:T(8,128)(2,1)S(1)}, bf16[512,512]{1,0:T(8,128)(2,1)S(1)}, u32[]{:S(2)}, u32[]{:S(2)}) collective-permute-start(bf16[512,512]{1,0:T(8,128)(2,1)S(1)} %dynamic-slice_convert_fusion.2), channel_id=1, source_target_pairs={{0,1},{1,0},{2,3},{3,2},{4,5},{5,4},{6,7},{7,6},{8,9},{9,8},{10,11... | collective-permute-start | bytes 1572872 | tf_op jit(solution)/shard_map/ppermute | solution.py:30
  62.4 7.4 %collective-permute-start.32 = (bf16[128,512]{1,0:T(8,128)(2,1)S(1)}, bf16[128,512]{1,0:T(8,128)(2,1)S(1)}, u32[]{:S(2)}, u32[]{:S(2)}) collective-permute-start(bf16[128,512]{1,0:T(8,128)(2,1)S(1)} %constant_dynamic-slice_fusion), channel_id=1, source_target_pairs={{0,16},{4,20},{8,24},{12,28},{16,0},{20,4},{24,8},{28,12},{1,17},{... | collective-permute-start | bytes 393224 | tf_op jit(solution)/shard_map/ppermute | solution.py:30
  69.5 10.5 %collective-permute-start.13 = (bf16[512,512]{1,0:T(8,128)(2,1)S(1)}, bf16[512,512]{1,0:T(8,128)(2,1)S(1)}, u32[]{:S(2)}, u32[]{:S(2)}) collective-permute-start(bf16[512,512]{1,0:T(8,128)(2,1)S(1)} %add_convert_fusion.5), channel_id=1, source_target_pairs={{0,1},{1,0},{2,3},{3,2},{4,5},{5,4},{6,7},{7,6},{8,9},{9,8},{10,11... | collective-permute-start | bytes 1572872 | tf_op jit(solution)/shard_map/ppermute | solution.py:30
  69.8 9.4 %collective-permute-start.33 = (bf16[128,512]{1,0:T(8,128)(2,1)S(1)}, bf16[128,512]{1,0:T(8,128)(2,1)S(1)}, u32[]{:S(2)}, u32[]{:S(2)}) collective-permute-start(bf16[128,512]{1,0:T(8,128)(2,1)S(1)} %add_convert_fusion.13), channel_id=1, source_target_pairs={{0,16},{4,20},{8,24},{12,28},{16,0},{20,4},{24,8},{28,12},{1,17},{... | collective-permute-start | bytes 393224 | tf_op jit(solution)/shard_map/ppermute | solution.py:30
  73.4 53.2 %collective-permute-start.9 = (bf16[512,512]{1,0:T(8,128)(2,1)}, bf16[512,512]{1,0:T(8,128)(2,1)}, u32[]{:S(2)}, u32[]{:S(2)}) collective-permute-start(bf16[512,512]{1,0:T(8,128)(2,1)} %add_convert_fusion.8), channel_id=1, source_target_pairs={{0,2},{1,3},{2,0},{3,1},{4,6},{5,7},{6,4},{7,5},{8,10},{9,11},{10,... | collective-permute-start | bytes 1572872 | tf_op jit(solution)/shard_map/ppermute | solution.py:30
  80.0 54.4 %collective-permute-start.34 = (bf16[256,512]{1,0:T(8,128)(2,1)}, bf16[256,512]{1,0:T(8,128)(2,1)}, u32[]{:S(2)}, u32[]{:S(2)}) collective-permute-start(bf16[256,512]{1,0:T(8,128)(2,1)} %maximum_select_fusion.7), channel_id=1, source_target_pairs={{0,8},{4,12},{8,0},{12,4},{16,24},{20,28},{24,16},{28,20},{1,9},{5... | collective-permute-start | bytes 786440 | tf_op jit(solution)/shard_map/ppermute | solution.py:30
  86.4 5.4 %copy-start.12 = (bf16[8,128,2,64]{1,3,0,2:T(8,128)(2,1)S(1)}, bf16[8,128,2,64]{1,3,0,2:T(8,128)(2,1)}, u32[]{:S(2)}) copy-start(bf16[8,128,2,64]{1,3,0,2:T(8,128)(2,1)} %copy-done.11) | copy-start | bytes 786436
  88.8 3.3 %copy-start.25 = (bf16[4,2,2,8,64]{4,3,0,2,1:T(8,128)(2,1)S(1)}, bf16[4,2,2,8,64]{4,3,0,2,1:T(8,128)(2,1)}, u32[]{:S(2)}) copy-start(bf16[4,2,2,8,64]{4,3,0,2,1:T(8,128)(2,1)} %copy-done.24) | copy-start | bytes 49156
  88.8 4.7 %copy-start.16 = (f32[2,8,128,32]{2,3,1,0:T(8,128)S(1)}, f32[2,8,128,32]{2,3,1,0:T(8,128)}, u32[]{:S(2)}) copy-start(f32[2,8,128,32]{2,3,1,0:T(8,128)} %copy-done.15) | copy-start | bytes 786436
  94.0 4.4 %copy-start.21 = (bf16[2,8,128,160]{2,3,1,0:T(8,128)(2,1)}, bf16[2,8,128,160]{2,3,1,0:T(8,128)(2,1)S(1)}, u32[]{:S(2)}) copy-start(bf16[2,8,128,160]{2,3,1,0:T(8,128)(2,1)S(1)} %fusion.15) | copy-start | bytes 1966084
  95.7 13.0 %copy-start.14 = (bf16[2,8,128,160]{2,3,1,0:T(8,128)(2,1)S(1)}, bf16[2,8,128,160]{2,3,1,0:T(8,128)(2,1)}, u32[]{:S(2)}) copy-start(bf16[2,8,128,160]{2,3,1,0:T(8,128)(2,1)} %copy-done.13) | copy-start | bytes 1966084
  95.8 13.0 %copy-start.18 = (bf16[16,8,8,128]{3,2,1,0:T(8,128)(2,1)S(1)}, bf16[16,8,8,128]{3,2,1,0:T(8,128)(2,1)}, u32[]{:S(2)}) copy-start(bf16[16,8,8,128]{3,2,1,0:T(8,128)(2,1)} %copy-done.17) | copy-start | bytes 786436
  96.4 7.0 %collective-permute-start.14 = (f32[2,2,2,8,64]{4,3,2,1,0:T(8,128)}, f32[2,2,2,8,64]{4,3,2,1,0:T(8,128)S(1)}, u32[]{:S(2)}, u32[]{:S(2)}) collective-permute-start(f32[2,2,2,8,64]{4,3,2,1,0:T(8,128)} %slice.118), channel_id=1, source_target_pairs={{0,8},{4,12},{8,0},{12,4},{16,24},{20,28},{24,16},{28,20},{1,9},{5... | collective-permute-start | bytes 49160 | tf_op jit(solution)/shard_map/ppermute | solution.py:30
  104.0 3.9 %collective-permute-start.15 = (f32[1,2,2,8,64]{4,3,2,1,0:T(8,128)}, f32[1,2,2,8,64]{4,3,2,1,0:T(8,128)S(1)}, u32[]{:S(2)}, u32[]{:S(2)}) collective-permute-start(f32[1,2,2,8,64]{4,3,2,1,0:T(8,128)} %slice.120), channel_id=1, source_target_pairs={{0,4},{4,0},{8,12},{12,8},{16,20},{20,16},{24,28},{28,24},{1,5},{5... | collective-permute-start | bytes 24584 | tf_op jit(solution)/shard_map/ppermute | solution.py:30
  111.4 3.6 %copy-start.31 = (f32[1024]{0:T(1024)S(1)}, f32[1024]{0:T(1024)}, u32[]{:S(2)}) copy-start(f32[1024]{0:T(1024)} %copy-done.30) | copy-start | bytes 12292
  115.1 3.9 %copy-start.7 = (bf16[1024,512]{1,0:T(8,128)(2,1)S(1)}, bf16[1024,512]{1,0:T(8,128)(2,1)}, u32[]{:S(2)}) copy-start(bf16[1024,512]{1,0:T(8,128)(2,1)} %param.13) | copy-start | bytes 3145732
  115.1 3.9 %copy-start.27 = (bf16[3,1024,128]{2,1,0:T(8,128)(2,1)S(1)}, bf16[3,1024,128]{2,1,0:T(8,128)(2,1)}, u32[]{:S(2)}) copy-start(bf16[3,1024,128]{2,1,0:T(8,128)(2,1)} %constant_dynamic-update-slice_fusion) | copy-start | bytes 2359300
  115.1 3.9 %copy-start.33 = (f32[512]{0:T(512)S(1)}, f32[512]{0:T(512)}, u32[]{:S(2)}) copy-start(f32[512]{0:T(512)} %param.14) | copy-start | bytes 6148
  115.1 3.9 %copy-start.39 = (f32[1024]{0:T(1024)S(1)}, f32[1024]{0:T(1024)}, u32[]{:S(2)}) copy-start(f32[1024]{0:T(1024)} %copy-done.38) | copy-start | bytes 12292
  115.1 3.9 %copy-start.47 = (f32[512]{0:T(512)S(1)}, f32[512]{0:T(512)}, u32[]{:S(2)}) copy-start(f32[512]{0:T(512)} %param.15) | copy-start | bytes 6148
  119.0 7.6 %copy-start.41 = (f32[512]{0:T(512)S(1)}, f32[512]{0:T(512)}, u32[]{:S(2)}) copy-start(f32[512]{0:T(512)} %param.24) | copy-start | bytes 6148
  120.7 8.0 %copy-start.34 = (f32[512]{0:T(512)S(1)}, f32[512]{0:T(512)}, u32[]{:S(2)}) copy-start(f32[512]{0:T(512)} %get-tuple-element.13) | copy-start | bytes 6148
  120.7 8.0 %copy-start.35 = (f32[512]{0:T(512)S(1)}, f32[512]{0:T(512)}, u32[]{:S(2)}) copy-start(f32[512]{0:T(512)} %get-tuple-element.19) | copy-start | bytes 6148
  120.7 8.0 %copy-start.36 = (f32[512]{0:T(512)S(1)}, f32[512]{0:T(512)}, u32[]{:S(2)}) copy-start(f32[512]{0:T(512)} %get-tuple-element.22) | copy-start | bytes 6148
  120.7 8.1 %copy-start.37 = (f32[512]{0:T(512)S(1)}, f32[512]{0:T(512)}, u32[]{:S(2)}) copy-start(f32[512]{0:T(512)} %get-tuple-element.30) | copy-start | bytes 6148
  120.7 8.1 %copy-start.42 = (f32[512]{0:T(512)S(1)}, f32[512]{0:T(512)}, u32[]{:S(2)}) copy-start(f32[512]{0:T(512)} %get-tuple-element.20) | copy-start | bytes 6148
  122.0 3.0 %collective-permute-start.19 = (f32[2,512]{1,0:T(2,128)S(1)}, f32[2,512]{1,0:T(2,128)S(1)}, u32[]{:S(2)}, u32[]{:S(2)}) collective-permute-start(f32[2,512]{1,0:T(2,128)S(1)} %pad_maximum_fusion.6), channel_id=1, source_target_pairs={{0,1},{1,0},{2,3},{3,2},{4,5},{5,4},{6,7},{7,6},{8,9},{9,8},{10,11... | collective-permute-start | bytes 12296 | tf_op jit(solution)/shard_map/ppermute | solution.py:30
  123.5 9.2 %collective-permute-start.24 = (bf16[1024,128]{1,0:T(8,128)(2,1)}, bf16[1024,128]{1,0:T(8,128)(2,1)}, u32[]{:S(2)}, u32[]{:S(2)}) collective-permute-start(bf16[1024,128]{1,0:T(8,128)(2,1)} %fusion.47), channel_id=1, source_target_pairs={{0,4},{4,0},{8,12},{12,8},{16,20},{20,16},{24,28},{28,24},{1,5},{5... | collective-permute-start | bytes 786440 | tf_op jit(solution)/shard_map/ppermute | solution.py:30
  125.0 3.7 %collective-permute-start.20 = (f32[2,512]{1,0:T(2,128)S(1)}, f32[2,512]{1,0:T(2,128)S(1)}, u32[]{:S(2)}, u32[]{:S(2)}) collective-permute-start(f32[2,512]{1,0:T(2,128)S(1)} %fusion.80), channel_id=1, source_target_pairs={{0,2},{1,3},{2,0},{3,1},{4,6},{5,7},{6,4},{7,5},{8,10},{9,11},{10,... | collective-permute-start | bytes 12296 | tf_op jit(solution)/shard_map/ppermute | solution.py:30
  128.0 16.4 %collective-permute-start.10 = (bf16[512,512]{1,0:T(8,128)(2,1)S(1)}, bf16[512,512]{1,0:T(8,128)(2,1)S(1)}, u32[]{:S(2)}, u32[]{:S(2)}) collective-permute-start(bf16[512,512]{1,0:T(8,128)(2,1)S(1)} %add_convert_fusion.7), channel_id=1, source_target_pairs={{0,1},{1,0},{2,3},{3,2},{4,5},{5,4},{6,7},{7,6},{8,9},{9,8},{10,11... | collective-permute-start | bytes 1572872 | tf_op jit(solution)/shard_map/ppermute | solution.py:30
  128.8 8.6 %collective-permute-start.21 = (f32[8,512]{1,0:T(8,128)S(1)}, f32[8,512]{1,0:T(8,128)S(1)}, u32[]{:S(2)}, u32[]{:S(2)}) collective-permute-start(f32[8,512]{1,0:T(8,128)S(1)} %concatenate.89), channel_id=1, source_target_pairs={{0,4},{4,0},{8,12},{12,8},{16,20},{20,16},{24,28},{28,24},{1,5},{5... | collective-permute-start | bytes 49160 | tf_op jit(solution)/shard_map/ppermute | solution.py:30
  134.3 10.0 %collective-permute-start.25 = (bf16[512,128]{1,0:T(8,128)(2,1)S(1)}, bf16[512,128]{1,0:T(8,128)(2,1)S(1)}, u32[]{:S(2)}, u32[]{:S(2)}) collective-permute-start(bf16[512,128]{1,0:T(8,128)(2,1)S(1)} %constant_dynamic-slice_fusion.3), channel_id=1, source_target_pairs={{0,8},{4,12},{8,0},{12,4},{16,24},{20,28},{24,16},{28,20},{1,9},{5... | collective-permute-start | bytes 393224 | tf_op jit(solution)/shard_map/ppermute | solution.py:30
  135.8 14.1 %copy-start.19 = (f32[1024,512]{1,0:T(8,128)S(1)}, f32[1024,512]{1,0:T(8,128)}, u32[]{:S(2)}) copy-start(f32[1024,512]{1,0:T(8,128)} %get-tuple-element.49) | copy-start | bytes 6291460
  135.8 19.5 %collective-permute-start.35 = (bf16[512,512]{1,0:T(8,128)(2,1)S(1)}, bf16[512,512]{1,0:T(8,128)(2,1)S(1)}, u32[]{:S(2)}, u32[]{:S(2)}) collective-permute-start(bf16[512,512]{1,0:T(8,128)(2,1)S(1)} %maximum_select_fusion.5), channel_id=1, source_target_pairs={{0,4},{4,0},{8,12},{12,8},{16,20},{20,16},{24,28},{28,24},{1,5},{5... | collective-permute-start | bytes 1572872 | tf_op jit(solution)/shard_map/ppermute | solution.py:30
  137.4 3.8 %collective-permute-start.22 = (f32[8,512]{1,0:T(8,128)S(1)}, f32[8,512]{1,0:T(8,128)S(1)}, u32[]{:S(2)}, u32[]{:S(2)}) collective-permute-start(f32[8,512]{1,0:T(8,128)S(1)} %add.352), channel_id=1, source_target_pairs={{0,8},{4,12},{8,0},{12,4},{16,24},{20,28},{24,16},{28,20},{1,9},{5... | collective-permute-start | bytes 49160 | tf_op jit(solution)/shard_map/ppermute | solution.py:30
  140.7 9.1 %collective-permute-start.16 = (bf16[512,512]{1,0:T(8,128)(2,1)S(1)}, bf16[512,512]{1,0:T(8,128)(2,1)S(1)}, u32[]{:S(2)}, u32[]{:S(2)}) collective-permute-start(bf16[512,512]{1,0:T(8,128)(2,1)S(1)} %dynamic-slice_convert_fusion), channel_id=1, source_target_pairs={{0,1},{1,0},{2,3},{3,2},{4,5},{5,4},{6,7},{7,6},{8,9},{9,8},{10,11... | collective-permute-start | bytes 1572872 | tf_op jit(solution)/shard_map/ppermute | solution.py:30
  141.2 5.0 %collective-permute-start.23 = (f32[8,512]{1,0:T(8,128)S(1)}, f32[8,512]{1,0:T(8,128)S(1)}, u32[]{:S(2)}, u32[]{:S(2)}) collective-permute-start(f32[8,512]{1,0:T(8,128)S(1)} %add.353), channel_id=1, source_target_pairs={{0,16},{4,20},{8,24},{12,28},{16,0},{20,4},{24,8},{28,12},{1,17},{... | collective-permute-start | bytes 49160 | tf_op jit(solution)/shard_map/ppermute | solution.py:30
  144.4 5.4 %collective-permute-start.26 = (bf16[256,128]{1,0:T(8,128)(2,1)S(1)}, bf16[256,128]{1,0:T(8,128)(2,1)S(1)}, u32[]{:S(2)}, u32[]{:S(2)}) collective-permute-start(bf16[256,128]{1,0:T(8,128)(2,1)S(1)} %constant_dynamic-slice_fusion.2), channel_id=1, source_target_pairs={{0,16},{4,20},{8,24},{12,28},{16,0},{20,4},{24,8},{28,12},{1,17},{... | collective-permute-start | bytes 196616 | tf_op jit(solution)/shard_map/ppermute | solution.py:30
  149.8 5.4 %collective-permute-start.27 = (bf16[256,128]{1,0:T(8,128)(2,1)S(1)}, bf16[256,128]{1,0:T(8,128)(2,1)S(1)}, u32[]{:S(2)}, u32[]{:S(2)}) collective-permute-start(bf16[256,128]{1,0:T(8,128)(2,1)S(1)} %add_convert_fusion.15), channel_id=1, source_target_pairs={{0,16},{4,20},{8,24},{12,28},{16,0},{20,4},{24,8},{28,12},{1,17},{... | collective-permute-start | bytes 196616 | tf_op jit(solution)/shard_map/ppermute | solution.py:30
  150.1 12.0 %copy-start.8 = (f32[1024,512]{1,0:T(8,128)S(1)}, f32[1024,512]{1,0:T(8,128)}, u32[]{:S(2)}) copy-start(f32[1024,512]{1,0:T(8,128)} %convert_element_type.196) | copy-start | bytes 6291460
  150.1 12.0 %copy-start.29 = (f32[512]{0:T(512)S(1)}, f32[512]{0:T(512)}, u32[]{:S(2)}) copy-start(f32[512]{0:T(512)} %broadcast_multiply_fusion.2) | copy-start | bytes 6148
  150.1 12.0 %collective-permute-start.17 = (bf16[512,512]{1,0:T(8,128)(2,1)S(1)}, bf16[512,512]{1,0:T(8,128)(2,1)S(1)}, u32[]{:S(2)}, u32[]{:S(2)}) collective-permute-start(bf16[512,512]{1,0:T(8,128)(2,1)S(1)} %add_convert_fusion.4), channel_id=1, source_target_pairs={{0,2},{1,3},{2,0},{3,1},{4,6},{5,7},{6,4},{7,5},{8,10},{9,11},{10,... | collective-permute-start | bytes 1572872 | tf_op jit(solution)/shard_map/ppermute | solution.py:30
  155.2 5.0 %collective-permute-start.28 = (bf16[512,128]{1,0:T(8,128)(2,1)S(1)}, bf16[512,128]{1,0:T(8,128)(2,1)S(1)}, u32[]{:S(2)}, u32[]{:S(2)}) collective-permute-start(bf16[512,128]{1,0:T(8,128)(2,1)S(1)} %maximum_select_fusion.8), channel_id=1, source_target_pairs={{0,8},{4,12},{8,0},{12,4},{16,24},{20,28},{24,16},{28,20},{1,9},{5... | collective-permute-start | bytes 393224 | tf_op jit(solution)/shard_map/ppermute | solution.py:30
  160.3 6.4 %collective-permute-start.29 = (bf16[1024,128]{1,0:T(8,128)(2,1)S(1)}, bf16[1024,128]{1,0:T(8,128)(2,1)S(1)}, u32[]{:S(2)}, u32[]{:S(2)}) collective-permute-start(bf16[1024,128]{1,0:T(8,128)(2,1)S(1)} %maximum_select_fusion.6), channel_id=1, source_target_pairs={{0,4},{4,0},{8,12},{12,8},{16,20},{20,16},{24,28},{28,24},{1,5},{5... | collective-permute-start | bytes 786440 | tf_op jit(solution)/shard_map/ppermute | solution.py:30
  164.3 4.3 %collective-permute-start.18 = (bf16[512,512]{1,0:T(8,128)(2,1)S(1)}, bf16[512,512]{1,0:T(8,128)(2,1)S(1)}, u32[]{:S(2)}, u32[]{:S(2)}) collective-permute-start(bf16[512,512]{1,0:T(8,128)(2,1)S(1)} %add_convert_fusion.3), channel_id=1, source_target_pairs={{0,1},{1,0},{2,3},{3,2},{4,5},{5,4},{6,7},{7,6},{8,9},{9,8},{10,11... | collective-permute-start | bytes 1572872 | tf_op jit(solution)/shard_map/ppermute | solution.py:30
  (20 other events, 29.7 us)

commit v2 on v1

v2 whole, which is shorter than its diff:
```python
import functools
import math

import jax
import jax.numpy as jnp
from jax import lax
from jax.experimental import pallas as pl
from jax.experimental.pallas import tpu as pltpu
from jax.sharding import PartitionSpec as P

HEAD_DIM = 64
SPAN = 128
LENGTH = 4096
EPSILON = 1e-05
SCALE = HEAD_DIM ** (-0.5)
LOW = -1e30

f32 = jnp.float32
bf16 = jnp.bfloat16
i32 = jnp.int32
VMEM = pl.BlockSpec(memory_space=pltpu.VMEM)
SMEM = pl.BlockSpec(memory_space=pltpu.SMEM)


def masks_of(count):
    return [1 << i for i in range(count.bit_length() - 1)]


def params(mib=60):
    return pltpu.CompilerParams(vmem_limit_bytes=mib * 1024 * 1024)


def cost():
    return pl.CostEstimate(flops=115_000_000_000, bytes_accessed=1, transcendentals=0)


def nt(a, b):
    return lax.dot_general(a, b, (((1,), (1,)), ((), ())), preferred_element_type=f32)


def tn(a, b):
    return lax.dot_general(a, b, (((0,), (0,)), ((), ())), preferred_element_type=f32)


def nn(a, b):
    return jnp.dot(a, b, preferred_element_type=f32)


def normed(x):
    c = x - jnp.mean(x, axis=-1, keepdims=True)
    r = lax.rsqrt(jnp.mean(c * c, axis=-1, keepdims=True) + EPSILON)
    return c * r, r


def norm_back(e, n, r, gain):
    k = e * gain
    return r * (
        k - jnp.mean(k, axis=-1, keepdims=True) - n * jnp.mean(k * n, axis=-1, keepdims=True)
    )


def fold(x):
    return jnp.sum(x.reshape(-1, 8, x.shape[-1]), axis=0)


def head_mask(shape, h, dtype):
    lane = lax.broadcasted_iota(i32, shape, len(shape) - 1)
    return jnp.where(lane // HEAD_DIM == h, 1.0, 0.0).astype(dtype)


def spread(x, factor):
    heads = x.shape[1] // HEAD_DIM
    return jnp.concatenate(
        [x * (head_mask((1, x.shape[1]), h, f32) * factor).astype(x.dtype) for h in range(heads)]
    )


def collect(x, factor):
    width = x.shape[1]
    heads = width // HEAD_DIM
    rows = x.shape[0] // heads
    total = x[:rows] * (head_mask((1, width), 0, f32) * factor)
    for h in range(1, heads):
        total = total + x[h * rows : (h + 1) * rows] * (head_mask((1, width), h, f32) * factor)
    return total


def to_low(v, cols):
    v = jnp.concatenate([v[:, i : i + cols] for i in range(0, v.shape[1], cols)])
    high = v.astype(bf16)
    return jnp.concatenate([high, (v - high.astype(f32)).astype(bf16)])


def from_low(x, dim):
    half = x.shape[0] // 2
    v = x[:half].astype(f32) + x[half:].astype(f32)
    count = dim // x.shape[1]
    return jnp.concatenate([v[i * 8 : (i + 1) * 8] for i in range(count)], axis=1)


def columns_of(sums_ref, start, count):
    slots, _, blocks, width = sums_ref.shape
    parts = [sums_ref[:, start + j].reshape(slots * blocks, width) for j in range(count)]
    return jnp.concatenate(parts, axis=1)


def project_kernel(tile, tok_ref, gain_ref, bias_ref, w_ref, first_ref, qkv_ref, sum_ref, wcat):
    width = w_ref.shape[2]
    for s in range(3):
        wcat[:, s * width : (s + 1) * width] = w_ref[s]
    per = tile // SPAN
    for i in range(tok_ref.shape[0] // tile):
        at = slice(i * tile, (i + 1) * tile)
        n, _ = normed(tok_ref[at].astype(f32))
        first = (n * gain_ref[...] + bias_ref[...]).astype(bf16)
        first_ref[at] = first
        both = nn(first, wcat[...]).astype(bf16)
        for s in range(3):
            part = both[:, s * width : (s + 1) * width]
            qkv_ref[s, at] = part
            if s:
                mean = jnp.mean(part.astype(f32).reshape(per, SPAN, width), axis=1)
                sum_ref[s - 1, i * per : (i + 1) * per] = mean.astype(bf16).astype(f32)
        sums = [jnp.sum(x.reshape(per, SPAN, -1), axis=1) for x in (first.astype(f32), n)]
        total = jnp.concatenate(sums, axis=1)
        for j in range(sum_ref.shape[0] - 2):
            sum_ref[2 + j, i * per : (i + 1) * per] = total[:, j * width : (j + 1) * width]


def local_kernel(qkv_ref, exp_ref, stat_ref):
    blocks = exp_ref.shape[0]
    lanes = exp_ref.shape[2]
    key = lax.broadcasted_iota(i32, (SPAN, lanes), 0)
    query = lax.broadcasted_iota(i32, (SPAN, lanes), 1) % SPAN
    keep = key <= query
    for b in range(blocks):
        at = slice(b * SPAN, (b + 1) * SPAN)
        s = nt(qkv_ref[1, at], spread(qkv_ref[0, at], SCALE))
        s = jnp.where(keep, s, LOW)
        top = jnp.max(s, axis=0, keepdims=True)
        e = jnp.exp(s - top)
        exp_ref[b] = e
        stat_ref[b, 0:1] = top
        stat_ref[b, 1:2] = jnp.sum(e, axis=0, keepdims=True)


def attend_kernel(place_ref, qkv_ref, exp_ref, stat_ref, sums_ref, prob_ref, att_ref):
    blocks = exp_ref.shape[0]
    lanes = exp_ref.shape[2]
    slots = sums_ref.shape[0]
    place = place_ref[0]
    keys = sums_ref[:, 0].reshape(slots * blocks, -1).astype(bf16)
    values = sums_ref[:, 1].reshape(slots * blocks, -1).astype(bf16)
    row = lax.broadcasted_iota(i32, (slots * blocks, lanes), 0)
    at_block = ((row // blocks) ^ place) * blocks + row % blocks
    for b in range(blocks):
        at = slice(b * SPAN, (b + 1) * SPAN)
        s = nt(keys, spread(qkv_ref[0, at], SCALE)) + math.log(SPAN)
        s = jnp.where(at_block < place * blocks + b, s, LOW)
        mine = stat_ref[b, 0:1]
        top = jnp.maximum(mine, jnp.max(s, axis=0, keepdims=True))
        e = jnp.exp(s - top)
        shrink = jnp.exp(mine - top)
        scale = 1.0 / (stat_ref[b, 1:2] * shrink + jnp.sum(e, axis=0, keepdims=True))
        p = jnp.concatenate([exp_ref[b] * (shrink * scale), e * scale])
        prob_ref[b] = p
        a = tn(p.astype(bf16), jnp.concatenate([qkv_ref[2, at], values]))
        att_ref[at] = collect(a, 1.0).astype(bf16)


def feed_kernel(
    count, pos_ref, tok_ref, *refs
):
    att = refs[:count]
    wo = refs[count : 2 * count]
    (
        b_out_ref,
        gain_ref,
        bias_ref,
        up_ref,
        b_up_ref,
        down_ref,
        cot_ref,
        mid_ref,
        second_ref,
        active_ref,
        grad_ref,
        theirs_ref,
        mine_ref,
        vec_ref,
        wcat,
    ) = refs[2 * count :]
    step = pl.program_id(0)
    me = pos_ref[0]
    width = wo[0].shape[0]

    def in_order(arrays):
        arrays = list(arrays)
        for m in masks_of(count):
            flip = (me & m) != 0
            arrays = [jnp.where(flip, arrays[j ^ m], arrays[j]) for j in range(count)]
        return arrays

    @pl.when(step == 0)
    def _():
        for j in range(count):
            wcat[pl.ds(pl.multiple_of((me ^ j) * width, width), width)] = wo[j][...]
        vec_ref[...] = jnp.zeros_like(vec_ref)

    attended = jnp.concatenate(in_order([a[...] for a in att]), axis=1)
    mid = tok_ref[...].astype(f32) + nn(attended, wcat[...]) + b_out_ref[...]
    mid_ref[...] = mid
    n, _ = normed(mid)
    second = (n * gain_ref[...] + bias_ref[...]).astype(bf16)
    second_ref[...] = second
    u = nn(second, up_ref[...]) + b_up_ref[...]
    root = math.sqrt(2.0 / math.pi)
    square = u * u
    t = jnp.tanh(u * (root + root * 0.044715 * square))
    half = 0.5 + 0.5 * t
    active_ref[...] = (u * half).astype(bf16)
    slope = half + (0.5 * u) * (1.0 - t * t) * (root + (3.0 * root * 0.044715) * square)
    grad = nt(cot_ref[...], down_ref[...]) * slope
    low = grad.astype(bf16)
    grad_ref[...] = low
    out = nt(low, up_ref[...]).astype(bf16)
    steps = pl.num_programs(0)

    @pl.when(step < steps // 2)
    def _():
        theirs_ref[...] = out

    @pl.when(step >= steps // 2)
    def _():
        mine_ref[...] = out

    vec_ref[0:8] += fold(low.astype(f32))


def weights_kernel(
    pos_ref,
    active_ref,
    second_ref,
    grad_ref,
    cot_ref,
    down_ref,
    out_theirs_ref,
    out_mine_ref,
    theirs_ref,
    mine_ref,
    down_acc,
    up_acc,
):
    step = pl.program_id(0)
    terms = nn(active_ref[...], down_ref[...]).astype(bf16)
    down = tn(active_ref[...], cot_ref[...])
    up = tn(second_ref[...], grad_ref[...])

    @pl.when(step == 0)
    def _():
        out_theirs_ref[...] = terms
        down_acc[...] = down
        up_acc[...] = up

    @pl.when(step == 1)
    def _():
        out_mine_ref[...] = terms
        first = (down_acc[...] + down).astype(bf16)
        then = (up_acc[...] + up).astype(bf16).reshape(first.shape)
        low = pos_ref[3] == 0
        theirs_ref[...] = jnp.where(low, then, first)
        mine_ref[...] = jnp.where(low, first, then)


def rest_kernel(
    bit_ref, first_ref, gqkv_ref, low_ref, att_ref, slot_ref, sums_ref, theirs_ref, mine_ref
):
    slots, _, blocks, width = slot_ref.shape
    dim = first_ref.shape[1]
    size = dim // 2
    rows = [slot_ref[:, s].reshape(slots * blocks, width) for s in range(2)]
    far_rows = (jnp.concatenate(rows, axis=1) * (1.0 / SPAN)).astype(bf16)
    far_first = columns_of(sums_ref, 2, dim // width).astype(bf16)
    out = []
    for h in range(2):
        at = slice(h * size, (h + 1) * size)
        main = tn(first_ref[:, at], gqkv_ref[...])
        far = tn(far_first[:, at], far_rows)
        last = tn(low_ref[:, at], att_ref[...])
        out.append(
            jnp.concatenate([main[:, :width], main[:, width:] + far, last], axis=1).astype(bf16)
        )
    low = bit_ref[0] == 0
    theirs_ref[...] = jnp.where(low, out[1], out[0])
    mine_ref[...] = jnp.where(low, out[0], out[1])


def split_kernel(bit_ref, a_ref, b_ref, theirs_ref, mine_ref):
    total = (a_ref[...].astype(f32) + b_ref[...].astype(f32)).astype(bf16)
    size = total.shape[0] // 2
    low = bit_ref[0] == 0
    theirs_ref[...] = jnp.where(low, total[size:], total[:size])
    mine_ref[...] = jnp.where(low, total[:size], total[size:])


def two_halves(refs, half, core):
    own, far, other, other_far = refs
    mine = half == core
    a = jnp.where(mine, own[...], other[...])
    b = jnp.where(mine, far[...], other_far[...])
    return a.astype(f32) + b.astype(f32)


def back_kernel(
    pos_ref,
    own_ref,
    far_ref,
    other_ref,
    other_far_ref,
    mid_ref,
    cot_ref,
    gain_ref,
    wo_ref,
    qkv_ref,
    prob_ref,
    sums_ref,
    low_ref,
    gqkv_ref,
    slot_ref,
    vec_ref,
):
    step = pl.program_id(0)
    slots = sums_ref.shape[0]
    width = wo_ref.shape[0]

    @pl.when(step == 0)
    def _():
        slot_ref[...] = jnp.zeros_like(slot_ref)
        vec_ref[...] = jnp.zeros_like(vec_ref)

    e = two_halves((own_ref, far_ref, other_ref, other_far_ref), step, pos_ref[1])
    n, r = normed(mid_ref[...])
    cot = cot_ref[...].astype(f32)
    grad_mid = cot + norm_back(e, n, r, gain_ref[...])
    low = grad_mid.astype(bf16)
    low_ref[...] = low
    vec_ref[0:8] += fold(grad_mid)
    vec_ref[8:16] += fold(e * n)
    vec_ref[16:24] += fold(e)
    vec_ref[24:32] += fold(cot)

    grad_att = nt(low, wo_ref[...]).astype(bf16)
    far_keys = sums_ref[:, 0].reshape(-1, width).astype(bf16)
    far_values = sums_ref[:, 1].reshape(-1, width).astype(bf16)
    far_gk = jnp.zeros(far_keys.shape, f32)
    far_gv = jnp.zeros(far_keys.shape, f32)
    for b in range(prob_ref.shape[0]):
        at = slice(b * SPAN, (b + 1) * SPAN)
        da = spread(grad_att[at], 1.0)
        query = spread(qkv_ref[0, at], SCALE)
        keys = jnp.concatenate([qkv_ref[1, at], far_keys])
        values = jnp.concatenate([qkv_ref[2, at], far_values])
        p = prob_ref[b]
        dp = nt(values, da)
        ds = (p * (dp - jnp.sum(p * dp, axis=0, keepdims=True))).astype(bf16)
        gq = collect(tn(ds, keys), SCALE)
        gk = nn(ds, query)
        gv = nn(p.astype(bf16), da)
        gqkv_ref[at, :width] = gq.astype(bf16)
        gqkv_ref[at, width : 2 * width] = gk[:SPAN].astype(bf16)
        gqkv_ref[at, 2 * width :] = gv[:SPAN].astype(bf16)
        far_gk = far_gk + gk[SPAN:]
        far_gv = far_gv + gv[SPAN:]
    slot_ref[:, 0] += far_gk.reshape(slots, -1, width)
    slot_ref[:, 1] += far_gv.reshape(slots, -1, width)


def first_kernel(
    pos_ref, gqkv_ref, slot_ref, sums_ref, w_ref, tok_ref, theirs_ref, mine_ref, wcat, vec
):
    step = pl.program_id(0)
    steps = pl.num_programs(0)
    dim, width = w_ref.shape[1:]
    tile = gqkv_ref.shape[0]
    half = tile * (steps // 2)

    @pl.when(step == 0)
    def _():
        vec[...] = jnp.zeros_like(vec)
        for s in range(3):
            wcat[:, s * width : (s + 1) * width] = w_ref[s]

    e = nt(gqkv_ref[...], wcat[...])
    n, _ = normed(tok_ref[...].astype(f32))
    vec[0:8] += fold(e * n)
    vec[8:16] += fold(e)
    out = e.astype(bf16)
    at = pl.ds(pl.multiple_of((step % (steps // 2)) * tile, tile), tile)

    @pl.when(step < steps // 2)
    def _():
        theirs_ref[at] = out

    @pl.when(step >= steps // 2)
    def _():
        mine_ref[at] = out

    @pl.when(step == steps - 1)
    def _():
        rows = [
            (slot_ref[:, s].reshape(-1, width) * (1.0 / SPAN)).astype(bf16) for s in range(2)
        ]
        far = nt(rows[0], w_ref[1]) + nt(rows[1], w_ref[2])
        normal = columns_of(sums_ref, 2 + dim // width, dim // width)
        gain = jnp.sum(vec[0:8], axis=0, keepdims=True) + jnp.sum(
            far * normal, axis=0, keepdims=True
        )
        offset = jnp.sum(vec[8:16], axis=0, keepdims=True) + SPAN * jnp.sum(
            far, axis=0, keepdims=True
        )
        low = to_low(jnp.concatenate([gain, offset, jnp.zeros((6, dim), f32)]), dim)
        theirs_ref[half:] = low
        mine_ref[half:] = low


def pair_kernel(a_ref, b_ref, out_ref):
    dim = a_ref.shape[1]
    rows = a_ref.shape[0] - 16
    out_ref[:rows] = (a_ref[:rows].astype(f32) + b_ref[:rows].astype(f32)).astype(bf16)
    out_ref[rows:] = to_low(from_low(a_ref[rows:], dim) + from_low(b_ref[rows:], dim), dim)


def extra_kernel(a_ref, b_ref, w_ref, out_ref):
    own = ((a_ref[0] + b_ref[0]) * (1.0 / SPAN)).astype(bf16)
    out_ref[...] = nt(own[0], w_ref[1]) + nt(own[1], w_ref[2])


def piece_kernel(mine_ref, got_ref, near_ref, far_ref, back_ref, up_ref, out_ref):
    dim = near_ref.shape[1]
    hidden = up_ref.shape[1]
    rows, cols = mine_ref.shape
    out_ref[:rows] = (mine_ref[...].astype(f32) + got_ref[...].astype(f32)).astype(bf16)
    last = near_ref.shape[0] - 16
    first = (from_low(near_ref[last:], dim) + from_low(far_ref[last:], dim))[:2]
    vectors = [first]
    for k in range(4):
        vectors.append(jnp.sum(back_ref[8 * k : 8 * k + 8], axis=0, keepdims=True))
    up = jnp.sum(up_ref[...], axis=0, keepdims=True)
    if hidden < dim:
        up = jnp.concatenate([up, jnp.zeros((1, dim - hidden), f32)], axis=1)
    vectors += [up, jnp.zeros((1, dim), f32)]
    out_ref[rows:] = to_low(jnp.concatenate(vectors), cols)


def merge_kernel(dim, a_ref, b_ref, out_ref):
    cols = a_ref.shape[1]
    rows = a_ref.shape[0] - 16 * (dim // cols)
    out_ref[:rows] = a_ref[:rows]
    out_ref[rows : 2 * rows] = b_ref[:rows]
    out_ref[2 * rows :] = to_low(from_low(a_ref[rows:], dim) + from_low(b_ref[rows:], dim), cols)


def last_kernel(
    pos_ref,
    own_ref,
    far_ref,
    other_ref,
    other_far_ref,
    extra_ref,
    tok_ref,
    low_ref,
    gain_ref,
    out_ref,
):
    step = pl.program_id(0)
    half = step // (pl.num_programs(0) // 2)
    e = two_halves((own_ref, far_ref, other_ref, other_far_ref), half, pos_ref[1])
    per = e.shape[0] // SPAN
    pieces = []
    for i in range(per):
        pieces.append(e[i * SPAN : (i + 1) * SPAN] + extra_ref[pl.ds(step * per + i, 1)])
    e = jnp.concatenate(pieces)
    n, r = normed(tok_ref[...].astype(f32))
    out_ref[...] = (low_ref[...].astype(f32) + norm_back(e, n, r, gain_ref[...])).astype(bf16)


def add_kernel(parts, a_ref, b_ref, *out_refs):
    size = a_ref.shape[0] // parts
    for k in range(parts):
        at = slice(k * size, (k + 1) * size)
        out_refs[k][...] = (a_ref[at].astype(f32) + b_ref[at].astype(f32)).astype(bf16)


def slot_kernel(a_ref, b_ref, out_ref):
    out_ref[...] = a_ref[: out_ref.shape[0]] + b_ref[...]


def spacer_kernel(x_ref, out_ref):
    out_ref[...] = x_ref[...] * 0.5


def concat_kernel(a_ref, b_ref, out_ref):
    rows = a_ref.shape[0]
    out_ref[:rows] = a_ref[...]
    out_ref[rows:] = b_ref[...]


def output_kernel(
    pos_ref, own_ref, far_ref, other_ref, other_far_ref, mid_ref, b_ref, out_ref
):
    half = pl.program_id(0) // (pl.num_programs(0) // 2)
    e = two_halves((own_ref, far_ref, other_ref, other_far_ref), half, pos_ref[1])
    out_ref[...] = (mid_ref[...] + e + b_ref[...]).astype(bf16)


def feed_unpack_kernel(count, at_ref, near_ref, far_ref, down_ref, up_ref):
    rows = 2 * near_ref.shape[0] // count
    part = count // 2
    top = at_ref[0] // part
    low = at_ref[0] % part
    for step, out_ref in enumerate((down_ref, up_ref)):

        @pl.when(pl.program_id(0) == step)
        def _():
            for k in range(part):
                at = pl.ds(pl.multiple_of((k ^ low) * rows, rows), rows)
                x = jnp.where(top == step, near_ref[at], far_ref[at])
                out_ref[k * rows : (k + 1) * rows] = x.astype(f32)


def rest_unpack_kernel(
    count, dim, at_ref, near_ref, far_ref, spare_ref, qkv_ref, out_ref, vec_ref, scratch
):
    cols = near_ref.shape[1]
    last = near_ref.shape[0] - 16 * (dim // cols)
    rows = 2 * last // count
    width = qkv_ref.shape[2]
    part = count // 2
    top = at_ref[0] // part
    low = at_ref[0] % part
    for k in range(count):
        start = pl.multiple_of(((k % part) ^ low) * rows, rows)
        is_near = top == k // part
        x = jnp.where(is_near, near_ref[pl.ds(start, rows)], far_ref[pl.ds(start, rows)])
        x = x.astype(f32)
        for s in range(3):
            qkv_ref[s, k * rows : (k + 1) * rows] = x[:, s * width : (s + 1) * width]
        scratch[k * rows : (k + 1) * rows] = x[:, 3 * width :]
    out_ref[...] = scratch[...].T
    vec_ref[...] = from_low(near_ref[last:], dim) + from_low(far_ref[last:], dim)


def build(n_dp, n_mp):
    def swap(x, axis, mask, label):
        n = n_dp if axis == "dp" else n_mp
        with jax.named_scope(label):
            return lax.ppermute(x, axis, [(i, i ^ mask) for i in range(n)])

    def pick(x, index, rows):
        return lax.dynamic_slice_in_dim(x, index * rows, rows, 0)

    def halves(x, mask, axis):
        bit = jnp.where((lax.axis_index(axis) & mask) == 0, 0, 1)
        size = x.shape[0] // 2
        return pick(x, 1 - bit, size), pick(x, bit, size)

    def after(x, *others):
        return lax.optimization_barrier((x, others))[0]

    far_masks = masks_of(n_mp)[1:]
    dp_masks = masks_of(n_dp)
    feed_masks = [dp_masks[1], dp_masks[0]] + dp_masks[2:]

    class Line:
        def __init__(self):
            self.last = ()

        def __call__(self, work, *inputs):
            if self.last:
                inputs = after(inputs, *self.last)
            result = work(*inputs)
            first = result[-1] if isinstance(result, (tuple, list)) else result
            self.last = (first,)
            return result

        def space(self, x=None):
            if x is not None:
                self.spare = x
            self.spare = self(spacer, self.spare)

    def add_parts(parts, a, b):
        part = jax.ShapeDtypeStruct((a.shape[0] // parts, *a.shape[1:]), bf16)
        return pl.pallas_call(
            functools.partial(add_kernel, parts),
            out_shape=(part,) * parts,
            in_specs=[VMEM, VMEM],
            out_specs=(VMEM,) * parts,
            compiler_params=params(16),
            cost_estimate=cost(),
            name="add",
        )(a, b)

    def add_low(a, b):
        return add_parts(1, a, b)[0]

    def spacer(x):
        return pl.pallas_call(
            spacer_kernel,
            out_shape=jax.ShapeDtypeStruct(x.shape, x.dtype),
            in_specs=[VMEM],
            out_specs=VMEM,
            compiler_params=params(16),
            cost_estimate=cost(),
            name="spacer",
        )(x)

    def split_sum(bit, mine, got):
        size = mine.shape[0] // 2
        half = jax.ShapeDtypeStruct((size, mine.shape[1]), bf16)
        return pl.pallas_call(
            split_kernel,
            out_shape=(half, half),
            in_specs=[SMEM, VMEM, VMEM],
            out_specs=(VMEM, VMEM),
            compiler_params=params(16),
            cost_estimate=cost(),
            name="split",
        )(bit, mine, got)

    def bit_of(mask):
        return jnp.where((lax.axis_index("dp") & mask) == 0, 0, 1).astype(i32)[None]

    class Scatter:
        def __init__(self, line, theirs, mine, masks, label):
            self.line, self.label = line, label
            self.rest = list(masks)
            self.mine = mine
            self.got = swap(theirs, "dp", self.rest.pop(0), label)

        def step(self):
            mask = self.rest.pop(0)
            theirs, self.mine = self.line(split_sum, bit_of(mask), self.mine, self.got)
            self.got = swap(theirs, "dp", mask, self.label)

    def per_device(
        tokens,
        ln1_gain,
        ln1_bias,
        w_qkv,
        w_out,
        b_out,
        ln2_gain,
        ln2_bias,
        w_up,
        b_up,
        w_down,
        b_down,
        cotangent,
    ):
        rows, dim = tokens.shape
        width = w_qkv.shape[2]
        hidden = w_up.shape[1]
        heads = width // HEAD_DIM
        blocks = rows // SPAN
        lanes = heads * SPAN
        group = LENGTH // rows
        entries = SPAN + group * blocks
        seq_masks = masks_of(group)
        me = lax.axis_index("mp")
        place = lax.axis_index("dp") % group
        first_bit = bit_of(dp_masks[0])
        pos = jnp.concatenate(
            [jnp.stack([me, me & 1, place]).astype(i32), bit_of(feed_masks[0])]
        )
        half = rows // 2
        tile = half // 2
        tiles = 4
        sds = jax.ShapeDtypeStruct

        def rolled(i, pos):
            return ((i + (1 - pos[1]) * (tiles // 2)) % tiles, 0)

        def theirs_row(i, pos):
            return (jnp.minimum(i, tiles // 2 - 1), 0)

        def mine_row(i, pos):
            return (jnp.maximum(i - tiles // 2, 0), 0)

        def half_rolled(i, pos):
            return (jnp.where(i == 0, 1 - pos[1], pos[1]), 0)

        def whole(*_):
            return (0, 0)

        def by_row(i, *_):
            return (i, 0)

        def zeros(n):
            return lambda *_: (0,) * n

        def block(shape, index):
            return pl.BlockSpec(shape, index)

        def plain(kernel, name, in_specs, out_shape, scratch=()):
            return pl.pallas_call(
                kernel,
                out_shape=out_shape,
                in_specs=in_specs,
                out_specs=tuple(VMEM for _ in out_shape),
                scratch_shapes=list(scratch),
                compiler_params=params(24),
                cost_estimate=cost(),
                name=name,
            )

        def gridded(
            kernel, name, grid, in_specs, out_specs, out_shape, scratch=(), mib=60, aliases=None
        ):
            return pl.pallas_call(
                kernel,
                grid_spec=pltpu.PrefetchScalarGridSpec(
                    num_scalar_prefetch=1,
                    grid=(grid,),
                    in_specs=in_specs,
                    out_specs=out_specs,
                    scratch_shapes=list(scratch),
                ),
                out_shape=out_shape,
                input_output_aliases=aliases or {},
                compiler_params=params(mib),
                cost_estimate=cost(),
                name=name,
            )

        row_block = block((tile, dim), rolled)
        row_vector = block((1, dim), whole)
        tile_block = block((tile, dim), by_row)
        one_tile = block((tile, dim), whole)

        project = plain(
            functools.partial(project_kernel, tile),
            "project",
            [VMEM] * 4,
            (
                sds((rows, dim), bf16),
                sds((3, rows, width), bf16),
                sds((2 + 2 * (dim // width), blocks, width), f32),
            ),
            [pltpu.VMEM((dim, 3 * width), bf16)],
        )
        local = plain(
            local_kernel,
            "local",
            [VMEM],
            (sds((blocks, SPAN, lanes), f32), sds((blocks, 2, lanes), f32)),
        )
        attend = plain(
            attend_kernel,
            "attend",
            [SMEM] + [VMEM] * 4,
            (sds((blocks, entries, lanes), f32), sds((rows, width), bf16)),
        )
        feed = gridded(
            functools.partial(feed_kernel, n_mp),
            "feed",
            tiles,
            [row_block]
            + [block((tile, width), rolled)] * n_mp
            + [block((width, dim), whole)] * n_mp
            + [row_vector] * 3
            + [
                block((dim, hidden), whole),
                block((1, hidden), whole),
                block((hidden, dim), whole),
                row_block,
            ],
            [
                row_block,
                row_block,
                block((tile, hidden), rolled),
                block((tile, hidden), rolled),
                block((tile, dim), theirs_row),
                block((tile, dim), mine_row),
                block((8, hidden), whole),
            ],
            (
                sds((rows, dim), f32),
                sds((rows, dim), bf16),
                sds((rows, hidden), bf16),
                sds((rows, hidden), bf16),
                sds((half, dim), bf16),
                sds((half, dim), bf16),
                sds((8, hidden), f32),
            ),
            [pltpu.VMEM((dim, dim), bf16)],
        )
        half_rows = block((half, dim), half_rolled)
        half_hidden = block((half, hidden), half_rolled)
        weights = gridded(
            weights_kernel,
            "weights",
            2,
            [half_hidden, half_rows, half_hidden, half_rows, block((hidden, dim), whole)],
            [block((half, dim), whole)] * 2 + [block((hidden, dim), whole)] * 2,
            (
                sds((half, dim), bf16),
                sds((half, dim), bf16),
                sds((hidden, dim), bf16),
                sds((hidden, dim), bf16),
            ),
            [pltpu.VMEM((hidden, dim), f32), pltpu.VMEM((dim, hidden), f32)],
        )
        rest_weights = plain(
            rest_kernel,
            "rest_weights",
            [SMEM] + [VMEM] * 6,
            (sds((dim // 2, 4 * width), bf16), sds((dim // 2, 4 * width), bf16)),
        )
        slot_shape = (group, 2, blocks, width)
        sums_shape = (group, 2 + 2 * (dim // width), blocks, width)
        back = gridded(
            back_kernel,
            "back",
            2,
            [block((half, dim), whole)] * 4
            + [
                block((half, dim), by_row),
                block((half, dim), by_row),
                row_vector,
                block((width, dim), whole),
                block((3, half, width), lambda i, pos: (0, i, 0)),
                block((blocks // 2, entries, lanes), lambda i, pos: (i, 0, 0)),
                block(sums_shape, zeros(4)),
            ],
            [
                block((half, dim), by_row),
                block((half, 3 * width), by_row),
                block(slot_shape, zeros(4)),
                block((32, dim), whole),
            ],
            (
                sds((rows, dim), bf16),
                sds((rows, 3 * width), bf16),
                sds(slot_shape, f32),
                sds((32, dim), f32),
            ),
        )
        first_block = block((half + 16, dim), whole)
        first_grad = gridded(
            first_kernel,
            "first",
            tiles,
            [
                block((tile, 3 * width), rolled),
                block(slot_shape, zeros(4)),
                block(sums_shape, zeros(4)),
                block((3, dim, width), zeros(3)),
                row_block,
            ],
            [first_block, first_block],
            (sds((half + 16, dim), bf16), sds((half + 16, dim), bf16)),
            [pltpu.VMEM((dim, 3 * width), bf16), pltpu.VMEM((16, dim), f32)],
        )
        def own_tile(i, pos):
            return (jnp.clip(i - pos[1] * (tiles // 2), 0, tiles // 2 - 1), 0)

        def other_tile(i, pos):
            return (jnp.clip(i - (1 - pos[1]) * (tiles // 2), 0, tiles // 2 - 1), 0)

        terms_specs = [block((tile, dim), own_tile)] * 2 + [block((tile, dim), other_tile)] * 2
        last = gridded(
            last_kernel,
            "last",
            tiles,
            terms_specs + [block((blocks, dim), whole), tile_block, tile_block, row_vector],
            tile_block,
            sds((rows, dim), bf16),
        )
        output_sum = gridded(
            output_kernel,
            "output",
            tiles,
            terms_specs + [tile_block, row_vector],
            tile_block,
            sds((rows, dim), bf16),
        )
        feed_unpack = gridded(
            functools.partial(feed_unpack_kernel, n_dp),
            "feed_unpack",
            2,
            [block((hidden, dim), whole)] * 2,
            [block((hidden, dim), whole)] * 2,
            (sds((hidden, dim), f32), sds((hidden, dim), f32)),
        )
        rest_unpack = plain(
            functools.partial(rest_unpack_kernel, n_dp, dim),
            "rest_unpack",
            [SMEM, VMEM, VMEM, VMEM],
            (sds((3, dim, width), f32), sds((width, dim), f32), sds((8, dim), f32)),
            [pltpu.VMEM((dim, width), f32)],
        )

        def like(kernel, name, shape, dtype, *operands):
            specs = [VMEM] * len(operands)
            return plain(kernel, name, specs, (sds(shape, dtype),))(*operands)[0]

        def pair(a, b):
            return like(pair_kernel, "pair", a.shape, bf16, a, b)

        def slot_add(a, b):
            return like(slot_kernel, "slots", b.shape, f32, a, b)

        def extra_of(a, b, w):
            return like(extra_kernel, "extra", (blocks, dim), f32, a, b, w)

        def concat(a, b):
            return like(concat_kernel, "concat", (2 * a.shape[0], a.shape[1]), bf16, a, b)

        def pl_add(a, b):
            return like(slot_kernel, "plus", a.shape, f32, a, b)

        vec_rows = 16 * (dim // (4 * width))

        def piece_of(mine, *operands):
            shape = (mine.shape[0] + vec_rows, 4 * width)
            return like(piece_kernel, "piece", shape, bf16, mine, *operands)

        def merge(a, b):
            shape = (2 * a.shape[0] - vec_rows, 4 * width)
            return like(functools.partial(merge_kernel, dim), "merge", shape, bf16, a, b)

        def place_of(masks):
            at = jnp.zeros((1,), i32)
            for m in masks:
                at = at * 2 + bit_of(m)
            return at


        def wait(*arrived):
            return line(lambda *x: x, *arrived)

        def near_sum(total, label):
            for m in far_masks[:-1]:
                total = line(add_low, total, swap(total, "mp", m, label))
            return total

        last_far = far_masks[-1]

        line = Line()

        out_slots = {0: w_out}
        for m in far_masks:
            out_slots.update(
                {j ^ m: swap(x, "mp", m, "gather_w_out") for j, x in list(out_slots.items())}
            )
        line.spare = ln1_gain[None]
        first, qkv, summary = line(project, tokens, ln1_gain[None], ln1_bias[None], w_qkv)
        out_list = list(out_slots.items())
        sums = after(summary, *[x for _, x in out_list])[None]
        for i, m in enumerate(seq_masks):
            got = swap(sums, "dp", m, "summaries")
            if i == 0:
                exps, stats = line(local, qkv)
                for j, x in out_list:
                    out_slots[j ^ 1] = swap(after(x, stats), "mp", 1, "gather_w_out")
            sums = line(lambda a, b: jnp.concatenate([a, b]), sums, got)
        probs, attended = line(attend, place[None].astype(i32), qkv, exps, stats, sums)

        att_slots = {0: attended}
        for m in far_masks:
            att_slots.update(
                {j ^ m: swap(x, "mp", m, "gather_attended") for j, x in list(att_slots.items())}
            )
        for j, x in list(att_slots.items()):
            att_slots[j ^ 1] = swap(x, "mp", 1, "gather_attended")
        mid, second, active, grad_upper, theirs, mine, up_vec = line(
            feed,
            pos,
            tokens,
            *[att_slots[j] for j in range(n_mp)],
            *[out_slots[j] for j in range(n_mp)],
            b_out[None],
            ln2_gain[None],
            ln2_bias[None],
            w_up,
            b_up[None],
            w_down,
            cotangent,
        )

        total = near_sum(line(add_low, mine, swap(theirs, "mp", 1, "sum_second")), "sum_second")
        far = swap(total, "mp", last_far, "sum_second")
        other = swap(total, "mp", 1, "sum_second")
        out_theirs, out_mine, theirs, mine = line(
            weights, pos, active, second, grad_upper, cotangent, w_down
        )
        feed_sum = Scatter(line, theirs, mine, feed_masks, "feed_weights")
        out_got = swap(out_theirs, "mp", 1, "sum_output")
        (far,) = wait(far)
        other_far = swap(far, "mp", 1, "sum_second")
        out_total = near_sum(line(add_low, out_mine, out_got), "sum_output")
        out_far = swap(out_total, "mp", last_far, "sum_output")
        out_other = swap(out_total, "mp", 1, "sum_output")
        grad_low, gqkv, back_vec, slot_grad = line(
            lambda *a: (lambda r: (r[0], r[1], r[3], r[2]))(back(*a)),
            pos,
            total,
            far,
            other,
            other_far,
            mid,
            cotangent,
            ln2_gain[None],
            w_out,
            qkv,
            probs,
            sums,
        )

        following = list(reversed(seq_masks))
        slot_part = slot_grad
        slot_got = swap(slot_part[following[0] :], "dp", following[0], "sum_slots")
        (out_other,) = wait(out_other)
        theirs, mine = line(
            rest_weights, first_bit, first, gqkv, grad_low, attended, slot_grad, sums
        )
        rest_sum = Scatter(line, theirs, mine, dp_masks, "rest_weights")
        feed_sum.step()
        for low in following[1:]:
            slot_part = line(slot_add, slot_part, slot_got)
            slot_got = swap(slot_part[low:], "dp", low, "sum_slots")
        (out_far,) = wait(out_far)
        out_other_far = swap(out_far, "mp", 1, "sum_output")
        theirs, mine = line(first_grad, pos, gqkv, slot_grad, sums, w_qkv, tokens)
        got = swap(theirs, "mp", 1, "sum_first")
        (out_other_far,) = wait(out_other_far)
        extra = line(extra_of, slot_part, slot_got, w_qkv)
        extra_got = swap(extra, "mp", 1, "sum_extra")
        total = line(pair, mine, got)
        for m in far_masks[:-1]:
            total = line(pair, total, swap(total, "mp", m, "sum_first"))
        far = swap(total, "mp", last_far, "sum_first")
        rest_sum.step()
        for m in far_masks:
            extra = line(pl_add, extra, extra_got)
            extra_got = swap(extra, "mp", m, "sum_extra")
        feed_sum.step()
        output = line(
            output_sum, pos, out_total, out_far, out_other, out_other_far, mid, b_down[None]
        )
        for m in dp_masks[2:]:
            rest_sum.step()
        line.space()
        for m in feed_masks[3:]:
            feed_sum.step()
        feed_all = line(add_low, feed_sum.mine, feed_sum.got)
        feed_got = swap(feed_all, "dp", feed_masks[-1], "feed_weights")
        (far,) = wait(far)
        other = swap(after(total, far), "mp", 1, "sum_first")
        other_far = swap(far, "mp", 1, "sum_first")
        rest_all = line(
            piece_of, rest_sum.mine, rest_sum.got, total, far, back_vec, up_vec
        )
        rest_got = swap(rest_all, "dp", dp_masks[-1], "rest_weights")
        extra = line(pl_add, extra, extra_got)
        grad_tokens = line(
            last, pos, total, far, other, other_far, extra, tokens, grad_low, ln1_gain[None]
        )
        feed_next = list(reversed(feed_masks))[1:]
        rest_next = list(reversed(dp_masks))[1:]
        for feed_mask, rest_mask in zip(feed_next, rest_next):
            feed_all = line(concat, feed_all, feed_got)
            feed_got = swap(feed_all, "dp", feed_mask, "feed_weights")
            rest_all = line(merge, rest_all, rest_got)
            rest_got = swap(rest_all, "dp", rest_mask, "rest_weights")
            line.space()
        grad_w_qkv, grad_w_out, vectors = line(
            rest_unpack, place_of(dp_masks), rest_all, rest_got, line.spare
        )
        grad_w_down, grad_w_up = line(feed_unpack, place_of(feed_masks), feed_all, feed_got)
        return (
            output,
            grad_tokens,
            vectors[0],
            vectors[1],
            grad_w_qkv,
            grad_w_out,
            vectors[2],
            vectors[3],
            vectors[4],
            grad_w_up.reshape(dim, hidden),
            vectors[6, :hidden],
            grad_w_down,
            vectors[5],
        )

    return per_device


def solution(mesh):
    return jax.shard_map(
        build(mesh.shape["dp"], mesh.shape["mp"]),
        mesh=mesh,
        in_specs=(
            P("dp", None),
            P(),
            P(),
            P(None, None, "mp"),
            P("mp", None),
            P(),
            P(),
            P(),
            P(None, "mp"),
            P("mp"),
            P("mp", None),
            P(),
            P("dp", None),
        ),
        out_specs=(
            P("dp", None),
            P("dp", None),
            P(),
            P(),
            P(None, None, "mp"),
            P("mp", None),
            P(),
            P(),
            P(),
            P(None, "mp"),
            P("mp"),
            P("mp", None),
            P(),
        ),
        check_vma=False,
    )
```

time: 171 us -> 160 us (0.936)
  Pallas kernels: 0 us -> 69 us
  other arithmetic: 32 us -> 0.59 us
  matrix products: 25.4 us -> 0 us
  local copies, waits for them, and re-layouts: 27.9 us -> 15.1 us
  waiting for transfers between devices: 46 us -> 36.8 us
    pallas_call x0 -> x32, Pallas kernels: none -> 69 us  [the longest x11 41.2 us: __call__(): result = work(*inputs)]
    dot_general x27 -> x0, matrix products: 25.4 us -> none  [the longest x1 3.85 us: per_device(): jnp.einsum('ste,sde->td', grad_qkv, w_qkv, preferred_element_type=f32)]
    reduce_sum x12 -> x0, other arithmetic: 13.4 us -> none  [the longest x4 4.04 us: layer_norm(): center = values - jnp.mean(values, axis=-1, keepdims=True)]
    ppermute x36, waiting for transfers between devices: 46 us -> 36.8 us  [swap(): return lax.ppermute(x, axis, [(i, i ^ mask) for i in range(n)])]
    another operation x14 -> x0, local copies, waits for them, and re-layouts: 8.81 us -> none  [the longest x7 6.88 us: per_device(): jnp.stack([heads_last(grad_query.astype(bf16)), heads_last(grad_keys.asty...]
    convert_element_type x17 -> x0, other arithmetic: 8.05 us -> none  [the longest x6 2.67 us: reduce_dp(): x = (pick(x, bit, half).astype(f32) + got.astype(f32)).astype(bf16)]
    unnamed x100 -> x76, local copies, waits for them, and re-layouts: 9.04 us -> 14.5 us
    select_n x6 -> x0, other arithmetic: 5.08 us -> none  [join(): jnp.where(bit == 0, jnp.concatenate([own, other]), jnp.concatenate([other...]
  transfers between devices with their start and end apart: 36 -> 36, of which waited for: 18 -> 14; matrix products, arithmetic and copies ran while one was open for 37% -> 1% of each run, Pallas kernels for 0% -> 34%
where the time goes in v2:
time: 160 us; the launch traced here: 159 us
  Pallas kernels  69 us (43%)
  waiting for transfers between devices  36.8 us (23%)
  starting transfers between devices  36.7 us (23%)
  local copies, waits for them, and re-layouts  15.1 us (9%)
    pallas_call x11, Pallas kernels, __call__(): result = work(*inputs)  41.2 us
    ppermute x36, waiting for transfers between devices, swap(): return lax.ppermute(x, axis, [(i, i ^ mask) for i in range(n)])  36.8 us
    ppermute x36, starting transfers between devices, swap(): return lax.ppermute(x, axis, [(i, i ^ mask) for i in range(n)])  36.7 us
    unnamed x76, local copies, waits for them, and re-layouts  14.5 us
    pallas_call x10, Pallas kernels, like(): return plain(kernel, name, specs, (sds(shape, dtype),))(*operands)[0]  11.9 us
    pallas_call x1, Pallas kernels, per_device(): back(*a)  8.67 us
    pallas_call x4, Pallas kernels, split_sum(): pl.pallas_call(split_kernel, out_shape=(half, half), in_specs=[SMEM, VMEM...  4.63 us
  transfers between devices with their start and end apart: 36, of which 14 were waited for; matrix products, arithmetic and copies ran while one was open for 1% of the time, Pallas kernels for 34%

profile of v2, /device:TPU:0, one launch (start us, length us, event | category | flops | bytes accessed | tf_op | source)
XLA Modules:
  0.0 159.2 jit_solution(105484622648341987)
XLA Ops:
  0.6 3.0 %collective-permute-start = (bf16[128,512]{1,0:T(8,128)(2,1)}, bf16[128,512]{1,0:T(8,128)(2,1)S(1)}, u32[]{:S(2)}, u32[]{:S(2)}) collective-permute-start(bf16[128,512]{1,0:T(8,128)(2,1)} %wo_ref), channel_id=1, source_target_pairs={{0,2},{1,3},{2,0},{3,1},{4,6},{5,7},{6,4},{7,5},{8,10},{9,11},{10,... | collective-permute-start | bytes 393224 | tf_op jit(solution)/shard_map/gather_w_out/ppermute | solution.py:557
  3.7 1.2 copy-done.3
  4.9 1.0 copy-done.5
  5.9 0.7 copy-done.9
  6.6 0.7 copy-done.10
  7.3 1.5 project.1
  8.8 1.6 collective-permute-start.1
  10.8 2.0 %collective-permute-done.1 = f32[1,10,8,128]{3,2,1,0:T(8,128)S(1)} collective-permute-done((f32[1,10,8,128]{3,2,1,0:T(8,128)S(1)}, f32[1,10,8,128]{3,2,1,0:T(8,128)S(1)}, u32[]{:S(2)}, u32[]{:S(2)}) %collective-permute-start.1) | collective-permute-done | bytes 40992 | tf_op jit(solution)/shard_map/summaries/ppermute | solution.py:557
  12.9 1.6 %collective-permute-start.2 = (f32[2,10,8,128]{3,2,1,0:T(8,128)S(1)}, f32[2,10,8,128]{3,2,1,0:T(8,128)S(1)}, u32[]{:S(2)}, u32[]{:S(2)}) collective-permute-start(f32[2,10,8,128]{3,2,1,0:T(8,128)S(1)} %constant_dynamic-update-slice_fusion), channel_id=1, source_target_pairs={{0,8},{4,12},{8,0},{12,4},{16,24},{20,28},{24,16},{28,20},{1,9},{5... | collective-permute-start | bytes 245768 | tf_op jit(solution)/shard_map/summaries/ppermute | solution.py:557
  14.5 2.9 %collective-permute-done.2 = f32[2,10,8,128]{3,2,1,0:T(8,128)S(1)} collective-permute-done((f32[2,10,8,128]{3,2,1,0:T(8,128)S(1)}, f32[2,10,8,128]{3,2,1,0:T(8,128)S(1)}, u32[]{:S(2)}, u32[]{:S(2)}) %collective-permute-start.2) | collective-permute-done | bytes 81952 | tf_op jit(solution)/shard_map/summaries/ppermute | solution.py:557
  17.4 1.5 attend.1
  19.0 1.1 copy-done.12
  20.3 6.1 %collective-permute-done.4.refs_2_ = bf16[1024,128]{1,0:T(8,128)(2,1)S(1)} collective-permute-done((bf16[1024,128]{1,0:T(8,128)(2,1)S(1)}, bf16[1024,128]{1,0:T(8,128)(2,1)S(1)}, u32[]{:S(2)}, u32[]{:S(2)}) %collective-permute-start.4) | collective-permute-done | bytes 262176 | tf_op jit(solution)/shard_map/gather_attended/ppermute | solution.py:557
  29.2 9.8 %feed.1 = (f32[1024,512]{1,0:T(8,128)}, bf16[1024,512]{1,0:T(8,128)(2,1)}, bf16[1024,512]{1,0:T(8,128)(2,1)}, bf16[1024,512]{1,0:T(8,128)(2,1)}, bf16[512,512]{1...) custom-call(s32[4]{0:T(128)} %pad_add_fusion.pos_ref, bf16[1024,512]{1,0:T(8,128)(2,1)} %tok_ref.4, ...), custom_call_target="tpu_custom_call" | custom-call | flops 115000000512 | bytes 1 | tf_op jit(solution)/shard_map/feed/pallas_call | solution.py:581
  39.2 2.0 %collective-permute-done.8.b_ref = bf16[512,512]{1,0:T(8,128)(2,1)S(1)} collective-permute-done((bf16[512,512]{1,0:T(8,128)(2,1)}, bf16[512,512]{1,0:T(8,128)(2,1)S(1)}, u32[]{:S(2)}, u32[]{:S(2)}) %collective-permute-start.8) | collective-permute-done | bytes 524320 | tf_op jit(solution)/shard_map/sum_second/ppermute | solution.py:557
  41.2 1.0 copy-done.17
  42.7 6.3 %weights.1 = (bf16[512,512]{1,0:T(8,128)(2,1)}, bf16[512,512]{1,0:T(8,128)(2,1)}, bf16[512,512]{1,0:T(8,128)(2,1)}, bf16[512,512]{1,0:T(8,128)(2,1)}) custom-call(s32[4]{0:T(128)} %pad_add_fusion.pos_ref, bf16[1024,512]{1,0:T(8,128)(2,1)} %get-tuple-element.232.active_ref, bf16[1024,512]{1,0:T(8,128)(2,1)} %get-tuple-element.233.second_ref, ...), custom_call_target="tpu_custom_call" | custom-call | flops 115000000512 | bytes 1 | tf_op jit(solution)/shard_map/weights/pallas_call | solution.py:581
  49.5 1.8 %collective-permute-start.15 = (bf16[512,512]{1,0:T(8,128)(2,1)}, bf16[512,512]{1,0:T(8,128)(2,1)}, u32[]{:S(2)}, u32[]{:S(2)}) collective-permute-start(bf16[512,512]{1,0:T(8,128)(2,1)} %get-tuple-element.258), channel_id=1, source_target_pairs={{0,8},{4,12},{8,0},{12,4},{16,24},{20,28},{24,16},{28,20},{1,9},{5... | collective-permute-start | bytes 1572872 | tf_op jit(solution)/shard_map/feed_weights/ppermute | solution.py:557
  51.3 5.0 %collective-permute-done.10.far_ref = bf16[512,512]{1,0:T(8,128)(2,1)S(1)} collective-permute-done((bf16[512,512]{1,0:T(8,128)(2,1)S(1)}, bf16[512,512]{1,0:T(8,128)(2,1)S(1)}, u32[]{:S(2)}, u32[]{:S(2)}) %collective-permute-start.10) | collective-permute-done | bytes 524320 | tf_op jit(solution)/shard_map/sum_second/ppermute | solution.py:557
  56.4 1.2 copy-done.19
  57.6 0.9 add.31.own_ref
  59.2 0.8 copy-done.28
  60.1 8.7 %back.1 = (bf16[1024,512]{1,0:T(8,128)(2,1)}, bf16[1024,384]{1,0:T(8,128)(2,1)}, f32[4,2,8,128]{3,2,1,0:T(8,128)}, f32[32,512]{1,0:T(8,128)}) custom-call(s32[4]{0:T(128)} %pad_add_fusion.pos_ref, bf16[512,512]{1,0:T(8,128)(2,1)} %copy-done.4, bf16[512,512]{1,0:T(8,128)(2,1)} %copy-done.25, bf16[512,512]{1,0:T(8,128)(2,1)} %copy-done.27, ...), custom_call_target="tpu_custom_call" | custom-call | flops 115000000512 | bytes 1 | tf_op jit(solution)/shard_map/back/pallas_call | solution.py:1005
  68.8 0.8 copy-done.24
  69.6 0.8 copy-done.2
  70.3 1.2 copy-done.13
  71.6 1.1 copy-done.15
  72.7 1.8 %rest_weights.1 = (bf16[256,512]{1,0:T(8,128)(2,1)}, bf16[256,512]{1,0:T(8,128)(2,1)S(1)}) custom-call(s32[1]{0:T(128)} %bitcast.11.bit_ref, bf16[1024,512]{1,0:T(8,128)(2,1)S(1)} %get-tuple-element.264.first_ref, bf16[1024,384]{1,0:T(8,128)(2,1)S(1)} %copy-done.15, bf16[1024,512]{1,0:T(8,128)(2,1)S(1)} %copy-done.13, bf16[1024,128]{1,0:T(8,128)(2,1)S(1)} %copy-done.8, ...), custom_call_target="tpu_custom_call" | custom-call | flops 115000000512 | bytes 1 | tf_op jit(solution)/shard_map/rest_weights/pallas_call | solution.py:581
  74.5 1.8 %collective-permute-start.14 = (f32[2,2,8,128]{3,2,1,0:T(8,128)S(1)}, f32[2,2,8,128]{3,2,1,0:T(8,128)S(1)}, u32[]{:S(2)}, u32[]{:S(2)}) collective-permute-start(f32[2,2,8,128]{3,2,1,0:T(8,128)S(1)} %slice.27), channel_id=1, source_target_pairs={{0,8},{4,12},{8,0},{12,4},{16,24},{20,28},{24,16},{28,20},{1,9},{5... | collective-permute-start | bytes 49160 | tf_op jit(solution)/shard_map/sum_slots/ppermute | solution.py:557
  76.3 1.5 collective-permute-start.21
  77.8 1.9 %split.4 = (bf16[256,512]{1,0:T(8,128)(2,1)}, bf16[256,512]{1,0:T(8,128)(2,1)S(1)}) custom-call(s32[1]{0:T(128)} %bitcast.11.bit_ref, bf16[512,512]{1,0:T(8,128)(2,1)S(1)} %copy-done.18, bf16[512,512]{1,0:T(8,128)(2,1)} %collective-permute-done.15.b_ref), custom_call_target="tpu_custom_call" | custom-call | flops 115000000512 | bytes 1 | tf_op jit(solution)/shard_map/split/pallas_call | solution.py:620
  80.3 1.5 collective-permute-start.19
  81.9 5.6 %first.1 = (bf16[528,512]{1,0:T(8,128)(2,1)}, bf16[528,512]{1,0:T(8,128)(2,1)}) custom-call(s32[4]{0:T(128)} %pad_add_fusion.pos_ref, bf16[1024,384]{1,0:T(8,128)(2,1)} %get-tuple-element.279.gqkv_ref, f32[4,2,8,128]{3,2,1,0:T(8,128)} %get-tuple-element.280.slot_ref.a_ref, f32[4,10,8,128]{3,2,1,0:T(8,128)} %copy-done, bf16[3,512,128]{2,1,0:T(8,128)(2,1)} %w_ref.3, ...), custom_call_target="tpu_custom_call" | custom-call | flops 115000000512 | bytes 1 | tf_op jit(solution)/shard_map/first/pallas_call | solution.py:581
  87.6 2.6 %collective-permute-done.19.b_ref = f32[1,2,8,128]{3,2,1,0:T(8,128)S(1)} collective-permute-done((f32[1,2,8,128]{3,2,1,0:T(8,128)S(1)}, f32[1,2,8,128]{3,2,1,0:T(8,128)S(1)}, u32[]{:S(2)}, u32[]{:S(2)}) %collective-permute-start.19) | collective-permute-done | bytes 8224 | tf_op jit(solution)/shard_map/sum_slots/ppermute | solution.py:557
  90.2 0.8 extra.1.a_ref
  91.0 0.9 pair.1.near_ref.own_ref
  91.9 1.5 collective-permute-start.23
  93.4 1.0 split.5
  94.5 1.3 plus.2.a_ref
  96.3 1.7 %split.6 = (bf16[128,512]{1,0:T(8,128)(2,1)}, bf16[128,512]{1,0:T(8,128)(2,1)S(1)}) custom-call(s32[1]{0:T(128)} %bitcast.13.bit_ref, bf16[256,512]{1,0:T(8,128)(2,1)S(1)} %get-tuple-element.301.a_ref, bf16[256,512]{1,0:T(8,128)(2,1)} %collective-permute-done.18.b_ref), custom_call_target="tpu_custom_call" | custom-call | flops 115000000512 | bytes 1 | tf_op jit(solution)/shard_map/split/pallas_call | solution.py:620
  98.4 2.7 %collective-permute-start.24 = (bf16[128,512]{1,0:T(8,128)(2,1)}, bf16[128,512]{1,0:T(8,128)(2,1)}, u32[]{:S(2)}, u32[]{:S(2)}) collective-permute-start(bf16[128,512]{1,0:T(8,128)(2,1)} %get-tuple-element.311), channel_id=1, source_target_pairs={{0,16},{4,20},{8,24},{12,28},{16,0},{20,4},{24,8},{28,12},{1,17},{... | collective-permute-start | bytes 393224 | tf_op jit(solution)/shard_map/feed_weights/ppermute | solution.py:557
  101.0 4.9 %output.1 = bf16[1024,512]{1,0:T(8,128)(2,1)} custom-call(s32[4]{0:T(128)} %pad_add_fusion.pos_ref, bf16[512,512]{1,0:T(8,128)(2,1)} %add.31.own_ref, bf16[512,512]{1,0:T(8,128)(2,1)} %collective-permute-done.11.far_ref, bf16[512,512]{1,0:T(8,128)(2,1)} %copy-done.24, bf16[512,512]{1,0:T(8,128)(2,1)} %copy-done.26, f32[1024,512]{1,0:T(8,128)} %get-tuple-element.309.mid_ref, ...), custom_call_target="tpu_custom_call" | custom-call | flops 115000000512 | bytes 1 | tf_op jit(solution)/shard_map/output/pallas_call | solution.py:581
  106.7 0.9 collective-permute-start.29
  107.6 1.6 add.32.a_ref
  109.2 2.1 %collective-permute-start.31 = (bf16[128,512]{1,0:T(8,128)(2,1)}, bf16[128,512]{1,0:T(8,128)(2,1)}, u32[]{:S(2)}, u32[]{:S(2)}) collective-permute-start(bf16[128,512]{1,0:T(8,128)(2,1)} %add.32.a_ref), channel_id=1, source_target_pairs={{0,16},{4,20},{8,24},{12,28},{16,0},{20,4},{24,8},{28,12},{1,17},{... | collective-permute-start | bytes 393224 | tf_op jit(solution)/shard_map/feed_weights/ppermute | solution.py:557
  111.3 2.4 %collective-permute-done.29.got_ref = bf16[64,512]{1,0:T(8,128)(2,1)S(1)} collective-permute-done((bf16[64,512]{1,0:T(8,128)(2,1)S(1)}, bf16[64,512]{1,0:T(8,128)(2,1)S(1)}, u32[]{:S(2)}, u32[]{:S(2)}) %collective-permute-start.29) | collective-permute-done | bytes 65568 | tf_op jit(solution)/shard_map/rest_weights/ppermute | solution.py:557
  113.7 1.9 %piece.1.a_ref = bf16[80,512]{1,0:T(8,128)(2,1)} custom-call(bf16[64,512]{1,0:T(8,128)(2,1)S(1)} %get-tuple-element.324.mine_ref, bf16[64,512]{1,0:T(8,128)(2,1)S(1)} %collective-permute-done.29.got_ref, bf16[528,512]{1,0:T(8,128)(2,1)} %pair.1.near_ref.own_ref, bf16[528,512]{1,0:T(8,128)(2,1)} %collective-permute-done.23.far_ref, f32[32,512]{1,0:T(8,128)S(1)} %copy-done.20, ...), custom_call_target="tpu_custom_call" | custom-call | flops 115000000512 | bytes 1 | tf_op jit(solution)/shard_map/piece/pallas_call | solution.py:905
  115.6 0.7 plus.3.extra_ref
  116.9 0.8 collective-permute-done.26.other_ref
  117.7 0.8 copy-done.23
  118.5 5.6 %last.1 = bf16[1024,512]{1,0:T(8,128)(2,1)} custom-call(s32[4]{0:T(128)} %pad_add_fusion.pos_ref, bf16[528,512]{1,0:T(8,128)(2,1)} %pair.1.near_ref.own_ref, bf16[528,512]{1,0:T(8,128)(2,1)} %collective-permute-done.23.far_ref, bf16[528,512]{1,0:T(8,128)(2,1)} %copy-done.23, bf16[528,512]{1,0:T(8,128)(2,1)} %collective-permute-done.27.other_far_ref, ...), custom_call_target="tpu_custom_call" | custom-call | flops 115000000512 | bytes 1 | tf_op jit(solution)/shard_map/last/pallas_call | solution.py:581
  124.1 1.7 %concat.2.a_ref = bf16[256,512]{1,0:T(8,128)(2,1)} custom-call(bf16[128,512]{1,0:T(8,128)(2,1)} %add.32.a_ref, bf16[128,512]{1,0:T(8,128)(2,1)} %collective-permute-done.31.b_ref), custom_call_target="tpu_custom_call" | custom-call | flops 115000000512 | bytes 1 | tf_op jit(solution)/shard_map/concat/pallas_call | solution.py:905
  125.8 1.4 collective-permute-start.33
  127.2 1.6 %merge.2.a_ref = bf16[144,512]{1,0:T(8,128)(2,1)} custom-call(bf16[80,512]{1,0:T(8,128)(2,1)} %piece.1.a_ref, bf16[80,512]{1,0:T(8,128)(2,1)} %collective-permute-done.30.b_ref), custom_call_target="tpu_custom_call" | custom-call | flops 115000000512 | bytes 1 | tf_op jit(solution)/shard_map/merge/pallas_call | solution.py:905
  128.8 6.3 %collective-permute-start.32 = (bf16[144,512]{1,0:T(8,128)(2,1)}, bf16[144,512]{1,0:T(8,128)(2,1)}, u32[]{:S(2)}, u32[]{:S(2)}) collective-permute-start(bf16[144,512]{1,0:T(8,128)(2,1)} %merge.2.a_ref), channel_id=1, source_target_pairs={{0,8},{4,12},{8,0},{12,4},{16,24},{20,28},{24,16},{28,20},{1,9},{5... | collective-permute-start | bytes 442376 | tf_op jit(solution)/shard_map/rest_weights/ppermute | solution.py:557
  135.1 1.9 %concat.3.near_ref = bf16[512,512]{1,0:T(8,128)(2,1)} custom-call(bf16[256,512]{1,0:T(8,128)(2,1)} %concat.2.a_ref, bf16[256,512]{1,0:T(8,128)(2,1)} %collective-permute-done.33.b_ref), custom_call_target="tpu_custom_call" | custom-call | flops 115000000512 | bytes 1 | tf_op jit(solution)/shard_map/concat/pallas_call | solution.py:905
  136.9 2.3 %collective-permute-done.32.b_ref = bf16[144,512]{1,0:T(8,128)(2,1)} collective-permute-done((bf16[144,512]{1,0:T(8,128)(2,1)}, bf16[144,512]{1,0:T(8,128)(2,1)}, u32[]{:S(2)}, u32[]{:S(2)}) %collective-permute-start.32) | collective-permute-done | bytes 147488 | tf_op jit(solution)/shard_map/rest_weights/ppermute | solution.py:557
  139.2 1.0 merge.3.near_ref
  140.3 1.5 collective-permute-start.34
  141.7 3.3 %collective-permute-start.35 = (bf16[512,512]{1,0:T(8,128)(2,1)}, bf16[512,512]{1,0:T(8,128)(2,1)}, u32[]{:S(2)}, u32[]{:S(2)}) collective-permute-start(bf16[512,512]{1,0:T(8,128)(2,1)} %concat.3.near_ref), channel_id=1, source_target_pairs={{0,8},{4,12},{8,0},{12,4},{16,24},{20,28},{24,16},{28,20},{1,9},{5... | collective-permute-start | bytes 1572872 | tf_op jit(solution)/shard_map/feed_weights/ppermute | solution.py:557
  145.1 3.1 %collective-permute-done.34.far_ref = bf16[272,512]{1,0:T(8,128)(2,1)S(1)} collective-permute-done((bf16[272,512]{1,0:T(8,128)(2,1)S(1)}, bf16[272,512]{1,0:T(8,128)(2,1)S(1)}, u32[]{:S(2)}, u32[]{:S(2)}) %collective-permute-start.34) | collective-permute-done | bytes 278560 | tf_op jit(solution)/shard_map/rest_weights/ppermute | solution.py:557
  148.2 1.0 rest_unpack.1
  149.8 6.6 %collective-permute-done.35.far_ref = bf16[512,512]{1,0:T(8,128)(2,1)} collective-permute-done((bf16[512,512]{1,0:T(8,128)(2,1)}, bf16[512,512]{1,0:T(8,128)(2,1)}, u32[]{:S(2)}, u32[]{:S(2)}) %collective-permute-start.35) | collective-permute-done | bytes 524320 | tf_op jit(solution)/shard_map/feed_weights/ppermute | solution.py:557
  156.5 2.7 %feed_unpack.1 = (f32[512,512]{1,0:T(8,128)}, f32[512,512]{1,0:T(8,128)}) custom-call(s32[1]{0:T(128)S(6)} %add.23.at_ref, bf16[512,512]{1,0:T(8,128)(2,1)} %concat.3.near_ref, bf16[512,512]{1,0:T(8,128)(2,1)} %collective-permute-done.35.far_ref), custom_call_target="tpu_custom_call" | custom-call | flops 115000000512 | bytes 1 | tf_op jit(solution)/shard_map/feed_unpack/pallas_call | solution.py:581
  (122 shorter events, 9.1 us)
Async XLA Ops:
  0.6 8.1 %collective-permute-start = (bf16[128,512]{1,0:T(8,128)(2,1)}, bf16[128,512]{1,0:T(8,128)(2,1)S(1)}, u32[]{:S(2)}, u32[]{:S(2)}) collective-permute-start(bf16[128,512]{1,0:T(8,128)(2,1)} %wo_ref), channel_id=1, source_target_pairs={{0,2},{1,3},{2,0},{3,1},{4,6},{5,7},{6,4},{7,5},{8,10},{9,11},{10,... | collective-permute-start | bytes 393224 | tf_op jit(solution)/shard_map/gather_w_out/ppermute | solution.py:557
  3.7 1.2 copy-start.3
  4.9 1.0 copy-start.5
  8.7 8.6 %copy-start.14 = (bf16[3,1024,128]{2,1,0:T(8,128)(2,1)}, bf16[3,1024,128]{2,1,0:T(8,128)(2,1)S(1)}, u32[]{:S(2)}) copy-start(bf16[3,1024,128]{2,1,0:T(8,128)(2,1)S(1)} %get-tuple-element.254.qkv_ref) | copy-start | bytes 2359300
  8.8 2.0 %copy-start.33 = (bf16[128,512]{1,0:T(8,128)(2,1)}, bf16[128,512]{1,0:T(8,128)(2,1)S(1)}, u32[]{:S(2)}) copy-start(bf16[128,512]{1,0:T(8,128)(2,1)S(1)} %collective-permute-done.refs_6_) | copy-start | bytes 393220
  8.8 4.1 %collective-permute-start.1 = (f32[1,10,8,128]{3,2,1,0:T(8,128)S(1)}, f32[1,10,8,128]{3,2,1,0:T(8,128)S(1)}, u32[]{:S(2)}, u32[]{:S(2)}) collective-permute-start(f32[1,10,8,128]{3,2,1,0:T(8,128)S(1)} %bitcast.21), channel_id=1, source_target_pairs={{0,4},{4,0},{8,12},{12,8},{16,20},{20,16},{24,28},{28,24},{1,5},{5... | collective-permute-start | bytes 122888 | tf_op jit(solution)/shard_map/summaries/ppermute | solution.py:557
  12.9 4.5 %collective-permute-start.2 = (f32[2,10,8,128]{3,2,1,0:T(8,128)S(1)}, f32[2,10,8,128]{3,2,1,0:T(8,128)S(1)}, u32[]{:S(2)}, u32[]{:S(2)}) collective-permute-start(f32[2,10,8,128]{3,2,1,0:T(8,128)S(1)} %constant_dynamic-update-slice_fusion), channel_id=1, source_target_pairs={{0,8},{4,12},{8,0},{12,4},{16,24},{20,28},{24,16},{28,20},{1,9},{5... | collective-permute-start | bytes 245768 | tf_op jit(solution)/shard_map/summaries/ppermute | solution.py:557
  17.4 1.6 copy-start
  17.4 9.0 %copy-start.32 = (bf16[128,512]{1,0:T(8,128)(2,1)S(1)}, bf16[128,512]{1,0:T(8,128)(2,1)}, u32[]{:S(2)}) copy-start(bf16[128,512]{1,0:T(8,128)(2,1)} %wo_ref) | copy-start | bytes 393220
  17.4 9.5 %copy-start.34 = (bf16[128,512]{1,0:T(8,128)(2,1)S(1)}, bf16[128,512]{1,0:T(8,128)(2,1)}, u32[]{:S(2)}) copy-start(bf16[128,512]{1,0:T(8,128)(2,1)} %copy-done.33) | copy-start | bytes 393220
  19.0 1.1 copy-start.12
  20.0 8.3 %copy-start.7 = (bf16[1024,128]{1,0:T(8,128)(2,1)}, bf16[1024,128]{1,0:T(8,128)(2,1)S(1)}, u32[]{:S(2)}) copy-start(bf16[1024,128]{1,0:T(8,128)(2,1)S(1)} %get-tuple-element.267.refs_0_.att_ref) | copy-start | bytes 786436
  20.0 6.4 %collective-permute-start.4 = (bf16[1024,128]{1,0:T(8,128)(2,1)S(1)}, bf16[1024,128]{1,0:T(8,128)(2,1)S(1)}, u32[]{:S(2)}, u32[]{:S(2)}) collective-permute-start(bf16[1024,128]{1,0:T(8,128)(2,1)S(1)} %get-tuple-element.267.refs_0_.att_ref), channel_id=1, source_target_pairs={{0,2},{1,3},{2,0},{3,1},{4,6},{5,7},{6,4},{7,5},{8,10},{9,11},{10,... | collective-permute-start | bytes 786440 | tf_op jit(solution)/shard_map/gather_attended/ppermute | solution.py:557
  20.3 8.0 %collective-permute-start.3 = (bf16[1024,128]{1,0:T(8,128)(2,1)S(1)}, bf16[1024,128]{1,0:T(8,128)(2,1)S(1)}, u32[]{:S(2)}, u32[]{:S(2)}) collective-permute-start(bf16[1024,128]{1,0:T(8,128)(2,1)S(1)} %get-tuple-element.267.refs_0_.att_ref), channel_id=1, source_target_pairs={{0,1},{1,0},{2,3},{3,2},{4,5},{5,4},{6,7},{7,6},{8,9},{9,8},{10,11... | collective-permute-start | bytes 786440 | tf_op jit(solution)/shard_map/gather_attended/ppermute | solution.py:557
  26.4 1.9 %copy-start.29 = (bf16[1024,128]{1,0:T(8,128)(2,1)}, bf16[1024,128]{1,0:T(8,128)(2,1)S(1)}, u32[]{:S(2)}) copy-start(bf16[1024,128]{1,0:T(8,128)(2,1)S(1)} %collective-permute-done.4.refs_2_) | copy-start | bytes 786436
  26.4 1.9 %collective-permute-start.5 = (bf16[1024,128]{1,0:T(8,128)(2,1)S(1)}, bf16[1024,128]{1,0:T(8,128)(2,1)S(1)}, u32[]{:S(2)}, u32[]{:S(2)}) collective-permute-start(bf16[1024,128]{1,0:T(8,128)(2,1)S(1)} %collective-permute-done.4.refs_2_), channel_id=1, source_target_pairs={{0,1},{1,0},{2,3},{3,2},{4,5},{5,4},{6,7},{7,6},{8,9},{9,8},{10,11... | collective-permute-start | bytes 786440 | tf_op jit(solution)/shard_map/gather_attended/ppermute | solution.py:557
  26.4 1.7 %collective-permute-start.6 = (bf16[128,512]{1,0:T(8,128)(2,1)S(1)}, bf16[128,512]{1,0:T(8,128)(2,1)S(1)}, u32[]{:S(2)}, u32[]{:S(2)}) collective-permute-start(bf16[128,512]{1,0:T(8,128)(2,1)S(1)} %copy-done.32), channel_id=1, source_target_pairs={{0,1},{1,0},{2,3},{3,2},{4,5},{5,4},{6,7},{7,6},{8,9},{9,8},{10,11... | collective-permute-start | bytes 393224 | tf_op jit(solution)/shard_map/gather_w_out/ppermute | solution.py:557
  26.9 1.4 collective-permute-start.7
  28.3 0.8 copy-start.31
  39.0 2.2 %collective-permute-start.8 = (bf16[512,512]{1,0:T(8,128)(2,1)}, bf16[512,512]{1,0:T(8,128)(2,1)S(1)}, u32[]{:S(2)}, u32[]{:S(2)}) collective-permute-start(bf16[512,512]{1,0:T(8,128)(2,1)} %get-tuple-element.227), channel_id=1, source_target_pairs={{0,1},{1,0},{2,3},{3,2},{4,5},{5,4},{6,7},{7,6},{8,9},{9,8},{10,11... | collective-permute-start | bytes 1572872 | tf_op jit(solution)/shard_map/sum_second/ppermute | solution.py:557
  41.1 1.0 copy-start.17
  42.3 6.7 %copy-start.4 = (bf16[512,512]{1,0:T(8,128)(2,1)}, bf16[512,512]{1,0:T(8,128)(2,1)S(1)}, u32[]{:S(2)}) copy-start(bf16[512,512]{1,0:T(8,128)(2,1)S(1)} %add.30.own_ref) | copy-start | bytes 1572868
  42.3 14.0 %collective-permute-start.10 = (bf16[512,512]{1,0:T(8,128)(2,1)S(1)}, bf16[512,512]{1,0:T(8,128)(2,1)S(1)}, u32[]{:S(2)}, u32[]{:S(2)}) collective-permute-start(bf16[512,512]{1,0:T(8,128)(2,1)S(1)} %add.30.own_ref), channel_id=1, source_target_pairs={{0,2},{1,3},{2,0},{3,1},{4,6},{5,7},{6,4},{7,5},{8,10},{9,11},{10,... | collective-permute-start | bytes 1572872 | tf_op jit(solution)/shard_map/sum_second/ppermute | solution.py:557
  49.0 7.3 %collective-permute-start.9 = (bf16[512,512]{1,0:T(8,128)(2,1)}, bf16[512,512]{1,0:T(8,128)(2,1)S(1)}, u32[]{:S(2)}, u32[]{:S(2)}) collective-permute-start(bf16[512,512]{1,0:T(8,128)(2,1)} %get-tuple-element.238), channel_id=1, source_target_pairs={{0,1},{1,0},{2,3},{3,2},{4,5},{5,4},{6,7},{7,6},{8,9},{9,8},{10,11... | collective-permute-start | bytes 1572872 | tf_op jit(solution)/shard_map/sum_output/ppermute | solution.py:557
  49.0 10.1 %collective-permute-start.12 = (bf16[512,512]{1,0:T(8,128)(2,1)S(1)}, bf16[512,512]{1,0:T(8,128)(2,1)S(1)}, u32[]{:S(2)}, u32[]{:S(2)}) collective-permute-start(bf16[512,512]{1,0:T(8,128)(2,1)S(1)} %add.30.own_ref), channel_id=1, source_target_pairs={{0,1},{1,0},{2,3},{3,2},{4,5},{5,4},{6,7},{7,6},{8,9},{9,8},{10,11... | collective-permute-start | bytes 1572872 | tf_op jit(solution)/shard_map/sum_second/ppermute | solution.py:557
  49.5 25.0 %collective-permute-start.15 = (bf16[512,512]{1,0:T(8,128)(2,1)}, bf16[512,512]{1,0:T(8,128)(2,1)}, u32[]{:S(2)}, u32[]{:S(2)}) collective-permute-start(bf16[512,512]{1,0:T(8,128)(2,1)} %get-tuple-element.258), channel_id=1, source_target_pairs={{0,8},{4,12},{8,0},{12,4},{16,24},{20,28},{24,16},{28,20},{1,9},{5... | collective-permute-start | bytes 1572872 | tf_op jit(solution)/shard_map/feed_weights/ppermute | solution.py:557
  56.4 2.2 %copy-start.25 = (bf16[512,512]{1,0:T(8,128)(2,1)}, bf16[512,512]{1,0:T(8,128)(2,1)S(1)}, u32[]{:S(2)}) copy-start(bf16[512,512]{1,0:T(8,128)(2,1)S(1)} %collective-permute-done.10.far_ref) | copy-start | bytes 1572868
  56.4 2.8 %collective-permute-start.13 = (bf16[512,512]{1,0:T(8,128)(2,1)S(1)}, bf16[512,512]{1,0:T(8,128)(2,1)S(1)}, u32[]{:S(2)}, u32[]{:S(2)}) collective-permute-start(bf16[512,512]{1,0:T(8,128)(2,1)S(1)} %collective-permute-done.10.far_ref), channel_id=1, source_target_pairs={{0,1},{1,0},{2,3},{3,2},{4,5},{5,4},{6,7},{7,6},{8,9},{9,8},{10,11... | collective-permute-start | bytes 1572872 | tf_op jit(solution)/shard_map/sum_second/ppermute | solution.py:557
  56.4 1.2 copy-start.19
  58.5 10.3 %collective-permute-start.16 = (bf16[512,512]{1,0:T(8,128)(2,1)}, bf16[512,512]{1,0:T(8,128)(2,1)S(1)}, u32[]{:S(2)}, u32[]{:S(2)}) collective-permute-start(bf16[512,512]{1,0:T(8,128)(2,1)} %add.31.own_ref), channel_id=1, source_target_pairs={{0,1},{1,0},{2,3},{3,2},{4,5},{5,4},{6,7},{7,6},{8,9},{9,8},{10,11... | collective-permute-start | bytes 1572872 | tf_op jit(solution)/shard_map/sum_output/ppermute | solution.py:557
  58.8 21.4 %collective-permute-start.11 = (bf16[512,512]{1,0:T(8,128)(2,1)}, bf16[512,512]{1,0:T(8,128)(2,1)}, u32[]{:S(2)}, u32[]{:S(2)}) collective-permute-start(bf16[512,512]{1,0:T(8,128)(2,1)} %add.31.own_ref), channel_id=1, source_target_pairs={{0,2},{1,3},{2,0},{3,1},{4,6},{5,7},{6,4},{7,5},{8,10},{9,11},{10,... | collective-permute-start | bytes 1572872 | tf_op jit(solution)/shard_map/sum_output/ppermute | solution.py:557
  59.1 1.0 copy-start.27
  59.1 0.9 copy-start.28
  60.1 9.5 %copy-start.1 = (f32[4,10,8,128]{3,2,1,0:T(8,128)S(1)}, f32[4,10,8,128]{3,2,1,0:T(8,128)}, u32[]{:S(2)}) copy-start(f32[4,10,8,128]{3,2,1,0:T(8,128)} %copy-done) | copy-start | bytes 491524
  60.1 9.5 %copy-start.8 = (bf16[1024,128]{1,0:T(8,128)(2,1)S(1)}, bf16[1024,128]{1,0:T(8,128)(2,1)}, u32[]{:S(2)}) copy-start(bf16[1024,128]{1,0:T(8,128)(2,1)} %copy-done.7) | copy-start | bytes 786436
  70.3 1.2 copy-start.13
  71.6 1.1 copy-start.15
  72.7 5.1 %copy-start.18 = (bf16[512,512]{1,0:T(8,128)(2,1)S(1)}, bf16[512,512]{1,0:T(8,128)(2,1)}, u32[]{:S(2)}) copy-start(bf16[512,512]{1,0:T(8,128)(2,1)} %get-tuple-element.272.a_ref) | copy-start | bytes 1572868
  74.5 5.7 %collective-permute-start.14 = (f32[2,2,8,128]{3,2,1,0:T(8,128)S(1)}, f32[2,2,8,128]{3,2,1,0:T(8,128)S(1)}, u32[]{:S(2)}, u32[]{:S(2)}) collective-permute-start(f32[2,2,8,128]{3,2,1,0:T(8,128)S(1)} %slice.27), channel_id=1, source_target_pairs={{0,8},{4,12},{8,0},{12,4},{16,24},{20,28},{24,16},{28,20},{1,9},{5... | collective-permute-start | bytes 49160 | tf_op jit(solution)/shard_map/sum_slots/ppermute | solution.py:557
  76.3 17.1 %collective-permute-start.21 = (bf16[256,512]{1,0:T(8,128)(2,1)}, bf16[256,512]{1,0:T(8,128)(2,1)}, u32[]{:S(2)}, u32[]{:S(2)}) collective-permute-start(bf16[256,512]{1,0:T(8,128)(2,1)} %get-tuple-element.290), channel_id=1, source_target_pairs={{0,4},{4,0},{8,12},{12,8},{16,20},{20,16},{24,28},{28,24},{1,5},{5... | collective-permute-start | bytes 786440 | tf_op jit(solution)/shard_map/rest_weights/ppermute | solution.py:557
  79.7 16.7 %collective-permute-start.18 = (bf16[256,512]{1,0:T(8,128)(2,1)}, bf16[256,512]{1,0:T(8,128)(2,1)}, u32[]{:S(2)}, u32[]{:S(2)}) collective-permute-start(bf16[256,512]{1,0:T(8,128)(2,1)} %get-tuple-element.286), channel_id=1, source_target_pairs={{0,4},{4,0},{8,12},{12,8},{16,20},{20,16},{24,28},{28,24},{1,5},{5... | collective-permute-start | bytes 786440 | tf_op jit(solution)/shard_map/feed_weights/ppermute | solution.py:557
  80.2 7.4 %collective-permute-start.17 = (bf16[512,512]{1,0:T(8,128)(2,1)}, bf16[512,512]{1,0:T(8,128)(2,1)S(1)}, u32[]{:S(2)}, u32[]{:S(2)}) collective-permute-start(bf16[512,512]{1,0:T(8,128)(2,1)} %collective-permute-done.11.far_ref), channel_id=1, source_target_pairs={{0,1},{1,0},{2,3},{3,2},{4,5},{5,4},{6,7},{7,6},{8,9},{9,8},{10,11... | collective-permute-start | bytes 1572872 | tf_op jit(solution)/shard_map/sum_output/ppermute | solution.py:557
  80.3 9.9 %copy-start.6 = (bf16[3,512,128]{2,1,0:T(8,128)(2,1)S(1)}, bf16[3,512,128]{2,1,0:T(8,128)(2,1)}, u32[]{:S(2)}) copy-start(bf16[3,512,128]{2,1,0:T(8,128)(2,1)} %w_ref.3) | copy-start | bytes 1179652
  80.3 9.8 %collective-permute-start.19 = (f32[1,2,8,128]{3,2,1,0:T(8,128)S(1)}, f32[1,2,8,128]{3,2,1,0:T(8,128)S(1)}, u32[]{:S(2)}, u32[]{:S(2)}) collective-permute-start(f32[1,2,8,128]{3,2,1,0:T(8,128)S(1)} %slice.36), channel_id=1, source_target_pairs={{0,4},{4,0},{8,12},{12,8},{16,20},{20,16},{24,28},{28,24},{1,5},{5... | collective-permute-start | bytes 24584 | tf_op jit(solution)/shard_map/sum_slots/ppermute | solution.py:557
  87.4 3.5 %collective-permute-start.22 = (bf16[528,512]{1,0:T(8,128)(2,1)}, bf16[528,512]{1,0:T(8,128)(2,1)S(1)}, u32[]{:S(2)}, u32[]{:S(2)}) collective-permute-start(bf16[528,512]{1,0:T(8,128)(2,1)} %get-tuple-element.291), channel_id=1, source_target_pairs={{0,1},{1,0},{2,3},{3,2},{4,5},{5,4},{6,7},{7,6},{8,9},{9,8},{10,11... | collective-permute-start | bytes 1622024 | tf_op jit(solution)/shard_map/sum_first/ppermute | solution.py:557
  87.6 3.4 %copy-start.26 = (bf16[512,512]{1,0:T(8,128)(2,1)}, bf16[512,512]{1,0:T(8,128)(2,1)S(1)}, u32[]{:S(2)}) copy-start(bf16[512,512]{1,0:T(8,128)(2,1)S(1)} %collective-permute-done.17.other_far_ref) | copy-start | bytes 1572868
  87.6 3.4 %copy-start.16 = (bf16[528,512]{1,0:T(8,128)(2,1)S(1)}, bf16[528,512]{1,0:T(8,128)(2,1)}, u32[]{:S(2)}) copy-start(bf16[528,512]{1,0:T(8,128)(2,1)} %get-tuple-element.292.a_ref) | copy-start | bytes 1622020
  91.0 3.5 %collective-permute-start.20 = (f32[8,512]{1,0:T(8,128)}, f32[8,512]{1,0:T(8,128)}, u32[]{:S(2)}, u32[]{:S(2)}) collective-permute-start(f32[8,512]{1,0:T(8,128)} %extra.1.a_ref), channel_id=1, source_target_pairs={{0,1},{1,0},{2,3},{3,2},{4,5},{5,4},{6,7},{7,6},{8,9},{9,8},{10,11... | collective-permute-start | bytes 49160 | tf_op jit(solution)/shard_map/sum_extra/ppermute | solution.py:557
  91.9 19.4 %collective-permute-start.23 = (bf16[528,512]{1,0:T(8,128)(2,1)}, bf16[528,512]{1,0:T(8,128)(2,1)}, u32[]{:S(2)}, u32[]{:S(2)}) collective-permute-start(bf16[528,512]{1,0:T(8,128)(2,1)} %pair.1.near_ref.own_ref), channel_id=1, source_target_pairs={{0,2},{1,3},{2,0},{3,1},{4,6},{5,7},{6,4},{7,5},{8,10},{9,11},{10,... | collective-permute-start | bytes 1622024 | tf_op jit(solution)/shard_map/sum_first/ppermute | solution.py:557
  95.8 19.8 %collective-permute-start.28 = (f32[8,512]{1,0:T(8,128)}, f32[8,512]{1,0:T(8,128)}, u32[]{:S(2)}, u32[]{:S(2)}) collective-permute-start(f32[8,512]{1,0:T(8,128)} %plus.2.a_ref), channel_id=1, source_target_pairs={{0,2},{1,3},{2,0},{3,1},{4,6},{5,7},{6,4},{7,5},{8,10},{9,11},{10,... | collective-permute-start | bytes 49160 | tf_op jit(solution)/shard_map/sum_extra/ppermute | solution.py:557
  98.0 8.1 %collective-permute-start.25 = (bf16[128,512]{1,0:T(8,128)(2,1)S(1)}, bf16[128,512]{1,0:T(8,128)(2,1)S(1)}, u32[]{:S(2)}, u32[]{:S(2)}) collective-permute-start(bf16[128,512]{1,0:T(8,128)(2,1)S(1)} %get-tuple-element.312), channel_id=1, source_target_pairs={{0,8},{4,12},{8,0},{12,4},{16,24},{20,28},{24,16},{28,20},{1,9},{5... | collective-permute-start | bytes 393224 | tf_op jit(solution)/shard_map/rest_weights/ppermute | solution.py:557
  98.4 8.3 %collective-permute-start.24 = (bf16[128,512]{1,0:T(8,128)(2,1)}, bf16[128,512]{1,0:T(8,128)(2,1)}, u32[]{:S(2)}, u32[]{:S(2)}) collective-permute-start(bf16[128,512]{1,0:T(8,128)(2,1)} %get-tuple-element.311), channel_id=1, source_target_pairs={{0,16},{4,20},{8,24},{12,28},{16,0},{20,4},{24,8},{28,12},{1,17},{... | collective-permute-start | bytes 393224 | tf_op jit(solution)/shard_map/feed_weights/ppermute | solution.py:557
  106.7 7.0 %copy-start.20 = (f32[32,512]{1,0:T(8,128)S(1)}, f32[32,512]{1,0:T(8,128)}, u32[]{:S(2)}) copy-start(f32[32,512]{1,0:T(8,128)} %get-tuple-element.328.back_ref) | copy-start | bytes 196612
  106.7 7.0 %copy-start.22 = (f32[8,512]{1,0:T(8,128)S(1)}, f32[8,512]{1,0:T(8,128)}, u32[]{:S(2)}) copy-start(f32[8,512]{1,0:T(8,128)} %get-tuple-element.329.up_ref) | copy-start | bytes 49156
  106.7 7.0 %collective-permute-start.29 = (bf16[64,512]{1,0:T(8,128)(2,1)S(1)}, bf16[64,512]{1,0:T(8,128)(2,1)S(1)}, u32[]{:S(2)}, u32[]{:S(2)}) collective-permute-start(bf16[64,512]{1,0:T(8,128)(2,1)S(1)} %get-tuple-element.322), channel_id=1, source_target_pairs={{0,16},{4,20},{8,24},{12,28},{16,0},{20,4},{24,8},{28,12},{1,17},{... | collective-permute-start | bytes 196616 | tf_op jit(solution)/shard_map/rest_weights/ppermute | solution.py:557
  109.2 14.9 %collective-permute-start.31 = (bf16[128,512]{1,0:T(8,128)(2,1)}, bf16[128,512]{1,0:T(8,128)(2,1)}, u32[]{:S(2)}, u32[]{:S(2)}) collective-permute-start(bf16[128,512]{1,0:T(8,128)(2,1)} %add.32.a_ref), channel_id=1, source_target_pairs={{0,16},{4,20},{8,24},{12,28},{16,0},{20,4},{24,8},{28,12},{1,17},{... | collective-permute-start | bytes 393224 | tf_op jit(solution)/shard_map/feed_weights/ppermute | solution.py:557
  111.3 6.5 %collective-permute-start.27 = (bf16[528,512]{1,0:T(8,128)(2,1)}, bf16[528,512]{1,0:T(8,128)(2,1)}, u32[]{:S(2)}, u32[]{:S(2)}) collective-permute-start(bf16[528,512]{1,0:T(8,128)(2,1)} %collective-permute-done.23.far_ref), channel_id=1, source_target_pairs={{0,1},{1,0},{2,3},{3,2},{4,5},{5,4},{6,7},{7,6},{8,9},{9,8},{10,11... | collective-permute-start | bytes 1622024 | tf_op jit(solution)/shard_map/sum_first/ppermute | solution.py:557
  115.6 11.6 %collective-permute-start.30 = (bf16[80,512]{1,0:T(8,128)(2,1)}, bf16[80,512]{1,0:T(8,128)(2,1)}, u32[]{:S(2)}, u32[]{:S(2)}) collective-permute-start(bf16[80,512]{1,0:T(8,128)(2,1)} %piece.1.a_ref), channel_id=1, source_target_pairs={{0,16},{4,20},{8,24},{12,28},{16,0},{20,4},{24,8},{28,12},{1,17},{... | collective-permute-start | bytes 245768 | tf_op jit(solution)/shard_map/rest_weights/ppermute | solution.py:557
  115.6 2.1 %collective-permute-start.26 = (bf16[528,512]{1,0:T(8,128)(2,1)}, bf16[528,512]{1,0:T(8,128)(2,1)S(1)}, u32[]{:S(2)}, u32[]{:S(2)}) collective-permute-start(bf16[528,512]{1,0:T(8,128)(2,1)} %pair.1.near_ref.own_ref), channel_id=1, source_target_pairs={{0,1},{1,0},{2,3},{3,2},{4,5},{5,4},{6,7},{7,6},{8,9},{9,8},{10,11... | collective-permute-start | bytes 1622024 | tf_op jit(solution)/shard_map/sum_first/ppermute | solution.py:557
  117.7 0.8 copy-start.23
  125.8 9.3 %collective-permute-start.33 = (bf16[256,512]{1,0:T(8,128)(2,1)}, bf16[256,512]{1,0:T(8,128)(2,1)}, u32[]{:S(2)}, u32[]{:S(2)}) collective-permute-start(bf16[256,512]{1,0:T(8,128)(2,1)} %concat.2.a_ref), channel_id=1, source_target_pairs={{0,4},{4,0},{8,12},{12,8},{16,20},{20,16},{24,28},{28,24},{1,5},{5... | collective-permute-start | bytes 786440 | tf_op jit(solution)/shard_map/feed_weights/ppermute | solution.py:557
  128.8 10.5 %collective-permute-start.32 = (bf16[144,512]{1,0:T(8,128)(2,1)}, bf16[144,512]{1,0:T(8,128)(2,1)}, u32[]{:S(2)}, u32[]{:S(2)}) collective-permute-start(bf16[144,512]{1,0:T(8,128)(2,1)} %merge.2.a_ref), channel_id=1, source_target_pairs={{0,8},{4,12},{8,0},{12,4},{16,24},{20,28},{24,16},{28,20},{1,9},{5... | collective-permute-start | bytes 442376 | tf_op jit(solution)/shard_map/rest_weights/ppermute | solution.py:557
  140.3 7.9 %collective-permute-start.34 = (bf16[272,512]{1,0:T(8,128)(2,1)S(1)}, bf16[272,512]{1,0:T(8,128)(2,1)S(1)}, u32[]{:S(2)}, u32[]{:S(2)}) collective-permute-start(bf16[272,512]{1,0:T(8,128)(2,1)S(1)} %merge.3.near_ref), channel_id=1, source_target_pairs={{0,4},{4,0},{8,12},{12,8},{16,20},{20,16},{24,28},{28,24},{1,5},{5... | collective-permute-start | bytes 835592 | tf_op jit(solution)/shard_map/rest_weights/ppermute | solution.py:557
  141.7 14.8 %collective-permute-start.35 = (bf16[512,512]{1,0:T(8,128)(2,1)}, bf16[512,512]{1,0:T(8,128)(2,1)}, u32[]{:S(2)}, u32[]{:S(2)}) collective-permute-start(bf16[512,512]{1,0:T(8,128)(2,1)} %concat.3.near_ref), channel_id=1, source_target_pairs={{0,8},{4,12},{8,0},{12,4},{16,24},{20,28},{24,16},{28,20},{1,9},{5... | collective-permute-start | bytes 1572872 | tf_op jit(solution)/shard_map/feed_weights/ppermute | solution.py:557
  (9 other events, 6.2 us)

commit v3 on v2

--- a/solution.py
+++ b/solution.py
@@ -595,7 +595,7 @@
             out_shape=(part,) * parts,
             in_specs=[VMEM, VMEM],
             out_specs=(VMEM,) * parts,
-            compiler_params=params(16),
+            compiler_params=params(60),
             cost_estimate=cost(),
             name="add",
         )(a, b)
@@ -701,14 +701,14 @@
         def block(shape, index):
             return pl.BlockSpec(shape, index)
 
-        def plain(kernel, name, in_specs, out_shape, scratch=()):
+        def plain(kernel, name, in_specs, out_shape, scratch=(), mib=24):
             return pl.pallas_call(
                 kernel,
                 out_shape=out_shape,
                 in_specs=in_specs,
                 out_specs=tuple(VMEM for _ in out_shape),
                 scratch_shapes=list(scratch),
-                compiler_params=params(24),
+                compiler_params=params(mib),
                 cost_estimate=cost(),
                 name=name,
             )
@@ -727,7 +727,7 @@
                 ),
                 out_shape=out_shape,
                 input_output_aliases=aliases or {},
-                compiler_params=params(mib),
+                compiler_params=params(60 if name in ('feed',) else 30 if name in ('back', 'weights') else 20),
                 cost_estimate=cost(),
                 name=name,
             )
@@ -747,6 +747,7 @@
                 sds((2 + 2 * (dim // width), blocks, width), f32),
             ),
             [pltpu.VMEM((dim, 3 * width), bf16)],
+            60,
         )
         local = plain(
             local_kernel,
@@ -815,6 +816,7 @@
             "rest_weights",
             [SMEM] + [VMEM] * 6,
             (sds((dim // 2, 4 * width), bf16), sds((dim // 2, 4 * width), bf16)),
+            mib=60,
         )
         slot_shape = (group, 2, blocks, width)
         sums_shape = (group, 2 + 2 * (dim // width), blocks, width)
@@ -849,13 +851,13 @@
         first_grad = gridded(
             first_kernel,
             "first",
-            tiles,
+            2,
             [
-                block((tile, 3 * width), rolled),
+                block((half, 3 * width), half_rolled),
                 block(slot_shape, zeros(4)),
                 block(sums_shape, zeros(4)),
                 block((3, dim, width), zeros(3)),
-                row_block,
+                half_rows,
             ],
             [first_block, first_block],
             (sds((half + 16, dim), bf16), sds((half + 16, dim), bf16)),
@@ -867,11 +869,12 @@
         def other_tile(i, pos):
             return (jnp.clip(i - (1 - pos[1]) * (tiles // 2), 0, tiles // 2 - 1), 0)
 
-        terms_specs = [block((tile, dim), own_tile)] * 2 + [block((tile, dim), other_tile)] * 2
+        terms_specs = [block((half, dim), whole)] * 4
+        tile_block = block((half, dim), by_row)
         last = gridded(
             last_kernel,
             "last",
-            tiles,
+            2,
             terms_specs + [block((blocks, dim), whole), tile_block, tile_block, row_vector],
             tile_block,
             sds((rows, dim), bf16),
@@ -879,7 +882,7 @@
         output_sum = gridded(
             output_kernel,
             "output",
-            tiles,
+            2,
             terms_specs + [tile_block, row_vector],
             tile_block,
             sds((rows, dim), bf16),
@@ -954,6 +957,7 @@
                 {j ^ m: swap(x, "mp", m, "gather_w_out") for j, x in list(out_slots.items())}
             )
         line.spare = ln1_gain[None]
+        pos, place = wait(pos, place[None].astype(i32))
         first, qkv, summary = line(project, tokens, ln1_gain[None], ln1_bias[None], w_qkv)
         out_list = list(out_slots.items())
         sums = after(summary, *[x for _, x in out_list])[None]
@@ -964,7 +968,7 @@
                 for j, x in out_list:
                     out_slots[j ^ 1] = swap(after(x, stats), "mp", 1, "gather_w_out")
             sums = line(lambda a, b: jnp.concatenate([a, b]), sums, got)
-        probs, attended = line(attend, place[None].astype(i32), qkv, exps, stats, sums)
+        probs, attended = line(attend, place, qkv, exps, stats, sums)
 
         att_slots = {0: attended}
         for m in far_masks:
@@ -996,11 +1000,14 @@
         )
         feed_sum = Scatter(line, theirs, mine, feed_masks, "feed_weights")
         out_got = swap(out_theirs, "mp", 1, "sum_output")
+        line.space()
+        out_total = near_sum(line(add_low, out_mine, out_got), "sum_output")
         (far,) = wait(far)
         other_far = swap(far, "mp", 1, "sum_second")
-        out_total = near_sum(line(add_low, out_mine, out_got), "sum_output")
-        out_far = swap(out_total, "mp", last_far, "sum_output")
-        out_other = swap(out_total, "mp", 1, "sum_output")
+        out_send = after(out_total, far)
+        out_far = swap(out_send, "mp", last_far, "sum_output")
+        out_other = swap(out_send, "mp", 1, "sum_output")
+        line.space()
         grad_low, gqkv, back_vec, slot_grad = line(
             lambda *a: (lambda r: (r[0], r[1], r[3], r[2]))(back(*a)),
             pos,
@@ -1020,55 +1027,58 @@
         following = list(reversed(seq_masks))
         slot_part = slot_grad
         slot_got = swap(slot_part[following[0] :], "dp", following[0], "sum_slots")
+        feed_sum.step()
         (out_other,) = wait(out_other)
-        theirs, mine = line(
+        theirs, mine = line(first_grad, pos, gqkv, slot_grad, sums, w_qkv, tokens)
+        got = swap(theirs, "mp", 1, "sum_first")
+        theirs_w, mine_w = line(
             rest_weights, first_bit, first, gqkv, grad_low, attended, slot_grad, sums
         )
-        rest_sum = Scatter(line, theirs, mine, dp_masks, "rest_weights")
-        feed_sum.step()
+        total = line(pair, mine, got)
+        for m in far_masks[:-1]:
+            total = line(pair, total, swap(total, "mp", m, "sum_first"))
+        far = swap(total, "mp", last_far, "sum_first")
+        rest_sum = Scatter(line, theirs_w, mine_w, dp_masks, "rest_weights")
         for low in following[1:]:
             slot_part = line(slot_add, slot_part, slot_got)
             slot_got = swap(slot_part[low:], "dp", low, "sum_slots")
         (out_far,) = wait(out_far)
         out_other_far = swap(out_far, "mp", 1, "sum_output")
-        theirs, mine = line(first_grad, pos, gqkv, slot_grad, sums, w_qkv, tokens)
-        got = swap(theirs, "mp", 1, "sum_first")
-        (out_other_far,) = wait(out_other_far)
+        feed_sum.step()
         extra = line(extra_of, slot_part, slot_got, w_qkv)
         extra_got = swap(extra, "mp", 1, "sum_extra")
-        total = line(pair, mine, got)
-        for m in far_masks[:-1]:
-            total = line(pair, total, swap(total, "mp", m, "sum_first"))
-        far = swap(total, "mp", last_far, "sum_first")
         rest_sum.step()
+        output = line(
+            output_sum, pos, out_total, out_far, out_other, out_other_far, mid, b_down[None]
+        )
         for m in far_masks:
             extra = line(pl_add, extra, extra_got)
             extra_got = swap(extra, "mp", m, "sum_extra")
-        feed_sum.step()
-        output = line(
-            output_sum, pos, out_total, out_far, out_other, out_other_far, mid, b_down[None]
-        )
-        for m in dp_masks[2:]:
-            rest_sum.step()
-        line.space()
         for m in feed_masks[3:]:
             feed_sum.step()
-        feed_all = line(add_low, feed_sum.mine, feed_sum.got)
-        feed_got = swap(feed_all, "dp", feed_masks[-1], "feed_weights")
         (far,) = wait(far)
         other = swap(after(total, far), "mp", 1, "sum_first")
         other_far = swap(far, "mp", 1, "sum_first")
-        rest_all = line(
-            piece_of, rest_sum.mine, rest_sum.got, total, far, back_vec, up_vec
-        )
-        rest_got = swap(rest_all, "dp", dp_masks[-1], "rest_weights")
+        feed_all = line(add_low, feed_sum.mine, feed_sum.got)
+        feed_got = swap(feed_all, "dp", feed_masks[-1], "feed_weights")
+        for m in dp_masks[2:]:
+            rest_sum.step()
         extra = line(pl_add, extra, extra_got)
         grad_tokens = line(
             last, pos, total, far, other, other_far, extra, tokens, grad_low, ln1_gain[None]
         )
         feed_next = list(reversed(feed_masks))[1:]
         rest_next = list(reversed(dp_masks))[1:]
-        for feed_mask, rest_mask in zip(feed_next, rest_next):
+        feed_all = line(concat, feed_all, feed_got)
+        feed_got = swap(feed_all, "dp", feed_next[0], "feed_weights")
+        rest_all = line(
+            piece_of, rest_sum.mine, rest_sum.got, total, far, back_vec, up_vec
+        )
+        rest_got = swap(rest_all, "dp", dp_masks[-1], "rest_weights")
+        line.space()
+        rest_all = line(merge, rest_all, rest_got)
+        rest_got = swap(rest_all, "dp", rest_next[0], "rest_weights")
+        for feed_mask, rest_mask in zip(feed_next[1:], rest_next[1:]):
             feed_all = line(concat, feed_all, feed_got)
             feed_got = swap(feed_all, "dp", feed_mask, "feed_weights")
             rest_all = line(merge, rest_all, rest_got)

time: 160 us -> 144 us (0.900)
  local copies, waits for them, and re-layouts: 15.1 us -> 8.57 us
  starting transfers between devices: 36.7 us -> 31.9 us
  Pallas kernels: 69 us -> 66.3 us
  waiting for transfers between devices: 36.8 us -> 34.6 us
    unnamed x76 -> x104, local copies, waits for them, and re-layouts: 14.5 us -> 7.35 us
    ppermute x36, starting transfers between devices: 36.7 us -> 31.9 us  [swap(): return lax.ppermute(x, axis, [(i, i ^ mask) for i in range(n)])]
    pallas_call x11, Pallas kernels: 41.2 us -> 36.8 us  [__call__(): result = work(*inputs)]
    pallas_call x3, Pallas kernels: 2.63 us -> 6.05 us  [add_parts(): pl.pallas_call(functools.partial(add_kernel, parts), out_shape=(part,) *...]
    pallas_call x4, Pallas kernels: 4.63 us -> 7.47 us  [split_sum(): pl.pallas_call(split_kernel, out_shape=(half, half), in_specs=[SMEM, VMEM...]
    pallas_call x10, Pallas kernels: 11.9 us -> 9.32 us  [like(): return plain(kernel, name, specs, (sds(shape, dtype),))(*operands)[0]]
    ppermute x36, waiting for transfers between devices: 36.8 us -> 34.6 us  [swap(): return lax.ppermute(x, axis, [(i, i ^ mask) for i in range(n)])]
    pallas_call x1, Pallas kernels: 8.67 us -> 6.67 us  [per_device(): back(*a)]
  transfers between devices with their start and end apart: 36 -> 36, of which waited for: 14 -> 15; matrix products, arithmetic and copies ran while one was open for 1% -> 1% of each run, Pallas kernels for 34% -> 34%
where the time goes in v3:
time: 144 us; the launch traced here: 143 us
  Pallas kernels  66.3 us (46%)
  waiting for transfers between devices  34.6 us (24%)
  starting transfers between devices  31.9 us (22%)
  local copies, waits for them, and re-layouts  8.57 us (6%)
    pallas_call x11, Pallas kernels, __call__(): result = work(*inputs)  36.8 us
    ppermute x36, waiting for transfers between devices, swap(): return lax.ppermute(x, axis, [(i, i ^ mask) for i in range(n)])  34.6 us
    ppermute x36, starting transfers between devices, swap(): return lax.ppermute(x, axis, [(i, i ^ mask) for i in range(n)])  31.9 us
    pallas_call x10, Pallas kernels, like(): return plain(kernel, name, specs, (sds(shape, dtype),))(*operands)[0]  9.32 us
    pallas_call x4, Pallas kernels, split_sum(): pl.pallas_call(split_kernel, out_shape=(half, half), in_specs=[SMEM, VMEM...  7.47 us
    unnamed x104, local copies, waits for them, and re-layouts  7.35 us
    pallas_call x1, Pallas kernels, per_device(): back(*a)  6.67 us
    pallas_call x3, Pallas kernels, add_parts(): pl.pallas_call(functools.partial(add_kernel, parts), out_shape=(part,) *...  6.05 us
  transfers between devices with their start and end apart: 36, of which 15 were waited for; matrix products, arithmetic and copies ran while one was open for 1% of the time, Pallas kernels for 34%

profile of v3, /device:TPU:0, one launch (start us, length us, event | category | flops | bytes accessed | tf_op | source)
XLA Modules:
  0.0 143.1 jit_solution(12353336211088614007)
XLA Ops:
  0.6 3.0 %collective-permute-start = (bf16[128,512]{1,0:T(8,128)(2,1)}, bf16[128,512]{1,0:T(8,128)(2,1)S(1)}, u32[]{:S(2)}, u32[]{:S(2)}) collective-permute-start(bf16[128,512]{1,0:T(8,128)(2,1)} %wo_ref), channel_id=1, source_target_pairs={{0,2},{1,3},{2,0},{3,1},{4,6},{5,7},{6,4},{7,5},{8,10},{9,11},{10,... | collective-permute-start | bytes 393224 | tf_op jit(solution)/shard_map/gather_w_out/ppermute | solution.py:557
  3.7 3.9 %project.1 = (bf16[1024,512]{1,0:T(8,128)(2,1)}, bf16[3,1024,128]{2,1,0:T(8,128)(2,1)}, f32[10,8,128]{2,1,0:T(8,128)}) custom-call(bf16[1024,512]{1,0:T(8,128)(2,1)} %tok_ref.3, f32[1,512]{1,0:T(1,128)} %bitcast.24, f32[1,512]{1,0:T(1,128)} %bitcast.36, bf16[3,512,128]{2,1,0:T(8,128)(2,1)} %w_ref.2), custom_call_target="tpu_custom_call" | custom-call | flops 115000000512 | bytes 1 | tf_op jit(solution)/shard_map/project/pallas_call | solution.py:581
  7.6 1.5 %collective-permute-start.1 = (f32[1,10,8,128]{3,2,1,0:T(8,128)}, f32[1,10,8,128]{3,2,1,0:T(8,128)S(1)}, u32[]{:S(2)}, u32[]{:S(2)}) collective-permute-start(f32[1,10,8,128]{3,2,1,0:T(8,128)} %bitcast.27), channel_id=1, source_target_pairs={{0,4},{4,0},{8,12},{12,8},{16,20},{20,16},{24,28},{28,24},{1,5},{5... | collective-permute-start | bytes 122888 | tf_op jit(solution)/shard_map/summaries/ppermute | solution.py:557
  9.1 1.1 copy-done.32
  10.7 1.1 collective-permute-done.1
  11.8 1.7 %collective-permute-start.2 = (f32[2,10,8,128]{3,2,1,0:T(8,128)S(1)}, f32[2,10,8,128]{3,2,1,0:T(8,128)S(1)}, u32[]{:S(2)}, u32[]{:S(2)}) collective-permute-start(f32[2,10,8,128]{3,2,1,0:T(8,128)S(1)} %constant_dynamic-update-slice_fusion), channel_id=1, source_target_pairs={{0,8},{4,12},{8,0},{12,4},{16,24},{20,28},{24,16},{28,20},{1,9},{5... | collective-permute-start | bytes 245768 | tf_op jit(solution)/shard_map/summaries/ppermute | solution.py:557
  13.5 2.9 %collective-permute-done.2 = f32[2,10,8,128]{3,2,1,0:T(8,128)S(1)} collective-permute-done((f32[2,10,8,128]{3,2,1,0:T(8,128)S(1)}, f32[2,10,8,128]{3,2,1,0:T(8,128)S(1)}, u32[]{:S(2)}, u32[]{:S(2)}) %collective-permute-start.2) | collective-permute-done | bytes 81952 | tf_op jit(solution)/shard_map/summaries/ppermute | solution.py:557
  16.4 1.5 %attend.1 = (f32[8,160,256]{2,1,0:T(8,128)S(1)}, bf16[1024,128]{1,0:T(8,128)(2,1)S(1)}) custom-call(s32[1]{0:T(128)} %bitcast.2.place_ref, bf16[3,1024,128]{2,1,0:T(8,128)(2,1)S(1)} %copy-done.32, f32[8,128,256]{2,1,0:T(8,128)S(1)} %get-tuple-element.209.exp_ref, f32[8,2,256]{2,1,0:T(2,128)S(1)} %get-tuple-element.210.stat_ref, ...), custom_call_target="tpu_custom_call" | custom-call | flops 115000000512 | bytes 1 | tf_op jit(solution)/shard_map/attend/pallas_call | solution.py:581
  17.9 1.6 %collective-permute-start.4 = (bf16[1024,128]{1,0:T(8,128)(2,1)S(1)}, bf16[1024,128]{1,0:T(8,128)(2,1)S(1)}, u32[]{:S(2)}, u32[]{:S(2)}) collective-permute-start(bf16[1024,128]{1,0:T(8,128)(2,1)S(1)} %get-tuple-element.291.refs_0_.att_ref), channel_id=1, source_target_pairs={{0,2},{1,3},{2,0},{3,1},{4,6},{5,7},{6,4},{7,5},{8,10},{9,11},{10,... | collective-permute-start | bytes 786440 | tf_op jit(solution)/shard_map/gather_attended/ppermute | solution.py:557
  19.5 4.8 %collective-permute-done.4.refs_2_ = bf16[1024,128]{1,0:T(8,128)(2,1)S(1)} collective-permute-done((bf16[1024,128]{1,0:T(8,128)(2,1)S(1)}, bf16[1024,128]{1,0:T(8,128)(2,1)S(1)}, u32[]{:S(2)}, u32[]{:S(2)}) %collective-permute-start.4) | collective-permute-done | bytes 262176 | tf_op jit(solution)/shard_map/gather_attended/ppermute | solution.py:557
  24.9 0.6 pad_add_fusion.pos_ref
  27.1 9.8 %feed.1 = (f32[1024,512]{1,0:T(8,128)}, bf16[1024,512]{1,0:T(8,128)(2,1)}, bf16[1024,512]{1,0:T(8,128)(2,1)}, bf16[1024,512]{1,0:T(8,128)(2,1)}, bf16[512,512]{1...) custom-call(s32[4]{0:T(128)} %pad_add_fusion.pos_ref, bf16[1024,512]{1,0:T(8,128)(2,1)} %tok_ref.3, ...), custom_call_target="tpu_custom_call" | custom-call | flops 115000000512 | bytes 1 | tf_op jit(solution)/shard_map/feed/pallas_call | solution.py:581
  37.1 2.0 %collective-permute-done.8.b_ref = bf16[512,512]{1,0:T(8,128)(2,1)S(1)} collective-permute-done((bf16[512,512]{1,0:T(8,128)(2,1)}, bf16[512,512]{1,0:T(8,128)(2,1)S(1)}, u32[]{:S(2)}, u32[]{:S(2)}) %collective-permute-start.8) | collective-permute-done | bytes 524320 | tf_op jit(solution)/shard_map/sum_second/ppermute | solution.py:557
  39.1 0.8 copy-done.42
  39.9 2.3 %add.30.own_ref = bf16[512,512]{1,0:T(8,128)(2,1)} custom-call(bf16[512,512]{1,0:T(8,128)(2,1)} %get-tuple-element.238.a_ref, bf16[512,512]{1,0:T(8,128)(2,1)} %copy-done.42), custom_call_target="tpu_custom_call" | custom-call | flops 115000000512 | bytes 1 | tf_op jit(solution)/shard_map/add/pallas_call | solution.py:593
  42.2 1.5 %collective-permute-start.10 = (bf16[512,512]{1,0:T(8,128)(2,1)}, bf16[512,512]{1,0:T(8,128)(2,1)}, u32[]{:S(2)}, u32[]{:S(2)}) collective-permute-start(bf16[512,512]{1,0:T(8,128)(2,1)} %add.30.own_ref), channel_id=1, source_target_pairs={{0,2},{1,3},{2,0},{3,1},{4,6},{5,7},{6,4},{7,5},{8,10},{9,11},{10,... | collective-permute-start | bytes 1572872 | tf_op jit(solution)/shard_map/sum_second/ppermute | solution.py:557
  43.8 1.2 copy-done.30
  45.0 1.2 copy-done.31
  46.2 3.8 %weights.1 = (bf16[512,512]{1,0:T(8,128)(2,1)S(1)}, bf16[512,512]{1,0:T(8,128)(2,1)S(1)}, bf16[512,512]{1,0:T(8,128)(2,1)}, bf16[512,512]{1,0:T(8,128)(2,1)S(1)}) custom-call(s32[4]{0:T(128)S(1)} %copy-done.4, bf16[1024,512]{1,0:T(8,128)(2,1)S(1)} %copy-done.30, bf16[1024,512]{1,0:T(8,128)(2,1)S(1)} %copy-done.29, bf16[1024,512]{1,0:T(8,128)(2,1)S(1)} %copy-done.31, ...), custom_call_target="tpu_custom_call" | custom-call | flops 115000000512 | bytes 1 | tf_op jit(solution)/shard_map/weights/pallas_call | solution.py:581
  51.0 1.6 %collective-permute-start.16 = (bf16[512,512]{1,0:T(8,128)(2,1)}, bf16[512,512]{1,0:T(8,128)(2,1)}, u32[]{:S(2)}, u32[]{:S(2)}) collective-permute-start(bf16[512,512]{1,0:T(8,128)(2,1)} %get-tuple-element.271), channel_id=1, source_target_pairs={{0,8},{4,12},{8,0},{12,4},{16,24},{20,28},{24,16},{28,20},{1,9},{5... | collective-permute-start | bytes 1572872 | tf_op jit(solution)/shard_map/feed_weights/ppermute | solution.py:557
  52.6 0.8 copy-done.43
  53.4 2.1 %add.31.own_ref = bf16[512,512]{1,0:T(8,128)(2,1)} custom-call(bf16[512,512]{1,0:T(8,128)(2,1)} %copy-done.37, bf16[512,512]{1,0:T(8,128)(2,1)} %copy-done.43), custom_call_target="tpu_custom_call" | custom-call | flops 115000000512 | bytes 1 | tf_op jit(solution)/shard_map/add/pallas_call | solution.py:593
  55.5 0.9 collective-permute-done.10.far_ref
  57.0 1.5 %collective-permute-start.11 = (bf16[512,512]{1,0:T(8,128)(2,1)}, bf16[512,512]{1,0:T(8,128)(2,1)}, u32[]{:S(2)}, u32[]{:S(2)}) collective-permute-start(bf16[512,512]{1,0:T(8,128)(2,1)} %add.31.own_ref), channel_id=1, source_target_pairs={{0,2},{1,3},{2,0},{3,1},{4,6},{5,7},{6,4},{7,5},{8,10},{9,11},{10,... | collective-permute-start | bytes 1572872 | tf_op jit(solution)/shard_map/sum_output/ppermute | solution.py:557
  58.5 0.8 collective-permute-done.13.other_far_ref
  59.4 6.7 %back.1 = (bf16[1024,512]{1,0:T(8,128)(2,1)S(1)}, bf16[1024,384]{1,0:T(8,128)(2,1)S(1)}, f32[4,2,8,128]{3,2,1,0:T(8,128)S(1)}, f32[32,512]{1,0:T(8,128)S(1)}) custom-call(s32[4]{0:T(128)S(1)} %copy-done.5, bf16[512,512]{1,0:T(8,128)(2,1)S(1)} %copy-done.14, bf16[512,512]{1,0:T(8,128)(2,1)} %collective-permute-done.10.far_ref, ...), custom_call_target="tpu_custom_call" | custom-call | flops 115000000512 | bytes 1 | tf_op jit(solution)/shard_map/back/pallas_call | solution.py:1012
  66.1 2.4 %split.4 = (bf16[256,512]{1,0:T(8,128)(2,1)}, bf16[256,512]{1,0:T(8,128)(2,1)S(1)}) custom-call(s32[1]{0:T(128)} %bitcast.11.bit_ref, bf16[512,512]{1,0:T(8,128)(2,1)S(1)} %copy-done.36, bf16[512,512]{1,0:T(8,128)(2,1)} %collective-permute-done.16.b_ref), custom_call_target="tpu_custom_call" | custom-call | flops 115000000512 | bytes 1 | tf_op jit(solution)/shard_map/split/pallas_call | solution.py:620
  68.5 0.6 slice.27
  69.2 2.0 %first.1 = (bf16[528,512]{1,0:T(8,128)(2,1)S(1)}, bf16[528,512]{1,0:T(8,128)(2,1)S(1)}) custom-call(s32[4]{0:T(128)S(1)} %copy-done.5, bf16[1024,384]{1,0:T(8,128)(2,1)S(1)} %get-tuple-element.289.gqkv_ref, f32[4,2,8,128]{3,2,1,0:T(8,128)S(1)} %get-tuple-element.297.slot_ref.a_ref, f32[4,10,8,128]{3,2,1,0:T(8,128)S(1)} %copy-done.1, ...), custom_call_target="tpu_custom_call" | custom-call | flops 115000000512 | bytes 1 | tf_op jit(solution)/shard_map/first/pallas_call | solution.py:581
  71.4 1.6 %collective-permute-start.14 = (f32[2,2,8,128]{3,2,1,0:T(8,128)}, f32[2,2,8,128]{3,2,1,0:T(8,128)}, u32[]{:S(2)}, u32[]{:S(2)}) collective-permute-start(f32[2,2,8,128]{3,2,1,0:T(8,128)} %slice.27), channel_id=1, source_target_pairs={{0,8},{4,12},{8,0},{12,4},{16,24},{20,28},{24,16},{28,20},{1,9},{5... | collective-permute-start | bytes 49160 | tf_op jit(solution)/shard_map/sum_slots/ppermute | solution.py:557
  73.0 1.5 %collective-permute-start.21 = (bf16[256,512]{1,0:T(8,128)(2,1)}, bf16[256,512]{1,0:T(8,128)(2,1)}, u32[]{:S(2)}, u32[]{:S(2)}) collective-permute-start(bf16[256,512]{1,0:T(8,128)(2,1)} %get-tuple-element.301), channel_id=1, source_target_pairs={{0,4},{4,0},{8,12},{12,8},{16,20},{20,16},{24,28},{28,24},{1,5},{5... | collective-permute-start | bytes 786440 | tf_op jit(solution)/shard_map/feed_weights/ppermute | solution.py:557
  74.5 3.8 %rest_weights.1 = (bf16[256,512]{1,0:T(8,128)(2,1)}, bf16[256,512]{1,0:T(8,128)(2,1)}) custom-call(s32[1]{0:T(128)} %bitcast.11.bit_ref, bf16[1024,512]{1,0:T(8,128)(2,1)} %get-tuple-element.288.first_ref, bf16[1024,384]{1,0:T(8,128)(2,1)} %copy-done.34, bf16[1024,512]{1,0:T(8,128)(2,1)} %copy-done.27, bf16[1024,128]{1,0:T(8,128)(2,1)} %copy-done.17, ...), custom_call_target="tpu_custom_call" | custom-call | flops 115000000512 | bytes 1 | tf_op jit(solution)/shard_map/rest_weights/pallas_call | solution.py:581
  78.8 0.9 pair.1.own_ref.near_ref
  79.7 1.5 %collective-permute-start.22 = (bf16[528,512]{1,0:T(8,128)(2,1)}, bf16[528,512]{1,0:T(8,128)(2,1)}, u32[]{:S(2)}, u32[]{:S(2)}) collective-permute-start(bf16[528,512]{1,0:T(8,128)(2,1)} %pair.1.own_ref.near_ref), channel_id=1, source_target_pairs={{0,2},{1,3},{2,0},{3,1},{4,6},{5,7},{6,4},{7,5},{8,10},{9,11},{10,... | collective-permute-start | bytes 1622024 | tf_op jit(solution)/shard_map/sum_first/ppermute | solution.py:557
  81.3 0.7 slots.1.a_ref
  82.2 1.8 %collective-permute-start.20 = (f32[1,2,8,128]{3,2,1,0:T(8,128)S(1)}, f32[1,2,8,128]{3,2,1,0:T(8,128)S(1)}, u32[]{:S(2)}, u32[]{:S(2)}) collective-permute-start(f32[1,2,8,128]{3,2,1,0:T(8,128)S(1)} %slice.36), channel_id=1, source_target_pairs={{0,4},{4,0},{8,12},{12,8},{16,20},{20,16},{24,28},{28,24},{1,5},{5... | collective-permute-start | bytes 24584 | tf_op jit(solution)/shard_map/sum_slots/ppermute | solution.py:557
  84.0 1.7 %split.5 = (bf16[128,512]{1,0:T(8,128)(2,1)}, bf16[128,512]{1,0:T(8,128)(2,1)S(1)}) custom-call(s32[1]{0:T(128)} %bitcast.13.bit_ref, bf16[256,512]{1,0:T(8,128)(2,1)S(1)} %get-tuple-element.303.a_ref, bf16[256,512]{1,0:T(8,128)(2,1)} %collective-permute-done.21.b_ref), custom_call_target="tpu_custom_call" | custom-call | flops 115000000512 | bytes 1 | tf_op jit(solution)/shard_map/split/pallas_call | solution.py:620
  85.7 0.7 copy-done.39
  86.3 2.6 %collective-permute-start.28 = (bf16[128,512]{1,0:T(8,128)(2,1)}, bf16[128,512]{1,0:T(8,128)(2,1)}, u32[]{:S(2)}, u32[]{:S(2)}) collective-permute-start(bf16[128,512]{1,0:T(8,128)(2,1)} %get-tuple-element.325), channel_id=1, source_target_pairs={{0,16},{4,20},{8,24},{12,28},{16,0},{20,4},{24,8},{28,12},{1,17},{... | collective-permute-start | bytes 393224 | tf_op jit(solution)/shard_map/feed_weights/ppermute | solution.py:557
  88.9 0.8 extra.1.a_ref
  89.9 1.8 %split.6 = (bf16[128,512]{1,0:T(8,128)(2,1)}, bf16[128,512]{1,0:T(8,128)(2,1)S(1)}) custom-call(s32[1]{0:T(128)} %bitcast.3.bit_ref, bf16[256,512]{1,0:T(8,128)(2,1)S(1)} %copy-done.38, bf16[256,512]{1,0:T(8,128)(2,1)} %collective-permute-done.19.b_ref), custom_call_target="tpu_custom_call" | custom-call | flops 115000000512 | bytes 1 | tf_op jit(solution)/shard_map/split/pallas_call | solution.py:620
  92.2 3.3 %output.1 = bf16[1024,512]{1,0:T(8,128)(2,1)} custom-call(s32[4]{0:T(128)S(1)} %copy-done.6, bf16[512,512]{1,0:T(8,128)(2,1)S(1)} %copy-done.13, bf16[512,512]{1,0:T(8,128)(2,1)} %collective-permute-done.11.far_ref, bf16[512,512]{1,0:T(8,128)(2,1)} %collective-permute-done.15.other_ref, bf16[512,512]{1,0:T(8,128)(2,1)} %collective-permute-done.18.other_far_ref, ...), custom_call_target="tpu_custom_call" | custom-call | flops 115000000512 | bytes 1 | tf_op jit(solution)/shard_map/output/pallas_call | solution.py:581
  95.5 1.3 plus.2.a_ref
  96.8 1.5 %collective-permute-start.26 = (f32[8,512]{1,0:T(8,128)}, f32[8,512]{1,0:T(8,128)}, u32[]{:S(2)}, u32[]{:S(2)}) collective-permute-start(f32[8,512]{1,0:T(8,128)} %plus.2.a_ref), channel_id=1, source_target_pairs={{0,2},{1,3},{2,0},{3,1},{4,6},{5,7},{6,4},{7,5},{8,10},{9,11},{10,... | collective-permute-start | bytes 49160 | tf_op jit(solution)/shard_map/sum_extra/ppermute | solution.py:557
  98.4 1.7 %add.32.a_ref = bf16[128,512]{1,0:T(8,128)(2,1)} custom-call(bf16[128,512]{1,0:T(8,128)(2,1)} %copy-done.39, bf16[128,512]{1,0:T(8,128)(2,1)} %collective-permute-done.28.b_ref), custom_call_target="tpu_custom_call" | custom-call | flops 115000000512 | bytes 1 | tf_op jit(solution)/shard_map/add/pallas_call | solution.py:593
  100.0 1.0 collective-permute-start.30
  101.0 1.6 %split.7 = (bf16[64,512]{1,0:T(8,128)(2,1)}, bf16[64,512]{1,0:T(8,128)(2,1)S(1)}) custom-call(s32[1]{0:T(128)} %bitcast.13.bit_ref, bf16[128,512]{1,0:T(8,128)(2,1)S(1)} %get-tuple-element.329.a_ref, bf16[128,512]{1,0:T(8,128)(2,1)} %collective-permute-done.27.b_ref), custom_call_target="tpu_custom_call" | custom-call | flops 115000000512 | bytes 1 | tf_op jit(solution)/shard_map/split/pallas_call | solution.py:620
  102.8 2.0 %collective-permute-start.29 = (bf16[64,512]{1,0:T(8,128)(2,1)}, bf16[64,512]{1,0:T(8,128)(2,1)}, u32[]{:S(2)}, u32[]{:S(2)}) collective-permute-start(bf16[64,512]{1,0:T(8,128)(2,1)} %get-tuple-element.343), channel_id=1, source_target_pairs={{0,16},{4,20},{8,24},{12,28},{16,0},{20,4},{24,8},{28,12},{1,17},{... | collective-permute-start | bytes 196616 | tf_op jit(solution)/shard_map/rest_weights/ppermute | solution.py:557
  104.8 0.7 plus.3.extra_ref
  105.6 4.4 %last.1 = bf16[1024,512]{1,0:T(8,128)(2,1)} custom-call(s32[4]{0:T(128)S(1)} %copy-done.7, bf16[528,512]{1,0:T(8,128)(2,1)} %pair.1.own_ref.near_ref, bf16[528,512]{1,0:T(8,128)(2,1)} %collective-permute-done.22.far_ref, bf16[528,512]{1,0:T(8,128)(2,1)S(1)} %collective-permute-done.24.other_ref, bf16[528,512]{1,0:T(8,128)(2,1)} %collective-permute-done.25.other_far_ref, ...), custom_call_target="tpu_custom_call" | custom-call | flops 115000000512 | bytes 1 | tf_op jit(solution)/shard_map/last/pallas_call | solution.py:581
  110.1 1.7 %collective-permute-done.30.b_ref = bf16[128,512]{1,0:T(8,128)(2,1)} collective-permute-done((bf16[128,512]{1,0:T(8,128)(2,1)}, bf16[128,512]{1,0:T(8,128)(2,1)}, u32[]{:S(2)}, u32[]{:S(2)}) %collective-permute-start.30) | collective-permute-done | bytes 131104 | tf_op jit(solution)/shard_map/feed_weights/ppermute | solution.py:557
  111.7 1.6 %concat.2.a_ref = bf16[256,512]{1,0:T(8,128)(2,1)} custom-call(bf16[128,512]{1,0:T(8,128)(2,1)S(1)} %copy-done.20, bf16[128,512]{1,0:T(8,128)(2,1)} %collective-permute-done.30.b_ref), custom_call_target="tpu_custom_call" | custom-call | flops 115000000512 | bytes 1 | tf_op jit(solution)/shard_map/concat/pallas_call | solution.py:908
  113.4 1.3 piece.1.a_ref
  114.7 0.8 collective-permute-start.33
  115.6 5.5 %collective-permute-done.31.b_ref = bf16[80,512]{1,0:T(8,128)(2,1)S(1)} collective-permute-done((bf16[80,512]{1,0:T(8,128)(2,1)S(1)}, bf16[80,512]{1,0:T(8,128)(2,1)S(1)}, u32[]{:S(2)}, u32[]{:S(2)}) %collective-permute-start.31) | collective-permute-done | bytes 81952 | tf_op jit(solution)/shard_map/rest_weights/ppermute | solution.py:557
  121.2 1.5 %collective-permute-done.33.b_ref = bf16[256,512]{1,0:T(8,128)(2,1)} collective-permute-done((bf16[256,512]{1,0:T(8,128)(2,1)}, bf16[256,512]{1,0:T(8,128)(2,1)}, u32[]{:S(2)}, u32[]{:S(2)}) %collective-permute-start.33) | collective-permute-done | bytes 262176 | tf_op jit(solution)/shard_map/feed_weights/ppermute | solution.py:557
  122.7 1.9 %concat.3.near_ref = bf16[512,512]{1,0:T(8,128)(2,1)} custom-call(bf16[256,512]{1,0:T(8,128)(2,1)} %concat.2.a_ref, bf16[256,512]{1,0:T(8,128)(2,1)} %collective-permute-done.33.b_ref), custom_call_target="tpu_custom_call" | custom-call | flops 115000000512 | bytes 1 | tf_op jit(solution)/shard_map/concat/pallas_call | solution.py:908
  124.5 2.4 %collective-permute-done.32.b_ref = bf16[144,512]{1,0:T(8,128)(2,1)S(1)} collective-permute-done((bf16[144,512]{1,0:T(8,128)(2,1)S(1)}, bf16[144,512]{1,0:T(8,128)(2,1)S(1)}, u32[]{:S(2)}, u32[]{:S(2)}) %collective-permute-start.32) | collective-permute-done | bytes 147488 | tf_op jit(solution)/shard_map/rest_weights/ppermute | solution.py:557
  127.0 1.5 %collective-permute-start.35 = (bf16[512,512]{1,0:T(8,128)(2,1)}, bf16[512,512]{1,0:T(8,128)(2,1)}, u32[]{:S(2)}, u32[]{:S(2)}) collective-permute-start(bf16[512,512]{1,0:T(8,128)(2,1)} %concat.3.near_ref), channel_id=1, source_target_pairs={{0,8},{4,12},{8,0},{12,4},{16,24},{20,28},{24,16},{28,20},{1,9},{5... | collective-permute-start | bytes 1572872 | tf_op jit(solution)/shard_map/feed_weights/ppermute | solution.py:557
  128.6 6.2 %collective-permute-done.34.far_ref = bf16[272,512]{1,0:T(8,128)(2,1)S(1)} collective-permute-done((bf16[272,512]{1,0:T(8,128)(2,1)S(1)}, bf16[272,512]{1,0:T(8,128)(2,1)S(1)}, u32[]{:S(2)}, u32[]{:S(2)}) %collective-permute-start.34) | collective-permute-done | bytes 278560 | tf_op jit(solution)/shard_map/rest_weights/ppermute | solution.py:557
  134.7 1.0 rest_unpack.1
  135.8 0.6 fusion
  136.4 4.0 %collective-permute-done.35.far_ref = bf16[512,512]{1,0:T(8,128)(2,1)} collective-permute-done((bf16[512,512]{1,0:T(8,128)(2,1)}, bf16[512,512]{1,0:T(8,128)(2,1)}, u32[]{:S(2)}, u32[]{:S(2)}) %collective-permute-start.35) | collective-permute-done | bytes 524320 | tf_op jit(solution)/shard_map/feed_weights/ppermute | solution.py:557
  140.4 2.7 %feed_unpack.1 = (f32[512,512]{1,0:T(8,128)}, f32[512,512]{1,0:T(8,128)}) custom-call(s32[1]{0:T(128)S(6)} %add.23.at_ref, bf16[512,512]{1,0:T(8,128)(2,1)} %concat.3.near_ref, bf16[512,512]{1,0:T(8,128)(2,1)} %collective-permute-done.35.far_ref), custom_call_target="tpu_custom_call" | custom-call | flops 115000000512 | bytes 1 | tf_op jit(solution)/shard_map/feed_unpack/pallas_call | solution.py:581
  (151 shorter events, 6.5 us)
Async XLA Ops:
  0.6 6.9 %collective-permute-start = (bf16[128,512]{1,0:T(8,128)(2,1)}, bf16[128,512]{1,0:T(8,128)(2,1)S(1)}, u32[]{:S(2)}, u32[]{:S(2)}) collective-permute-start(bf16[128,512]{1,0:T(8,128)(2,1)} %wo_ref), channel_id=1, source_target_pairs={{0,2},{1,3},{2,0},{3,1},{4,6},{5,7},{6,4},{7,5},{8,10},{9,11},{10,... | collective-permute-start | bytes 393224 | tf_op jit(solution)/shard_map/gather_w_out/ppermute | solution.py:557
  7.6 3.1 %copy-start.47 = (bf16[128,512]{1,0:T(8,128)(2,1)}, bf16[128,512]{1,0:T(8,128)(2,1)S(1)}, u32[]{:S(2)}) copy-start(bf16[128,512]{1,0:T(8,128)(2,1)S(1)} %collective-permute-done.refs_6_) | copy-start | bytes 393220
  7.6 4.2 %collective-permute-start.1 = (f32[1,10,8,128]{3,2,1,0:T(8,128)}, f32[1,10,8,128]{3,2,1,0:T(8,128)S(1)}, u32[]{:S(2)}, u32[]{:S(2)}) collective-permute-start(f32[1,10,8,128]{3,2,1,0:T(8,128)} %bitcast.27), channel_id=1, source_target_pairs={{0,4},{4,0},{8,12},{12,8},{16,20},{20,16},{24,28},{28,24},{1,5},{5... | collective-permute-start | bytes 122888 | tf_op jit(solution)/shard_map/summaries/ppermute | solution.py:557
  11.8 4.5 %collective-permute-start.2 = (f32[2,10,8,128]{3,2,1,0:T(8,128)S(1)}, f32[2,10,8,128]{3,2,1,0:T(8,128)S(1)}, u32[]{:S(2)}, u32[]{:S(2)}) collective-permute-start(f32[2,10,8,128]{3,2,1,0:T(8,128)S(1)} %constant_dynamic-update-slice_fusion), channel_id=1, source_target_pairs={{0,8},{4,12},{8,0},{12,4},{16,24},{20,28},{24,16},{28,20},{1,9},{5... | collective-permute-start | bytes 245768 | tf_op jit(solution)/shard_map/summaries/ppermute | solution.py:557
  16.4 8.0 %copy-start.18 = (bf16[128,512]{1,0:T(8,128)(2,1)S(1)}, bf16[128,512]{1,0:T(8,128)(2,1)}, u32[]{:S(2)}) copy-start(bf16[128,512]{1,0:T(8,128)(2,1)} %wo_ref) | copy-start | bytes 393220
  16.4 8.5 %copy-start.48 = (bf16[128,512]{1,0:T(8,128)(2,1)S(1)}, bf16[128,512]{1,0:T(8,128)(2,1)}, u32[]{:S(2)}) copy-start(bf16[128,512]{1,0:T(8,128)(2,1)} %copy-done.47) | copy-start | bytes 393220
  17.9 8.4 %copy-start.17 = (bf16[1024,128]{1,0:T(8,128)(2,1)}, bf16[1024,128]{1,0:T(8,128)(2,1)S(1)}, u32[]{:S(2)}) copy-start(bf16[1024,128]{1,0:T(8,128)(2,1)S(1)} %get-tuple-element.291.refs_0_.att_ref) | copy-start | bytes 786436
  17.9 6.4 %collective-permute-start.4 = (bf16[1024,128]{1,0:T(8,128)(2,1)S(1)}, bf16[1024,128]{1,0:T(8,128)(2,1)S(1)}, u32[]{:S(2)}, u32[]{:S(2)}) collective-permute-start(bf16[1024,128]{1,0:T(8,128)(2,1)S(1)} %get-tuple-element.291.refs_0_.att_ref), channel_id=1, source_target_pairs={{0,2},{1,3},{2,0},{3,1},{4,6},{5,7},{6,4},{7,5},{8,10},{9,11},{10,... | collective-permute-start | bytes 786440 | tf_op jit(solution)/shard_map/gather_attended/ppermute | solution.py:557
  19.5 6.7 %collective-permute-start.3 = (bf16[1024,128]{1,0:T(8,128)(2,1)S(1)}, bf16[1024,128]{1,0:T(8,128)(2,1)S(1)}, u32[]{:S(2)}, u32[]{:S(2)}) collective-permute-start(bf16[1024,128]{1,0:T(8,128)(2,1)S(1)} %get-tuple-element.291.refs_0_.att_ref), channel_id=1, source_target_pairs={{0,1},{1,0},{2,3},{3,2},{4,5},{5,4},{6,7},{7,6},{8,9},{9,8},{10,11... | collective-permute-start | bytes 786440 | tf_op jit(solution)/shard_map/gather_attended/ppermute | solution.py:557
  24.4 1.9 %collective-permute-start.5 = (bf16[1024,128]{1,0:T(8,128)(2,1)S(1)}, bf16[1024,128]{1,0:T(8,128)(2,1)S(1)}, u32[]{:S(2)}, u32[]{:S(2)}) collective-permute-start(bf16[1024,128]{1,0:T(8,128)(2,1)S(1)} %collective-permute-done.4.refs_2_), channel_id=1, source_target_pairs={{0,1},{1,0},{2,3},{3,2},{4,5},{5,4},{6,7},{7,6},{8,9},{9,8},{10,11... | collective-permute-start | bytes 786440 | tf_op jit(solution)/shard_map/gather_attended/ppermute | solution.py:557
  24.4 1.7 %collective-permute-start.6 = (bf16[128,512]{1,0:T(8,128)(2,1)S(1)}, bf16[128,512]{1,0:T(8,128)(2,1)S(1)}, u32[]{:S(2)}, u32[]{:S(2)}) collective-permute-start(bf16[128,512]{1,0:T(8,128)(2,1)S(1)} %copy-done.18), channel_id=1, source_target_pairs={{0,1},{1,0},{2,3},{3,2},{4,5},{5,4},{6,7},{7,6},{8,9},{9,8},{10,11... | collective-permute-start | bytes 393224 | tf_op jit(solution)/shard_map/gather_w_out/ppermute | solution.py:557
  24.9 1.4 collective-permute-start.7
  36.9 2.2 %collective-permute-start.8 = (bf16[512,512]{1,0:T(8,128)(2,1)}, bf16[512,512]{1,0:T(8,128)(2,1)S(1)}, u32[]{:S(2)}, u32[]{:S(2)}) collective-permute-start(bf16[512,512]{1,0:T(8,128)(2,1)} %get-tuple-element.236), channel_id=1, source_target_pairs={{0,1},{1,0},{2,3},{3,2},{4,5},{5,4},{6,7},{7,6},{8,9},{9,8},{10,11... | collective-permute-start | bytes 1572872 | tf_op jit(solution)/shard_map/sum_second/ppermute | solution.py:557
  39.9 3.8 %copy-start.4 = (s32[4]{0:T(128)S(1)}, s32[4]{0:T(128)}, u32[]{:S(2)}) copy-start(s32[4]{0:T(128)} %pad_add_fusion.pos_ref) | copy-start | bytes 52
  39.9 3.8 %copy-start.8 = (bf16[1024,512]{1,0:T(8,128)(2,1)S(1)}, bf16[1024,512]{1,0:T(8,128)(2,1)}, u32[]{:S(2)}) copy-start(bf16[1024,512]{1,0:T(8,128)(2,1)} %cot_ref.1) | copy-start | bytes 3145732
  39.9 3.8 %copy-start.12 = (bf16[512,512]{1,0:T(8,128)(2,1)S(1)}, bf16[512,512]{1,0:T(8,128)(2,1)}, u32[]{:S(2)}) copy-start(bf16[512,512]{1,0:T(8,128)(2,1)} %down_ref) | copy-start | bytes 1572868
  39.9 3.8 %copy-start.29 = (bf16[1024,512]{1,0:T(8,128)(2,1)S(1)}, bf16[1024,512]{1,0:T(8,128)(2,1)}, u32[]{:S(2)}) copy-start(bf16[1024,512]{1,0:T(8,128)(2,1)} %get-tuple-element.242.second_ref) | copy-start | bytes 3145732
  42.2 14.3 %collective-permute-start.10 = (bf16[512,512]{1,0:T(8,128)(2,1)}, bf16[512,512]{1,0:T(8,128)(2,1)}, u32[]{:S(2)}, u32[]{:S(2)}) collective-permute-start(bf16[512,512]{1,0:T(8,128)(2,1)} %add.30.own_ref), channel_id=1, source_target_pairs={{0,2},{1,3},{2,0},{3,1},{4,6},{5,7},{6,4},{7,5},{8,10},{9,11},{10,... | collective-permute-start | bytes 1572872 | tf_op jit(solution)/shard_map/sum_second/ppermute | solution.py:557
  43.7 14.8 %collective-permute-start.12 = (bf16[512,512]{1,0:T(8,128)(2,1)}, bf16[512,512]{1,0:T(8,128)(2,1)}, u32[]{:S(2)}, u32[]{:S(2)}) collective-permute-start(bf16[512,512]{1,0:T(8,128)(2,1)} %add.30.own_ref), channel_id=1, source_target_pairs={{0,1},{1,0},{2,3},{3,2},{4,5},{5,4},{6,7},{7,6},{8,9},{9,8},{10,11... | collective-permute-start | bytes 1572872 | tf_op jit(solution)/shard_map/sum_second/ppermute | solution.py:557
  46.2 4.3 %copy-start.23 = (f32[512]{0:T(512)S(1)}, f32[512]{0:T(512)}, u32[]{:S(2)}) copy-start(f32[512]{0:T(512)} %param.14) | copy-start | bytes 6148
  50.0 2.5 %collective-permute-start.9 = (bf16[512,512]{1,0:T(8,128)(2,1)S(1)}, bf16[512,512]{1,0:T(8,128)(2,1)S(1)}, u32[]{:S(2)}, u32[]{:S(2)}) collective-permute-start(bf16[512,512]{1,0:T(8,128)(2,1)S(1)} %get-tuple-element.247), channel_id=1, source_target_pairs={{0,1},{1,0},{2,3},{3,2},{4,5},{5,4},{6,7},{7,6},{8,9},{9,8},{10,11... | collective-permute-start | bytes 1572872 | tf_op jit(solution)/shard_map/sum_output/ppermute | solution.py:557
  51.0 15.1 %collective-permute-start.16 = (bf16[512,512]{1,0:T(8,128)(2,1)}, bf16[512,512]{1,0:T(8,128)(2,1)}, u32[]{:S(2)}, u32[]{:S(2)}) collective-permute-start(bf16[512,512]{1,0:T(8,128)(2,1)} %get-tuple-element.271), channel_id=1, source_target_pairs={{0,8},{4,12},{8,0},{12,4},{16,24},{20,28},{24,16},{28,20},{1,9},{5... | collective-permute-start | bytes 1572872 | tf_op jit(solution)/shard_map/feed_weights/ppermute | solution.py:557
  55.5 3.8 %copy-start.1 = (f32[4,10,8,128]{3,2,1,0:T(8,128)S(1)}, f32[4,10,8,128]{3,2,1,0:T(8,128)}, u32[]{:S(2)}) copy-start(f32[4,10,8,128]{3,2,1,0:T(8,128)} %copy-done) | copy-start | bytes 491524
  55.5 3.8 %copy-start.5 = (s32[4]{0:T(128)S(1)}, s32[4]{0:T(128)}, u32[]{:S(2)}) copy-start(s32[4]{0:T(128)} %pad_add_fusion.pos_ref) | copy-start | bytes 52
  55.5 3.8 %copy-start.9 = (bf16[1024,512]{1,0:T(8,128)(2,1)S(1)}, bf16[1024,512]{1,0:T(8,128)(2,1)}, u32[]{:S(2)}) copy-start(bf16[1024,512]{1,0:T(8,128)(2,1)} %cot_ref.1) | copy-start | bytes 3145732
  55.5 3.8 %copy-start.14 = (bf16[512,512]{1,0:T(8,128)(2,1)S(1)}, bf16[512,512]{1,0:T(8,128)(2,1)}, u32[]{:S(2)}) copy-start(bf16[512,512]{1,0:T(8,128)(2,1)} %add.30.own_ref) | copy-start | bytes 1572868
  55.5 3.8 %copy-start.19 = (bf16[128,512]{1,0:T(8,128)(2,1)S(1)}, bf16[128,512]{1,0:T(8,128)(2,1)}, u32[]{:S(2)}) copy-start(bf16[128,512]{1,0:T(8,128)(2,1)} %wo_ref) | copy-start | bytes 393220
  55.5 3.8 %copy-start.21 = (f32[512]{0:T(512)S(1)}, f32[512]{0:T(512)}, u32[]{:S(2)}) copy-start(f32[512]{0:T(512)} %param.19) | copy-start | bytes 6148
  55.5 3.8 %copy-start.25 = (f32[1024,512]{1,0:T(8,128)S(1)}, f32[1024,512]{1,0:T(8,128)}, u32[]{:S(2)}) copy-start(f32[1024,512]{1,0:T(8,128)} %get-tuple-element.318.mid_ref) | copy-start | bytes 6291460
  55.5 3.8 %copy-start.33 = (bf16[3,1024,128]{2,1,0:T(8,128)(2,1)S(1)}, bf16[3,1024,128]{2,1,0:T(8,128)(2,1)}, u32[]{:S(2)}) copy-start(bf16[3,1024,128]{2,1,0:T(8,128)(2,1)} %get-tuple-element.266.qkv_ref) | copy-start | bytes 2359300
  56.5 2.8 %collective-permute-start.13 = (bf16[512,512]{1,0:T(8,128)(2,1)}, bf16[512,512]{1,0:T(8,128)(2,1)S(1)}, u32[]{:S(2)}, u32[]{:S(2)}) collective-permute-start(bf16[512,512]{1,0:T(8,128)(2,1)} %collective-permute-done.10.far_ref), channel_id=1, source_target_pairs={{0,1},{1,0},{2,3},{3,2},{4,5},{5,4},{6,7},{7,6},{8,9},{9,8},{10,11... | collective-permute-start | bytes 1572872 | tf_op jit(solution)/shard_map/sum_second/ppermute | solution.py:557
  56.5 12.7 %collective-permute-start.15 = (bf16[512,512]{1,0:T(8,128)(2,1)}, bf16[512,512]{1,0:T(8,128)(2,1)}, u32[]{:S(2)}, u32[]{:S(2)}) collective-permute-start(bf16[512,512]{1,0:T(8,128)(2,1)} %add.31.own_ref), channel_id=1, source_target_pairs={{0,1},{1,0},{2,3},{3,2},{4,5},{5,4},{6,7},{7,6},{8,9},{9,8},{10,11... | collective-permute-start | bytes 1572872 | tf_op jit(solution)/shard_map/sum_output/ppermute | solution.py:557
  57.0 25.0 %collective-permute-start.11 = (bf16[512,512]{1,0:T(8,128)(2,1)}, bf16[512,512]{1,0:T(8,128)(2,1)}, u32[]{:S(2)}, u32[]{:S(2)}) collective-permute-start(bf16[512,512]{1,0:T(8,128)(2,1)} %add.31.own_ref), channel_id=1, source_target_pairs={{0,2},{1,3},{2,0},{3,1},{4,6},{5,7},{6,4},{7,5},{8,10},{9,11},{10,... | collective-permute-start | bytes 1572872 | tf_op jit(solution)/shard_map/sum_output/ppermute | solution.py:557
  59.4 6.7 %copy-start.36 = (bf16[512,512]{1,0:T(8,128)(2,1)S(1)}, bf16[512,512]{1,0:T(8,128)(2,1)}, u32[]{:S(2)}) copy-start(bf16[512,512]{1,0:T(8,128)(2,1)} %copy-done.35) | copy-start | bytes 1572868
  66.0 3.1 %copy-start.2 = (f32[4,2,8,128]{3,2,1,0:T(8,128)}, f32[4,2,8,128]{3,2,1,0:T(8,128)S(1)}, u32[]{:S(2)}) copy-start(f32[4,2,8,128]{3,2,1,0:T(8,128)S(1)} %get-tuple-element.297.slot_ref.a_ref) | copy-start | bytes 98308
  66.1 3.1 %copy-start.34 = (bf16[1024,384]{1,0:T(8,128)(2,1)}, bf16[1024,384]{1,0:T(8,128)(2,1)S(1)}, u32[]{:S(2)}) copy-start(bf16[1024,384]{1,0:T(8,128)(2,1)S(1)} %get-tuple-element.289.gqkv_ref) | copy-start | bytes 2359300
  66.1 3.1 %copy-start.10 = (bf16[1024,512]{1,0:T(8,128)(2,1)S(1)}, bf16[1024,512]{1,0:T(8,128)(2,1)}, u32[]{:S(2)}) copy-start(bf16[1024,512]{1,0:T(8,128)(2,1)} %tok_ref.3) | copy-start | bytes 3145732
  66.1 3.1 %copy-start.15 = (bf16[3,512,128]{2,1,0:T(8,128)(2,1)S(1)}, bf16[3,512,128]{2,1,0:T(8,128)(2,1)}, u32[]{:S(2)}) copy-start(bf16[3,512,128]{2,1,0:T(8,128)(2,1)} %w_ref.2) | copy-start | bytes 1179652
  71.2 7.6 %collective-permute-start.17 = (bf16[528,512]{1,0:T(8,128)(2,1)S(1)}, bf16[528,512]{1,0:T(8,128)(2,1)S(1)}, u32[]{:S(2)}, u32[]{:S(2)}) collective-permute-start(bf16[528,512]{1,0:T(8,128)(2,1)S(1)} %get-tuple-element.284), channel_id=1, source_target_pairs={{0,1},{1,0},{2,3},{3,2},{4,5},{5,4},{6,7},{7,6},{8,9},{9,8},{10,11... | collective-permute-start | bytes 1622024 | tf_op jit(solution)/shard_map/sum_first/ppermute | solution.py:557
  71.4 9.9 %collective-permute-start.14 = (f32[2,2,8,128]{3,2,1,0:T(8,128)}, f32[2,2,8,128]{3,2,1,0:T(8,128)}, u32[]{:S(2)}, u32[]{:S(2)}) collective-permute-start(f32[2,2,8,128]{3,2,1,0:T(8,128)} %slice.27), channel_id=1, source_target_pairs={{0,8},{4,12},{8,0},{12,4},{16,24},{20,28},{24,16},{28,20},{1,9},{5... | collective-permute-start | bytes 49160 | tf_op jit(solution)/shard_map/sum_slots/ppermute | solution.py:557
  73.0 9.2 %collective-permute-start.21 = (bf16[256,512]{1,0:T(8,128)(2,1)}, bf16[256,512]{1,0:T(8,128)(2,1)}, u32[]{:S(2)}, u32[]{:S(2)}) collective-permute-start(bf16[256,512]{1,0:T(8,128)(2,1)} %get-tuple-element.301), channel_id=1, source_target_pairs={{0,4},{4,0},{8,12},{12,8},{16,20},{20,16},{24,28},{28,24},{1,5},{5... | collective-permute-start | bytes 786440 | tf_op jit(solution)/shard_map/feed_weights/ppermute | solution.py:557
  78.3 11.5 %collective-permute-start.19 = (bf16[256,512]{1,0:T(8,128)(2,1)}, bf16[256,512]{1,0:T(8,128)(2,1)}, u32[]{:S(2)}, u32[]{:S(2)}) collective-permute-start(bf16[256,512]{1,0:T(8,128)(2,1)} %get-tuple-element.300), channel_id=1, source_target_pairs={{0,4},{4,0},{8,12},{12,8},{16,20},{20,16},{24,28},{28,24},{1,5},{5... | collective-permute-start | bytes 786440 | tf_op jit(solution)/shard_map/rest_weights/ppermute | solution.py:557
  79.7 18.6 %collective-permute-start.22 = (bf16[528,512]{1,0:T(8,128)(2,1)}, bf16[528,512]{1,0:T(8,128)(2,1)}, u32[]{:S(2)}, u32[]{:S(2)}) collective-permute-start(bf16[528,512]{1,0:T(8,128)(2,1)} %pair.1.own_ref.near_ref), channel_id=1, source_target_pairs={{0,2},{1,3},{2,0},{3,1},{4,6},{5,7},{6,4},{7,5},{8,10},{9,11},{10,... | collective-permute-start | bytes 1622024 | tf_op jit(solution)/shard_map/sum_first/ppermute | solution.py:557
  82.0 6.9 %copy-start.16 = (bf16[3,512,128]{2,1,0:T(8,128)(2,1)S(1)}, bf16[3,512,128]{2,1,0:T(8,128)(2,1)}, u32[]{:S(2)}) copy-start(bf16[3,512,128]{2,1,0:T(8,128)(2,1)} %w_ref.2) | copy-start | bytes 1179652
  82.0 10.1 %collective-permute-start.18 = (bf16[512,512]{1,0:T(8,128)(2,1)}, bf16[512,512]{1,0:T(8,128)(2,1)}, u32[]{:S(2)}, u32[]{:S(2)}) collective-permute-start(bf16[512,512]{1,0:T(8,128)(2,1)} %collective-permute-done.11.far_ref), channel_id=1, source_target_pairs={{0,1},{1,0},{2,3},{3,2},{4,5},{5,4},{6,7},{7,6},{8,9},{9,8},{10,11... | collective-permute-start | bytes 1572872 | tf_op jit(solution)/shard_map/sum_output/ppermute | solution.py:557
  82.2 6.7 %collective-permute-start.20 = (f32[1,2,8,128]{3,2,1,0:T(8,128)S(1)}, f32[1,2,8,128]{3,2,1,0:T(8,128)S(1)}, u32[]{:S(2)}, u32[]{:S(2)}) collective-permute-start(f32[1,2,8,128]{3,2,1,0:T(8,128)S(1)} %slice.36), channel_id=1, source_target_pairs={{0,4},{4,0},{8,12},{12,8},{16,20},{20,16},{24,28},{28,24},{1,5},{5... | collective-permute-start | bytes 24584 | tf_op jit(solution)/shard_map/sum_slots/ppermute | solution.py:557
  86.3 12.0 %collective-permute-start.28 = (bf16[128,512]{1,0:T(8,128)(2,1)}, bf16[128,512]{1,0:T(8,128)(2,1)}, u32[]{:S(2)}, u32[]{:S(2)}) collective-permute-start(bf16[128,512]{1,0:T(8,128)(2,1)} %get-tuple-element.325), channel_id=1, source_target_pairs={{0,16},{4,20},{8,24},{12,28},{16,0},{20,4},{24,8},{28,12},{1,17},{... | collective-permute-start | bytes 393224 | tf_op jit(solution)/shard_map/feed_weights/ppermute | solution.py:557
  89.7 5.8 %collective-permute-start.23 = (f32[8,512]{1,0:T(8,128)}, f32[8,512]{1,0:T(8,128)}, u32[]{:S(2)}, u32[]{:S(2)}) collective-permute-start(f32[8,512]{1,0:T(8,128)} %extra.1.a_ref), channel_id=1, source_target_pairs={{0,1},{1,0},{2,3},{3,2},{4,5},{5,4},{6,7},{7,6},{8,9},{9,8},{10,11... | collective-permute-start | bytes 49160 | tf_op jit(solution)/shard_map/sum_extra/ppermute | solution.py:557
  91.7 9.3 %collective-permute-start.27 = (bf16[128,512]{1,0:T(8,128)(2,1)}, bf16[128,512]{1,0:T(8,128)(2,1)}, u32[]{:S(2)}, u32[]{:S(2)}) collective-permute-start(bf16[128,512]{1,0:T(8,128)(2,1)} %get-tuple-element.324), channel_id=1, source_target_pairs={{0,8},{4,12},{8,0},{12,4},{16,24},{20,28},{24,16},{28,20},{1,9},{5... | collective-permute-start | bytes 393224 | tf_op jit(solution)/shard_map/rest_weights/ppermute | solution.py:557
  96.8 5.8 %collective-permute-start.26 = (f32[8,512]{1,0:T(8,128)}, f32[8,512]{1,0:T(8,128)}, u32[]{:S(2)}, u32[]{:S(2)}) collective-permute-start(f32[8,512]{1,0:T(8,128)} %plus.2.a_ref), channel_id=1, source_target_pairs={{0,2},{1,3},{2,0},{3,1},{4,6},{5,7},{6,4},{7,5},{8,10},{9,11},{10,... | collective-permute-start | bytes 49160 | tf_op jit(solution)/shard_map/sum_extra/ppermute | solution.py:557
  98.4 7.2 %collective-permute-start.25 = (bf16[528,512]{1,0:T(8,128)(2,1)}, bf16[528,512]{1,0:T(8,128)(2,1)}, u32[]{:S(2)}, u32[]{:S(2)}) collective-permute-start(bf16[528,512]{1,0:T(8,128)(2,1)} %collective-permute-done.22.far_ref), channel_id=1, source_target_pairs={{0,1},{1,0},{2,3},{3,2},{4,5},{5,4},{6,7},{7,6},{8,9},{9,8},{10,11... | collective-permute-start | bytes 1622024 | tf_op jit(solution)/shard_map/sum_first/ppermute | solution.py:557
  100.0 11.7 %collective-permute-start.30 = (bf16[128,512]{1,0:T(8,128)(2,1)}, bf16[128,512]{1,0:T(8,128)(2,1)}, u32[]{:S(2)}, u32[]{:S(2)}) collective-permute-start(bf16[128,512]{1,0:T(8,128)(2,1)} %add.32.a_ref), channel_id=1, source_target_pairs={{0,16},{4,20},{8,24},{12,28},{16,0},{20,4},{24,8},{28,12},{1,17},{... | collective-permute-start | bytes 393224 | tf_op jit(solution)/shard_map/feed_weights/ppermute | solution.py:557
  102.6 3.0 %collective-permute-start.24 = (bf16[528,512]{1,0:T(8,128)(2,1)}, bf16[528,512]{1,0:T(8,128)(2,1)S(1)}, u32[]{:S(2)}, u32[]{:S(2)}) collective-permute-start(bf16[528,512]{1,0:T(8,128)(2,1)} %pair.1.own_ref.near_ref), channel_id=1, source_target_pairs={{0,1},{1,0},{2,3},{3,2},{4,5},{5,4},{6,7},{7,6},{8,9},{9,8},{10,11... | collective-permute-start | bytes 1622024 | tf_op jit(solution)/shard_map/sum_first/ppermute | solution.py:557
  102.8 2.8 %copy-start.11 = (bf16[1024,512]{1,0:T(8,128)(2,1)S(1)}, bf16[1024,512]{1,0:T(8,128)(2,1)}, u32[]{:S(2)}) copy-start(bf16[1024,512]{1,0:T(8,128)(2,1)} %tok_ref.3) | copy-start | bytes 3145732
  102.8 2.8 %copy-start.24 = (f32[512]{0:T(512)S(1)}, f32[512]{0:T(512)}, u32[]{:S(2)}) copy-start(f32[512]{0:T(512)} %param.14) | copy-start | bytes 6148
  102.8 2.8 %copy-start.28 = (bf16[1024,512]{1,0:T(8,128)(2,1)S(1)}, bf16[1024,512]{1,0:T(8,128)(2,1)}, u32[]{:S(2)}) copy-start(bf16[1024,512]{1,0:T(8,128)(2,1)} %copy-done.27) | copy-start | bytes 3145732
  102.8 10.5 %collective-permute-start.29 = (bf16[64,512]{1,0:T(8,128)(2,1)}, bf16[64,512]{1,0:T(8,128)(2,1)}, u32[]{:S(2)}, u32[]{:S(2)}) collective-permute-start(bf16[64,512]{1,0:T(8,128)(2,1)} %get-tuple-element.343), channel_id=1, source_target_pairs={{0,16},{4,20},{8,24},{12,28},{16,0},{20,4},{24,8},{28,12},{1,17},{... | collective-permute-start | bytes 196616 | tf_op jit(solution)/shard_map/rest_weights/ppermute | solution.py:557
  105.6 6.2 %copy-start.20 = (bf16[128,512]{1,0:T(8,128)(2,1)S(1)}, bf16[128,512]{1,0:T(8,128)(2,1)}, u32[]{:S(2)}) copy-start(bf16[128,512]{1,0:T(8,128)(2,1)} %add.32.a_ref) | copy-start | bytes 393220
  110.1 3.3 %copy-start.40 = (f32[8,512]{1,0:T(8,128)S(1)}, f32[8,512]{1,0:T(8,128)}, u32[]{:S(2)}) copy-start(f32[8,512]{1,0:T(8,128)} %get-tuple-element.352.up_ref) | copy-start | bytes 49156
  114.7 6.4 %collective-permute-start.31 = (bf16[80,512]{1,0:T(8,128)(2,1)S(1)}, bf16[80,512]{1,0:T(8,128)(2,1)S(1)}, u32[]{:S(2)}, u32[]{:S(2)}) collective-permute-start(bf16[80,512]{1,0:T(8,128)(2,1)S(1)} %piece.1.a_ref), channel_id=1, source_target_pairs={{0,16},{4,20},{8,24},{12,28},{16,0},{20,4},{24,8},{28,12},{1,17},{... | collective-permute-start | bytes 245768 | tf_op jit(solution)/shard_map/rest_weights/ppermute | solution.py:557
  114.7 7.9 %collective-permute-start.33 = (bf16[256,512]{1,0:T(8,128)(2,1)}, bf16[256,512]{1,0:T(8,128)(2,1)}, u32[]{:S(2)}, u32[]{:S(2)}) collective-permute-start(bf16[256,512]{1,0:T(8,128)(2,1)} %concat.2.a_ref), channel_id=1, source_target_pairs={{0,4},{4,0},{8,12},{12,8},{16,20},{20,16},{24,28},{28,24},{1,5},{5... | collective-permute-start | bytes 786440 | tf_op jit(solution)/shard_map/feed_weights/ppermute | solution.py:557
  121.1 5.8 %collective-permute-start.32 = (bf16[144,512]{1,0:T(8,128)(2,1)S(1)}, bf16[144,512]{1,0:T(8,128)(2,1)S(1)}, u32[]{:S(2)}, u32[]{:S(2)}) collective-permute-start(bf16[144,512]{1,0:T(8,128)(2,1)S(1)} %merge.2.a_ref), channel_id=1, source_target_pairs={{0,8},{4,12},{8,0},{12,4},{16,24},{20,28},{24,16},{28,20},{1,9},{5... | collective-permute-start | bytes 442376 | tf_op jit(solution)/shard_map/rest_weights/ppermute | solution.py:557
  127.0 7.8 %collective-permute-start.34 = (bf16[272,512]{1,0:T(8,128)(2,1)S(1)}, bf16[272,512]{1,0:T(8,128)(2,1)S(1)}, u32[]{:S(2)}, u32[]{:S(2)}) collective-permute-start(bf16[272,512]{1,0:T(8,128)(2,1)S(1)} %merge.3.near_ref), channel_id=1, source_target_pairs={{0,4},{4,0},{8,12},{12,8},{16,20},{20,16},{24,28},{28,24},{1,5},{5... | collective-permute-start | bytes 835592 | tf_op jit(solution)/shard_map/rest_weights/ppermute | solution.py:557
  127.0 13.4 %collective-permute-start.35 = (bf16[512,512]{1,0:T(8,128)(2,1)}, bf16[512,512]{1,0:T(8,128)(2,1)}, u32[]{:S(2)}, u32[]{:S(2)}) collective-permute-start(bf16[512,512]{1,0:T(8,128)(2,1)} %concat.3.near_ref), channel_id=1, source_target_pairs={{0,8},{4,12},{8,0},{12,4},{16,24},{20,28},{24,16},{28,20},{1,9},{5... | collective-permute-start | bytes 1572872 | tf_op jit(solution)/shard_map/feed_weights/ppermute | solution.py:557
  (23 other events, 34.1 us)

commit v4 on v3

--- a/solution.py
+++ b/solution.py
@@ -162,9 +162,9 @@
         e = jnp.exp(s - top)
         shrink = jnp.exp(mine - top)
         scale = 1.0 / (stat_ref[b, 1:2] * shrink + jnp.sum(e, axis=0, keepdims=True))
-        p = jnp.concatenate([exp_ref[b] * (shrink * scale), e * scale])
+        p = jnp.concatenate([exp_ref[b] * (shrink * scale), e * scale]).astype(bf16)
         prob_ref[b] = p
-        a = tn(p.astype(bf16), jnp.concatenate([qkv_ref[2, at], values]))
+        a = tn(p, jnp.concatenate([qkv_ref[2, at], values]))
         att_ref[at] = collect(a, 1.0).astype(bf16)
 
 
@@ -360,12 +360,13 @@
         query = spread(qkv_ref[0, at], SCALE)
         keys = jnp.concatenate([qkv_ref[1, at], far_keys])
         values = jnp.concatenate([qkv_ref[2, at], far_values])
-        p = prob_ref[b]
+        p_low = prob_ref[b]
+        p = p_low.astype(f32)
         dp = nt(values, da)
         ds = (p * (dp - jnp.sum(p * dp, axis=0, keepdims=True))).astype(bf16)
         gq = collect(tn(ds, keys), SCALE)
         gk = nn(ds, query)
-        gv = nn(p.astype(bf16), da)
+        gv = nn(p_low, da)
         gqkv_ref[at, :width] = gq.astype(bf16)
         gqkv_ref[at, width : 2 * width] = gk[:SPAN].astype(bf16)
         gqkv_ref[at, 2 * width :] = gv[:SPAN].astype(bf16)
@@ -467,6 +468,7 @@
     other_ref,
     other_far_ref,
     extra_ref,
+    extra_far_ref,
     tok_ref,
     low_ref,
     gain_ref,
@@ -478,7 +480,8 @@
     per = e.shape[0] // SPAN
     pieces = []
     for i in range(per):
-        pieces.append(e[i * SPAN : (i + 1) * SPAN] + extra_ref[pl.ds(step * per + i, 1)])
+        at = pl.ds(step * per + i, 1)
+        pieces.append(e[i * SPAN : (i + 1) * SPAN] + (extra_ref[at] + extra_far_ref[at]))
     e = jnp.concatenate(pieces)
     n, r = normed(tok_ref[...].astype(f32))
     out_ref[...] = (low_ref[...].astype(f32) + norm_back(e, n, r, gain_ref[...])).astype(bf16)
@@ -513,18 +516,23 @@
     out_ref[...] = (mid_ref[...] + e + b_ref[...]).astype(bf16)
 
 
-def feed_unpack_kernel(count, at_ref, near_ref, far_ref, down_ref, up_ref):
-    rows = 2 * near_ref.shape[0] // count
-    part = count // 2
+def feed_unpack_kernel(
+    count, at_ref, own_ref, one_ref, two_ref, both_ref, down_ref, up_ref
+):
+    part = count // 4
+    rows = own_ref.shape[0] // part
     top = at_ref[0] // part
     low = at_ref[0] % part
     for step, out_ref in enumerate((down_ref, up_ref)):
 
         @pl.when(pl.program_id(0) == step)
         def _():
-            for k in range(part):
-                at = pl.ds(pl.multiple_of((k ^ low) * rows, rows), rows)
-                x = jnp.where(top == step, near_ref[at], far_ref[at])
+            for k in range(2 * part):
+                slot = top ^ (2 * step + k // part)
+                at = pl.ds(pl.multiple_of(((k % part) ^ low) * rows, rows), rows)
+                x = jnp.where(slot == 0, own_ref[at], one_ref[at])
+                far = jnp.where(slot == 2, two_ref[at], both_ref[at])
+                x = jnp.where(slot < 2, x, far)
                 out_ref[k * rows : (k + 1) * rows] = x.astype(f32)
 
 
@@ -595,7 +603,7 @@
             out_shape=(part,) * parts,
             in_specs=[VMEM, VMEM],
             out_specs=(VMEM,) * parts,
-            compiler_params=params(60),
+            compiler_params=params(16),
             cost_estimate=cost(),
             name="add",
         )(a, b)
@@ -759,29 +767,31 @@
             attend_kernel,
             "attend",
             [SMEM] + [VMEM] * 4,
-            (sds((blocks, entries, lanes), f32), sds((rows, width), bf16)),
-        )
+            (sds((blocks, entries, lanes), bf16), sds((rows, width), bf16)),
+        )
+        half_rows = block((half, dim), half_rolled)
+        half_hidden = block((half, hidden), half_rolled)
         feed = gridded(
             functools.partial(feed_kernel, n_mp),
             "feed",
-            tiles,
-            [row_block]
-            + [block((tile, width), rolled)] * n_mp
+            2,
+            [half_rows]
+            + [block((half, width), half_rolled)] * n_mp
             + [block((width, dim), whole)] * n_mp
             + [row_vector] * 3
             + [
                 block((dim, hidden), whole),
                 block((1, hidden), whole),
                 block((hidden, dim), whole),
-                row_block,
+                half_rows,
             ],
             [
-                row_block,
-                row_block,
-                block((tile, hidden), rolled),
-                block((tile, hidden), rolled),
-                block((tile, dim), theirs_row),
-                block((tile, dim), mine_row),
+                half_rows,
+                half_rows,
+                half_hidden,
+                half_hidden,
+                block((half, dim), whole),
+                block((half, dim), whole),
                 block((8, hidden), whole),
             ],
             (
@@ -795,8 +805,6 @@
             ),
             [pltpu.VMEM((dim, dim), bf16)],
         )
-        half_rows = block((half, dim), half_rolled)
-        half_hidden = block((half, hidden), half_rolled)
         weights = gridded(
             weights_kernel,
             "weights",
@@ -875,7 +883,7 @@
             last_kernel,
             "last",
             2,
-            terms_specs + [block((blocks, dim), whole), tile_block, tile_block, row_vector],
+            terms_specs + [block((blocks, dim), whole)] * 2 + [tile_block, tile_block, row_vector],
             tile_block,
             sds((rows, dim), bf16),
         )
@@ -891,7 +899,7 @@
             functools.partial(feed_unpack_kernel, n_dp),
             "feed_unpack",
             2,
-            [block((hidden, dim), whole)] * 2,
+            [block((hidden // 2, dim), whole)] * 4,
             [block((hidden, dim), whole)] * 2,
             (sds((hidden, dim), f32), sds((hidden, dim), f32)),
         )
@@ -968,6 +976,9 @@
                 for j, x in out_list:
                     out_slots[j ^ 1] = swap(after(x, stats), "mp", 1, "gather_w_out")
             sums = line(lambda a, b: jnp.concatenate([a, b]), sums, got)
+        cores = wait(*[out_slots[j ^ 1] for j, _ in out_list])
+        for (j, _), x in zip(out_list, cores):
+            out_slots[j ^ 1] = x
         probs, attended = line(attend, place, qkv, exps, stats, sums)
 
         att_slots = {0: attended}
@@ -1054,6 +1065,8 @@
         for m in far_masks:
             extra = line(pl_add, extra, extra_got)
             extra_got = swap(extra, "mp", m, "sum_extra")
+        for m in dp_masks[2:]:
+            rest_sum.step()
         for m in feed_masks[3:]:
             feed_sum.step()
         (far,) = wait(far)
@@ -1061,33 +1074,47 @@
         other_far = swap(far, "mp", 1, "sum_first")
         feed_all = line(add_low, feed_sum.mine, feed_sum.got)
         feed_got = swap(feed_all, "dp", feed_masks[-1], "feed_weights")
-        for m in dp_masks[2:]:
-            rest_sum.step()
-        extra = line(pl_add, extra, extra_got)
         grad_tokens = line(
-            last, pos, total, far, other, other_far, extra, tokens, grad_low, ln1_gain[None]
-        )
+            last,
+            pos,
+            total,
+            far,
+            other,
+            other_far,
+            extra,
+            extra_got,
+            tokens,
+            grad_low,
+            ln1_gain[None],
+        )
+        rest_all = line(
+            piece_of, rest_sum.mine, rest_sum.got, total, far, back_vec, up_vec
+        )
+        rest_got = swap(rest_all, "dp", dp_masks[-1], "rest_weights")
         feed_next = list(reversed(feed_masks))[1:]
         rest_next = list(reversed(dp_masks))[1:]
+        for m in feed_next[:-2]:
+            feed_all = line(concat, feed_all, feed_got)
+            feed_got = swap(feed_all, "dp", m, "feed_weights")
         feed_all = line(concat, feed_all, feed_got)
-        feed_got = swap(feed_all, "dp", feed_next[0], "feed_weights")
-        rest_all = line(
-            piece_of, rest_sum.mine, rest_sum.got, total, far, back_vec, up_vec
-        )
-        rest_got = swap(rest_all, "dp", dp_masks[-1], "rest_weights")
+        two = swap(feed_all, "dp", feed_masks[0], "feed_weights")
+        one = swap(feed_all, "dp", feed_masks[1], "feed_weights")
         line.space()
         rest_all = line(merge, rest_all, rest_got)
         rest_got = swap(rest_all, "dp", rest_next[0], "rest_weights")
-        for feed_mask, rest_mask in zip(feed_next[1:], rest_next[1:]):
-            feed_all = line(concat, feed_all, feed_got)
-            feed_got = swap(feed_all, "dp", feed_mask, "feed_weights")
+        (two,) = wait(two)
+        both = swap(two, "dp", feed_masks[1], "feed_weights")
+        for m in rest_next[1:]:
+            line.space()
             rest_all = line(merge, rest_all, rest_got)
-            rest_got = swap(rest_all, "dp", rest_mask, "rest_weights")
-            line.space()
+            rest_got = swap(rest_all, "dp", m, "rest_weights")
+        line.space()
+        grad_w_down, grad_w_up = line(
+            feed_unpack, place_of(feed_masks), feed_all, one, two, both
+        )
         grad_w_qkv, grad_w_out, vectors = line(
             rest_unpack, place_of(dp_masks), rest_all, rest_got, line.spare
         )
-        grad_w_down, grad_w_up = line(feed_unpack, place_of(feed_masks), feed_all, feed_got)
         return (
             output,
             grad_tokens,

time: 144 us -> 140 us (0.972)
  starting transfers between devices: 31.9 us -> 36.9 us
  local copies, waits for them, and re-layouts: 8.57 us -> 4.49 us
  Pallas kernels: 66.3 us -> 62.4 us
    ppermute x36 -> x37, starting transfers between devices: 31.9 us -> 36.9 us  [swap(): return lax.ppermute(x, axis, [(i, i ^ mask) for i in range(n)])]
    unnamed x104 -> x86, local copies, waits for them, and re-layouts: 7.35 us -> 3.27 us
    pallas_call x3, Pallas kernels: 6.05 us -> 3.5 us  [add_parts(): pl.pallas_call(functools.partial(add_kernel, parts), out_shape=(part,) *...]
    pallas_call x10 -> x8, Pallas kernels: 9.32 us -> 7.5 us  [like(): return plain(kernel, name, specs, (sds(shape, dtype),))(*operands)[0]]
    ppermute x36 -> x37, waiting for transfers between devices: 34.6 us -> 33.7 us  [swap(): return lax.ppermute(x, axis, [(i, i ^ mask) for i in range(n)])]
  transfers between devices with their start and end apart: 36 -> 37, of which waited for: 15 -> 14; matrix products, arithmetic and copies ran while one was open for 1% -> 1% of each run, Pallas kernels for 34% -> 34%
where the time goes in v4:
time: 140 us; the launch traced here: 139 us
  Pallas kernels  62.4 us (45%)
  starting transfers between devices  36.9 us (26%)
  waiting for transfers between devices  33.7 us (24%)
  local copies, waits for them, and re-layouts  4.49 us (3%)
    pallas_call x11, Pallas kernels, __call__(): result = work(*inputs)  37.1 us
    ppermute x37, starting transfers between devices, swap(): return lax.ppermute(x, axis, [(i, i ^ mask) for i in range(n)])  36.9 us
    ppermute x37, waiting for transfers between devices, swap(): return lax.ppermute(x, axis, [(i, i ^ mask) for i in range(n)])  33.7 us
    pallas_call x8, Pallas kernels, like(): return plain(kernel, name, specs, (sds(shape, dtype),))(*operands)[0]  7.5 us
    pallas_call x4, Pallas kernels, split_sum(): pl.pallas_call(split_kernel, out_shape=(half, half), in_specs=[SMEM, VMEM...  7.45 us
    pallas_call x1, Pallas kernels, per_device(): back(*a)  6.81 us
    pallas_call x3, Pallas kernels, add_parts(): pl.pallas_call(functools.partial(add_kernel, parts), out_shape=(part,) *...  3.5 us
    unnamed x86, local copies, waits for them, and re-layouts  3.27 us
  transfers between devices with their start and end apart: 37, of which 14 were waited for; matrix products, arithmetic and copies ran while one was open for 1% of the time, Pallas kernels for 34%

profile of v4, /device:TPU:0, one launch (start us, length us, event | category | flops | bytes accessed | tf_op | source)
XLA Modules:
  0.0 139.2 jit_solution(14519821587841867974)
XLA Ops:
  0.6 3.0 %collective-permute-start = (bf16[128,512]{1,0:T(8,128)(2,1)}, bf16[128,512]{1,0:T(8,128)(2,1)S(1)}, u32[]{:S(2)}, u32[]{:S(2)}) collective-permute-start(bf16[128,512]{1,0:T(8,128)(2,1)} %wo_ref), channel_id=1, source_target_pairs={{0,2},{1,3},{2,0},{3,1},{4,6},{5,7},{6,4},{7,5},{8,10},{9,11},{10,... | collective-permute-start | bytes 393224 | tf_op jit(solution)/shard_map/gather_w_out/ppermute | solution.py:565
  3.7 3.9 %project.1 = (bf16[1024,512]{1,0:T(8,128)(2,1)}, bf16[3,1024,128]{2,1,0:T(8,128)(2,1)}, f32[10,8,128]{2,1,0:T(8,128)}) custom-call(bf16[1024,512]{1,0:T(8,128)(2,1)} %tok_ref.3, f32[1,512]{1,0:T(1,128)} %bitcast.24, f32[1,512]{1,0:T(1,128)} %bitcast.36, bf16[3,512,128]{2,1,0:T(8,128)(2,1)} %w_ref.2), custom_call_target="tpu_custom_call" | custom-call | flops 115000000512 | bytes 1 | tf_op jit(solution)/shard_map/project/pallas_call | solution.py:589
  7.6 1.6 %collective-permute-start.1 = (f32[1,10,8,128]{3,2,1,0:T(8,128)}, f32[1,10,8,128]{3,2,1,0:T(8,128)S(1)}, u32[]{:S(2)}, u32[]{:S(2)}) collective-permute-start(f32[1,10,8,128]{3,2,1,0:T(8,128)} %bitcast.27), channel_id=1, source_target_pairs={{0,4},{4,0},{8,12},{12,8},{16,20},{20,16},{24,28},{28,24},{1,5},{5... | collective-permute-start | bytes 122888 | tf_op jit(solution)/shard_map/summaries/ppermute | solution.py:565
  9.2 1.1 copy-done.29
  10.8 1.1 collective-permute-done.1
  11.9 1.6 %collective-permute-start.2 = (f32[2,10,8,128]{3,2,1,0:T(8,128)S(1)}, f32[2,10,8,128]{3,2,1,0:T(8,128)S(1)}, u32[]{:S(2)}, u32[]{:S(2)}) collective-permute-start(f32[2,10,8,128]{3,2,1,0:T(8,128)S(1)} %constant_dynamic-update-slice_fusion), channel_id=1, source_target_pairs={{0,8},{4,12},{8,0},{12,4},{16,24},{20,28},{24,16},{28,20},{1,9},{5... | collective-permute-start | bytes 245768 | tf_op jit(solution)/shard_map/summaries/ppermute | solution.py:565
  14.1 2.3 %collective-permute-done.2 = f32[2,10,8,128]{3,2,1,0:T(8,128)S(1)} collective-permute-done((f32[2,10,8,128]{3,2,1,0:T(8,128)S(1)}, f32[2,10,8,128]{3,2,1,0:T(8,128)S(1)}, u32[]{:S(2)}, u32[]{:S(2)}) %collective-permute-start.2) | collective-permute-done | bytes 81952 | tf_op jit(solution)/shard_map/summaries/ppermute | solution.py:565
  16.5 1.5 %attend.1 = (bf16[8,160,256]{2,1,0:T(8,128)(2,1)S(1)}, bf16[1024,128]{1,0:T(8,128)(2,1)S(1)}) custom-call(s32[1]{0:T(128)} %bitcast.2.place_ref, bf16[3,1024,128]{2,1,0:T(8,128)(2,1)S(1)} %copy-done.29, f32[8,128,256]{2,1,0:T(8,128)S(1)} %get-tuple-element.215.exp_ref, f32[8,2,256]{2,1,0:T(2,128)S(1)} %get-tuple-element.216.stat_ref, ...), custom_call_target="tpu_custom_call" | custom-call | flops 115000000512 | bytes 1 | tf_op jit(solution)/shard_map/attend/pallas_call | solution.py:589
  18.0 1.5 %collective-permute-start.6 = (bf16[1024,128]{1,0:T(8,128)(2,1)S(1)}, bf16[1024,128]{1,0:T(8,128)(2,1)S(1)}, u32[]{:S(2)}, u32[]{:S(2)}) collective-permute-start(bf16[1024,128]{1,0:T(8,128)(2,1)S(1)} %get-tuple-element.296.refs_0_.att_ref), channel_id=1, source_target_pairs={{0,2},{1,3},{2,0},{3,1},{4,6},{5,7},{6,4},{7,5},{8,10},{9,11},{10,... | collective-permute-start | bytes 786440 | tf_op jit(solution)/shard_map/gather_attended/ppermute | solution.py:565
  19.6 5.7 %collective-permute-done.6.refs_2_ = bf16[1024,128]{1,0:T(8,128)(2,1)S(1)} collective-permute-done((bf16[1024,128]{1,0:T(8,128)(2,1)S(1)}, bf16[1024,128]{1,0:T(8,128)(2,1)S(1)}, u32[]{:S(2)}, u32[]{:S(2)}) %collective-permute-start.6) | collective-permute-done | bytes 262176 | tf_op jit(solution)/shard_map/gather_attended/ppermute | solution.py:565
  25.2 0.6 pad_add_fusion.pos_ref
  25.8 0.9 collective-permute-done.7.refs_3_
  26.8 0.7 copy-done.38
  27.5 8.9 %feed.1 = (f32[1024,512]{1,0:T(8,128)}, bf16[1024,512]{1,0:T(8,128)(2,1)}, bf16[1024,512]{1,0:T(8,128)(2,1)}, bf16[1024,512]{1,0:T(8,128)(2,1)}, bf16[512,512]{1...) custom-call(s32[4]{0:T(128)} %pad_add_fusion.pos_ref, bf16[1024,512]{1,0:T(8,128)(2,1)} %tok_ref.3, ...), custom_call_target="tpu_custom_call" | custom-call | flops 115000000512 | bytes 1 | tf_op jit(solution)/shard_map/feed/pallas_call | solution.py:589
  36.6 2.0 %collective-permute-done.8.b_ref = bf16[512,512]{1,0:T(8,128)(2,1)S(1)} collective-permute-done((bf16[512,512]{1,0:T(8,128)(2,1)}, bf16[512,512]{1,0:T(8,128)(2,1)S(1)}, u32[]{:S(2)}, u32[]{:S(2)}) %collective-permute-start.8) | collective-permute-done | bytes 524320 | tf_op jit(solution)/shard_map/sum_second/ppermute | solution.py:565
  38.6 1.0 copy-done.32
  39.7 0.9 add.30.own_ref
  40.6 1.5 %collective-permute-start.10 = (bf16[512,512]{1,0:T(8,128)(2,1)}, bf16[512,512]{1,0:T(8,128)(2,1)}, u32[]{:S(2)}, u32[]{:S(2)}) collective-permute-start(bf16[512,512]{1,0:T(8,128)(2,1)} %add.30.own_ref), channel_id=1, source_target_pairs={{0,2},{1,3},{2,0},{3,1},{4,6},{5,7},{6,4},{7,5},{8,10},{9,11},{10,... | collective-permute-start | bytes 1572872 | tf_op jit(solution)/shard_map/sum_second/ppermute | solution.py:565
  42.2 3.8 %weights.1 = (bf16[512,512]{1,0:T(8,128)(2,1)S(1)}, bf16[512,512]{1,0:T(8,128)(2,1)S(1)}, bf16[512,512]{1,0:T(8,128)(2,1)}, bf16[512,512]{1,0:T(8,128)(2,1)S(1)}) custom-call(s32[4]{0:T(128)S(1)} %copy-done.4, bf16[1024,512]{1,0:T(8,128)(2,1)S(1)} %copy-done.27, bf16[1024,512]{1,0:T(8,128)(2,1)S(1)} %copy-done.26, bf16[1024,512]{1,0:T(8,128)(2,1)S(1)} %copy-done.28, ...), custom_call_target="tpu_custom_call" | custom-call | flops 115000000512 | bytes 1 | tf_op jit(solution)/shard_map/weights/pallas_call | solution.py:589
  46.5 0.8 collective-permute-start.16
  47.3 0.7 collective-permute-done.9.b_ref
  48.0 0.9 add.31.own_ref
  49.0 5.9 %collective-permute-done.10.far_ref = bf16[512,512]{1,0:T(8,128)(2,1)} collective-permute-done((bf16[512,512]{1,0:T(8,128)(2,1)}, bf16[512,512]{1,0:T(8,128)(2,1)}, u32[]{:S(2)}, u32[]{:S(2)}) %collective-permute-start.10) | collective-permute-done | bytes 524320 | tf_op jit(solution)/shard_map/sum_second/ppermute | solution.py:565
  55.4 1.5 %collective-permute-start.11 = (bf16[512,512]{1,0:T(8,128)(2,1)}, bf16[512,512]{1,0:T(8,128)(2,1)}, u32[]{:S(2)}, u32[]{:S(2)}) collective-permute-start(bf16[512,512]{1,0:T(8,128)(2,1)} %add.31.own_ref), channel_id=1, source_target_pairs={{0,2},{1,3},{2,0},{3,1},{4,6},{5,7},{6,4},{7,5},{8,10},{9,11},{10,... | collective-permute-start | bytes 1572872 | tf_op jit(solution)/shard_map/sum_output/ppermute | solution.py:565
  56.9 0.9 collective-permute-done.13.other_far_ref
  57.8 6.8 %back.1 = (bf16[1024,512]{1,0:T(8,128)(2,1)S(1)}, bf16[1024,384]{1,0:T(8,128)(2,1)S(1)}, f32[4,2,8,128]{3,2,1,0:T(8,128)S(1)}, f32[32,512]{1,0:T(8,128)S(1)}) custom-call(s32[4]{0:T(128)S(1)} %copy-done.5, bf16[512,512]{1,0:T(8,128)(2,1)} %add.30.own_ref, bf16[512,512]{1,0:T(8,128)(2,1)} %collective-permute-done.10.far_ref, ...), custom_call_target="tpu_custom_call" | custom-call | flops 115000000512 | bytes 1 | tf_op jit(solution)/shard_map/back/pallas_call | solution.py:1023
  64.7 2.4 %split.4 = (bf16[256,512]{1,0:T(8,128)(2,1)}, bf16[256,512]{1,0:T(8,128)(2,1)S(1)}) custom-call(s32[1]{0:T(128)} %bitcast.11.bit_ref, bf16[512,512]{1,0:T(8,128)(2,1)S(1)} %get-tuple-element.278.a_ref, bf16[512,512]{1,0:T(8,128)(2,1)} %collective-permute-done.16.b_ref), custom_call_target="tpu_custom_call" | custom-call | flops 115000000512 | bytes 1 | tf_op jit(solution)/shard_map/split/pallas_call | solution.py:628
  67.1 0.6 slice.27
  67.7 2.0 %first.1 = (bf16[528,512]{1,0:T(8,128)(2,1)S(1)}, bf16[528,512]{1,0:T(8,128)(2,1)S(1)}) custom-call(s32[4]{0:T(128)S(1)} %copy-done.5, bf16[1024,384]{1,0:T(8,128)(2,1)S(1)} %get-tuple-element.294.gqkv_ref, f32[4,2,8,128]{3,2,1,0:T(8,128)S(1)} %get-tuple-element.302.slot_ref.a_ref, f32[4,10,8,128]{3,2,1,0:T(8,128)S(1)} %copy-done.1, ...), custom_call_target="tpu_custom_call" | custom-call | flops 115000000512 | bytes 1 | tf_op jit(solution)/shard_map/first/pallas_call | solution.py:589
  69.9 0.8 collective-permute-start.14
  70.8 1.5 %collective-permute-start.21 = (bf16[256,512]{1,0:T(8,128)(2,1)}, bf16[256,512]{1,0:T(8,128)(2,1)}, u32[]{:S(2)}, u32[]{:S(2)}) collective-permute-start(bf16[256,512]{1,0:T(8,128)(2,1)} %get-tuple-element.306), channel_id=1, source_target_pairs={{0,4},{4,0},{8,12},{12,8},{16,20},{20,16},{24,28},{28,24},{1,5},{5... | collective-permute-start | bytes 786440 | tf_op jit(solution)/shard_map/feed_weights/ppermute | solution.py:565
  72.3 3.8 %rest_weights.1 = (bf16[256,512]{1,0:T(8,128)(2,1)}, bf16[256,512]{1,0:T(8,128)(2,1)}) custom-call(s32[1]{0:T(128)} %bitcast.11.bit_ref, bf16[1024,512]{1,0:T(8,128)(2,1)} %get-tuple-element.293.first_ref, bf16[1024,384]{1,0:T(8,128)(2,1)} %copy-done.31, bf16[1024,512]{1,0:T(8,128)(2,1)} %copy-done.24, bf16[1024,128]{1,0:T(8,128)(2,1)} %copy-done.15, ...), custom_call_target="tpu_custom_call" | custom-call | flops 115000000512 | bytes 1 | tf_op jit(solution)/shard_map/rest_weights/pallas_call | solution.py:589
  76.6 0.9 pair.1.own_ref.near_ref
  77.5 1.5 %collective-permute-start.22 = (bf16[528,512]{1,0:T(8,128)(2,1)}, bf16[528,512]{1,0:T(8,128)(2,1)}, u32[]{:S(2)}, u32[]{:S(2)}) collective-permute-start(bf16[528,512]{1,0:T(8,128)(2,1)} %pair.1.own_ref.near_ref), channel_id=1, source_target_pairs={{0,2},{1,3},{2,0},{3,1},{4,6},{5,7},{6,4},{7,5},{8,10},{9,11},{10,... | collective-permute-start | bytes 1622024 | tf_op jit(solution)/shard_map/sum_first/ppermute | solution.py:565
  79.0 0.7 slots.1.a_ref
  79.9 1.8 %collective-permute-start.20 = (f32[1,2,8,128]{3,2,1,0:T(8,128)S(1)}, f32[1,2,8,128]{3,2,1,0:T(8,128)S(1)}, u32[]{:S(2)}, u32[]{:S(2)}) collective-permute-start(f32[1,2,8,128]{3,2,1,0:T(8,128)S(1)} %slice.36), channel_id=1, source_target_pairs={{0,4},{4,0},{8,12},{12,8},{16,20},{20,16},{24,28},{28,24},{1,5},{5... | collective-permute-start | bytes 24584 | tf_op jit(solution)/shard_map/sum_slots/ppermute | solution.py:565
  81.7 1.7 %split.5 = (bf16[128,512]{1,0:T(8,128)(2,1)}, bf16[128,512]{1,0:T(8,128)(2,1)S(1)}) custom-call(s32[1]{0:T(128)} %bitcast.13.bit_ref, bf16[256,512]{1,0:T(8,128)(2,1)S(1)} %get-tuple-element.308.a_ref, bf16[256,512]{1,0:T(8,128)(2,1)} %collective-permute-done.21.b_ref), custom_call_target="tpu_custom_call" | custom-call | flops 115000000512 | bytes 1 | tf_op jit(solution)/shard_map/split/pallas_call | solution.py:628
  83.4 2.6 %collective-permute-start.28 = (bf16[128,512]{1,0:T(8,128)(2,1)}, bf16[128,512]{1,0:T(8,128)(2,1)}, u32[]{:S(2)}, u32[]{:S(2)}) collective-permute-start(bf16[128,512]{1,0:T(8,128)(2,1)} %get-tuple-element.334), channel_id=1, source_target_pairs={{0,16},{4,20},{8,24},{12,28},{16,0},{20,4},{24,8},{28,12},{1,17},{... | collective-permute-start | bytes 393224 | tf_op jit(solution)/shard_map/feed_weights/ppermute | solution.py:565
  86.0 0.8 extra.1.a_ref
  86.9 1.8 %split.6 = (bf16[128,512]{1,0:T(8,128)(2,1)}, bf16[128,512]{1,0:T(8,128)(2,1)S(1)}) custom-call(s32[1]{0:T(128)} %bitcast.3.bit_ref, bf16[256,512]{1,0:T(8,128)(2,1)S(1)} %copy-done.33, bf16[256,512]{1,0:T(8,128)(2,1)} %collective-permute-done.19.b_ref), custom_call_target="tpu_custom_call" | custom-call | flops 115000000512 | bytes 1 | tf_op jit(solution)/shard_map/split/pallas_call | solution.py:628
  88.7 1.2 collective-permute-start.23
  90.0 3.5 %output.1 = bf16[1024,512]{1,0:T(8,128)(2,1)} custom-call(s32[4]{0:T(128)S(1)} %copy-done.6, bf16[512,512]{1,0:T(8,128)(2,1)} %add.31.own_ref, bf16[512,512]{1,0:T(8,128)(2,1)} %collective-permute-done.11.far_ref, bf16[512,512]{1,0:T(8,128)(2,1)} %collective-permute-done.15.other_ref, bf16[512,512]{1,0:T(8,128)(2,1)} %collective-permute-done.18.other_far_ref, ...), custom_call_target="tpu_custom_call" | custom-call | flops 115000000512 | bytes 1 | tf_op jit(solution)/shard_map/output/pallas_call | solution.py:589
  93.5 1.3 plus.1.extra_ref
  94.8 1.5 %collective-permute-start.27 = (f32[8,512]{1,0:T(8,128)}, f32[8,512]{1,0:T(8,128)}, u32[]{:S(2)}, u32[]{:S(2)}) collective-permute-start(f32[8,512]{1,0:T(8,128)} %plus.1.extra_ref), channel_id=1, source_target_pairs={{0,2},{1,3},{2,0},{3,1},{4,6},{5,7},{6,4},{7,5},{8,10},{9,11},{10,... | collective-permute-start | bytes 49160 | tf_op jit(solution)/shard_map/sum_extra/ppermute | solution.py:565
  96.3 1.6 %split.7 = (bf16[64,512]{1,0:T(8,128)(2,1)}, bf16[64,512]{1,0:T(8,128)(2,1)S(1)}) custom-call(s32[1]{0:T(128)} %bitcast.13.bit_ref, bf16[128,512]{1,0:T(8,128)(2,1)S(1)} %get-tuple-element.329.a_ref, bf16[128,512]{1,0:T(8,128)(2,1)} %collective-permute-done.23.b_ref), custom_call_target="tpu_custom_call" | custom-call | flops 115000000512 | bytes 1 | tf_op jit(solution)/shard_map/split/pallas_call | solution.py:628
  97.8 1.7 %collective-permute-start.29 = (bf16[64,512]{1,0:T(8,128)(2,1)}, bf16[64,512]{1,0:T(8,128)(2,1)}, u32[]{:S(2)}, u32[]{:S(2)}) collective-permute-start(bf16[64,512]{1,0:T(8,128)(2,1)} %get-tuple-element.347), channel_id=1, source_target_pairs={{0,16},{4,20},{8,24},{12,28},{16,0},{20,4},{24,8},{28,12},{1,17},{... | collective-permute-start | bytes 196616 | tf_op jit(solution)/shard_map/rest_weights/ppermute | solution.py:565
  100.1 1.7 %add.32.a_ref = bf16[128,512]{1,0:T(8,128)(2,1)} custom-call(bf16[128,512]{1,0:T(8,128)(2,1)S(1)} %get-tuple-element.335.a_ref, bf16[128,512]{1,0:T(8,128)(2,1)} %collective-permute-done.28.b_ref), custom_call_target="tpu_custom_call" | custom-call | flops 115000000512 | bytes 1 | tf_op jit(solution)/shard_map/add/pallas_call | solution.py:601
  101.8 1.3 collective-permute-start.31
  103.1 4.3 %last.1 = bf16[1024,512]{1,0:T(8,128)(2,1)} custom-call(s32[4]{0:T(128)S(1)} %copy-done.7, bf16[528,512]{1,0:T(8,128)(2,1)} %pair.1.own_ref.near_ref, bf16[528,512]{1,0:T(8,128)(2,1)} %collective-permute-done.22.far_ref, bf16[528,512]{1,0:T(8,128)(2,1)S(1)} %collective-permute-done.25.other_ref, bf16[528,512]{1,0:T(8,128)(2,1)S(1)} %collective-permute-done.26.other_far_ref, ...), custom_call_target="tpu_custom_call" | custom-call | flops 115000000512 | bytes 1 | tf_op jit(solution)/shard_map/last/pallas_call | solution.py:589
  107.4 1.3 piece.1.a_ref
  108.7 2.5 %collective-permute-done.31.b_ref = bf16[128,512]{1,0:T(8,128)(2,1)} collective-permute-done((bf16[128,512]{1,0:T(8,128)(2,1)}, bf16[128,512]{1,0:T(8,128)(2,1)}, u32[]{:S(2)}, u32[]{:S(2)}) %collective-permute-start.31) | collective-permute-done | bytes 131104 | tf_op jit(solution)/shard_map/feed_weights/ppermute | solution.py:565
  111.2 1.7 %concat.1.own_ref = bf16[256,512]{1,0:T(8,128)(2,1)} custom-call(bf16[128,512]{1,0:T(8,128)(2,1)} %add.32.a_ref, bf16[128,512]{1,0:T(8,128)(2,1)} %collective-permute-done.31.b_ref), custom_call_target="tpu_custom_call" | custom-call | flops 115000000512 | bytes 1 | tf_op jit(solution)/shard_map/concat/pallas_call | solution.py:916
  112.9 2.1 %collective-permute-start.30 = (bf16[80,512]{1,0:T(8,128)(2,1)S(1)}, bf16[80,512]{1,0:T(8,128)(2,1)S(1)}, u32[]{:S(2)}, u32[]{:S(2)}) collective-permute-start(bf16[80,512]{1,0:T(8,128)(2,1)S(1)} %piece.1.a_ref), channel_id=1, source_target_pairs={{0,16},{4,20},{8,24},{12,28},{16,0},{20,4},{24,8},{28,12},{1,17},{... | collective-permute-start | bytes 245768 | tf_op jit(solution)/shard_map/rest_weights/ppermute | solution.py:565
  115.5 4.7 %collective-permute-done.30.b_ref = bf16[80,512]{1,0:T(8,128)(2,1)S(1)} collective-permute-done((bf16[80,512]{1,0:T(8,128)(2,1)S(1)}, bf16[80,512]{1,0:T(8,128)(2,1)S(1)}, u32[]{:S(2)}, u32[]{:S(2)}) %collective-permute-start.30) | collective-permute-done | bytes 81952 | tf_op jit(solution)/shard_map/rest_weights/ppermute | solution.py:565
  120.2 2.6 %collective-permute-start.32 = (bf16[144,512]{1,0:T(8,128)(2,1)S(1)}, bf16[144,512]{1,0:T(8,128)(2,1)S(1)}, u32[]{:S(2)}, u32[]{:S(2)}) collective-permute-start(bf16[144,512]{1,0:T(8,128)(2,1)S(1)} %merge.2.a_ref), channel_id=1, source_target_pairs={{0,8},{4,12},{8,0},{12,4},{16,24},{20,28},{24,16},{28,20},{1,9},{5... | collective-permute-start | bytes 442376 | tf_op jit(solution)/shard_map/rest_weights/ppermute | solution.py:565
  122.9 1.8 %collective-permute-start.36 = (bf16[256,512]{1,0:T(8,128)(2,1)}, bf16[256,512]{1,0:T(8,128)(2,1)}, u32[]{:S(2)}, u32[]{:S(2)}) collective-permute-start(bf16[256,512]{1,0:T(8,128)(2,1)} %collective-permute-done.33.two_ref), channel_id=1, source_target_pairs={{0,4},{4,0},{8,12},{12,8},{16,20},{20,16},{24,28},{28,24},{1,5},{5... | collective-permute-start | bytes 786440 | tf_op jit(solution)/shard_map/feed_weights/ppermute | solution.py:565
  124.7 1.3 collective-permute-done.32.b_ref
  126.0 0.7 merge.3.near_ref
  126.7 1.5 %collective-permute-start.34 = (bf16[272,512]{1,0:T(8,128)(2,1)}, bf16[272,512]{1,0:T(8,128)(2,1)}, u32[]{:S(2)}, u32[]{:S(2)}) collective-permute-start(bf16[272,512]{1,0:T(8,128)(2,1)} %merge.3.near_ref), channel_id=1, source_target_pairs={{0,4},{4,0},{8,12},{12,8},{16,20},{20,16},{24,28},{28,24},{1,5},{5... | collective-permute-start | bytes 835592 | tf_op jit(solution)/shard_map/rest_weights/ppermute | solution.py:565
  128.3 4.2 %collective-permute-done.36.both_ref = bf16[256,512]{1,0:T(8,128)(2,1)} collective-permute-done((bf16[256,512]{1,0:T(8,128)(2,1)}, bf16[256,512]{1,0:T(8,128)(2,1)}, u32[]{:S(2)}, u32[]{:S(2)}) %collective-permute-start.36) | collective-permute-done | bytes 262176 | tf_op jit(solution)/shard_map/feed_weights/ppermute | solution.py:565
  132.4 2.8 %feed_unpack.1 = (f32[512,512]{1,0:T(8,128)}, f32[512,512]{1,0:T(8,128)}) custom-call(s32[1]{0:T(128)S(6)} %add.23.at_ref, bf16[256,512]{1,0:T(8,128)(2,1)} %concat.1.own_ref, bf16[256,512]{1,0:T(8,128)(2,1)} %collective-permute-done.35.one_ref, bf16[256,512]{1,0:T(8,128)(2,1)} %collective-permute-done.33.two_ref, ...), custom_call_target="tpu_custom_call" | custom-call | flops 115000000512 | bytes 1 | tf_op jit(solution)/shard_map/feed_unpack/pallas_call | solution.py:589
  135.2 1.3 collective-permute-done.34.far_ref
  136.5 2.1 %rest_unpack.1 = (f32[3,512,128]{2,1,0:T(8,128)}, f32[128,512]{1,0:T(8,128)}, f32[8,512]{1,0:T(8,128)S(1)}) custom-call(s32[1]{0:T(128)S(6)} %add.21.at_ref, bf16[272,512]{1,0:T(8,128)(2,1)} %merge.3.near_ref, bf16[272,512]{1,0:T(8,128)(2,1)} %collective-permute-done.34.far_ref, f32[1,512]{1,0:T(1,128)S(1)} %spacer.9.spare_ref), custom_call_target="tpu_custom_call" | custom-call | flops 115000000512 | bytes 1 | tf_op jit(solution)/shard_map/rest_unpack/pallas_call | solution.py:589
  138.6 0.6 fusion
  (134 shorter events, 4.7 us)
Async XLA Ops:
  0.6 6.9 %collective-permute-start = (bf16[128,512]{1,0:T(8,128)(2,1)}, bf16[128,512]{1,0:T(8,128)(2,1)S(1)}, u32[]{:S(2)}, u32[]{:S(2)}) collective-permute-start(bf16[128,512]{1,0:T(8,128)(2,1)} %wo_ref), channel_id=1, source_target_pairs={{0,2},{1,3},{2,0},{3,1},{4,6},{5,7},{6,4},{7,5},{8,10},{9,11},{10,... | collective-permute-start | bytes 393224 | tf_op jit(solution)/shard_map/gather_w_out/ppermute | solution.py:565
  7.6 6.0 %copy-start.39 = (bf16[128,512]{1,0:T(8,128)(2,1)}, bf16[128,512]{1,0:T(8,128)(2,1)S(1)}, u32[]{:S(2)}) copy-start(bf16[128,512]{1,0:T(8,128)(2,1)S(1)} %collective-permute-done.refs_6_) | copy-start | bytes 393220
  7.6 5.9 %copy-start.16 = (bf16[128,512]{1,0:T(8,128)(2,1)S(1)}, bf16[128,512]{1,0:T(8,128)(2,1)}, u32[]{:S(2)}) copy-start(bf16[128,512]{1,0:T(8,128)(2,1)} %wo_ref) | copy-start | bytes 393220
  7.6 4.3 %collective-permute-start.1 = (f32[1,10,8,128]{3,2,1,0:T(8,128)}, f32[1,10,8,128]{3,2,1,0:T(8,128)S(1)}, u32[]{:S(2)}, u32[]{:S(2)}) collective-permute-start(f32[1,10,8,128]{3,2,1,0:T(8,128)} %bitcast.27), channel_id=1, source_target_pairs={{0,4},{4,0},{8,12},{12,8},{16,20},{20,16},{24,28},{28,24},{1,5},{5... | collective-permute-start | bytes 122888 | tf_op jit(solution)/shard_map/summaries/ppermute | solution.py:565
  11.9 4.5 %collective-permute-start.2 = (f32[2,10,8,128]{3,2,1,0:T(8,128)S(1)}, f32[2,10,8,128]{3,2,1,0:T(8,128)S(1)}, u32[]{:S(2)}, u32[]{:S(2)}) collective-permute-start(f32[2,10,8,128]{3,2,1,0:T(8,128)S(1)} %constant_dynamic-update-slice_fusion), channel_id=1, source_target_pairs={{0,8},{4,12},{8,0},{12,4},{16,24},{20,28},{24,16},{28,20},{1,9},{5... | collective-permute-start | bytes 245768 | tf_op jit(solution)/shard_map/summaries/ppermute | solution.py:565
  13.5 2.9 %collective-permute-start.3 = (bf16[128,512]{1,0:T(8,128)(2,1)S(1)}, bf16[128,512]{1,0:T(8,128)(2,1)S(1)}, u32[]{:S(2)}, u32[]{:S(2)}) collective-permute-start(bf16[128,512]{1,0:T(8,128)(2,1)S(1)} %copy-done.16), channel_id=1, source_target_pairs={{0,1},{1,0},{2,3},{3,2},{4,5},{5,4},{6,7},{7,6},{8,9},{9,8},{10,11... | collective-permute-start | bytes 393224 | tf_op jit(solution)/shard_map/gather_w_out/ppermute | solution.py:565
  13.5 2.9 %collective-permute-start.4 = (bf16[128,512]{1,0:T(8,128)(2,1)S(1)}, bf16[128,512]{1,0:T(8,128)(2,1)S(1)}, u32[]{:S(2)}, u32[]{:S(2)}) collective-permute-start(bf16[128,512]{1,0:T(8,128)(2,1)S(1)} %collective-permute-done.refs_6_), channel_id=1, source_target_pairs={{0,1},{1,0},{2,3},{3,2},{4,5},{5,4},{6,7},{7,6},{8,9},{9,8},{10,11... | collective-permute-start | bytes 393224 | tf_op jit(solution)/shard_map/gather_w_out/ppermute | solution.py:565
  18.0 8.8 %copy-start.15 = (bf16[1024,128]{1,0:T(8,128)(2,1)}, bf16[1024,128]{1,0:T(8,128)(2,1)S(1)}, u32[]{:S(2)}) copy-start(bf16[1024,128]{1,0:T(8,128)(2,1)S(1)} %get-tuple-element.296.refs_0_.att_ref) | copy-start | bytes 786436
  18.0 7.2 %collective-permute-start.6 = (bf16[1024,128]{1,0:T(8,128)(2,1)S(1)}, bf16[1024,128]{1,0:T(8,128)(2,1)S(1)}, u32[]{:S(2)}, u32[]{:S(2)}) collective-permute-start(bf16[1024,128]{1,0:T(8,128)(2,1)S(1)} %get-tuple-element.296.refs_0_.att_ref), channel_id=1, source_target_pairs={{0,2},{1,3},{2,0},{3,1},{4,6},{5,7},{6,4},{7,5},{8,10},{9,11},{10,... | collective-permute-start | bytes 786440 | tf_op jit(solution)/shard_map/gather_attended/ppermute | solution.py:565
  19.6 6.3 %collective-permute-start.5 = (bf16[1024,128]{1,0:T(8,128)(2,1)S(1)}, bf16[1024,128]{1,0:T(8,128)(2,1)S(1)}, u32[]{:S(2)}, u32[]{:S(2)}) collective-permute-start(bf16[1024,128]{1,0:T(8,128)(2,1)S(1)} %get-tuple-element.296.refs_0_.att_ref), channel_id=1, source_target_pairs={{0,1},{1,0},{2,3},{3,2},{4,5},{5,4},{6,7},{7,6},{8,9},{9,8},{10,11... | collective-permute-start | bytes 786440 | tf_op jit(solution)/shard_map/gather_attended/ppermute | solution.py:565
  25.2 1.5 %collective-permute-start.7 = (bf16[1024,128]{1,0:T(8,128)(2,1)S(1)}, bf16[1024,128]{1,0:T(8,128)(2,1)S(1)}, u32[]{:S(2)}, u32[]{:S(2)}) collective-permute-start(bf16[1024,128]{1,0:T(8,128)(2,1)S(1)} %collective-permute-done.6.refs_2_), channel_id=1, source_target_pairs={{0,1},{1,0},{2,3},{3,2},{4,5},{5,4},{6,7},{7,6},{8,9},{9,8},{10,11... | collective-permute-start | bytes 786440 | tf_op jit(solution)/shard_map/gather_attended/ppermute | solution.py:565
  36.4 2.2 %collective-permute-start.8 = (bf16[512,512]{1,0:T(8,128)(2,1)}, bf16[512,512]{1,0:T(8,128)(2,1)S(1)}, u32[]{:S(2)}, u32[]{:S(2)}) collective-permute-start(bf16[512,512]{1,0:T(8,128)(2,1)} %get-tuple-element.241), channel_id=1, source_target_pairs={{0,1},{1,0},{2,3},{3,2},{4,5},{5,4},{6,7},{7,6},{8,9},{9,8},{10,11... | collective-permute-start | bytes 1572872 | tf_op jit(solution)/shard_map/sum_second/ppermute | solution.py:565
  39.7 2.4 %copy-start.27 = (bf16[1024,512]{1,0:T(8,128)(2,1)S(1)}, bf16[1024,512]{1,0:T(8,128)(2,1)}, u32[]{:S(2)}) copy-start(bf16[1024,512]{1,0:T(8,128)(2,1)} %get-tuple-element.246.active_ref) | copy-start | bytes 3145732
  39.7 2.5 %copy-start.28 = (bf16[1024,512]{1,0:T(8,128)(2,1)S(1)}, bf16[1024,512]{1,0:T(8,128)(2,1)}, u32[]{:S(2)}) copy-start(bf16[1024,512]{1,0:T(8,128)(2,1)} %get-tuple-element.248.grad_ref) | copy-start | bytes 3145732
  40.6 14.3 %collective-permute-start.10 = (bf16[512,512]{1,0:T(8,128)(2,1)}, bf16[512,512]{1,0:T(8,128)(2,1)}, u32[]{:S(2)}, u32[]{:S(2)}) collective-permute-start(bf16[512,512]{1,0:T(8,128)(2,1)} %add.30.own_ref), channel_id=1, source_target_pairs={{0,2},{1,3},{2,0},{3,1},{4,6},{5,7},{6,4},{7,5},{8,10},{9,11},{10,... | collective-permute-start | bytes 1572872 | tf_op jit(solution)/shard_map/sum_second/ppermute | solution.py:565
  42.1 14.8 %collective-permute-start.12 = (bf16[512,512]{1,0:T(8,128)(2,1)}, bf16[512,512]{1,0:T(8,128)(2,1)}, u32[]{:S(2)}, u32[]{:S(2)}) collective-permute-start(bf16[512,512]{1,0:T(8,128)(2,1)} %add.30.own_ref), channel_id=1, source_target_pairs={{0,1},{1,0},{2,3},{3,2},{4,5},{5,4},{6,7},{7,6},{8,9},{9,8},{10,11... | collective-permute-start | bytes 1572872 | tf_op jit(solution)/shard_map/sum_second/ppermute | solution.py:565
  42.2 4.3 %copy-start.20 = (f32[512]{0:T(512)S(1)}, f32[512]{0:T(512)}, u32[]{:S(2)}) copy-start(f32[512]{0:T(512)} %param.14) | copy-start | bytes 6148
  46.0 2.0 %collective-permute-start.9 = (bf16[512,512]{1,0:T(8,128)(2,1)S(1)}, bf16[512,512]{1,0:T(8,128)(2,1)S(1)}, u32[]{:S(2)}, u32[]{:S(2)}) collective-permute-start(bf16[512,512]{1,0:T(8,128)(2,1)S(1)} %get-tuple-element.252), channel_id=1, source_target_pairs={{0,1},{1,0},{2,3},{3,2},{4,5},{5,4},{6,7},{7,6},{8,9},{9,8},{10,11... | collective-permute-start | bytes 1572872 | tf_op jit(solution)/shard_map/sum_output/ppermute | solution.py:565
  46.5 18.2 %collective-permute-start.16 = (bf16[512,512]{1,0:T(8,128)(2,1)}, bf16[512,512]{1,0:T(8,128)(2,1)}, u32[]{:S(2)}, u32[]{:S(2)}) collective-permute-start(bf16[512,512]{1,0:T(8,128)(2,1)} %get-tuple-element.276), channel_id=1, source_target_pairs={{0,8},{4,12},{8,0},{12,4},{16,24},{20,28},{24,16},{28,20},{1,9},{5... | collective-permute-start | bytes 1572872 | tf_op jit(solution)/shard_map/feed_weights/ppermute | solution.py:565
  48.9 8.8 %copy-start.1 = (f32[4,10,8,128]{3,2,1,0:T(8,128)S(1)}, f32[4,10,8,128]{3,2,1,0:T(8,128)}, u32[]{:S(2)}) copy-start(f32[4,10,8,128]{3,2,1,0:T(8,128)} %copy-done) | copy-start | bytes 491524
  48.9 8.8 %copy-start.5 = (s32[4]{0:T(128)S(1)}, s32[4]{0:T(128)}, u32[]{:S(2)}) copy-start(s32[4]{0:T(128)} %pad_add_fusion.pos_ref) | copy-start | bytes 52
  48.9 8.8 %copy-start.9 = (bf16[1024,512]{1,0:T(8,128)(2,1)S(1)}, bf16[1024,512]{1,0:T(8,128)(2,1)}, u32[]{:S(2)}) copy-start(bf16[1024,512]{1,0:T(8,128)(2,1)} %cot_ref.1) | copy-start | bytes 3145732
  48.9 8.8 %copy-start.17 = (bf16[128,512]{1,0:T(8,128)(2,1)S(1)}, bf16[128,512]{1,0:T(8,128)(2,1)}, u32[]{:S(2)}) copy-start(bf16[128,512]{1,0:T(8,128)(2,1)} %wo_ref) | copy-start | bytes 393220
  48.9 8.8 %copy-start.18 = (f32[512]{0:T(512)S(1)}, f32[512]{0:T(512)}, u32[]{:S(2)}) copy-start(f32[512]{0:T(512)} %param.19) | copy-start | bytes 6148
  48.9 8.8 %copy-start.22 = (f32[1024,512]{1,0:T(8,128)S(1)}, f32[1024,512]{1,0:T(8,128)}, u32[]{:S(2)}) copy-start(f32[1024,512]{1,0:T(8,128)} %get-tuple-element.323.mid_ref) | copy-start | bytes 6291460
  48.9 8.8 %copy-start.30 = (bf16[3,1024,128]{2,1,0:T(8,128)(2,1)S(1)}, bf16[3,1024,128]{2,1,0:T(8,128)(2,1)}, u32[]{:S(2)}) copy-start(bf16[3,1024,128]{2,1,0:T(8,128)(2,1)} %get-tuple-element.271.qkv_ref) | copy-start | bytes 2359300
  54.9 2.8 %collective-permute-start.13 = (bf16[512,512]{1,0:T(8,128)(2,1)}, bf16[512,512]{1,0:T(8,128)(2,1)S(1)}, u32[]{:S(2)}, u32[]{:S(2)}) collective-permute-start(bf16[512,512]{1,0:T(8,128)(2,1)} %collective-permute-done.10.far_ref), channel_id=1, source_target_pairs={{0,1},{1,0},{2,3},{3,2},{4,5},{5,4},{6,7},{7,6},{8,9},{9,8},{10,11... | collective-permute-start | bytes 1572872 | tf_op jit(solution)/shard_map/sum_second/ppermute | solution.py:565
  54.9 12.8 %collective-permute-start.15 = (bf16[512,512]{1,0:T(8,128)(2,1)}, bf16[512,512]{1,0:T(8,128)(2,1)}, u32[]{:S(2)}, u32[]{:S(2)}) collective-permute-start(bf16[512,512]{1,0:T(8,128)(2,1)} %add.31.own_ref), channel_id=1, source_target_pairs={{0,1},{1,0},{2,3},{3,2},{4,5},{5,4},{6,7},{7,6},{8,9},{9,8},{10,11... | collective-permute-start | bytes 1572872 | tf_op jit(solution)/shard_map/sum_output/ppermute | solution.py:565
  55.4 24.3 %collective-permute-start.11 = (bf16[512,512]{1,0:T(8,128)(2,1)}, bf16[512,512]{1,0:T(8,128)(2,1)}, u32[]{:S(2)}, u32[]{:S(2)}) collective-permute-start(bf16[512,512]{1,0:T(8,128)(2,1)} %add.31.own_ref), channel_id=1, source_target_pairs={{0,2},{1,3},{2,0},{3,1},{4,6},{5,7},{6,4},{7,5},{8,10},{9,11},{10,... | collective-permute-start | bytes 1572872 | tf_op jit(solution)/shard_map/sum_output/ppermute | solution.py:565
  64.6 2.5 %copy-start.24 = (bf16[1024,512]{1,0:T(8,128)(2,1)}, bf16[1024,512]{1,0:T(8,128)(2,1)S(1)}, u32[]{:S(2)}) copy-start(bf16[1024,512]{1,0:T(8,128)(2,1)S(1)} %get-tuple-element.345.low_ref) | copy-start | bytes 3145732
  64.6 3.1 %copy-start.2 = (f32[4,2,8,128]{3,2,1,0:T(8,128)}, f32[4,2,8,128]{3,2,1,0:T(8,128)S(1)}, u32[]{:S(2)}) copy-start(f32[4,2,8,128]{3,2,1,0:T(8,128)S(1)} %get-tuple-element.302.slot_ref.a_ref) | copy-start | bytes 98308
  64.6 3.1 %copy-start.31 = (bf16[1024,384]{1,0:T(8,128)(2,1)}, bf16[1024,384]{1,0:T(8,128)(2,1)S(1)}, u32[]{:S(2)}) copy-start(bf16[1024,384]{1,0:T(8,128)(2,1)S(1)} %get-tuple-element.294.gqkv_ref) | copy-start | bytes 2359300
  64.7 3.0 %copy-start.10 = (bf16[1024,512]{1,0:T(8,128)(2,1)S(1)}, bf16[1024,512]{1,0:T(8,128)(2,1)}, u32[]{:S(2)}) copy-start(bf16[1024,512]{1,0:T(8,128)(2,1)} %tok_ref.3) | copy-start | bytes 3145732
  64.7 3.0 %copy-start.13 = (bf16[3,512,128]{2,1,0:T(8,128)(2,1)S(1)}, bf16[3,512,128]{2,1,0:T(8,128)(2,1)}, u32[]{:S(2)}) copy-start(bf16[3,512,128]{2,1,0:T(8,128)(2,1)} %w_ref.2) | copy-start | bytes 1179652
  69.7 6.8 %collective-permute-start.17 = (bf16[528,512]{1,0:T(8,128)(2,1)S(1)}, bf16[528,512]{1,0:T(8,128)(2,1)S(1)}, u32[]{:S(2)}, u32[]{:S(2)}) collective-permute-start(bf16[528,512]{1,0:T(8,128)(2,1)S(1)} %get-tuple-element.289), channel_id=1, source_target_pairs={{0,1},{1,0},{2,3},{3,2},{4,5},{5,4},{6,7},{7,6},{8,9},{9,8},{10,11... | collective-permute-start | bytes 1622024 | tf_op jit(solution)/shard_map/sum_first/ppermute | solution.py:565
  69.9 9.0 %collective-permute-start.14 = (f32[2,2,8,128]{3,2,1,0:T(8,128)}, f32[2,2,8,128]{3,2,1,0:T(8,128)}, u32[]{:S(2)}, u32[]{:S(2)}) collective-permute-start(f32[2,2,8,128]{3,2,1,0:T(8,128)} %slice.27), channel_id=1, source_target_pairs={{0,8},{4,12},{8,0},{12,4},{16,24},{20,28},{24,16},{28,20},{1,9},{5... | collective-permute-start | bytes 49160 | tf_op jit(solution)/shard_map/sum_slots/ppermute | solution.py:565
  70.8 9.2 %collective-permute-start.21 = (bf16[256,512]{1,0:T(8,128)(2,1)}, bf16[256,512]{1,0:T(8,128)(2,1)}, u32[]{:S(2)}, u32[]{:S(2)}) collective-permute-start(bf16[256,512]{1,0:T(8,128)(2,1)} %get-tuple-element.306), channel_id=1, source_target_pairs={{0,4},{4,0},{8,12},{12,8},{16,20},{20,16},{24,28},{28,24},{1,5},{5... | collective-permute-start | bytes 786440 | tf_op jit(solution)/shard_map/feed_weights/ppermute | solution.py:565
  76.0 10.8 %collective-permute-start.19 = (bf16[256,512]{1,0:T(8,128)(2,1)}, bf16[256,512]{1,0:T(8,128)(2,1)}, u32[]{:S(2)}, u32[]{:S(2)}) collective-permute-start(bf16[256,512]{1,0:T(8,128)(2,1)} %get-tuple-element.305), channel_id=1, source_target_pairs={{0,4},{4,0},{8,12},{12,8},{16,20},{20,16},{24,28},{28,24},{1,5},{5... | collective-permute-start | bytes 786440 | tf_op jit(solution)/shard_map/rest_weights/ppermute | solution.py:565
  77.5 22.0 %collective-permute-start.22 = (bf16[528,512]{1,0:T(8,128)(2,1)}, bf16[528,512]{1,0:T(8,128)(2,1)}, u32[]{:S(2)}, u32[]{:S(2)}) collective-permute-start(bf16[528,512]{1,0:T(8,128)(2,1)} %pair.1.own_ref.near_ref), channel_id=1, source_target_pairs={{0,2},{1,3},{2,0},{3,1},{4,6},{5,7},{6,4},{7,5},{8,10},{9,11},{10,... | collective-permute-start | bytes 1622024 | tf_op jit(solution)/shard_map/sum_first/ppermute | solution.py:565
  79.7 6.3 %copy-start.14 = (bf16[3,512,128]{2,1,0:T(8,128)(2,1)S(1)}, bf16[3,512,128]{2,1,0:T(8,128)(2,1)}, u32[]{:S(2)}) copy-start(bf16[3,512,128]{2,1,0:T(8,128)(2,1)} %w_ref.2) | copy-start | bytes 1179652
  79.7 10.3 %collective-permute-start.18 = (bf16[512,512]{1,0:T(8,128)(2,1)}, bf16[512,512]{1,0:T(8,128)(2,1)}, u32[]{:S(2)}, u32[]{:S(2)}) collective-permute-start(bf16[512,512]{1,0:T(8,128)(2,1)} %collective-permute-done.11.far_ref), channel_id=1, source_target_pairs={{0,1},{1,0},{2,3},{3,2},{4,5},{5,4},{6,7},{7,6},{8,9},{9,8},{10,11... | collective-permute-start | bytes 1572872 | tf_op jit(solution)/shard_map/sum_output/ppermute | solution.py:565
  79.9 6.1 %collective-permute-start.20 = (f32[1,2,8,128]{3,2,1,0:T(8,128)S(1)}, f32[1,2,8,128]{3,2,1,0:T(8,128)S(1)}, u32[]{:S(2)}, u32[]{:S(2)}) collective-permute-start(f32[1,2,8,128]{3,2,1,0:T(8,128)S(1)} %slice.36), channel_id=1, source_target_pairs={{0,4},{4,0},{8,12},{12,8},{16,20},{20,16},{24,28},{28,24},{1,5},{5... | collective-permute-start | bytes 24584 | tf_op jit(solution)/shard_map/sum_slots/ppermute | solution.py:565
  83.4 16.2 %collective-permute-start.28 = (bf16[128,512]{1,0:T(8,128)(2,1)}, bf16[128,512]{1,0:T(8,128)(2,1)}, u32[]{:S(2)}, u32[]{:S(2)}) collective-permute-start(bf16[128,512]{1,0:T(8,128)(2,1)} %get-tuple-element.334), channel_id=1, source_target_pairs={{0,16},{4,20},{8,24},{12,28},{16,0},{20,4},{24,8},{28,12},{1,17},{... | collective-permute-start | bytes 393224 | tf_op jit(solution)/shard_map/feed_weights/ppermute | solution.py:565
  86.8 3.2 %copy-start.6 = (s32[4]{0:T(128)S(1)}, s32[4]{0:T(128)}, u32[]{:S(2)}) copy-start(s32[4]{0:T(128)} %pad_add_fusion.pos_ref) | copy-start | bytes 52
  86.8 3.2 %copy-start.19 = (f32[512]{0:T(512)S(1)}, f32[512]{0:T(512)}, u32[]{:S(2)}) copy-start(f32[512]{0:T(512)} %param.24) | copy-start | bytes 6148
  86.8 3.2 %copy-start.23 = (f32[1024,512]{1,0:T(8,128)S(1)}, f32[1024,512]{1,0:T(8,128)}, u32[]{:S(2)}) copy-start(f32[1024,512]{1,0:T(8,128)} %get-tuple-element.323.mid_ref) | copy-start | bytes 6291460
  86.8 6.7 %collective-permute-start.24 = (f32[8,512]{1,0:T(8,128)}, f32[8,512]{1,0:T(8,128)}, u32[]{:S(2)}, u32[]{:S(2)}) collective-permute-start(f32[8,512]{1,0:T(8,128)} %extra.1.a_ref), channel_id=1, source_target_pairs={{0,1},{1,0},{2,3},{3,2},{4,5},{5,4},{6,7},{7,6},{8,9},{9,8},{10,11... | collective-permute-start | bytes 49160 | tf_op jit(solution)/shard_map/sum_extra/ppermute | solution.py:565
  88.7 7.5 %collective-permute-start.23 = (bf16[128,512]{1,0:T(8,128)(2,1)}, bf16[128,512]{1,0:T(8,128)(2,1)}, u32[]{:S(2)}, u32[]{:S(2)}) collective-permute-start(bf16[128,512]{1,0:T(8,128)(2,1)} %get-tuple-element.325), channel_id=1, source_target_pairs={{0,8},{4,12},{8,0},{12,4},{16,24},{20,28},{24,16},{28,20},{1,9},{5... | collective-permute-start | bytes 393224 | tf_op jit(solution)/shard_map/rest_weights/ppermute | solution.py:565
  94.8 8.2 %collective-permute-start.27 = (f32[8,512]{1,0:T(8,128)}, f32[8,512]{1,0:T(8,128)}, u32[]{:S(2)}, u32[]{:S(2)}) collective-permute-start(f32[8,512]{1,0:T(8,128)} %plus.1.extra_ref), channel_id=1, source_target_pairs={{0,2},{1,3},{2,0},{3,1},{4,6},{5,7},{6,4},{7,5},{8,10},{9,11},{10,... | collective-permute-start | bytes 49160 | tf_op jit(solution)/shard_map/sum_extra/ppermute | solution.py:565
  97.8 9.6 %collective-permute-start.29 = (bf16[64,512]{1,0:T(8,128)(2,1)}, bf16[64,512]{1,0:T(8,128)(2,1)}, u32[]{:S(2)}, u32[]{:S(2)}) collective-permute-start(bf16[64,512]{1,0:T(8,128)(2,1)} %get-tuple-element.347), channel_id=1, source_target_pairs={{0,16},{4,20},{8,24},{12,28},{16,0},{20,4},{24,8},{28,12},{1,17},{... | collective-permute-start | bytes 196616 | tf_op jit(solution)/shard_map/rest_weights/ppermute | solution.py:565
  99.5 3.5 %copy-start.7 = (s32[4]{0:T(128)S(1)}, s32[4]{0:T(128)}, u32[]{:S(2)}) copy-start(s32[4]{0:T(128)} %pad_add_fusion.pos_ref) | copy-start | bytes 52
  99.5 3.5 %copy-start.11 = (bf16[1024,512]{1,0:T(8,128)(2,1)S(1)}, bf16[1024,512]{1,0:T(8,128)(2,1)}, u32[]{:S(2)}) copy-start(bf16[1024,512]{1,0:T(8,128)(2,1)} %tok_ref.3) | copy-start | bytes 3145732
  99.5 3.5 %copy-start.21 = (f32[512]{0:T(512)S(1)}, f32[512]{0:T(512)}, u32[]{:S(2)}) copy-start(f32[512]{0:T(512)} %param.14) | copy-start | bytes 6148
  99.5 3.5 %copy-start.25 = (bf16[1024,512]{1,0:T(8,128)(2,1)S(1)}, bf16[1024,512]{1,0:T(8,128)(2,1)}, u32[]{:S(2)}) copy-start(bf16[1024,512]{1,0:T(8,128)(2,1)} %copy-done.24) | copy-start | bytes 3145732
  99.5 3.5 %collective-permute-start.26 = (bf16[528,512]{1,0:T(8,128)(2,1)}, bf16[528,512]{1,0:T(8,128)(2,1)S(1)}, u32[]{:S(2)}, u32[]{:S(2)}) collective-permute-start(bf16[528,512]{1,0:T(8,128)(2,1)} %collective-permute-done.22.far_ref), channel_id=1, source_target_pairs={{0,1},{1,0},{2,3},{3,2},{4,5},{5,4},{6,7},{7,6},{8,9},{9,8},{10,11... | collective-permute-start | bytes 1622024 | tf_op jit(solution)/shard_map/sum_first/ppermute | solution.py:565
  99.6 3.4 %collective-permute-start.25 = (bf16[528,512]{1,0:T(8,128)(2,1)}, bf16[528,512]{1,0:T(8,128)(2,1)S(1)}, u32[]{:S(2)}, u32[]{:S(2)}) collective-permute-start(bf16[528,512]{1,0:T(8,128)(2,1)} %pair.1.own_ref.near_ref), channel_id=1, source_target_pairs={{0,1},{1,0},{2,3},{3,2},{4,5},{5,4},{6,7},{7,6},{8,9},{9,8},{10,11... | collective-permute-start | bytes 1622024 | tf_op jit(solution)/shard_map/sum_first/ppermute | solution.py:565
  101.8 5.6 %copy-start.34 = (f32[8,512]{1,0:T(8,128)S(1)}, f32[8,512]{1,0:T(8,128)}, u32[]{:S(2)}) copy-start(f32[8,512]{1,0:T(8,128)} %get-tuple-element.354.up_ref) | copy-start | bytes 49156
  101.8 9.5 %collective-permute-start.31 = (bf16[128,512]{1,0:T(8,128)(2,1)}, bf16[128,512]{1,0:T(8,128)(2,1)}, u32[]{:S(2)}, u32[]{:S(2)}) collective-permute-start(bf16[128,512]{1,0:T(8,128)(2,1)} %add.32.a_ref), channel_id=1, source_target_pairs={{0,16},{4,20},{8,24},{12,28},{16,0},{20,4},{24,8},{28,12},{1,17},{... | collective-permute-start | bytes 393224 | tf_op jit(solution)/shard_map/feed_weights/ppermute | solution.py:565
  112.9 10.0 %collective-permute-start.33 = (bf16[256,512]{1,0:T(8,128)(2,1)}, bf16[256,512]{1,0:T(8,128)(2,1)}, u32[]{:S(2)}, u32[]{:S(2)}) collective-permute-start(bf16[256,512]{1,0:T(8,128)(2,1)} %concat.1.own_ref), channel_id=1, source_target_pairs={{0,8},{4,12},{8,0},{12,4},{16,24},{20,28},{24,16},{28,20},{1,9},{5... | collective-permute-start | bytes 786440 | tf_op jit(solution)/shard_map/feed_weights/ppermute | solution.py:565
  112.9 7.3 %collective-permute-start.30 = (bf16[80,512]{1,0:T(8,128)(2,1)S(1)}, bf16[80,512]{1,0:T(8,128)(2,1)S(1)}, u32[]{:S(2)}, u32[]{:S(2)}) collective-permute-start(bf16[80,512]{1,0:T(8,128)(2,1)S(1)} %piece.1.a_ref), channel_id=1, source_target_pairs={{0,16},{4,20},{8,24},{12,28},{16,0},{20,4},{24,8},{28,12},{1,17},{... | collective-permute-start | bytes 245768 | tf_op jit(solution)/shard_map/rest_weights/ppermute | solution.py:565
  115.0 13.3 %collective-permute-start.35 = (bf16[256,512]{1,0:T(8,128)(2,1)}, bf16[256,512]{1,0:T(8,128)(2,1)}, u32[]{:S(2)}, u32[]{:S(2)}) collective-permute-start(bf16[256,512]{1,0:T(8,128)(2,1)} %concat.1.own_ref), channel_id=1, source_target_pairs={{0,4},{4,0},{8,12},{12,8},{16,20},{20,16},{24,28},{28,24},{1,5},{5... | collective-permute-start | bytes 786440 | tf_op jit(solution)/shard_map/feed_weights/ppermute | solution.py:565
  120.2 5.8 %collective-permute-start.32 = (bf16[144,512]{1,0:T(8,128)(2,1)S(1)}, bf16[144,512]{1,0:T(8,128)(2,1)S(1)}, u32[]{:S(2)}, u32[]{:S(2)}) collective-permute-start(bf16[144,512]{1,0:T(8,128)(2,1)S(1)} %merge.2.a_ref), channel_id=1, source_target_pairs={{0,8},{4,12},{8,0},{12,4},{16,24},{20,28},{24,16},{28,20},{1,9},{5... | collective-permute-start | bytes 442376 | tf_op jit(solution)/shard_map/rest_weights/ppermute | solution.py:565
  122.9 9.6 %collective-permute-start.36 = (bf16[256,512]{1,0:T(8,128)(2,1)}, bf16[256,512]{1,0:T(8,128)(2,1)}, u32[]{:S(2)}, u32[]{:S(2)}) collective-permute-start(bf16[256,512]{1,0:T(8,128)(2,1)} %collective-permute-done.33.two_ref), channel_id=1, source_target_pairs={{0,4},{4,0},{8,12},{12,8},{16,20},{20,16},{24,28},{28,24},{1,5},{5... | collective-permute-start | bytes 786440 | tf_op jit(solution)/shard_map/feed_weights/ppermute | solution.py:565
  126.7 9.8 %collective-permute-start.34 = (bf16[272,512]{1,0:T(8,128)(2,1)}, bf16[272,512]{1,0:T(8,128)(2,1)}, u32[]{:S(2)}, u32[]{:S(2)}) collective-permute-start(bf16[272,512]{1,0:T(8,128)(2,1)} %merge.3.near_ref), channel_id=1, source_target_pairs={{0,4},{4,0},{8,12},{12,8},{16,20},{20,16},{24,28},{28,24},{1,5},{5... | collective-permute-start | bytes 835592 | tf_op jit(solution)/shard_map/rest_weights/ppermute | solution.py:565
  (15 other events, 24.7 us)

commit v5 on v4

--- a/solution.py
+++ b/solution.py
@@ -291,8 +291,39 @@
             jnp.concatenate([main[:, :width], main[:, width:] + far, last], axis=1).astype(bf16)
         )
     low = bit_ref[0] == 0
-    theirs_ref[...] = jnp.where(low, out[1], out[0])
-    mine_ref[...] = jnp.where(low, out[0], out[1])
+    theirs_ref[:size] = jnp.where(low, out[1], out[0])
+    mine_ref[:size] = jnp.where(low, out[0], out[1])
+    for ref, slot in ((theirs_ref, 2), (mine_ref, 0)):
+        parts = [slot_ref[j, s] for j in (slot, slot + 1) for s in range(2)]
+        ref[size:] = to_low(jnp.concatenate(parts, axis=1), 4 * width)
+
+
+def split_first_kernel(bit_ref, a_ref, b_ref, theirs_ref, mine_ref):
+    rows = a_ref.shape[0] - 16
+    cols = a_ref.shape[1]
+    size = rows // 2
+    total = (a_ref[:rows].astype(f32) + b_ref[:rows].astype(f32)).astype(bf16)
+    low = bit_ref[0] == 0
+    theirs_ref[:size] = jnp.where(low, total[size:], total[:size])
+    mine_ref[:size] = jnp.where(low, total[:size], total[size:])
+    slots = from_low(a_ref[rows:], cols) + from_low(b_ref[rows:], cols)
+    none = jnp.zeros((8, cols // 2), f32)
+    for ref, at in ((theirs_ref, slice(cols // 2, cols)), (mine_ref, slice(0, cols // 2))):
+        ref[size:] = to_low(jnp.concatenate([slots[:, at], none], axis=1), cols)
+
+
+def split_second_kernel(bit_ref, a_ref, b_ref, w_ref, theirs_ref, mine_ref, extra_ref):
+    rows = a_ref.shape[0] - 16
+    cols = a_ref.shape[1]
+    width = w_ref.shape[2]
+    size = rows // 2
+    total = (a_ref[:rows].astype(f32) + b_ref[:rows].astype(f32)).astype(bf16)
+    low = bit_ref[0] == 0
+    theirs_ref[...] = jnp.where(low, total[size:], total[:size])
+    mine_ref[...] = jnp.where(low, total[:size], total[size:])
+    own = from_low(a_ref[rows:], cols) + from_low(b_ref[rows:], cols)
+    own = (own * (1.0 / SPAN)).astype(bf16)
+    extra_ref[...] = nt(own[:, :width], w_ref[1]) + nt(own[:, width : 2 * width], w_ref[2])
 
 
 def split_kernel(bit_ref, a_ref, b_ref, theirs_ref, mine_ref):
@@ -431,11 +462,6 @@
     out_ref[rows:] = to_low(from_low(a_ref[rows:], dim) + from_low(b_ref[rows:], dim), dim)
 
 
-def extra_kernel(a_ref, b_ref, w_ref, out_ref):
-    own = ((a_ref[0] + b_ref[0]) * (1.0 / SPAN)).astype(bf16)
-    out_ref[...] = nt(own[0], w_ref[1]) + nt(own[1], w_ref[2])
-
-
 def piece_kernel(mine_ref, got_ref, near_ref, far_ref, back_ref, up_ref, out_ref):
     dim = near_ref.shape[1]
     hidden = up_ref.shape[1]
@@ -537,8 +563,9 @@
 
 
 def rest_unpack_kernel(
-    count, dim, at_ref, near_ref, far_ref, spare_ref, qkv_ref, out_ref, vec_ref, scratch
+    count, dim, at_ref, near_ref, far_ref, spare_ref, qkv_ref, out_ref, *refs
 ):
+    vec_refs, scratch = refs[:-1], refs[-1]
     cols = near_ref.shape[1]
     last = near_ref.shape[0] - 16 * (dim // cols)
     rows = 2 * last // count
@@ -555,7 +582,9 @@
             qkv_ref[s, k * rows : (k + 1) * rows] = x[:, s * width : (s + 1) * width]
         scratch[k * rows : (k + 1) * rows] = x[:, 3 * width :]
     out_ref[...] = scratch[...].T
-    vec_ref[...] = from_low(near_ref[last:], dim) + from_low(far_ref[last:], dim)
+    vectors = from_low(near_ref[last:], dim) + from_low(far_ref[last:], dim)
+    for k, ref in enumerate(vec_refs):
+        ref[...] = vectors[k : k + 1, : ref.shape[1]]
 
 
 def build(n_dp, n_mp):
@@ -676,7 +705,7 @@
         seq_masks = masks_of(group)
         me = lax.axis_index("mp")
         place = lax.axis_index("dp") % group
-        first_bit = bit_of(dp_masks[0])
+        first_bit = bit_of(feed_masks[0])
         pos = jnp.concatenate(
             [jnp.stack([me, me & 1, place]).astype(i32), bit_of(feed_masks[0])]
         )
@@ -823,7 +852,7 @@
             rest_kernel,
             "rest_weights",
             [SMEM] + [VMEM] * 6,
-            (sds((dim // 2, 4 * width), bf16), sds((dim // 2, 4 * width), bf16)),
+            (sds((dim // 2 + 16, 4 * width), bf16), sds((dim // 2 + 16, 4 * width), bf16)),
             mib=60,
         )
         slot_shape = (group, 2, blocks, width)
@@ -907,7 +936,9 @@
             functools.partial(rest_unpack_kernel, n_dp, dim),
             "rest_unpack",
             [SMEM, VMEM, VMEM, VMEM],
-            (sds((3, dim, width), f32), sds((width, dim), f32), sds((8, dim), f32)),
+            (sds((3, dim, width), f32), sds((width, dim), f32))
+            + (sds((1, dim), f32),) * 6
+            + (sds((1, hidden), f32),),
             [pltpu.VMEM((dim, width), f32)],
         )
 
@@ -918,17 +949,30 @@
         def pair(a, b):
             return like(pair_kernel, "pair", a.shape, bf16, a, b)
 
-        def slot_add(a, b):
-            return like(slot_kernel, "slots", b.shape, f32, a, b)
-
-        def extra_of(a, b, w):
-            return like(extra_kernel, "extra", (blocks, dim), f32, a, b, w)
-
         def concat(a, b):
             return like(concat_kernel, "concat", (2 * a.shape[0], a.shape[1]), bf16, a, b)
 
         def pl_add(a, b):
             return like(slot_kernel, "plus", a.shape, f32, a, b)
+
+        cols = 4 * width
+        quarter = dim // 4
+        split_first = plain(
+            split_first_kernel,
+            "split_first",
+            [SMEM, VMEM, VMEM],
+            (sds((quarter + 16, cols), bf16), sds((quarter + 16, cols), bf16)),
+        )
+        split_second = plain(
+            split_second_kernel,
+            "split_second",
+            [SMEM, VMEM, VMEM, VMEM],
+            (
+                sds((quarter // 2, cols), bf16),
+                sds((quarter // 2, cols), bf16),
+                sds((blocks, dim), f32),
+            ),
+        )
 
         vec_rows = 16 * (dim // (4 * width))
 
@@ -1035,45 +1079,43 @@
             sums,
         )
 
-        following = list(reversed(seq_masks))
-        slot_part = slot_grad
-        slot_got = swap(slot_part[following[0] :], "dp", following[0], "sum_slots")
         feed_sum.step()
         (out_other,) = wait(out_other)
         theirs, mine = line(first_grad, pos, gqkv, slot_grad, sums, w_qkv, tokens)
         got = swap(theirs, "mp", 1, "sum_first")
-        theirs_w, mine_w = line(
+        theirs_w, rest = line(
             rest_weights, first_bit, first, gqkv, grad_low, attended, slot_grad, sums
         )
+        rest_got = swap(theirs_w, "dp", feed_masks[0], "rest_weights")
         total = line(pair, mine, got)
         for m in far_masks[:-1]:
             total = line(pair, total, swap(total, "mp", m, "sum_first"))
         far = swap(total, "mp", last_far, "sum_first")
-        rest_sum = Scatter(line, theirs_w, mine_w, dp_masks, "rest_weights")
-        for low in following[1:]:
-            slot_part = line(slot_add, slot_part, slot_got)
-            slot_got = swap(slot_part[low:], "dp", low, "sum_slots")
         (out_far,) = wait(out_far)
         out_other_far = swap(out_far, "mp", 1, "sum_output")
         feed_sum.step()
-        extra = line(extra_of, slot_part, slot_got, w_qkv)
-        extra_got = swap(extra, "mp", 1, "sum_extra")
-        rest_sum.step()
+        theirs_w, rest = line(split_first, bit_of(feed_masks[1]), rest, rest_got)
+        rest_got = swap(theirs_w, "dp", feed_masks[1], "rest_weights")
         output = line(
             output_sum, pos, out_total, out_far, out_other, out_other_far, mid, b_down[None]
         )
+        for m in feed_masks[3:]:
+            feed_sum.step()
+        feed_all = line(add_low, feed_sum.mine, feed_sum.got)
+        feed_got = swap(feed_all, "dp", feed_masks[-1], "feed_weights")
+        theirs_w, rest, extra = line(split_second, bit_of(feed_masks[2]), rest, rest_got, w_qkv)
+        rest_got = swap(theirs_w, "dp", feed_masks[2], "rest_weights")
+        extra_got = swap(extra, "mp", 1, "sum_extra")
+        for m in feed_masks[3:]:
+            theirs_w, rest = line(split_sum, bit_of(m), rest, rest_got)
+            rest_got = swap(theirs_w, "dp", m, "rest_weights")
         for m in far_masks:
+            line.space()
             extra = line(pl_add, extra, extra_got)
             extra_got = swap(extra, "mp", m, "sum_extra")
-        for m in dp_masks[2:]:
-            rest_sum.step()
-        for m in feed_masks[3:]:
-            feed_sum.step()
         (far,) = wait(far)
         other = swap(after(total, far), "mp", 1, "sum_first")
         other_far = swap(far, "mp", 1, "sum_first")
-        feed_all = line(add_low, feed_sum.mine, feed_sum.got)
-        feed_got = swap(feed_all, "dp", feed_masks[-1], "feed_weights")
         grad_tokens = line(
             last,
             pos,
@@ -1087,18 +1129,18 @@
             grad_low,
             ln1_gain[None],
         )
-        rest_all = line(
-            piece_of, rest_sum.mine, rest_sum.got, total, far, back_vec, up_vec
-        )
-        rest_got = swap(rest_all, "dp", dp_masks[-1], "rest_weights")
         feed_next = list(reversed(feed_masks))[1:]
-        rest_next = list(reversed(dp_masks))[1:]
+        rest_next = list(reversed(feed_masks))[1:]
         for m in feed_next[:-2]:
             feed_all = line(concat, feed_all, feed_got)
             feed_got = swap(feed_all, "dp", m, "feed_weights")
         feed_all = line(concat, feed_all, feed_got)
         two = swap(feed_all, "dp", feed_masks[0], "feed_weights")
         one = swap(feed_all, "dp", feed_masks[1], "feed_weights")
+        rest_all = line(
+            piece_of, rest, rest_got, total, far, back_vec, up_vec
+        )
+        rest_got = swap(rest_all, "dp", feed_masks[-1], "rest_weights")
         line.space()
         rest_all = line(merge, rest_all, rest_got)
         rest_got = swap(rest_all, "dp", rest_next[0], "rest_weights")
@@ -1112,23 +1154,23 @@
         grad_w_down, grad_w_up = line(
             feed_unpack, place_of(feed_masks), feed_all, one, two, both
         )
-        grad_w_qkv, grad_w_out, vectors = line(
-            rest_unpack, place_of(dp_masks), rest_all, rest_got, line.spare
+        grad_w_qkv, grad_w_out, *vectors = line(
+            rest_unpack, place_of(feed_masks), rest_all, rest_got, line.spare
         )
         return (
             output,
             grad_tokens,
-            vectors[0],
-            vectors[1],
+            vectors[0][0],
+            vectors[1][0],
             grad_w_qkv,
             grad_w_out,
-            vectors[2],
-            vectors[3],
-            vectors[4],
+            vectors[2][0],
+            vectors[3][0],
+            vectors[4][0],
             grad_w_up.reshape(dim, hidden),
-            vectors[6, :hidden],
+            vectors[6][0],
             grad_w_down,
-            vectors[5],
+            vectors[5][0],
         )
 
     return per_device

time: 140 us -> 136 us (0.971)
  waiting for transfers between devices: 33.7 us -> 41 us
  starting transfers between devices: 36.9 us -> 31.4 us
  Pallas kernels: 62.4 us -> 57.8 us
    ppermute x37 -> x35, waiting for transfers between devices: 33.7 us -> 41 us  [swap(): return lax.ppermute(x, axis, [(i, i ^ mask) for i in range(n)])]
    ppermute x37 -> x35, starting transfers between devices: 36.9 us -> 31.4 us  [swap(): return lax.ppermute(x, axis, [(i, i ^ mask) for i in range(n)])]
    pallas_call x8 -> x6, Pallas kernels: 7.5 us -> 3.69 us  [like(): return plain(kernel, name, specs, (sds(shape, dtype),))(*operands)[0]]
    pallas_call x4 -> x2, Pallas kernels: 7.45 us -> 4.11 us  [split_sum(): pl.pallas_call(split_kernel, out_shape=(half, half), in_specs=[SMEM, VMEM...]
    pallas_call x11 -> x13, Pallas kernels: 37.1 us -> 40.4 us  [__call__(): result = work(*inputs)]
    unnamed x86 -> x82, local copies, waits for them, and re-layouts: 3.27 us -> 3.14 us
  transfers between devices with their start and end apart: 37 -> 35, of which waited for: 14 -> 19; matrix products, arithmetic and copies ran while one was open for 1% -> 0% of each run, Pallas kernels for 34% -> 32%
where the time goes in v5:
time: 136 us; the launch traced here: 135 us
  Pallas kernels  57.8 us (42%)
  waiting for transfers between devices  41 us (30%)
  starting transfers between devices  31.4 us (23%)
  local copies, waits for them, and re-layouts  3.15 us (2%)
    ppermute x35, waiting for transfers between devices, swap(): return lax.ppermute(x, axis, [(i, i ^ mask) for i in range(n)])  41 us
    pallas_call x13, Pallas kernels, __call__(): result = work(*inputs)  40.4 us
    ppermute x35, starting transfers between devices, swap(): return lax.ppermute(x, axis, [(i, i ^ mask) for i in range(n)])  31.4 us
    pallas_call x1, Pallas kernels, per_device(): back(*a)  6.81 us
    pallas_call x2, Pallas kernels, split_sum(): pl.pallas_call(split_kernel, out_shape=(half, half), in_specs=[SMEM, VMEM...  4.11 us
    pallas_call x6, Pallas kernels, like(): return plain(kernel, name, specs, (sds(shape, dtype),))(*operands)[0]  3.69 us
    unnamed x82, local copies, waits for them, and re-layouts  3.14 us
    pallas_call x3, Pallas kernels, add_parts(): pl.pallas_call(functools.partial(add_kernel, parts), out_shape=(part,) *...  2.75 us
  transfers between devices with their start and end apart: 35, of which 19 were waited for; matrix products, arithmetic and copies ran while one was open for 0% of the time, Pallas kernels for 32%

profile of v5, /device:TPU:0, one launch (start us, length us, event | category | flops | bytes accessed | tf_op | source)
XLA Modules:
  0.0 135.1 jit_solution(13379102861197640713)
XLA Ops:
  0.6 3.0 %collective-permute-start = (bf16[128,512]{1,0:T(8,128)(2,1)}, bf16[128,512]{1,0:T(8,128)(2,1)S(1)}, u32[]{:S(2)}, u32[]{:S(2)}) collective-permute-start(bf16[128,512]{1,0:T(8,128)(2,1)} %wo_ref), channel_id=1, source_target_pairs={{0,2},{1,3},{2,0},{3,1},{4,6},{5,7},{6,4},{7,5},{8,10},{9,11},{10,... | collective-permute-start | bytes 393224 | tf_op jit(solution)/shard_map/gather_w_out/ppermute | solution.py:594
  3.7 3.9 %project.1 = (bf16[1024,512]{1,0:T(8,128)(2,1)}, bf16[3,1024,128]{2,1,0:T(8,128)(2,1)}, f32[10,8,128]{2,1,0:T(8,128)}) custom-call(bf16[1024,512]{1,0:T(8,128)(2,1)} %tok_ref.3, f32[1,512]{1,0:T(1,128)} %bitcast.24, f32[1,512]{1,0:T(1,128)} %bitcast.29, bf16[3,512,128]{2,1,0:T(8,128)(2,1)} %w_ref.2), custom_call_target="tpu_custom_call" | custom-call | flops 115000000512 | bytes 1 | tf_op jit(solution)/shard_map/project/pallas_call | solution.py:618
  7.6 1.6 %collective-permute-start.1 = (f32[1,10,8,128]{3,2,1,0:T(8,128)}, f32[1,10,8,128]{3,2,1,0:T(8,128)S(1)}, u32[]{:S(2)}, u32[]{:S(2)}) collective-permute-start(f32[1,10,8,128]{3,2,1,0:T(8,128)} %bitcast.27), channel_id=1, source_target_pairs={{0,4},{4,0},{8,12},{12,8},{16,20},{20,16},{24,28},{28,24},{1,5},{5... | collective-permute-start | bytes 122888 | tf_op jit(solution)/shard_map/summaries/ppermute | solution.py:594
  9.2 1.1 copy-done.26
  10.3 0.5 local.1
  10.8 1.1 collective-permute-done.1
  11.9 1.6 %collective-permute-start.2 = (f32[2,10,8,128]{3,2,1,0:T(8,128)S(1)}, f32[2,10,8,128]{3,2,1,0:T(8,128)S(1)}, u32[]{:S(2)}, u32[]{:S(2)}) collective-permute-start(f32[2,10,8,128]{3,2,1,0:T(8,128)S(1)} %constant_dynamic-update-slice_fusion), channel_id=1, source_target_pairs={{0,8},{4,12},{8,0},{12,4},{16,24},{20,28},{24,16},{28,20},{1,9},{5... | collective-permute-start | bytes 245768 | tf_op jit(solution)/shard_map/summaries/ppermute | solution.py:594
  13.5 0.5 collective-permute-start.4
  14.1 2.3 %collective-permute-done.2 = f32[2,10,8,128]{3,2,1,0:T(8,128)S(1)} collective-permute-done((f32[2,10,8,128]{3,2,1,0:T(8,128)S(1)}, f32[2,10,8,128]{3,2,1,0:T(8,128)S(1)}, u32[]{:S(2)}, u32[]{:S(2)}) %collective-permute-start.2) | collective-permute-done | bytes 81952 | tf_op jit(solution)/shard_map/summaries/ppermute | solution.py:594
  16.5 1.5 %attend.1 = (bf16[8,160,256]{2,1,0:T(8,128)(2,1)S(1)}, bf16[1024,128]{1,0:T(8,128)(2,1)S(1)}) custom-call(s32[1]{0:T(128)} %bitcast.2.place_ref, bf16[3,1024,128]{2,1,0:T(8,128)(2,1)S(1)} %copy-done.26, f32[8,128,256]{2,1,0:T(8,128)S(1)} %get-tuple-element.219.exp_ref, f32[8,2,256]{2,1,0:T(2,128)S(1)} %get-tuple-element.220.stat_ref, ...), custom_call_target="tpu_custom_call" | custom-call | flops 115000000512 | bytes 1 | tf_op jit(solution)/shard_map/attend/pallas_call | solution.py:618
  18.0 1.5 %collective-permute-start.6 = (bf16[1024,128]{1,0:T(8,128)(2,1)S(1)}, bf16[1024,128]{1,0:T(8,128)(2,1)S(1)}, u32[]{:S(2)}, u32[]{:S(2)}) collective-permute-start(bf16[1024,128]{1,0:T(8,128)(2,1)S(1)} %get-tuple-element.300.refs_0_.att_ref), channel_id=1, source_target_pairs={{0,2},{1,3},{2,0},{3,1},{4,6},{5,7},{6,4},{7,5},{8,10},{9,11},{10,... | collective-permute-start | bytes 786440 | tf_op jit(solution)/shard_map/gather_attended/ppermute | solution.py:594
  19.6 5.7 %collective-permute-done.6.refs_2_ = bf16[1024,128]{1,0:T(8,128)(2,1)S(1)} collective-permute-done((bf16[1024,128]{1,0:T(8,128)(2,1)S(1)}, bf16[1024,128]{1,0:T(8,128)(2,1)S(1)}, u32[]{:S(2)}, u32[]{:S(2)}) %collective-permute-start.6) | collective-permute-done | bytes 262176 | tf_op jit(solution)/shard_map/gather_attended/ppermute | solution.py:594
  25.2 0.6 pad_add_fusion.pos_ref
  25.8 0.9 collective-permute-done.7.refs_3_
  26.8 0.7 copy-done.36
  27.5 8.9 %feed.1 = (f32[1024,512]{1,0:T(8,128)}, bf16[1024,512]{1,0:T(8,128)(2,1)}, bf16[1024,512]{1,0:T(8,128)(2,1)}, bf16[1024,512]{1,0:T(8,128)(2,1)}, bf16[512,512]{1...) custom-call(s32[4]{0:T(128)} %pad_add_fusion.pos_ref, bf16[1024,512]{1,0:T(8,128)(2,1)} %tok_ref.3, ...), custom_call_target="tpu_custom_call" | custom-call | flops 115000000512 | bytes 1 | tf_op jit(solution)/shard_map/feed/pallas_call | solution.py:618
  36.6 2.0 %collective-permute-done.8.b_ref = bf16[512,512]{1,0:T(8,128)(2,1)S(1)} collective-permute-done((bf16[512,512]{1,0:T(8,128)(2,1)}, bf16[512,512]{1,0:T(8,128)(2,1)S(1)}, u32[]{:S(2)}, u32[]{:S(2)}) %collective-permute-start.8) | collective-permute-done | bytes 524320 | tf_op jit(solution)/shard_map/sum_second/ppermute | solution.py:594
  38.6 1.0 copy-done.29
  39.7 0.9 add.24.own_ref
  40.6 1.5 %collective-permute-start.10 = (bf16[512,512]{1,0:T(8,128)(2,1)}, bf16[512,512]{1,0:T(8,128)(2,1)}, u32[]{:S(2)}, u32[]{:S(2)}) collective-permute-start(bf16[512,512]{1,0:T(8,128)(2,1)} %add.24.own_ref), channel_id=1, source_target_pairs={{0,2},{1,3},{2,0},{3,1},{4,6},{5,7},{6,4},{7,5},{8,10},{9,11},{10,... | collective-permute-start | bytes 1572872 | tf_op jit(solution)/shard_map/sum_second/ppermute | solution.py:594
  42.2 3.8 %weights.1 = (bf16[512,512]{1,0:T(8,128)(2,1)S(1)}, bf16[512,512]{1,0:T(8,128)(2,1)S(1)}, bf16[512,512]{1,0:T(8,128)(2,1)}, bf16[512,512]{1,0:T(8,128)(2,1)S(1)}) custom-call(s32[4]{0:T(128)S(1)} %copy-done.2, bf16[1024,512]{1,0:T(8,128)(2,1)S(1)} %copy-done.24, bf16[1024,512]{1,0:T(8,128)(2,1)S(1)} %copy-done.23, bf16[1024,512]{1,0:T(8,128)(2,1)S(1)} %copy-done.25, ...), custom_call_target="tpu_custom_call" | custom-call | flops 115000000512 | bytes 1 | tf_op jit(solution)/shard_map/weights/pallas_call | solution.py:618
  46.4 0.8 collective-permute-start.15
  47.2 0.7 collective-permute-done.9.b_ref
  48.0 0.9 add.25.own_ref
  48.9 5.9 %collective-permute-done.10.far_ref = bf16[512,512]{1,0:T(8,128)(2,1)} collective-permute-done((bf16[512,512]{1,0:T(8,128)(2,1)}, bf16[512,512]{1,0:T(8,128)(2,1)}, u32[]{:S(2)}, u32[]{:S(2)}) %collective-permute-start.10) | collective-permute-done | bytes 524320 | tf_op jit(solution)/shard_map/sum_second/ppermute | solution.py:594
  54.9 0.5 collective-permute-start.14
  55.4 1.5 %collective-permute-start.11 = (bf16[512,512]{1,0:T(8,128)(2,1)}, bf16[512,512]{1,0:T(8,128)(2,1)}, u32[]{:S(2)}, u32[]{:S(2)}) collective-permute-start(bf16[512,512]{1,0:T(8,128)(2,1)} %add.25.own_ref), channel_id=1, source_target_pairs={{0,2},{1,3},{2,0},{3,1},{4,6},{5,7},{6,4},{7,5},{8,10},{9,11},{10,... | collective-permute-start | bytes 1572872 | tf_op jit(solution)/shard_map/sum_output/ppermute | solution.py:594
  56.9 0.9 collective-permute-done.13.other_far_ref
  57.8 6.8 %back.1 = (bf16[1024,512]{1,0:T(8,128)(2,1)S(1)}, bf16[1024,384]{1,0:T(8,128)(2,1)S(1)}, f32[4,2,8,128]{3,2,1,0:T(8,128)S(1)}, f32[32,512]{1,0:T(8,128)S(1)}) custom-call(s32[4]{0:T(128)S(1)} %copy-done.3, bf16[512,512]{1,0:T(8,128)(2,1)} %add.24.own_ref, bf16[512,512]{1,0:T(8,128)(2,1)} %collective-permute-done.10.far_ref, ...), custom_call_target="tpu_custom_call" | custom-call | flops 115000000512 | bytes 1 | tf_op jit(solution)/shard_map/back/pallas_call | solution.py:1067
  64.6 2.4 %split.2 = (bf16[256,512]{1,0:T(8,128)(2,1)}, bf16[256,512]{1,0:T(8,128)(2,1)S(1)}) custom-call(s32[1]{0:T(128)} %bitcast.11.bit_ref, bf16[512,512]{1,0:T(8,128)(2,1)S(1)} %get-tuple-element.282.a_ref, bf16[512,512]{1,0:T(8,128)(2,1)} %collective-permute-done.15.b_ref), custom_call_target="tpu_custom_call" | custom-call | flops 115000000512 | bytes 1 | tf_op jit(solution)/shard_map/split/pallas_call | solution.py:657
  67.1 2.0 %first.1 = (bf16[528,512]{1,0:T(8,128)(2,1)S(1)}, bf16[528,512]{1,0:T(8,128)(2,1)S(1)}) custom-call(s32[4]{0:T(128)S(1)} %copy-done.3, bf16[1024,384]{1,0:T(8,128)(2,1)S(1)} %get-tuple-element.298.gqkv_ref, f32[4,2,8,128]{3,2,1,0:T(8,128)S(1)} %get-tuple-element.301.slot_ref, f32[4,10,8,128]{3,2,1,0:T(8,128)S(1)} %copy-done.1, ...), custom_call_target="tpu_custom_call" | custom-call | flops 115000000512 | bytes 1 | tf_op jit(solution)/shard_map/first/pallas_call | solution.py:618
  69.3 1.5 %collective-permute-start.19 = (bf16[256,512]{1,0:T(8,128)(2,1)}, bf16[256,512]{1,0:T(8,128)(2,1)}, u32[]{:S(2)}, u32[]{:S(2)}) collective-permute-start(bf16[256,512]{1,0:T(8,128)(2,1)} %get-tuple-element.308), channel_id=1, source_target_pairs={{0,4},{4,0},{8,12},{12,8},{16,20},{20,16},{24,28},{28,24},{1,5},{5... | collective-permute-start | bytes 786440 | tf_op jit(solution)/shard_map/feed_weights/ppermute | solution.py:594
  70.8 3.8 %rest_weights.1 = (bf16[272,512]{1,0:T(8,128)(2,1)}, bf16[272,512]{1,0:T(8,128)(2,1)}) custom-call(s32[1]{0:T(128)} %bitcast.3.bit_ref, bf16[1024,512]{1,0:T(8,128)(2,1)} %get-tuple-element.297.first_ref, bf16[1024,384]{1,0:T(8,128)(2,1)} %copy-done.28, bf16[1024,512]{1,0:T(8,128)(2,1)} %copy-done.21, bf16[1024,128]{1,0:T(8,128)(2,1)} %copy-done.12, ...), custom_call_target="tpu_custom_call" | custom-call | flops 115000000512 | bytes 1 | tf_op jit(solution)/shard_map/rest_weights/pallas_call | solution.py:618
  74.6 0.8 collective-permute-start.18
  75.4 0.9 pair.1.own_ref.near_ref
  76.4 1.5 %collective-permute-start.20 = (bf16[528,512]{1,0:T(8,128)(2,1)}, bf16[528,512]{1,0:T(8,128)(2,1)}, u32[]{:S(2)}, u32[]{:S(2)}) collective-permute-start(bf16[528,512]{1,0:T(8,128)(2,1)} %pair.1.own_ref.near_ref), channel_id=1, source_target_pairs={{0,2},{1,3},{2,0},{3,1},{4,6},{5,7},{6,4},{7,5},{8,10},{9,11},{10,... | collective-permute-start | bytes 1622024 | tf_op jit(solution)/shard_map/sum_first/ppermute | solution.py:594
  78.2 1.7 %split.3 = (bf16[128,512]{1,0:T(8,128)(2,1)}, bf16[128,512]{1,0:T(8,128)(2,1)S(1)}) custom-call(s32[1]{0:T(128)} %bitcast.13.bit_ref, bf16[256,512]{1,0:T(8,128)(2,1)S(1)} %get-tuple-element.310.a_ref, bf16[256,512]{1,0:T(8,128)(2,1)} %collective-permute-done.19.b_ref), custom_call_target="tpu_custom_call" | custom-call | flops 115000000512 | bytes 1 | tf_op jit(solution)/shard_map/split/pallas_call | solution.py:657
  79.9 3.6 %collective-permute-done.18.b_ref = bf16[272,512]{1,0:T(8,128)(2,1)} collective-permute-done((bf16[272,512]{1,0:T(8,128)(2,1)}, bf16[272,512]{1,0:T(8,128)(2,1)}, u32[]{:S(2)}, u32[]{:S(2)}) %collective-permute-start.18) | collective-permute-done | bytes 278560 | tf_op jit(solution)/shard_map/rest_weights/ppermute | solution.py:594
  83.6 2.6 %collective-permute-start.22 = (bf16[128,512]{1,0:T(8,128)(2,1)}, bf16[128,512]{1,0:T(8,128)(2,1)}, u32[]{:S(2)}, u32[]{:S(2)}) collective-permute-start(bf16[128,512]{1,0:T(8,128)(2,1)} %get-tuple-element.325), channel_id=1, source_target_pairs={{0,16},{4,20},{8,24},{12,28},{16,0},{20,4},{24,8},{28,12},{1,17},{... | collective-permute-start | bytes 393224 | tf_op jit(solution)/shard_map/feed_weights/ppermute | solution.py:594
  86.2 1.7 %split_first.1 = (bf16[144,512]{1,0:T(8,128)(2,1)}, bf16[144,512]{1,0:T(8,128)(2,1)S(1)}) custom-call(s32[1]{0:T(128)} %bitcast.11.bit_ref, bf16[272,512]{1,0:T(8,128)(2,1)S(1)} %copy-done.30, bf16[272,512]{1,0:T(8,128)(2,1)} %collective-permute-done.18.b_ref), custom_call_target="tpu_custom_call" | custom-call | flops 115000000512 | bytes 1 | tf_op jit(solution)/shard_map/split_first/pallas_call | solution.py:618
  87.9 0.5 collective-permute-start.21
  88.4 3.4 %output.1 = bf16[1024,512]{1,0:T(8,128)(2,1)} custom-call(s32[4]{0:T(128)S(1)} %copy-done.4, bf16[512,512]{1,0:T(8,128)(2,1)} %add.25.own_ref, bf16[512,512]{1,0:T(8,128)(2,1)} %collective-permute-done.11.far_ref, bf16[512,512]{1,0:T(8,128)(2,1)} %collective-permute-done.14.other_ref, bf16[512,512]{1,0:T(8,128)(2,1)} %collective-permute-done.17.other_far_ref, ...), custom_call_target="tpu_custom_call" | custom-call | flops 115000000512 | bytes 1 | tf_op jit(solution)/shard_map/output/pallas_call | solution.py:618
  92.2 0.9 add.26.a_ref
  93.3 1.6 %split_second.1 = (bf16[64,512]{1,0:T(8,128)(2,1)}, bf16[64,512]{1,0:T(8,128)(2,1)S(1)}, f32[8,512]{1,0:T(8,128)S(1)}) custom-call(s32[1]{0:T(128)} %bitcast.13.bit_ref, bf16[144,512]{1,0:T(8,128)(2,1)S(1)} %get-tuple-element.329.a_ref, bf16[144,512]{1,0:T(8,128)(2,1)} %collective-permute-done.21.b_ref, bf16[3,512,128]{2,1,0:T(8,128)(2,1)S(1)} %copy-done.11), custom_call_target="tpu_custom_call" | custom-call | flops 115000000512 | bytes 1 | tf_op jit(solution)/shard_map/split_second/pallas_call | solution.py:618
  95.0 1.1 collective-permute-done.23.b_ref
  96.7 1.5 %collective-permute-start.26 = (f32[8,512]{1,0:T(8,128)S(1)}, f32[8,512]{1,0:T(8,128)S(1)}, u32[]{:S(2)}, u32[]{:S(2)}) collective-permute-start(f32[8,512]{1,0:T(8,128)S(1)} %plus.1.extra_ref), channel_id=1, source_target_pairs={{0,2},{1,3},{2,0},{3,1},{4,6},{5,7},{6,4},{7,5},{8,10},{9,11},{10,... | collective-permute-start | bytes 49160 | tf_op jit(solution)/shard_map/sum_extra/ppermute | solution.py:594
  98.2 0.5 collective-permute-start.28
  98.7 2.4 %collective-permute-start.27 = (bf16[64,512]{1,0:T(8,128)(2,1)}, bf16[64,512]{1,0:T(8,128)(2,1)}, u32[]{:S(2)}, u32[]{:S(2)}) collective-permute-start(bf16[64,512]{1,0:T(8,128)(2,1)} %get-tuple-element.349), channel_id=1, source_target_pairs={{0,16},{4,20},{8,24},{12,28},{16,0},{20,4},{24,8},{28,12},{1,17},{... | collective-permute-start | bytes 196616 | tf_op jit(solution)/shard_map/rest_weights/ppermute | solution.py:594
  101.2 4.3 %last.1 = bf16[1024,512]{1,0:T(8,128)(2,1)} custom-call(s32[4]{0:T(128)S(1)} %copy-done.4, bf16[528,512]{1,0:T(8,128)(2,1)} %pair.1.own_ref.near_ref, bf16[528,512]{1,0:T(8,128)(2,1)} %collective-permute-done.20.far_ref, bf16[528,512]{1,0:T(8,128)(2,1)S(1)} %collective-permute-done.24.other_ref, bf16[528,512]{1,0:T(8,128)(2,1)S(1)} %collective-permute-done.25.other_far_ref, ...), custom_call_target="tpu_custom_call" | custom-call | flops 115000000512 | bytes 1 | tf_op jit(solution)/shard_map/last/pallas_call | solution.py:618
  105.5 3.5 %collective-permute-done.28.b_ref = bf16[128,512]{1,0:T(8,128)(2,1)S(1)} collective-permute-done((bf16[128,512]{1,0:T(8,128)(2,1)S(1)}, bf16[128,512]{1,0:T(8,128)(2,1)S(1)}, u32[]{:S(2)}, u32[]{:S(2)}) %collective-permute-start.28) | collective-permute-done | bytes 131104 | tf_op jit(solution)/shard_map/feed_weights/ppermute | solution.py:594
  108.9 0.7 concat.1.own_ref
  110.1 1.3 piece.1.a_ref
  111.4 2.0 %collective-permute-start.31 = (bf16[256,512]{1,0:T(8,128)(2,1)}, bf16[256,512]{1,0:T(8,128)(2,1)}, u32[]{:S(2)}, u32[]{:S(2)}) collective-permute-start(bf16[256,512]{1,0:T(8,128)(2,1)} %concat.1.own_ref), channel_id=1, source_target_pairs={{0,8},{4,12},{8,0},{12,4},{16,24},{20,28},{24,16},{28,20},{1,9},{5... | collective-permute-start | bytes 786440 | tf_op jit(solution)/shard_map/feed_weights/ppermute | solution.py:594
  113.4 1.1 collective-permute-start.33
  114.5 2.9 %collective-permute-done.29.b_ref = bf16[80,512]{1,0:T(8,128)(2,1)S(1)} collective-permute-done((bf16[80,512]{1,0:T(8,128)(2,1)S(1)}, bf16[80,512]{1,0:T(8,128)(2,1)S(1)}, u32[]{:S(2)}, u32[]{:S(2)}) %collective-permute-start.29) | collective-permute-done | bytes 81952 | tf_op jit(solution)/shard_map/rest_weights/ppermute | solution.py:594
  117.4 1.1 collective-permute-start.30
  118.5 3.2 %collective-permute-done.31.two_ref = bf16[256,512]{1,0:T(8,128)(2,1)} collective-permute-done((bf16[256,512]{1,0:T(8,128)(2,1)}, bf16[256,512]{1,0:T(8,128)(2,1)}, u32[]{:S(2)}, u32[]{:S(2)}) %collective-permute-start.31) | collective-permute-done | bytes 262176 | tf_op jit(solution)/shard_map/feed_weights/ppermute | solution.py:594
  121.7 1.1 collective-permute-start.34
  122.8 2.5 %collective-permute-done.30.b_ref = bf16[144,512]{1,0:T(8,128)(2,1)S(1)} collective-permute-done((bf16[144,512]{1,0:T(8,128)(2,1)S(1)}, bf16[144,512]{1,0:T(8,128)(2,1)S(1)}, u32[]{:S(2)}, u32[]{:S(2)}) %collective-permute-start.30) | collective-permute-done | bytes 147488 | tf_op jit(solution)/shard_map/rest_weights/ppermute | solution.py:594
  125.2 0.7 merge.3.near_ref
  126.0 0.9 collective-permute-start.32
  126.9 3.3 %collective-permute-done.34.both_ref = bf16[256,512]{1,0:T(8,128)(2,1)} collective-permute-done((bf16[256,512]{1,0:T(8,128)(2,1)}, bf16[256,512]{1,0:T(8,128)(2,1)}, u32[]{:S(2)}, u32[]{:S(2)}) %collective-permute-start.34) | collective-permute-done | bytes 262176 | tf_op jit(solution)/shard_map/feed_weights/ppermute | solution.py:594
  130.2 2.8 %feed_unpack.1 = (f32[512,512]{1,0:T(8,128)}, f32[512,512]{1,0:T(8,128)}) custom-call(s32[1]{0:T(128)S(6)} %add.17.at_ref, bf16[256,512]{1,0:T(8,128)(2,1)} %concat.1.own_ref, bf16[256,512]{1,0:T(8,128)(2,1)} %collective-permute-done.33.one_ref, bf16[256,512]{1,0:T(8,128)(2,1)} %collective-permute-done.31.two_ref, ...), custom_call_target="tpu_custom_call" | custom-call | flops 115000000512 | bytes 1 | tf_op jit(solution)/shard_map/feed_unpack/pallas_call | solution.py:618
  133.0 2.1 %rest_unpack.1 = (f32[3,512,128]{2,1,0:T(8,128)}, f32[128,512]{1,0:T(8,128)}, f32[1,512]{1,0:T(1,128)}, f32[1,512]{1,0:T(1,128)}, f32[1,512]{1,0:T(1,128)}, /*in...) custom-call(s32[1]{0:T(128)S(6)} %add.17.at_ref, bf16[272,512]{1,0:T(8,128)(2,1)} %merge.3.near_ref, ...), custom_call_target="tpu_custom_call" | custom-call | flops 115000000512 | bytes 1 | tf_op jit(solution)/shard_map/rest_unpack/pallas_call | solution.py:618
  (122 shorter events, 3.2 us)
Async XLA Ops:
  0.6 6.9 %collective-permute-start = (bf16[128,512]{1,0:T(8,128)(2,1)}, bf16[128,512]{1,0:T(8,128)(2,1)S(1)}, u32[]{:S(2)}, u32[]{:S(2)}) collective-permute-start(bf16[128,512]{1,0:T(8,128)(2,1)} %wo_ref), channel_id=1, source_target_pairs={{0,2},{1,3},{2,0},{3,1},{4,6},{5,7},{6,4},{7,5},{8,10},{9,11},{10,... | collective-permute-start | bytes 393224 | tf_op jit(solution)/shard_map/gather_w_out/ppermute | solution.py:594
  7.6 6.0 %copy-start.37 = (bf16[128,512]{1,0:T(8,128)(2,1)}, bf16[128,512]{1,0:T(8,128)(2,1)S(1)}, u32[]{:S(2)}) copy-start(bf16[128,512]{1,0:T(8,128)(2,1)S(1)} %collective-permute-done.refs_6_) | copy-start | bytes 393220
  7.6 5.9 %copy-start.13 = (bf16[128,512]{1,0:T(8,128)(2,1)S(1)}, bf16[128,512]{1,0:T(8,128)(2,1)}, u32[]{:S(2)}) copy-start(bf16[128,512]{1,0:T(8,128)(2,1)} %wo_ref) | copy-start | bytes 393220
  7.6 4.3 %collective-permute-start.1 = (f32[1,10,8,128]{3,2,1,0:T(8,128)}, f32[1,10,8,128]{3,2,1,0:T(8,128)S(1)}, u32[]{:S(2)}, u32[]{:S(2)}) collective-permute-start(f32[1,10,8,128]{3,2,1,0:T(8,128)} %bitcast.27), channel_id=1, source_target_pairs={{0,4},{4,0},{8,12},{12,8},{16,20},{20,16},{24,28},{28,24},{1,5},{5... | collective-permute-start | bytes 122888 | tf_op jit(solution)/shard_map/summaries/ppermute | solution.py:594
  11.9 4.5 %collective-permute-start.2 = (f32[2,10,8,128]{3,2,1,0:T(8,128)S(1)}, f32[2,10,8,128]{3,2,1,0:T(8,128)S(1)}, u32[]{:S(2)}, u32[]{:S(2)}) collective-permute-start(f32[2,10,8,128]{3,2,1,0:T(8,128)S(1)} %constant_dynamic-update-slice_fusion), channel_id=1, source_target_pairs={{0,8},{4,12},{8,0},{12,4},{16,24},{20,28},{24,16},{28,20},{1,9},{5... | collective-permute-start | bytes 245768 | tf_op jit(solution)/shard_map/summaries/ppermute | solution.py:594
  13.5 2.9 %collective-permute-start.3 = (bf16[128,512]{1,0:T(8,128)(2,1)S(1)}, bf16[128,512]{1,0:T(8,128)(2,1)S(1)}, u32[]{:S(2)}, u32[]{:S(2)}) collective-permute-start(bf16[128,512]{1,0:T(8,128)(2,1)S(1)} %copy-done.13), channel_id=1, source_target_pairs={{0,1},{1,0},{2,3},{3,2},{4,5},{5,4},{6,7},{7,6},{8,9},{9,8},{10,11... | collective-permute-start | bytes 393224 | tf_op jit(solution)/shard_map/gather_w_out/ppermute | solution.py:594
  13.5 2.9 %collective-permute-start.4 = (bf16[128,512]{1,0:T(8,128)(2,1)S(1)}, bf16[128,512]{1,0:T(8,128)(2,1)S(1)}, u32[]{:S(2)}, u32[]{:S(2)}) collective-permute-start(bf16[128,512]{1,0:T(8,128)(2,1)S(1)} %collective-permute-done.refs_6_), channel_id=1, source_target_pairs={{0,1},{1,0},{2,3},{3,2},{4,5},{5,4},{6,7},{7,6},{8,9},{9,8},{10,11... | collective-permute-start | bytes 393224 | tf_op jit(solution)/shard_map/gather_w_out/ppermute | solution.py:594
  18.0 8.8 %copy-start.12 = (bf16[1024,128]{1,0:T(8,128)(2,1)}, bf16[1024,128]{1,0:T(8,128)(2,1)S(1)}, u32[]{:S(2)}) copy-start(bf16[1024,128]{1,0:T(8,128)(2,1)S(1)} %get-tuple-element.300.refs_0_.att_ref) | copy-start | bytes 786436
  18.0 7.2 %collective-permute-start.6 = (bf16[1024,128]{1,0:T(8,128)(2,1)S(1)}, bf16[1024,128]{1,0:T(8,128)(2,1)S(1)}, u32[]{:S(2)}, u32[]{:S(2)}) collective-permute-start(bf16[1024,128]{1,0:T(8,128)(2,1)S(1)} %get-tuple-element.300.refs_0_.att_ref), channel_id=1, source_target_pairs={{0,2},{1,3},{2,0},{3,1},{4,6},{5,7},{6,4},{7,5},{8,10},{9,11},{10,... | collective-permute-start | bytes 786440 | tf_op jit(solution)/shard_map/gather_attended/ppermute | solution.py:594
  19.6 6.3 %collective-permute-start.5 = (bf16[1024,128]{1,0:T(8,128)(2,1)S(1)}, bf16[1024,128]{1,0:T(8,128)(2,1)S(1)}, u32[]{:S(2)}, u32[]{:S(2)}) collective-permute-start(bf16[1024,128]{1,0:T(8,128)(2,1)S(1)} %get-tuple-element.300.refs_0_.att_ref), channel_id=1, source_target_pairs={{0,1},{1,0},{2,3},{3,2},{4,5},{5,4},{6,7},{7,6},{8,9},{9,8},{10,11... | collective-permute-start | bytes 786440 | tf_op jit(solution)/shard_map/gather_attended/ppermute | solution.py:594
  25.2 1.5 %collective-permute-start.7 = (bf16[1024,128]{1,0:T(8,128)(2,1)S(1)}, bf16[1024,128]{1,0:T(8,128)(2,1)S(1)}, u32[]{:S(2)}, u32[]{:S(2)}) collective-permute-start(bf16[1024,128]{1,0:T(8,128)(2,1)S(1)} %collective-permute-done.6.refs_2_), channel_id=1, source_target_pairs={{0,1},{1,0},{2,3},{3,2},{4,5},{5,4},{6,7},{7,6},{8,9},{9,8},{10,11... | collective-permute-start | bytes 786440 | tf_op jit(solution)/shard_map/gather_attended/ppermute | solution.py:594
  36.4 2.2 %collective-permute-start.8 = (bf16[512,512]{1,0:T(8,128)(2,1)}, bf16[512,512]{1,0:T(8,128)(2,1)S(1)}, u32[]{:S(2)}, u32[]{:S(2)}) collective-permute-start(bf16[512,512]{1,0:T(8,128)(2,1)} %get-tuple-element.245), channel_id=1, source_target_pairs={{0,1},{1,0},{2,3},{3,2},{4,5},{5,4},{6,7},{7,6},{8,9},{9,8},{10,11... | collective-permute-start | bytes 1572872 | tf_op jit(solution)/shard_map/sum_second/ppermute | solution.py:594
  39.7 2.4 %copy-start.5 = (bf16[1024,512]{1,0:T(8,128)(2,1)S(1)}, bf16[1024,512]{1,0:T(8,128)(2,1)}, u32[]{:S(2)}) copy-start(bf16[1024,512]{1,0:T(8,128)(2,1)} %cot_ref.1) | copy-start | bytes 3145732
  39.7 2.4 %copy-start.9 = (bf16[512,512]{1,0:T(8,128)(2,1)S(1)}, bf16[512,512]{1,0:T(8,128)(2,1)}, u32[]{:S(2)}) copy-start(bf16[512,512]{1,0:T(8,128)(2,1)} %down_ref) | copy-start | bytes 1572868
  39.7 2.4 %copy-start.23 = (bf16[1024,512]{1,0:T(8,128)(2,1)S(1)}, bf16[1024,512]{1,0:T(8,128)(2,1)}, u32[]{:S(2)}) copy-start(bf16[1024,512]{1,0:T(8,128)(2,1)} %get-tuple-element.251.second_ref) | copy-start | bytes 3145732
  39.7 2.4 %copy-start.24 = (bf16[1024,512]{1,0:T(8,128)(2,1)S(1)}, bf16[1024,512]{1,0:T(8,128)(2,1)}, u32[]{:S(2)}) copy-start(bf16[1024,512]{1,0:T(8,128)(2,1)} %get-tuple-element.250.active_ref) | copy-start | bytes 3145732
  39.7 2.5 %copy-start.25 = (bf16[1024,512]{1,0:T(8,128)(2,1)S(1)}, bf16[1024,512]{1,0:T(8,128)(2,1)}, u32[]{:S(2)}) copy-start(bf16[1024,512]{1,0:T(8,128)(2,1)} %get-tuple-element.252.grad_ref) | copy-start | bytes 3145732
  40.6 14.3 %collective-permute-start.10 = (bf16[512,512]{1,0:T(8,128)(2,1)}, bf16[512,512]{1,0:T(8,128)(2,1)}, u32[]{:S(2)}, u32[]{:S(2)}) collective-permute-start(bf16[512,512]{1,0:T(8,128)(2,1)} %add.24.own_ref), channel_id=1, source_target_pairs={{0,2},{1,3},{2,0},{3,1},{4,6},{5,7},{6,4},{7,5},{8,10},{9,11},{10,... | collective-permute-start | bytes 1572872 | tf_op jit(solution)/shard_map/sum_second/ppermute | solution.py:594
  42.1 14.8 %collective-permute-start.12 = (bf16[512,512]{1,0:T(8,128)(2,1)}, bf16[512,512]{1,0:T(8,128)(2,1)}, u32[]{:S(2)}, u32[]{:S(2)}) collective-permute-start(bf16[512,512]{1,0:T(8,128)(2,1)} %add.24.own_ref), channel_id=1, source_target_pairs={{0,1},{1,0},{2,3},{3,2},{4,5},{5,4},{6,7},{7,6},{8,9},{9,8},{10,11... | collective-permute-start | bytes 1572872 | tf_op jit(solution)/shard_map/sum_second/ppermute | solution.py:594
  42.2 4.3 %copy-start.17 = (f32[512]{0:T(512)S(1)}, f32[512]{0:T(512)}, u32[]{:S(2)}) copy-start(f32[512]{0:T(512)} %param.14) | copy-start | bytes 6148
  46.0 2.0 %collective-permute-start.9 = (bf16[512,512]{1,0:T(8,128)(2,1)S(1)}, bf16[512,512]{1,0:T(8,128)(2,1)S(1)}, u32[]{:S(2)}, u32[]{:S(2)}) collective-permute-start(bf16[512,512]{1,0:T(8,128)(2,1)S(1)} %get-tuple-element.256), channel_id=1, source_target_pairs={{0,1},{1,0},{2,3},{3,2},{4,5},{5,4},{6,7},{7,6},{8,9},{9,8},{10,11... | collective-permute-start | bytes 1572872 | tf_op jit(solution)/shard_map/sum_output/ppermute | solution.py:594
  46.4 18.2 %collective-permute-start.15 = (bf16[512,512]{1,0:T(8,128)(2,1)}, bf16[512,512]{1,0:T(8,128)(2,1)}, u32[]{:S(2)}, u32[]{:S(2)}) collective-permute-start(bf16[512,512]{1,0:T(8,128)(2,1)} %get-tuple-element.280), channel_id=1, source_target_pairs={{0,8},{4,12},{8,0},{12,4},{16,24},{20,28},{24,16},{28,20},{1,9},{5... | collective-permute-start | bytes 1572872 | tf_op jit(solution)/shard_map/feed_weights/ppermute | solution.py:594
  48.9 8.8 %copy-start.1 = (f32[4,10,8,128]{3,2,1,0:T(8,128)S(1)}, f32[4,10,8,128]{3,2,1,0:T(8,128)}, u32[]{:S(2)}) copy-start(f32[4,10,8,128]{3,2,1,0:T(8,128)} %copy-done) | copy-start | bytes 491524
  48.9 8.8 %copy-start.3 = (s32[4]{0:T(128)S(1)}, s32[4]{0:T(128)}, u32[]{:S(2)}) copy-start(s32[4]{0:T(128)} %pad_add_fusion.pos_ref) | copy-start | bytes 52
  48.9 8.8 %copy-start.6 = (bf16[1024,512]{1,0:T(8,128)(2,1)S(1)}, bf16[1024,512]{1,0:T(8,128)(2,1)}, u32[]{:S(2)}) copy-start(bf16[1024,512]{1,0:T(8,128)(2,1)} %cot_ref.1) | copy-start | bytes 3145732
  48.9 8.8 %copy-start.14 = (bf16[128,512]{1,0:T(8,128)(2,1)S(1)}, bf16[128,512]{1,0:T(8,128)(2,1)}, u32[]{:S(2)}) copy-start(bf16[128,512]{1,0:T(8,128)(2,1)} %wo_ref) | copy-start | bytes 393220
  48.9 8.8 %copy-start.15 = (f32[512]{0:T(512)S(1)}, f32[512]{0:T(512)}, u32[]{:S(2)}) copy-start(f32[512]{0:T(512)} %param.19) | copy-start | bytes 6148
  48.9 8.8 %copy-start.19 = (f32[1024,512]{1,0:T(8,128)S(1)}, f32[1024,512]{1,0:T(8,128)}, u32[]{:S(2)}) copy-start(f32[1024,512]{1,0:T(8,128)} %get-tuple-element.322.mid_ref) | copy-start | bytes 6291460
  48.9 8.8 %copy-start.27 = (bf16[3,1024,128]{2,1,0:T(8,128)(2,1)S(1)}, bf16[3,1024,128]{2,1,0:T(8,128)(2,1)}, u32[]{:S(2)}) copy-start(bf16[3,1024,128]{2,1,0:T(8,128)(2,1)} %get-tuple-element.275.qkv_ref) | copy-start | bytes 2359300
  54.9 2.8 %collective-permute-start.13 = (bf16[512,512]{1,0:T(8,128)(2,1)}, bf16[512,512]{1,0:T(8,128)(2,1)S(1)}, u32[]{:S(2)}, u32[]{:S(2)}) collective-permute-start(bf16[512,512]{1,0:T(8,128)(2,1)} %collective-permute-done.10.far_ref), channel_id=1, source_target_pairs={{0,1},{1,0},{2,3},{3,2},{4,5},{5,4},{6,7},{7,6},{8,9},{9,8},{10,11... | collective-permute-start | bytes 1572872 | tf_op jit(solution)/shard_map/sum_second/ppermute | solution.py:594
  54.9 12.2 %collective-permute-start.14 = (bf16[512,512]{1,0:T(8,128)(2,1)}, bf16[512,512]{1,0:T(8,128)(2,1)}, u32[]{:S(2)}, u32[]{:S(2)}) collective-permute-start(bf16[512,512]{1,0:T(8,128)(2,1)} %add.25.own_ref), channel_id=1, source_target_pairs={{0,1},{1,0},{2,3},{3,2},{4,5},{5,4},{6,7},{7,6},{8,9},{9,8},{10,11... | collective-permute-start | bytes 1572872 | tf_op jit(solution)/shard_map/sum_output/ppermute | solution.py:594
  55.4 22.4 %collective-permute-start.11 = (bf16[512,512]{1,0:T(8,128)(2,1)}, bf16[512,512]{1,0:T(8,128)(2,1)}, u32[]{:S(2)}, u32[]{:S(2)}) collective-permute-start(bf16[512,512]{1,0:T(8,128)(2,1)} %add.25.own_ref), channel_id=1, source_target_pairs={{0,2},{1,3},{2,0},{3,1},{4,6},{5,7},{6,4},{7,5},{8,10},{9,11},{10,... | collective-permute-start | bytes 1572872 | tf_op jit(solution)/shard_map/sum_output/ppermute | solution.py:594
  64.6 2.5 %copy-start.21 = (bf16[1024,512]{1,0:T(8,128)(2,1)}, bf16[1024,512]{1,0:T(8,128)(2,1)S(1)}, u32[]{:S(2)}) copy-start(bf16[1024,512]{1,0:T(8,128)(2,1)S(1)} %get-tuple-element.346.low_ref) | copy-start | bytes 3145732
  64.6 2.5 %copy-start.28 = (bf16[1024,384]{1,0:T(8,128)(2,1)}, bf16[1024,384]{1,0:T(8,128)(2,1)S(1)}, u32[]{:S(2)}) copy-start(bf16[1024,384]{1,0:T(8,128)(2,1)S(1)} %get-tuple-element.298.gqkv_ref) | copy-start | bytes 2359300
  64.6 2.5 %copy-start.31 = (f32[4,2,8,128]{3,2,1,0:T(8,128)}, f32[4,2,8,128]{3,2,1,0:T(8,128)S(1)}, u32[]{:S(2)}) copy-start(f32[4,2,8,128]{3,2,1,0:T(8,128)S(1)} %get-tuple-element.301.slot_ref) | copy-start | bytes 98308
  64.6 2.4 %copy-start.7 = (bf16[1024,512]{1,0:T(8,128)(2,1)S(1)}, bf16[1024,512]{1,0:T(8,128)(2,1)}, u32[]{:S(2)}) copy-start(bf16[1024,512]{1,0:T(8,128)(2,1)} %tok_ref.3) | copy-start | bytes 3145732
  64.6 2.4 %copy-start.10 = (bf16[3,512,128]{2,1,0:T(8,128)(2,1)S(1)}, bf16[3,512,128]{2,1,0:T(8,128)(2,1)}, u32[]{:S(2)}) copy-start(bf16[3,512,128]{2,1,0:T(8,128)(2,1)} %w_ref.2) | copy-start | bytes 1179652
  69.1 6.3 %collective-permute-start.16 = (bf16[528,512]{1,0:T(8,128)(2,1)S(1)}, bf16[528,512]{1,0:T(8,128)(2,1)S(1)}, u32[]{:S(2)}, u32[]{:S(2)}) collective-permute-start(bf16[528,512]{1,0:T(8,128)(2,1)S(1)} %get-tuple-element.293), channel_id=1, source_target_pairs={{0,1},{1,0},{2,3},{3,2},{4,5},{5,4},{6,7},{7,6},{8,9},{9,8},{10,11... | collective-permute-start | bytes 1622024 | tf_op jit(solution)/shard_map/sum_first/ppermute | solution.py:594
  69.3 8.9 %collective-permute-start.19 = (bf16[256,512]{1,0:T(8,128)(2,1)}, bf16[256,512]{1,0:T(8,128)(2,1)}, u32[]{:S(2)}, u32[]{:S(2)}) collective-permute-start(bf16[256,512]{1,0:T(8,128)(2,1)} %get-tuple-element.308), channel_id=1, source_target_pairs={{0,4},{4,0},{8,12},{12,8},{16,20},{20,16},{24,28},{28,24},{1,5},{5... | collective-permute-start | bytes 786440 | tf_op jit(solution)/shard_map/feed_weights/ppermute | solution.py:594
  74.6 9.0 %collective-permute-start.18 = (bf16[272,512]{1,0:T(8,128)(2,1)}, bf16[272,512]{1,0:T(8,128)(2,1)}, u32[]{:S(2)}, u32[]{:S(2)}) collective-permute-start(bf16[272,512]{1,0:T(8,128)(2,1)} %get-tuple-element.307), channel_id=1, source_target_pairs={{0,8},{4,12},{8,0},{12,4},{16,24},{20,28},{24,16},{28,20},{1,9},{5... | collective-permute-start | bytes 835592 | tf_op jit(solution)/shard_map/rest_weights/ppermute | solution.py:594
  76.4 19.8 %collective-permute-start.20 = (bf16[528,512]{1,0:T(8,128)(2,1)}, bf16[528,512]{1,0:T(8,128)(2,1)}, u32[]{:S(2)}, u32[]{:S(2)}) collective-permute-start(bf16[528,512]{1,0:T(8,128)(2,1)} %pair.1.own_ref.near_ref), channel_id=1, source_target_pairs={{0,2},{1,3},{2,0},{3,1},{4,6},{5,7},{6,4},{7,5},{8,10},{9,11},{10,... | collective-permute-start | bytes 1622024 | tf_op jit(solution)/shard_map/sum_first/ppermute | solution.py:594
  77.8 10.6 %collective-permute-start.17 = (bf16[512,512]{1,0:T(8,128)(2,1)}, bf16[512,512]{1,0:T(8,128)(2,1)}, u32[]{:S(2)}, u32[]{:S(2)}) collective-permute-start(bf16[512,512]{1,0:T(8,128)(2,1)} %collective-permute-done.11.far_ref), channel_id=1, source_target_pairs={{0,1},{1,0},{2,3},{3,2},{4,5},{5,4},{6,7},{7,6},{8,9},{9,8},{10,11... | collective-permute-start | bytes 1572872 | tf_op jit(solution)/shard_map/sum_output/ppermute | solution.py:594
  78.2 7.9 %copy-start.30 = (bf16[272,512]{1,0:T(8,128)(2,1)S(1)}, bf16[272,512]{1,0:T(8,128)(2,1)}, u32[]{:S(2)}) copy-start(bf16[272,512]{1,0:T(8,128)(2,1)} %get-tuple-element.314.a_ref) | copy-start | bytes 835588
  83.6 4.8 %copy-start.4 = (s32[4]{0:T(128)S(1)}, s32[4]{0:T(128)}, u32[]{:S(2)}) copy-start(s32[4]{0:T(128)} %pad_add_fusion.pos_ref) | copy-start | bytes 52
  83.6 4.8 %copy-start.16 = (f32[512]{0:T(512)S(1)}, f32[512]{0:T(512)}, u32[]{:S(2)}) copy-start(f32[512]{0:T(512)} %param.24) | copy-start | bytes 6148
  83.6 4.8 %copy-start.20 = (f32[1024,512]{1,0:T(8,128)S(1)}, f32[1024,512]{1,0:T(8,128)}, u32[]{:S(2)}) copy-start(f32[1024,512]{1,0:T(8,128)} %get-tuple-element.322.mid_ref) | copy-start | bytes 6291460
  83.6 8.7 %collective-permute-start.22 = (bf16[128,512]{1,0:T(8,128)(2,1)}, bf16[128,512]{1,0:T(8,128)(2,1)}, u32[]{:S(2)}, u32[]{:S(2)}) collective-permute-start(bf16[128,512]{1,0:T(8,128)(2,1)} %get-tuple-element.325), channel_id=1, source_target_pairs={{0,16},{4,20},{8,24},{12,28},{16,0},{20,4},{24,8},{28,12},{1,17},{... | collective-permute-start | bytes 393224 | tf_op jit(solution)/shard_map/feed_weights/ppermute | solution.py:594
  87.9 5.5 %collective-permute-start.21 = (bf16[144,512]{1,0:T(8,128)(2,1)}, bf16[144,512]{1,0:T(8,128)(2,1)}, u32[]{:S(2)}, u32[]{:S(2)}) collective-permute-start(bf16[144,512]{1,0:T(8,128)(2,1)} %get-tuple-element.324), channel_id=1, source_target_pairs={{0,4},{4,0},{8,12},{12,8},{16,20},{20,16},{24,28},{28,24},{1,5},{5... | collective-permute-start | bytes 442376 | tf_op jit(solution)/shard_map/rest_weights/ppermute | solution.py:594
  95.0 1.2 collective-permute-start.23
  95.0 6.2 %copy-start.8 = (bf16[1024,512]{1,0:T(8,128)(2,1)S(1)}, bf16[1024,512]{1,0:T(8,128)(2,1)}, u32[]{:S(2)}) copy-start(bf16[1024,512]{1,0:T(8,128)(2,1)} %tok_ref.3) | copy-start | bytes 3145732
  95.0 6.2 %copy-start.18 = (f32[512]{0:T(512)S(1)}, f32[512]{0:T(512)}, u32[]{:S(2)}) copy-start(f32[512]{0:T(512)} %param.14) | copy-start | bytes 6148
  95.0 6.2 %copy-start.22 = (bf16[1024,512]{1,0:T(8,128)(2,1)S(1)}, bf16[1024,512]{1,0:T(8,128)(2,1)}, u32[]{:S(2)}) copy-start(bf16[1024,512]{1,0:T(8,128)(2,1)} %copy-done.21) | copy-start | bytes 3145732
  96.2 5.0 %collective-permute-start.24 = (bf16[528,512]{1,0:T(8,128)(2,1)}, bf16[528,512]{1,0:T(8,128)(2,1)S(1)}, u32[]{:S(2)}, u32[]{:S(2)}) collective-permute-start(bf16[528,512]{1,0:T(8,128)(2,1)} %pair.1.own_ref.near_ref), channel_id=1, source_target_pairs={{0,1},{1,0},{2,3},{3,2},{4,5},{5,4},{6,7},{7,6},{8,9},{9,8},{10,11... | collective-permute-start | bytes 1622024 | tf_op jit(solution)/shard_map/sum_first/ppermute | solution.py:594
  96.3 4.8 %collective-permute-start.25 = (bf16[528,512]{1,0:T(8,128)(2,1)}, bf16[528,512]{1,0:T(8,128)(2,1)S(1)}, u32[]{:S(2)}, u32[]{:S(2)}) collective-permute-start(bf16[528,512]{1,0:T(8,128)(2,1)} %collective-permute-done.20.far_ref), channel_id=1, source_target_pairs={{0,1},{1,0},{2,3},{3,2},{4,5},{5,4},{6,7},{7,6},{8,9},{9,8},{10,11... | collective-permute-start | bytes 1622024 | tf_op jit(solution)/shard_map/sum_first/ppermute | solution.py:594
  96.7 4.4 %collective-permute-start.26 = (f32[8,512]{1,0:T(8,128)S(1)}, f32[8,512]{1,0:T(8,128)S(1)}, u32[]{:S(2)}, u32[]{:S(2)}) collective-permute-start(f32[8,512]{1,0:T(8,128)S(1)} %plus.1.extra_ref), channel_id=1, source_target_pairs={{0,2},{1,3},{2,0},{3,1},{4,6},{5,7},{6,4},{7,5},{8,10},{9,11},{10,... | collective-permute-start | bytes 49160 | tf_op jit(solution)/shard_map/sum_extra/ppermute | solution.py:594
  98.2 10.7 %collective-permute-start.28 = (bf16[128,512]{1,0:T(8,128)(2,1)S(1)}, bf16[128,512]{1,0:T(8,128)(2,1)S(1)}, u32[]{:S(2)}, u32[]{:S(2)}) collective-permute-start(bf16[128,512]{1,0:T(8,128)(2,1)S(1)} %add.26.a_ref), channel_id=1, source_target_pairs={{0,16},{4,20},{8,24},{12,28},{16,0},{20,4},{24,8},{28,12},{1,17},{... | collective-permute-start | bytes 393224 | tf_op jit(solution)/shard_map/feed_weights/ppermute | solution.py:594
  98.7 11.3 %collective-permute-start.27 = (bf16[64,512]{1,0:T(8,128)(2,1)}, bf16[64,512]{1,0:T(8,128)(2,1)}, u32[]{:S(2)}, u32[]{:S(2)}) collective-permute-start(bf16[64,512]{1,0:T(8,128)(2,1)} %get-tuple-element.349), channel_id=1, source_target_pairs={{0,16},{4,20},{8,24},{12,28},{16,0},{20,4},{24,8},{28,12},{1,17},{... | collective-permute-start | bytes 196616 | tf_op jit(solution)/shard_map/rest_weights/ppermute | solution.py:594
  105.4 4.6 %copy-start.32 = (f32[8,512]{1,0:T(8,128)S(1)}, f32[8,512]{1,0:T(8,128)}, u32[]{:S(2)}) copy-start(f32[8,512]{1,0:T(8,128)} %get-tuple-element.358.up_ref) | copy-start | bytes 49156
  111.3 6.0 %collective-permute-start.29 = (bf16[80,512]{1,0:T(8,128)(2,1)S(1)}, bf16[80,512]{1,0:T(8,128)(2,1)S(1)}, u32[]{:S(2)}, u32[]{:S(2)}) collective-permute-start(bf16[80,512]{1,0:T(8,128)(2,1)S(1)} %piece.1.a_ref), channel_id=1, source_target_pairs={{0,16},{4,20},{8,24},{12,28},{16,0},{20,4},{24,8},{28,12},{1,17},{... | collective-permute-start | bytes 245768 | tf_op jit(solution)/shard_map/rest_weights/ppermute | solution.py:594
  111.4 10.3 %collective-permute-start.31 = (bf16[256,512]{1,0:T(8,128)(2,1)}, bf16[256,512]{1,0:T(8,128)(2,1)}, u32[]{:S(2)}, u32[]{:S(2)}) collective-permute-start(bf16[256,512]{1,0:T(8,128)(2,1)} %concat.1.own_ref), channel_id=1, source_target_pairs={{0,8},{4,12},{8,0},{12,4},{16,24},{20,28},{24,16},{28,20},{1,9},{5... | collective-permute-start | bytes 786440 | tf_op jit(solution)/shard_map/feed_weights/ppermute | solution.py:594
  113.4 13.4 %collective-permute-start.33 = (bf16[256,512]{1,0:T(8,128)(2,1)}, bf16[256,512]{1,0:T(8,128)(2,1)}, u32[]{:S(2)}, u32[]{:S(2)}) collective-permute-start(bf16[256,512]{1,0:T(8,128)(2,1)} %concat.1.own_ref), channel_id=1, source_target_pairs={{0,4},{4,0},{8,12},{12,8},{16,20},{20,16},{24,28},{28,24},{1,5},{5... | collective-permute-start | bytes 786440 | tf_op jit(solution)/shard_map/feed_weights/ppermute | solution.py:594
  117.4 7.9 %collective-permute-start.30 = (bf16[144,512]{1,0:T(8,128)(2,1)S(1)}, bf16[144,512]{1,0:T(8,128)(2,1)S(1)}, u32[]{:S(2)}, u32[]{:S(2)}) collective-permute-start(bf16[144,512]{1,0:T(8,128)(2,1)S(1)} %merge.2.a_ref), channel_id=1, source_target_pairs={{0,4},{4,0},{8,12},{12,8},{16,20},{20,16},{24,28},{28,24},{1,5},{5... | collective-permute-start | bytes 442376 | tf_op jit(solution)/shard_map/rest_weights/ppermute | solution.py:594
  121.7 8.5 %collective-permute-start.34 = (bf16[256,512]{1,0:T(8,128)(2,1)}, bf16[256,512]{1,0:T(8,128)(2,1)}, u32[]{:S(2)}, u32[]{:S(2)}) collective-permute-start(bf16[256,512]{1,0:T(8,128)(2,1)} %collective-permute-done.31.two_ref), channel_id=1, source_target_pairs={{0,4},{4,0},{8,12},{12,8},{16,20},{20,16},{24,28},{28,24},{1,5},{5... | collective-permute-start | bytes 786440 | tf_op jit(solution)/shard_map/feed_weights/ppermute | solution.py:594
  126.0 7.0 %collective-permute-start.32 = (bf16[272,512]{1,0:T(8,128)(2,1)}, bf16[272,512]{1,0:T(8,128)(2,1)}, u32[]{:S(2)}, u32[]{:S(2)}) collective-permute-start(bf16[272,512]{1,0:T(8,128)(2,1)} %merge.3.near_ref), channel_id=1, source_target_pairs={{0,8},{4,12},{8,0},{12,4},{16,24},{20,28},{24,16},{28,20},{1,9},{5... | collective-permute-start | bytes 835592 | tf_op jit(solution)/shard_map/rest_weights/ppermute | solution.py:594
  (11 other events, 15.5 us)

commit v6 on v5

--- a/solution.py
+++ b/solution.py
@@ -542,24 +542,41 @@
     out_ref[...] = (mid_ref[...] + e + b_ref[...]).astype(bf16)
 
 
-def feed_unpack_kernel(
-    count, at_ref, own_ref, one_ref, two_ref, both_ref, down_ref, up_ref
-):
-    part = count // 4
-    rows = own_ref.shape[0] // part
-    top = at_ref[0] // part
-    low = at_ref[0] % part
-    for step, out_ref in enumerate((down_ref, up_ref)):
-
-        @pl.when(pl.program_id(0) == step)
-        def _():
-            for k in range(2 * part):
-                slot = top ^ (2 * step + k // part)
-                at = pl.ds(pl.multiple_of(((k % part) ^ low) * rows, rows), rows)
-                x = jnp.where(slot == 0, own_ref[at], one_ref[at])
-                far = jnp.where(slot == 2, two_ref[at], both_ref[at])
-                x = jnp.where(slot < 2, x, far)
-                out_ref[k * rows : (k + 1) * rows] = x.astype(f32)
+def feed_unpack_kernel(pieces, far, at_ref, own_ref, one_ref, *refs):
+    down_ref, up_ref, scratch, sems = refs[-4:]
+    rows = own_ref.shape[0]
+    size = rows // pieces
+    top = at_ref[0] // pieces
+    low = at_ref[0] % pieces
+
+    def copies(ref):
+        return [
+            pltpu.make_async_copy(
+                scratch.at[pl.ds(q * rows, rows)], ref.at[pl.ds(q * rows, rows)], sems.at[q]
+            )
+            for q in range(2)
+        ]
+
+    def fill(ref):
+        out = copies(ref)
+        for q in range(2):
+            for k in range(pieces):
+                at = pl.ds(pl.multiple_of((k ^ low) * size, size), size)
+                x = jnp.where(top % 2 == q, own_ref[at], one_ref[at])
+                scratch[q * rows + k * size : q * rows + (k + 1) * size] = x.astype(f32)
+            out[q].start()
+        for q in range(2):
+            out[q].wait()
+
+    is_down = top // 2 == far
+
+    @pl.when(is_down)
+    def _():
+        fill(down_ref)
+
+    @pl.when(jnp.logical_not(is_down))
+    def _():
+        fill(up_ref)
 
 
 def rest_unpack_kernel(
@@ -924,14 +941,20 @@
             tile_block,
             sds((rows, dim), bf16),
         )
-        feed_unpack = gridded(
-            functools.partial(feed_unpack_kernel, n_dp),
-            "feed_unpack",
-            2,
-            [block((hidden // 2, dim), whole)] * 4,
-            [block((hidden, dim), whole)] * 2,
-            (sds((hidden, dim), f32), sds((hidden, dim), f32)),
-        )
+        def feed_unpack(at, own, one, *held):
+            anywhere = pl.BlockSpec(memory_space=pl.ANY)
+            return pl.pallas_call(
+                functools.partial(feed_unpack_kernel, n_dp // 4, 1 if held else 0),
+                out_shape=(sds((hidden, dim), f32), sds((hidden, dim), f32)),
+                in_specs=[SMEM, VMEM, VMEM] + [anywhere] * len(held),
+                out_specs=(anywhere, anywhere),
+                scratch_shapes=[pltpu.VMEM((hidden, dim), f32), pltpu.SemaphoreType.DMA((2,))],
+                input_output_aliases={3 + k: k for k in range(len(held))},
+                compiler_params=params(20),
+                cost_estimate=cost(),
+                name="feed_unpack",
+            )(at, own, one, *held)
+
         rest_unpack = plain(
             functools.partial(rest_unpack_kernel, n_dp, dim),
             "rest_unpack",
@@ -1081,41 +1104,54 @@
 
         feed_sum.step()
         (out_other,) = wait(out_other)
+        theirs_w, rest = line(
+            rest_weights, first_bit, first, gqkv, grad_low, attended, slot_grad, sums
+        )
+        rest_got = swap(theirs_w, "dp", feed_masks[0], "rest_weights")
+        (out_far,) = wait(out_far)
+        out_other_far = swap(out_far, "mp", 1, "sum_output")
         theirs, mine = line(first_grad, pos, gqkv, slot_grad, sums, w_qkv, tokens)
         got = swap(theirs, "mp", 1, "sum_first")
-        theirs_w, rest = line(
-            rest_weights, first_bit, first, gqkv, grad_low, attended, slot_grad, sums
-        )
-        rest_got = swap(theirs_w, "dp", feed_masks[0], "rest_weights")
+        feed_sum.step()
         total = line(pair, mine, got)
         for m in far_masks[:-1]:
             total = line(pair, total, swap(total, "mp", m, "sum_first"))
         far = swap(total, "mp", last_far, "sum_first")
-        (out_far,) = wait(out_far)
-        out_other_far = swap(out_far, "mp", 1, "sum_output")
-        feed_sum.step()
         theirs_w, rest = line(split_first, bit_of(feed_masks[1]), rest, rest_got)
         rest_got = swap(theirs_w, "dp", feed_masks[1], "rest_weights")
         output = line(
             output_sum, pos, out_total, out_far, out_other, out_other_far, mid, b_down[None]
         )
-        for m in feed_masks[3:]:
-            feed_sum.step()
-        feed_all = line(add_low, feed_sum.mine, feed_sum.got)
-        feed_got = swap(feed_all, "dp", feed_masks[-1], "feed_weights")
         theirs_w, rest, extra = line(split_second, bit_of(feed_masks[2]), rest, rest_got, w_qkv)
         rest_got = swap(theirs_w, "dp", feed_masks[2], "rest_weights")
         extra_got = swap(extra, "mp", 1, "sum_extra")
         for m in feed_masks[3:]:
             theirs_w, rest = line(split_sum, bit_of(m), rest, rest_got)
             rest_got = swap(theirs_w, "dp", m, "rest_weights")
-        for m in far_masks:
-            line.space()
-            extra = line(pl_add, extra, extra_got)
-            extra_got = swap(extra, "mp", m, "sum_extra")
+        for m in feed_masks[3:]:
+            feed_sum.step()
+        feed_all = line(add_low, feed_sum.mine, feed_sum.got)
+        feed_got = swap(feed_all, "dp", feed_masks[-1], "feed_weights")
         (far,) = wait(far)
         other = swap(after(total, far), "mp", 1, "sum_first")
         other_far = swap(far, "mp", 1, "sum_first")
+        for m in far_masks:
+            extra = line(pl_add, extra, extra_got)
+            extra_got = swap(extra, "mp", m, "sum_extra")
+        rest_all = line(
+            piece_of, rest, rest_got, total, far, back_vec, up_vec
+        )
+        rest_got = swap(rest_all, "dp", feed_masks[-1], "rest_weights")
+        feed_next = list(reversed(feed_masks))[1:]
+        rest_next = list(reversed(feed_masks))[1:]
+        for m in feed_next[:-2]:
+            feed_all = line(concat, feed_all, feed_got)
+            feed_got = swap(feed_all, "dp", m, "feed_weights")
+        feed_all = line(concat, feed_all, feed_got)
+        two = swap(feed_all, "dp", feed_masks[0], "feed_weights")
+        one = swap(feed_all, "dp", feed_masks[1], "feed_weights")
+        rest_all = line(merge, rest_all, rest_got)
+        rest_got = swap(rest_all, "dp", rest_next[0], "rest_weights")
         grad_tokens = line(
             last,
             pos,
@@ -1129,30 +1165,15 @@
             grad_low,
             ln1_gain[None],
         )
-        feed_next = list(reversed(feed_masks))[1:]
-        rest_next = list(reversed(feed_masks))[1:]
-        for m in feed_next[:-2]:
-            feed_all = line(concat, feed_all, feed_got)
-            feed_got = swap(feed_all, "dp", m, "feed_weights")
-        feed_all = line(concat, feed_all, feed_got)
-        two = swap(feed_all, "dp", feed_masks[0], "feed_weights")
-        one = swap(feed_all, "dp", feed_masks[1], "feed_weights")
-        rest_all = line(
-            piece_of, rest, rest_got, total, far, back_vec, up_vec
-        )
-        rest_got = swap(rest_all, "dp", feed_masks[-1], "rest_weights")
-        line.space()
-        rest_all = line(merge, rest_all, rest_got)
-        rest_got = swap(rest_all, "dp", rest_next[0], "rest_weights")
         (two,) = wait(two)
         both = swap(two, "dp", feed_masks[1], "feed_weights")
         for m in rest_next[1:]:
             line.space()
             rest_all = line(merge, rest_all, rest_got)
             rest_got = swap(rest_all, "dp", m, "rest_weights")
-        line.space()
+        held = line(feed_unpack, place_of(feed_masks), feed_all, one)
         grad_w_down, grad_w_up = line(
-            feed_unpack, place_of(feed_masks), feed_all, one, two, both
+            feed_unpack, place_of(feed_masks), two, both, *held
         )
         grad_w_qkv, grad_w_out, *vectors = line(
             rest_unpack, place_of(feed_masks), rest_all, rest_got, line.spare

time: 136 us -> 131 us (0.963)
  waiting for transfers between devices: 41 us -> 33.6 us
  Pallas kernels: 57.8 us -> 60 us
    ppermute x35, waiting for transfers between devices: 41 us -> 33.6 us  [swap(): return lax.ppermute(x, axis, [(i, i ^ mask) for i in range(n)])]
    pallas_call x0 -> x2, Pallas kernels: none -> 4.14 us  [feed_unpack(): pl.pallas_call(functools.partial(feed_unpack_kernel, n_dp // 4, 1 if held...]
    pallas_call x13 -> x12, Pallas kernels: 40.4 us -> 36.4 us  [__call__(): result = work(*inputs)]
    pallas_call x6, Pallas kernels: 3.69 us -> 6.9 us  [like(): return plain(kernel, name, specs, (sds(shape, dtype),))(*operands)[0]]
    pallas_call x2, Pallas kernels: 4.11 us -> 2.34 us  [split_sum(): pl.pallas_call(split_kernel, out_shape=(half, half), in_specs=[SMEM, VMEM...]
    unnamed x82 -> x84, local copies, waits for them, and re-layouts: 3.14 us -> 3.12 us
  transfers between devices with their start and end apart: 35 -> 35, of which waited for: 19 -> 16; matrix products, arithmetic and copies ran while one was open for 0% -> 0% of each run, Pallas kernels for 32% -> 36%
where the time goes in v6:
time: 131 us; the launch traced here: 130 us
  Pallas kernels  60 us (46%)
  waiting for transfers between devices  33.6 us (26%)
  starting transfers between devices  31.5 us (24%)
  local copies, waits for them, and re-layouts  3.13 us (2%)
    pallas_call x12, Pallas kernels, __call__(): result = work(*inputs)  36.4 us
    ppermute x35, waiting for transfers between devices, swap(): return lax.ppermute(x, axis, [(i, i ^ mask) for i in range(n)])  33.6 us
    ppermute x35, starting transfers between devices, swap(): return lax.ppermute(x, axis, [(i, i ^ mask) for i in range(n)])  31.5 us
    pallas_call x6, Pallas kernels, like(): return plain(kernel, name, specs, (sds(shape, dtype),))(*operands)[0]  6.9 us
    pallas_call x1, Pallas kernels, per_device(): back(*a)  6.81 us
    pallas_call x2, Pallas kernels, feed_unpack(): pl.pallas_call(functools.partial(feed_unpack_kernel, n_dp // 4, 1 if held...  4.14 us
    pallas_call x3, Pallas kernels, add_parts(): pl.pallas_call(functools.partial(add_kernel, parts), out_shape=(part,) *...  3.42 us
    unnamed x84, local copies, waits for them, and re-layouts  3.12 us
  transfers between devices with their start and end apart: 35, of which 16 were waited for; matrix products, arithmetic and copies ran while one was open for 0% of the time, Pallas kernels for 36%

profile of v6, /device:TPU:0, one launch (start us, length us, event | category | flops | bytes accessed | tf_op | source)
XLA Modules:
  0.0 130.1 jit_solution(1485878664927356303)
XLA Ops:
  0.6 3.0 %collective-permute-start = (bf16[128,512]{1,0:T(8,128)(2,1)}, bf16[128,512]{1,0:T(8,128)(2,1)S(1)}, u32[]{:S(2)}, u32[]{:S(2)}) collective-permute-start(bf16[128,512]{1,0:T(8,128)(2,1)} %wo_ref), channel_id=1, source_target_pairs={{0,2},{1,3},{2,0},{3,1},{4,6},{5,7},{6,4},{7,5},{8,10},{9,11},{10,... | collective-permute-start | bytes 393224 | tf_op jit(solution)/shard_map/gather_w_out/ppermute | solution.py:611
  3.7 3.9 %project.1 = (bf16[1024,512]{1,0:T(8,128)(2,1)}, bf16[3,1024,128]{2,1,0:T(8,128)(2,1)}, f32[10,8,128]{2,1,0:T(8,128)}) custom-call(bf16[1024,512]{1,0:T(8,128)(2,1)} %tok_ref.3, f32[1,512]{1,0:T(1,128)} %bitcast.24, f32[1,512]{1,0:T(1,128)} %bitcast.29, bf16[3,512,128]{2,1,0:T(8,128)(2,1)} %w_ref.2), custom_call_target="tpu_custom_call" | custom-call | flops 115000000512 | bytes 1 | tf_op jit(solution)/shard_map/project/pallas_call | solution.py:635
  7.6 1.6 %collective-permute-start.1 = (f32[1,10,8,128]{3,2,1,0:T(8,128)}, f32[1,10,8,128]{3,2,1,0:T(8,128)S(1)}, u32[]{:S(2)}, u32[]{:S(2)}) collective-permute-start(f32[1,10,8,128]{3,2,1,0:T(8,128)} %bitcast.27), channel_id=1, source_target_pairs={{0,4},{4,0},{8,12},{12,8},{16,20},{20,16},{24,28},{28,24},{1,5},{5... | collective-permute-start | bytes 122888 | tf_op jit(solution)/shard_map/summaries/ppermute | solution.py:611
  9.2 1.1 copy-done.25
  10.8 1.1 collective-permute-done.1
  11.9 1.6 %collective-permute-start.2 = (f32[2,10,8,128]{3,2,1,0:T(8,128)S(1)}, f32[2,10,8,128]{3,2,1,0:T(8,128)S(1)}, u32[]{:S(2)}, u32[]{:S(2)}) collective-permute-start(f32[2,10,8,128]{3,2,1,0:T(8,128)S(1)} %constant_dynamic-update-slice_fusion), channel_id=1, source_target_pairs={{0,8},{4,12},{8,0},{12,4},{16,24},{20,28},{24,16},{28,20},{1,9},{5... | collective-permute-start | bytes 245768 | tf_op jit(solution)/shard_map/summaries/ppermute | solution.py:611
  13.5 0.5 collective-permute-start.4
  14.1 2.3 %collective-permute-done.2 = f32[2,10,8,128]{3,2,1,0:T(8,128)S(1)} collective-permute-done((f32[2,10,8,128]{3,2,1,0:T(8,128)S(1)}, f32[2,10,8,128]{3,2,1,0:T(8,128)S(1)}, u32[]{:S(2)}, u32[]{:S(2)}) %collective-permute-start.2) | collective-permute-done | bytes 81952 | tf_op jit(solution)/shard_map/summaries/ppermute | solution.py:611
  16.5 1.5 %attend.1 = (bf16[8,160,256]{2,1,0:T(8,128)(2,1)S(1)}, bf16[1024,128]{1,0:T(8,128)(2,1)S(1)}) custom-call(s32[1]{0:T(128)} %bitcast.2.place_ref, bf16[3,1024,128]{2,1,0:T(8,128)(2,1)S(1)} %copy-done.25, f32[8,128,256]{2,1,0:T(8,128)S(1)} %get-tuple-element.221.exp_ref, f32[8,2,256]{2,1,0:T(2,128)S(1)} %get-tuple-element.222.stat_ref, ...), custom_call_target="tpu_custom_call" | custom-call | flops 115000000512 | bytes 1 | tf_op jit(solution)/shard_map/attend/pallas_call | solution.py:635
  18.0 1.5 %collective-permute-start.6 = (bf16[1024,128]{1,0:T(8,128)(2,1)S(1)}, bf16[1024,128]{1,0:T(8,128)(2,1)S(1)}, u32[]{:S(2)}, u32[]{:S(2)}) collective-permute-start(bf16[1024,128]{1,0:T(8,128)(2,1)S(1)} %get-tuple-element.294.refs_0_.att_ref), channel_id=1, source_target_pairs={{0,2},{1,3},{2,0},{3,1},{4,6},{5,7},{6,4},{7,5},{8,10},{9,11},{10,... | collective-permute-start | bytes 786440 | tf_op jit(solution)/shard_map/gather_attended/ppermute | solution.py:611
  19.6 5.7 %collective-permute-done.6.refs_2_ = bf16[1024,128]{1,0:T(8,128)(2,1)S(1)} collective-permute-done((bf16[1024,128]{1,0:T(8,128)(2,1)S(1)}, bf16[1024,128]{1,0:T(8,128)(2,1)S(1)}, u32[]{:S(2)}, u32[]{:S(2)}) %collective-permute-start.6) | collective-permute-done | bytes 262176 | tf_op jit(solution)/shard_map/gather_attended/ppermute | solution.py:611
  25.2 0.6 pad_add_fusion.pos_ref
  25.8 0.9 collective-permute-done.7.refs_3_
  26.8 0.7 copy-done.37
  27.5 8.9 %feed.1 = (f32[1024,512]{1,0:T(8,128)}, bf16[1024,512]{1,0:T(8,128)(2,1)}, bf16[1024,512]{1,0:T(8,128)(2,1)}, bf16[1024,512]{1,0:T(8,128)(2,1)}, bf16[512,512]{1...) custom-call(s32[4]{0:T(128)} %pad_add_fusion.pos_ref, bf16[1024,512]{1,0:T(8,128)(2,1)} %tok_ref.3, ...), custom_call_target="tpu_custom_call" | custom-call | flops 115000000512 | bytes 1 | tf_op jit(solution)/shard_map/feed/pallas_call | solution.py:635
  36.6 2.0 %collective-permute-done.8.b_ref = bf16[512,512]{1,0:T(8,128)(2,1)S(1)} collective-permute-done((bf16[512,512]{1,0:T(8,128)(2,1)}, bf16[512,512]{1,0:T(8,128)(2,1)S(1)}, u32[]{:S(2)}, u32[]{:S(2)}) %collective-permute-start.8) | collective-permute-done | bytes 524320 | tf_op jit(solution)/shard_map/sum_second/ppermute | solution.py:611
  38.6 1.0 copy-done.29
  39.7 0.9 add.26.own_ref
  40.6 1.5 %collective-permute-start.10 = (bf16[512,512]{1,0:T(8,128)(2,1)}, bf16[512,512]{1,0:T(8,128)(2,1)}, u32[]{:S(2)}, u32[]{:S(2)}) collective-permute-start(bf16[512,512]{1,0:T(8,128)(2,1)} %add.26.own_ref), channel_id=1, source_target_pairs={{0,2},{1,3},{2,0},{3,1},{4,6},{5,7},{6,4},{7,5},{8,10},{9,11},{10,... | collective-permute-start | bytes 1572872 | tf_op jit(solution)/shard_map/sum_second/ppermute | solution.py:611
  42.2 3.8 %weights.1 = (bf16[512,512]{1,0:T(8,128)(2,1)S(1)}, bf16[512,512]{1,0:T(8,128)(2,1)S(1)}, bf16[512,512]{1,0:T(8,128)(2,1)}, bf16[512,512]{1,0:T(8,128)(2,1)S(1)}) custom-call(s32[4]{0:T(128)S(1)} %copy-done.3, bf16[1024,512]{1,0:T(8,128)(2,1)S(1)} %copy-done.23, bf16[1024,512]{1,0:T(8,128)(2,1)S(1)} %copy-done.22, bf16[1024,512]{1,0:T(8,128)(2,1)S(1)} %copy-done.24, ...), custom_call_target="tpu_custom_call" | custom-call | flops 115000000512 | bytes 1 | tf_op jit(solution)/shard_map/weights/pallas_call | solution.py:635
  46.5 0.8 collective-permute-start.15
  47.3 0.7 collective-permute-done.9.b_ref
  48.0 0.9 add.27.own_ref
  48.9 5.9 %collective-permute-done.10.far_ref = bf16[512,512]{1,0:T(8,128)(2,1)} collective-permute-done((bf16[512,512]{1,0:T(8,128)(2,1)}, bf16[512,512]{1,0:T(8,128)(2,1)}, u32[]{:S(2)}, u32[]{:S(2)}) %collective-permute-start.10) | collective-permute-done | bytes 524320 | tf_op jit(solution)/shard_map/sum_second/ppermute | solution.py:611
  54.9 0.5 collective-permute-start.14
  55.4 1.5 %collective-permute-start.11 = (bf16[512,512]{1,0:T(8,128)(2,1)}, bf16[512,512]{1,0:T(8,128)(2,1)}, u32[]{:S(2)}, u32[]{:S(2)}) collective-permute-start(bf16[512,512]{1,0:T(8,128)(2,1)} %add.27.own_ref), channel_id=1, source_target_pairs={{0,2},{1,3},{2,0},{3,1},{4,6},{5,7},{6,4},{7,5},{8,10},{9,11},{10,... | collective-permute-start | bytes 1572872 | tf_op jit(solution)/shard_map/sum_output/ppermute | solution.py:611
  56.9 0.9 collective-permute-done.13.other_far_ref
  57.8 6.8 %back.1 = (bf16[1024,512]{1,0:T(8,128)(2,1)S(1)}, bf16[1024,384]{1,0:T(8,128)(2,1)S(1)}, f32[4,2,8,128]{3,2,1,0:T(8,128)S(1)}, f32[32,512]{1,0:T(8,128)S(1)}) custom-call(s32[4]{0:T(128)S(1)} %copy-done.4, bf16[512,512]{1,0:T(8,128)(2,1)} %add.26.own_ref, bf16[512,512]{1,0:T(8,128)(2,1)} %collective-permute-done.10.far_ref, ...), custom_call_target="tpu_custom_call" | custom-call | flops 115000000512 | bytes 1 | tf_op jit(solution)/shard_map/back/pallas_call | solution.py:1090
  64.6 1.6 %split.2 = (bf16[256,512]{1,0:T(8,128)(2,1)S(1)}, bf16[256,512]{1,0:T(8,128)(2,1)S(1)}) custom-call(s32[1]{0:T(128)} %bitcast.11.bit_ref, bf16[512,512]{1,0:T(8,128)(2,1)S(1)} %get-tuple-element.286.a_ref, bf16[512,512]{1,0:T(8,128)(2,1)} %collective-permute-done.15.b_ref), custom_call_target="tpu_custom_call" | custom-call | flops 115000000512 | bytes 1 | tf_op jit(solution)/shard_map/split/pallas_call | solution.py:674
  66.4 3.9 %rest_weights.1 = (bf16[272,512]{1,0:T(8,128)(2,1)}, bf16[272,512]{1,0:T(8,128)(2,1)}) custom-call(s32[1]{0:T(128)} %bitcast.3.bit_ref, bf16[1024,512]{1,0:T(8,128)(2,1)} %get-tuple-element.291.first_ref, bf16[1024,384]{1,0:T(8,128)(2,1)} %copy-done.27, bf16[1024,512]{1,0:T(8,128)(2,1)} %copy-done.20, bf16[1024,128]{1,0:T(8,128)(2,1)} %copy-done.11, ...), custom_call_target="tpu_custom_call" | custom-call | flops 115000000512 | bytes 1 | tf_op jit(solution)/shard_map/rest_weights/pallas_call | solution.py:635
  70.4 1.5 %collective-permute-start.19 = (bf16[256,512]{1,0:T(8,128)(2,1)S(1)}, bf16[256,512]{1,0:T(8,128)(2,1)S(1)}, u32[]{:S(2)}, u32[]{:S(2)}) collective-permute-start(bf16[256,512]{1,0:T(8,128)(2,1)S(1)} %get-tuple-element.308), channel_id=1, source_target_pairs={{0,4},{4,0},{8,12},{12,8},{16,20},{20,16},{24,28},{28,24},{1,5},{5... | collective-permute-start | bytes 786440 | tf_op jit(solution)/shard_map/feed_weights/ppermute | solution.py:611
  72.0 2.0 %first.1 = (bf16[528,512]{1,0:T(8,128)(2,1)S(1)}, bf16[528,512]{1,0:T(8,128)(2,1)S(1)}) custom-call(s32[4]{0:T(128)S(1)} %copy-done.5, bf16[1024,384]{1,0:T(8,128)(2,1)S(1)} %copy-done.28, f32[4,2,8,128]{3,2,1,0:T(8,128)S(1)} %copy-done.32, f32[4,10,8,128]{3,2,1,0:T(8,128)S(1)} %copy-done.2, bf16[3,512,128]{2,1,0:T(8,128)(2,1)S(1)} %copy-done.10, ...), custom_call_target="tpu_custom_call" | custom-call | flops 115000000512 | bytes 1 | tf_op jit(solution)/shard_map/first/pallas_call | solution.py:635
  74.2 0.8 collective-permute-start.17
  75.0 4.0 %collective-permute-done.19.b_ref = bf16[256,512]{1,0:T(8,128)(2,1)S(1)} collective-permute-done((bf16[256,512]{1,0:T(8,128)(2,1)S(1)}, bf16[256,512]{1,0:T(8,128)(2,1)S(1)}, u32[]{:S(2)}, u32[]{:S(2)}) %collective-permute-start.19) | collective-permute-done | bytes 262176 | tf_op jit(solution)/shard_map/feed_weights/ppermute | solution.py:611
  79.0 0.7 split.3
  79.7 2.6 %collective-permute-start.21 = (bf16[128,512]{1,0:T(8,128)(2,1)}, bf16[128,512]{1,0:T(8,128)(2,1)}, u32[]{:S(2)}, u32[]{:S(2)}) collective-permute-start(bf16[128,512]{1,0:T(8,128)(2,1)} %get-tuple-element.326), channel_id=1, source_target_pairs={{0,16},{4,20},{8,24},{12,28},{16,0},{20,4},{24,8},{28,12},{1,17},{... | collective-permute-start | bytes 393224 | tf_op jit(solution)/shard_map/feed_weights/ppermute | solution.py:611
  82.3 0.9 pair.1.near_ref.own_ref
  83.3 1.5 %collective-permute-start.20 = (bf16[528,512]{1,0:T(8,128)(2,1)}, bf16[528,512]{1,0:T(8,128)(2,1)}, u32[]{:S(2)}, u32[]{:S(2)}) collective-permute-start(bf16[528,512]{1,0:T(8,128)(2,1)} %pair.1.near_ref.own_ref), channel_id=1, source_target_pairs={{0,2},{1,3},{2,0},{3,1},{4,6},{5,7},{6,4},{7,5},{8,10},{9,11},{10,... | collective-permute-start | bytes 1622024 | tf_op jit(solution)/shard_map/sum_first/ppermute | solution.py:611
  84.7 0.7 collective-permute-done.17.b_ref
  85.5 1.1 split_first.1
  86.5 0.8 collective-permute-start.22
  87.4 3.4 %output.1 = bf16[1024,512]{1,0:T(8,128)(2,1)} custom-call(s32[4]{0:T(128)S(1)} %copy-done.5, bf16[512,512]{1,0:T(8,128)(2,1)} %add.27.own_ref, bf16[512,512]{1,0:T(8,128)(2,1)} %collective-permute-done.11.far_ref, bf16[512,512]{1,0:T(8,128)(2,1)} %collective-permute-done.14.other_ref, bf16[512,512]{1,0:T(8,128)(2,1)} %collective-permute-done.16.other_far_ref, ...), custom_call_target="tpu_custom_call" | custom-call | flops 115000000512 | bytes 1 | tf_op jit(solution)/shard_map/output/pallas_call | solution.py:635
  90.8 0.9 collective-permute-done.22.b_ref
  91.7 0.7 split_second.1
  92.5 1.1 collective-permute-start.27
  93.5 1.6 %add.28.a_ref = bf16[128,512]{1,0:T(8,128)(2,1)} custom-call(bf16[128,512]{1,0:T(8,128)(2,1)S(1)} %get-tuple-element.333.a_ref, bf16[128,512]{1,0:T(8,128)(2,1)} %collective-permute-done.21.b_ref), custom_call_target="tpu_custom_call" | custom-call | flops 115000000512 | bytes 1 | tf_op jit(solution)/shard_map/add/pallas_call | solution.py:647
  95.1 1.9 %collective-permute-start.29 = (bf16[128,512]{1,0:T(8,128)(2,1)}, bf16[128,512]{1,0:T(8,128)(2,1)}, u32[]{:S(2)}, u32[]{:S(2)}) collective-permute-start(bf16[128,512]{1,0:T(8,128)(2,1)} %add.28.a_ref), channel_id=1, source_target_pairs={{0,16},{4,20},{8,24},{12,28},{16,0},{20,4},{24,8},{28,12},{1,17},{... | collective-permute-start | bytes 393224 | tf_op jit(solution)/shard_map/feed_weights/ppermute | solution.py:611
  97.2 0.6 plus.1.extra_ref
  97.8 1.5 %collective-permute-start.26 = (f32[8,512]{1,0:T(8,128)}, f32[8,512]{1,0:T(8,128)}, u32[]{:S(2)}, u32[]{:S(2)}) collective-permute-start(f32[8,512]{1,0:T(8,128)} %plus.1.extra_ref), channel_id=1, source_target_pairs={{0,2},{1,3},{2,0},{3,1},{4,6},{5,7},{6,4},{7,5},{8,10},{9,11},{10,... | collective-permute-start | bytes 49160 | tf_op jit(solution)/shard_map/sum_extra/ppermute | solution.py:611
  99.2 1.3 piece.1.a_ref
  100.5 1.0 collective-permute-start.28
  101.5 5.4 %collective-permute-done.29.b_ref = bf16[128,512]{1,0:T(8,128)(2,1)} collective-permute-done((bf16[128,512]{1,0:T(8,128)(2,1)}, bf16[128,512]{1,0:T(8,128)(2,1)}, u32[]{:S(2)}, u32[]{:S(2)}) %collective-permute-start.29) | collective-permute-done | bytes 131104 | tf_op jit(solution)/shard_map/feed_weights/ppermute | solution.py:611
  106.9 1.7 %concat.1.own_ref = bf16[256,512]{1,0:T(8,128)(2,1)} custom-call(bf16[128,512]{1,0:T(8,128)(2,1)} %add.28.a_ref, bf16[128,512]{1,0:T(8,128)(2,1)} %collective-permute-done.29.b_ref), custom_call_target="tpu_custom_call" | custom-call | flops 115000000512 | bytes 1 | tf_op jit(solution)/shard_map/concat/pallas_call | solution.py:970
  108.7 0.7 merge.2.a_ref
  109.4 1.9 %collective-permute-start.30 = (bf16[144,512]{1,0:T(8,128)(2,1)}, bf16[144,512]{1,0:T(8,128)(2,1)}, u32[]{:S(2)}, u32[]{:S(2)}) collective-permute-start(bf16[144,512]{1,0:T(8,128)(2,1)} %merge.2.a_ref), channel_id=1, source_target_pairs={{0,4},{4,0},{8,12},{12,8},{16,20},{20,16},{24,28},{28,24},{1,5},{5... | collective-permute-start | bytes 442376 | tf_op jit(solution)/shard_map/rest_weights/ppermute | solution.py:611
  111.4 4.5 %last.1 = bf16[1024,512]{1,0:T(8,128)(2,1)} custom-call(s32[4]{0:T(128)S(1)} %copy-done.5, bf16[528,512]{1,0:T(8,128)(2,1)} %pair.1.near_ref.own_ref, bf16[528,512]{1,0:T(8,128)(2,1)} %collective-permute-done.20.far_ref, bf16[528,512]{1,0:T(8,128)(2,1)S(1)} %collective-permute-done.23.other_ref, bf16[528,512]{1,0:T(8,128)(2,1)} %collective-permute-done.24.other_far_ref, ...), custom_call_target="tpu_custom_call" | custom-call | flops 115000000512 | bytes 1 | tf_op jit(solution)/shard_map/last/pallas_call | solution.py:635
  115.9 1.4 %collective-permute-start.33 = (bf16[256,512]{1,0:T(8,128)(2,1)}, bf16[256,512]{1,0:T(8,128)(2,1)}, u32[]{:S(2)}, u32[]{:S(2)}) collective-permute-start(bf16[256,512]{1,0:T(8,128)(2,1)} %collective-permute-done.31.own_ref), channel_id=1, source_target_pairs={{0,4},{4,0},{8,12},{12,8},{16,20},{20,16},{24,28},{28,24},{1,5},{5... | collective-permute-start | bytes 786440 | tf_op jit(solution)/shard_map/feed_weights/ppermute | solution.py:611
  117.3 1.2 collective-permute-done.30.b_ref
  118.5 1.7 %merge.3.near_ref = bf16[272,512]{1,0:T(8,128)(2,1)} custom-call(bf16[144,512]{1,0:T(8,128)(2,1)} %merge.2.a_ref, bf16[144,512]{1,0:T(8,128)(2,1)} %collective-permute-done.30.b_ref), custom_call_target="tpu_custom_call" | custom-call | flops 115000000512 | bytes 1 | tf_op jit(solution)/shard_map/merge/pallas_call | solution.py:970
  120.2 2.0 %collective-permute-start.32 = (bf16[272,512]{1,0:T(8,128)(2,1)}, bf16[272,512]{1,0:T(8,128)(2,1)}, u32[]{:S(2)}, u32[]{:S(2)}) collective-permute-start(bf16[272,512]{1,0:T(8,128)(2,1)} %merge.3.near_ref), channel_id=1, source_target_pairs={{0,8},{4,12},{8,0},{12,4},{16,24},{20,28},{24,16},{28,20},{1,9},{5... | collective-permute-start | bytes 835592 | tf_op jit(solution)/shard_map/rest_weights/ppermute | solution.py:611
  122.2 2.1 %feed_unpack.2 = (f32[512,512]{1,0:T(8,128)}, f32[512,512]{1,0:T(8,128)}) custom-call(s32[1]{0:T(128)S(6)} %add.19.at_ref, bf16[256,512]{1,0:T(8,128)(2,1)} %concat.1.own_ref, bf16[256,512]{1,0:T(8,128)(2,1)} %collective-permute-done.34.one_ref), custom_call_target="tpu_custom_call" | custom-call | flops 115000000512 | bytes 1 | tf_op jit(solution)/shard_map/feed_unpack/pallas_call | solution.py:946
  124.6 2.1 %feed_unpack.3 = (f32[512,512]{1,0:T(8,128)}, f32[512,512]{1,0:T(8,128)}) custom-call(s32[1]{0:T(128)S(6)} %add.19.at_ref, bf16[256,512]{1,0:T(8,128)(2,1)} %collective-permute-done.31.own_ref, bf16[256,512]{1,0:T(8,128)(2,1)} %collective-permute-done.33.one_ref, ...), custom_call_target="tpu_custom_call", output_to_operand_aliasing={{0}: (3, {}), {1}: (4, {})} | custom-call | flops 115000000512 | bytes 1 | tf_op jit(solution)/shard_map/feed_unpack/pallas_call | solution.py:946
  126.7 1.3 collective-permute-done.32.far_ref
  128.0 2.1 %rest_unpack.1 = (f32[3,512,128]{2,1,0:T(8,128)}, f32[128,512]{1,0:T(8,128)}, f32[1,512]{1,0:T(1,128)}, f32[1,512]{1,0:T(1,128)}, f32[1,512]{1,0:T(1,128)}, /*in...) custom-call(s32[1]{0:T(128)S(6)} %add.19.at_ref, bf16[272,512]{1,0:T(8,128)(2,1)} %merge.3.near_ref, ...), custom_call_target="tpu_custom_call" | custom-call | flops 115000000512 | bytes 1 | tf_op jit(solution)/shard_map/rest_unpack/pallas_call | solution.py:635
  (122 shorter events, 2.4 us)
Async XLA Ops:
  0.6 6.9 %collective-permute-start = (bf16[128,512]{1,0:T(8,128)(2,1)}, bf16[128,512]{1,0:T(8,128)(2,1)S(1)}, u32[]{:S(2)}, u32[]{:S(2)}) collective-permute-start(bf16[128,512]{1,0:T(8,128)(2,1)} %wo_ref), channel_id=1, source_target_pairs={{0,2},{1,3},{2,0},{3,1},{4,6},{5,7},{6,4},{7,5},{8,10},{9,11},{10,... | collective-permute-start | bytes 393224 | tf_op jit(solution)/shard_map/gather_w_out/ppermute | solution.py:611
  7.6 6.0 %copy-start.38 = (bf16[128,512]{1,0:T(8,128)(2,1)}, bf16[128,512]{1,0:T(8,128)(2,1)S(1)}, u32[]{:S(2)}) copy-start(bf16[128,512]{1,0:T(8,128)(2,1)S(1)} %collective-permute-done.refs_6_) | copy-start | bytes 393220
  7.6 5.9 %copy-start.12 = (bf16[128,512]{1,0:T(8,128)(2,1)S(1)}, bf16[128,512]{1,0:T(8,128)(2,1)}, u32[]{:S(2)}) copy-start(bf16[128,512]{1,0:T(8,128)(2,1)} %wo_ref) | copy-start | bytes 393220
  7.6 4.3 %collective-permute-start.1 = (f32[1,10,8,128]{3,2,1,0:T(8,128)}, f32[1,10,8,128]{3,2,1,0:T(8,128)S(1)}, u32[]{:S(2)}, u32[]{:S(2)}) collective-permute-start(f32[1,10,8,128]{3,2,1,0:T(8,128)} %bitcast.27), channel_id=1, source_target_pairs={{0,4},{4,0},{8,12},{12,8},{16,20},{20,16},{24,28},{28,24},{1,5},{5... | collective-permute-start | bytes 122888 | tf_op jit(solution)/shard_map/summaries/ppermute | solution.py:611
  11.9 4.5 %collective-permute-start.2 = (f32[2,10,8,128]{3,2,1,0:T(8,128)S(1)}, f32[2,10,8,128]{3,2,1,0:T(8,128)S(1)}, u32[]{:S(2)}, u32[]{:S(2)}) collective-permute-start(f32[2,10,8,128]{3,2,1,0:T(8,128)S(1)} %constant_dynamic-update-slice_fusion), channel_id=1, source_target_pairs={{0,8},{4,12},{8,0},{12,4},{16,24},{20,28},{24,16},{28,20},{1,9},{5... | collective-permute-start | bytes 245768 | tf_op jit(solution)/shard_map/summaries/ppermute | solution.py:611
  13.5 2.9 %collective-permute-start.3 = (bf16[128,512]{1,0:T(8,128)(2,1)S(1)}, bf16[128,512]{1,0:T(8,128)(2,1)S(1)}, u32[]{:S(2)}, u32[]{:S(2)}) collective-permute-start(bf16[128,512]{1,0:T(8,128)(2,1)S(1)} %copy-done.12), channel_id=1, source_target_pairs={{0,1},{1,0},{2,3},{3,2},{4,5},{5,4},{6,7},{7,6},{8,9},{9,8},{10,11... | collective-permute-start | bytes 393224 | tf_op jit(solution)/shard_map/gather_w_out/ppermute | solution.py:611
  13.5 2.9 %collective-permute-start.4 = (bf16[128,512]{1,0:T(8,128)(2,1)S(1)}, bf16[128,512]{1,0:T(8,128)(2,1)S(1)}, u32[]{:S(2)}, u32[]{:S(2)}) collective-permute-start(bf16[128,512]{1,0:T(8,128)(2,1)S(1)} %collective-permute-done.refs_6_), channel_id=1, source_target_pairs={{0,1},{1,0},{2,3},{3,2},{4,5},{5,4},{6,7},{7,6},{8,9},{9,8},{10,11... | collective-permute-start | bytes 393224 | tf_op jit(solution)/shard_map/gather_w_out/ppermute | solution.py:611
  18.0 8.8 %copy-start.11 = (bf16[1024,128]{1,0:T(8,128)(2,1)}, bf16[1024,128]{1,0:T(8,128)(2,1)S(1)}, u32[]{:S(2)}) copy-start(bf16[1024,128]{1,0:T(8,128)(2,1)S(1)} %get-tuple-element.294.refs_0_.att_ref) | copy-start | bytes 786436
  18.0 7.2 %collective-permute-start.6 = (bf16[1024,128]{1,0:T(8,128)(2,1)S(1)}, bf16[1024,128]{1,0:T(8,128)(2,1)S(1)}, u32[]{:S(2)}, u32[]{:S(2)}) collective-permute-start(bf16[1024,128]{1,0:T(8,128)(2,1)S(1)} %get-tuple-element.294.refs_0_.att_ref), channel_id=1, source_target_pairs={{0,2},{1,3},{2,0},{3,1},{4,6},{5,7},{6,4},{7,5},{8,10},{9,11},{10,... | collective-permute-start | bytes 786440 | tf_op jit(solution)/shard_map/gather_attended/ppermute | solution.py:611
  19.6 6.3 %collective-permute-start.5 = (bf16[1024,128]{1,0:T(8,128)(2,1)S(1)}, bf16[1024,128]{1,0:T(8,128)(2,1)S(1)}, u32[]{:S(2)}, u32[]{:S(2)}) collective-permute-start(bf16[1024,128]{1,0:T(8,128)(2,1)S(1)} %get-tuple-element.294.refs_0_.att_ref), channel_id=1, source_target_pairs={{0,1},{1,0},{2,3},{3,2},{4,5},{5,4},{6,7},{7,6},{8,9},{9,8},{10,11... | collective-permute-start | bytes 786440 | tf_op jit(solution)/shard_map/gather_attended/ppermute | solution.py:611
  25.2 1.5 %collective-permute-start.7 = (bf16[1024,128]{1,0:T(8,128)(2,1)S(1)}, bf16[1024,128]{1,0:T(8,128)(2,1)S(1)}, u32[]{:S(2)}, u32[]{:S(2)}) collective-permute-start(bf16[1024,128]{1,0:T(8,128)(2,1)S(1)} %collective-permute-done.6.refs_2_), channel_id=1, source_target_pairs={{0,1},{1,0},{2,3},{3,2},{4,5},{5,4},{6,7},{7,6},{8,9},{9,8},{10,11... | collective-permute-start | bytes 786440 | tf_op jit(solution)/shard_map/gather_attended/ppermute | solution.py:611
  36.4 2.2 %collective-permute-start.8 = (bf16[512,512]{1,0:T(8,128)(2,1)}, bf16[512,512]{1,0:T(8,128)(2,1)S(1)}, u32[]{:S(2)}, u32[]{:S(2)}) collective-permute-start(bf16[512,512]{1,0:T(8,128)(2,1)} %get-tuple-element.247), channel_id=1, source_target_pairs={{0,1},{1,0},{2,3},{3,2},{4,5},{5,4},{6,7},{7,6},{8,9},{9,8},{10,11... | collective-permute-start | bytes 1572872 | tf_op jit(solution)/shard_map/sum_second/ppermute | solution.py:611
  39.6 2.4 %copy-start.3 = (s32[4]{0:T(128)S(1)}, s32[4]{0:T(128)}, u32[]{:S(2)}) copy-start(s32[4]{0:T(128)} %pad_add_fusion.pos_ref) | copy-start | bytes 52
  39.7 2.4 %copy-start.6 = (bf16[1024,512]{1,0:T(8,128)(2,1)S(1)}, bf16[1024,512]{1,0:T(8,128)(2,1)}, u32[]{:S(2)}) copy-start(bf16[1024,512]{1,0:T(8,128)(2,1)} %cot_ref.1) | copy-start | bytes 3145732
  39.7 2.4 %copy-start.9 = (bf16[512,512]{1,0:T(8,128)(2,1)S(1)}, bf16[512,512]{1,0:T(8,128)(2,1)}, u32[]{:S(2)}) copy-start(bf16[512,512]{1,0:T(8,128)(2,1)} %down_ref) | copy-start | bytes 1572868
  39.7 2.4 %copy-start.22 = (bf16[1024,512]{1,0:T(8,128)(2,1)S(1)}, bf16[1024,512]{1,0:T(8,128)(2,1)}, u32[]{:S(2)}) copy-start(bf16[1024,512]{1,0:T(8,128)(2,1)} %get-tuple-element.253.second_ref) | copy-start | bytes 3145732
  39.7 2.4 %copy-start.23 = (bf16[1024,512]{1,0:T(8,128)(2,1)S(1)}, bf16[1024,512]{1,0:T(8,128)(2,1)}, u32[]{:S(2)}) copy-start(bf16[1024,512]{1,0:T(8,128)(2,1)} %get-tuple-element.252.active_ref) | copy-start | bytes 3145732
  39.7 2.5 %copy-start.24 = (bf16[1024,512]{1,0:T(8,128)(2,1)S(1)}, bf16[1024,512]{1,0:T(8,128)(2,1)}, u32[]{:S(2)}) copy-start(bf16[1024,512]{1,0:T(8,128)(2,1)} %get-tuple-element.254.grad_ref) | copy-start | bytes 3145732
  40.6 14.3 %collective-permute-start.10 = (bf16[512,512]{1,0:T(8,128)(2,1)}, bf16[512,512]{1,0:T(8,128)(2,1)}, u32[]{:S(2)}, u32[]{:S(2)}) collective-permute-start(bf16[512,512]{1,0:T(8,128)(2,1)} %add.26.own_ref), channel_id=1, source_target_pairs={{0,2},{1,3},{2,0},{3,1},{4,6},{5,7},{6,4},{7,5},{8,10},{9,11},{10,... | collective-permute-start | bytes 1572872 | tf_op jit(solution)/shard_map/sum_second/ppermute | solution.py:611
  42.1 14.8 %collective-permute-start.12 = (bf16[512,512]{1,0:T(8,128)(2,1)}, bf16[512,512]{1,0:T(8,128)(2,1)}, u32[]{:S(2)}, u32[]{:S(2)}) collective-permute-start(bf16[512,512]{1,0:T(8,128)(2,1)} %add.26.own_ref), channel_id=1, source_target_pairs={{0,1},{1,0},{2,3},{3,2},{4,5},{5,4},{6,7},{7,6},{8,9},{9,8},{10,11... | collective-permute-start | bytes 1572872 | tf_op jit(solution)/shard_map/sum_second/ppermute | solution.py:611
  42.2 4.3 %copy-start.16 = (f32[512]{0:T(512)S(1)}, f32[512]{0:T(512)}, u32[]{:S(2)}) copy-start(f32[512]{0:T(512)} %param.14) | copy-start | bytes 6148
  46.0 2.0 %collective-permute-start.9 = (bf16[512,512]{1,0:T(8,128)(2,1)S(1)}, bf16[512,512]{1,0:T(8,128)(2,1)S(1)}, u32[]{:S(2)}, u32[]{:S(2)}) collective-permute-start(bf16[512,512]{1,0:T(8,128)(2,1)S(1)} %get-tuple-element.258), channel_id=1, source_target_pairs={{0,1},{1,0},{2,3},{3,2},{4,5},{5,4},{6,7},{7,6},{8,9},{9,8},{10,11... | collective-permute-start | bytes 1572872 | tf_op jit(solution)/shard_map/sum_output/ppermute | solution.py:611
  46.5 18.2 %collective-permute-start.15 = (bf16[512,512]{1,0:T(8,128)(2,1)}, bf16[512,512]{1,0:T(8,128)(2,1)}, u32[]{:S(2)}, u32[]{:S(2)}) collective-permute-start(bf16[512,512]{1,0:T(8,128)(2,1)} %get-tuple-element.284), channel_id=1, source_target_pairs={{0,8},{4,12},{8,0},{12,4},{16,24},{20,28},{24,16},{28,20},{1,9},{5... | collective-permute-start | bytes 1572872 | tf_op jit(solution)/shard_map/feed_weights/ppermute | solution.py:611
  48.9 8.8 %copy-start.1 = (f32[4,10,8,128]{3,2,1,0:T(8,128)S(1)}, f32[4,10,8,128]{3,2,1,0:T(8,128)}, u32[]{:S(2)}) copy-start(f32[4,10,8,128]{3,2,1,0:T(8,128)} %copy-done) | copy-start | bytes 491524
  48.9 8.8 %copy-start.4 = (s32[4]{0:T(128)S(1)}, s32[4]{0:T(128)}, u32[]{:S(2)}) copy-start(s32[4]{0:T(128)} %pad_add_fusion.pos_ref) | copy-start | bytes 52
  48.9 8.8 %copy-start.7 = (bf16[1024,512]{1,0:T(8,128)(2,1)S(1)}, bf16[1024,512]{1,0:T(8,128)(2,1)}, u32[]{:S(2)}) copy-start(bf16[1024,512]{1,0:T(8,128)(2,1)} %cot_ref.1) | copy-start | bytes 3145732
  48.9 8.8 %copy-start.13 = (bf16[128,512]{1,0:T(8,128)(2,1)S(1)}, bf16[128,512]{1,0:T(8,128)(2,1)}, u32[]{:S(2)}) copy-start(bf16[128,512]{1,0:T(8,128)(2,1)} %wo_ref) | copy-start | bytes 393220
  48.9 8.8 %copy-start.14 = (f32[512]{0:T(512)S(1)}, f32[512]{0:T(512)}, u32[]{:S(2)}) copy-start(f32[512]{0:T(512)} %param.19) | copy-start | bytes 6148
  48.9 8.8 %copy-start.18 = (f32[1024,512]{1,0:T(8,128)S(1)}, f32[1024,512]{1,0:T(8,128)}, u32[]{:S(2)}) copy-start(f32[1024,512]{1,0:T(8,128)} %get-tuple-element.324.mid_ref) | copy-start | bytes 6291460
  48.9 8.8 %copy-start.26 = (bf16[3,1024,128]{2,1,0:T(8,128)(2,1)S(1)}, bf16[3,1024,128]{2,1,0:T(8,128)(2,1)}, u32[]{:S(2)}) copy-start(bf16[3,1024,128]{2,1,0:T(8,128)(2,1)} %get-tuple-element.278.qkv_ref) | copy-start | bytes 2359300
  54.9 2.8 %collective-permute-start.13 = (bf16[512,512]{1,0:T(8,128)(2,1)}, bf16[512,512]{1,0:T(8,128)(2,1)S(1)}, u32[]{:S(2)}, u32[]{:S(2)}) collective-permute-start(bf16[512,512]{1,0:T(8,128)(2,1)} %collective-permute-done.10.far_ref), channel_id=1, source_target_pairs={{0,1},{1,0},{2,3},{3,2},{4,5},{5,4},{6,7},{7,6},{8,9},{9,8},{10,11... | collective-permute-start | bytes 1572872 | tf_op jit(solution)/shard_map/sum_second/ppermute | solution.py:611
  54.9 11.4 %collective-permute-start.14 = (bf16[512,512]{1,0:T(8,128)(2,1)}, bf16[512,512]{1,0:T(8,128)(2,1)}, u32[]{:S(2)}, u32[]{:S(2)}) collective-permute-start(bf16[512,512]{1,0:T(8,128)(2,1)} %add.27.own_ref), channel_id=1, source_target_pairs={{0,1},{1,0},{2,3},{3,2},{4,5},{5,4},{6,7},{7,6},{8,9},{9,8},{10,11... | collective-permute-start | bytes 1572872 | tf_op jit(solution)/shard_map/sum_output/ppermute | solution.py:611
  55.4 14.9 %collective-permute-start.11 = (bf16[512,512]{1,0:T(8,128)(2,1)}, bf16[512,512]{1,0:T(8,128)(2,1)}, u32[]{:S(2)}, u32[]{:S(2)}) collective-permute-start(bf16[512,512]{1,0:T(8,128)(2,1)} %add.27.own_ref), channel_id=1, source_target_pairs={{0,2},{1,3},{2,0},{3,1},{4,6},{5,7},{6,4},{7,5},{8,10},{9,11},{10,... | collective-permute-start | bytes 1572872 | tf_op jit(solution)/shard_map/sum_output/ppermute | solution.py:611
  66.3 5.6 %copy-start.2 = (f32[4,10,8,128]{3,2,1,0:T(8,128)S(1)}, f32[4,10,8,128]{3,2,1,0:T(8,128)}, u32[]{:S(2)}) copy-start(f32[4,10,8,128]{3,2,1,0:T(8,128)} %copy-done) | copy-start | bytes 491524
  66.3 5.6 %copy-start.5 = (s32[4]{0:T(128)S(1)}, s32[4]{0:T(128)}, u32[]{:S(2)}) copy-start(s32[4]{0:T(128)} %pad_add_fusion.pos_ref) | copy-start | bytes 52
  66.3 5.6 %copy-start.8 = (bf16[1024,512]{1,0:T(8,128)(2,1)S(1)}, bf16[1024,512]{1,0:T(8,128)(2,1)}, u32[]{:S(2)}) copy-start(bf16[1024,512]{1,0:T(8,128)(2,1)} %tok_ref.3) | copy-start | bytes 3145732
  66.3 5.6 %copy-start.10 = (bf16[3,512,128]{2,1,0:T(8,128)(2,1)S(1)}, bf16[3,512,128]{2,1,0:T(8,128)(2,1)}, u32[]{:S(2)}) copy-start(bf16[3,512,128]{2,1,0:T(8,128)(2,1)} %w_ref.2) | copy-start | bytes 1179652
  66.3 5.6 %copy-start.28 = (bf16[1024,384]{1,0:T(8,128)(2,1)S(1)}, bf16[1024,384]{1,0:T(8,128)(2,1)}, u32[]{:S(2)}) copy-start(bf16[1024,384]{1,0:T(8,128)(2,1)} %copy-done.27) | copy-start | bytes 2359300
  66.3 5.6 %copy-start.32 = (f32[4,2,8,128]{3,2,1,0:T(8,128)S(1)}, f32[4,2,8,128]{3,2,1,0:T(8,128)}, u32[]{:S(2)}) copy-start(f32[4,2,8,128]{3,2,1,0:T(8,128)} %copy-done.31) | copy-start | bytes 98308
  70.3 16.2 %collective-permute-start.16 = (bf16[512,512]{1,0:T(8,128)(2,1)}, bf16[512,512]{1,0:T(8,128)(2,1)}, u32[]{:S(2)}, u32[]{:S(2)}) collective-permute-start(bf16[512,512]{1,0:T(8,128)(2,1)} %collective-permute-done.11.far_ref), channel_id=1, source_target_pairs={{0,1},{1,0},{2,3},{3,2},{4,5},{5,4},{6,7},{7,6},{8,9},{9,8},{10,11... | collective-permute-start | bytes 1572872 | tf_op jit(solution)/shard_map/sum_output/ppermute | solution.py:611
  70.4 8.6 %collective-permute-start.19 = (bf16[256,512]{1,0:T(8,128)(2,1)S(1)}, bf16[256,512]{1,0:T(8,128)(2,1)S(1)}, u32[]{:S(2)}, u32[]{:S(2)}) collective-permute-start(bf16[256,512]{1,0:T(8,128)(2,1)S(1)} %get-tuple-element.308), channel_id=1, source_target_pairs={{0,4},{4,0},{8,12},{12,8},{16,20},{20,16},{24,28},{28,24},{1,5},{5... | collective-permute-start | bytes 786440 | tf_op jit(solution)/shard_map/feed_weights/ppermute | solution.py:611
  74.0 8.3 %collective-permute-start.18 = (bf16[528,512]{1,0:T(8,128)(2,1)S(1)}, bf16[528,512]{1,0:T(8,128)(2,1)S(1)}, u32[]{:S(2)}, u32[]{:S(2)}) collective-permute-start(bf16[528,512]{1,0:T(8,128)(2,1)S(1)} %get-tuple-element.307), channel_id=1, source_target_pairs={{0,1},{1,0},{2,3},{3,2},{4,5},{5,4},{6,7},{7,6},{8,9},{9,8},{10,11... | collective-permute-start | bytes 1622024 | tf_op jit(solution)/shard_map/sum_first/ppermute | solution.py:611
  74.2 11.3 %collective-permute-start.17 = (bf16[272,512]{1,0:T(8,128)(2,1)}, bf16[272,512]{1,0:T(8,128)(2,1)}, u32[]{:S(2)}, u32[]{:S(2)}) collective-permute-start(bf16[272,512]{1,0:T(8,128)(2,1)} %get-tuple-element.299), channel_id=1, source_target_pairs={{0,8},{4,12},{8,0},{12,4},{16,24},{20,28},{24,16},{28,20},{1,9},{5... | collective-permute-start | bytes 835592 | tf_op jit(solution)/shard_map/rest_weights/ppermute | solution.py:611
  79.7 12.7 %collective-permute-start.21 = (bf16[128,512]{1,0:T(8,128)(2,1)}, bf16[128,512]{1,0:T(8,128)(2,1)}, u32[]{:S(2)}, u32[]{:S(2)}) collective-permute-start(bf16[128,512]{1,0:T(8,128)(2,1)} %get-tuple-element.326), channel_id=1, source_target_pairs={{0,16},{4,20},{8,24},{12,28},{16,0},{20,4},{24,8},{28,12},{1,17},{... | collective-permute-start | bytes 393224 | tf_op jit(solution)/shard_map/feed_weights/ppermute | solution.py:611
  82.3 3.1 %copy-start.30 = (bf16[272,512]{1,0:T(8,128)(2,1)S(1)}, bf16[272,512]{1,0:T(8,128)(2,1)}, u32[]{:S(2)}) copy-start(bf16[272,512]{1,0:T(8,128)(2,1)} %get-tuple-element.316.a_ref) | copy-start | bytes 835588
  83.3 4.1 %copy-start.15 = (f32[512]{0:T(512)S(1)}, f32[512]{0:T(512)}, u32[]{:S(2)}) copy-start(f32[512]{0:T(512)} %param.24) | copy-start | bytes 6148
  83.3 4.1 %copy-start.19 = (f32[1024,512]{1,0:T(8,128)S(1)}, f32[1024,512]{1,0:T(8,128)}, u32[]{:S(2)}) copy-start(f32[1024,512]{1,0:T(8,128)} %get-tuple-element.324.mid_ref) | copy-start | bytes 6291460
  83.3 13.9 %collective-permute-start.20 = (bf16[528,512]{1,0:T(8,128)(2,1)}, bf16[528,512]{1,0:T(8,128)(2,1)}, u32[]{:S(2)}, u32[]{:S(2)}) collective-permute-start(bf16[528,512]{1,0:T(8,128)(2,1)} %pair.1.near_ref.own_ref), channel_id=1, source_target_pairs={{0,2},{1,3},{2,0},{3,1},{4,6},{5,7},{6,4},{7,5},{8,10},{9,11},{10,... | collective-permute-start | bytes 1622024 | tf_op jit(solution)/shard_map/sum_first/ppermute | solution.py:611
  86.5 5.2 %collective-permute-start.22 = (bf16[144,512]{1,0:T(8,128)(2,1)S(1)}, bf16[144,512]{1,0:T(8,128)(2,1)S(1)}, u32[]{:S(2)}, u32[]{:S(2)}) collective-permute-start(bf16[144,512]{1,0:T(8,128)(2,1)S(1)} %get-tuple-element.327), channel_id=1, source_target_pairs={{0,4},{4,0},{8,12},{12,8},{16,20},{20,16},{24,28},{28,24},{1,5},{5... | collective-permute-start | bytes 442376 | tf_op jit(solution)/shard_map/rest_weights/ppermute | solution.py:611
  92.5 4.7 %collective-permute-start.25 = (f32[8,512]{1,0:T(8,128)S(1)}, f32[8,512]{1,0:T(8,128)S(1)}, u32[]{:S(2)}, u32[]{:S(2)}) collective-permute-start(f32[8,512]{1,0:T(8,128)S(1)} %get-tuple-element.337.a_ref), channel_id=1, source_target_pairs={{0,1},{1,0},{2,3},{3,2},{4,5},{5,4},{6,7},{7,6},{8,9},{9,8},{10,11... | collective-permute-start | bytes 49160 | tf_op jit(solution)/shard_map/sum_extra/ppermute | solution.py:611
  92.5 6.8 %collective-permute-start.27 = (bf16[64,512]{1,0:T(8,128)(2,1)}, bf16[64,512]{1,0:T(8,128)(2,1)}, u32[]{:S(2)}, u32[]{:S(2)}) collective-permute-start(bf16[64,512]{1,0:T(8,128)(2,1)} %get-tuple-element.340), channel_id=1, source_target_pairs={{0,16},{4,20},{8,24},{12,28},{16,0},{20,4},{24,8},{28,12},{1,17},{... | collective-permute-start | bytes 196616 | tf_op jit(solution)/shard_map/rest_weights/ppermute | solution.py:611
  95.1 4.1 %copy-start.33 = (f32[8,512]{1,0:T(8,128)S(1)}, f32[8,512]{1,0:T(8,128)}, u32[]{:S(2)}) copy-start(f32[8,512]{1,0:T(8,128)} %get-tuple-element.347.up_ref) | copy-start | bytes 49156
  95.1 11.7 %collective-permute-start.29 = (bf16[128,512]{1,0:T(8,128)(2,1)}, bf16[128,512]{1,0:T(8,128)(2,1)}, u32[]{:S(2)}, u32[]{:S(2)}) collective-permute-start(bf16[128,512]{1,0:T(8,128)(2,1)} %add.28.a_ref), channel_id=1, source_target_pairs={{0,16},{4,20},{8,24},{12,28},{16,0},{20,4},{24,8},{28,12},{1,17},{... | collective-permute-start | bytes 393224 | tf_op jit(solution)/shard_map/feed_weights/ppermute | solution.py:611
  97.2 14.2 %collective-permute-start.24 = (bf16[528,512]{1,0:T(8,128)(2,1)}, bf16[528,512]{1,0:T(8,128)(2,1)}, u32[]{:S(2)}, u32[]{:S(2)}) collective-permute-start(bf16[528,512]{1,0:T(8,128)(2,1)} %collective-permute-done.20.far_ref), channel_id=1, source_target_pairs={{0,1},{1,0},{2,3},{3,2},{4,5},{5,4},{6,7},{7,6},{8,9},{9,8},{10,11... | collective-permute-start | bytes 1622024 | tf_op jit(solution)/shard_map/sum_first/ppermute | solution.py:611
  97.8 11.7 %collective-permute-start.26 = (f32[8,512]{1,0:T(8,128)}, f32[8,512]{1,0:T(8,128)}, u32[]{:S(2)}, u32[]{:S(2)}) collective-permute-start(f32[8,512]{1,0:T(8,128)} %plus.1.extra_ref), channel_id=1, source_target_pairs={{0,2},{1,3},{2,0},{3,1},{4,6},{5,7},{6,4},{7,5},{8,10},{9,11},{10,... | collective-permute-start | bytes 49160 | tf_op jit(solution)/shard_map/sum_extra/ppermute | solution.py:611
  100.5 8.1 %collective-permute-start.28 = (bf16[80,512]{1,0:T(8,128)(2,1)S(1)}, bf16[80,512]{1,0:T(8,128)(2,1)S(1)}, u32[]{:S(2)}, u32[]{:S(2)}) collective-permute-start(bf16[80,512]{1,0:T(8,128)(2,1)S(1)} %piece.1.a_ref), channel_id=1, source_target_pairs={{0,16},{4,20},{8,24},{12,28},{16,0},{20,4},{24,8},{28,12},{1,17},{... | collective-permute-start | bytes 245768 | tf_op jit(solution)/shard_map/rest_weights/ppermute | solution.py:611
  108.6 2.8 %copy-start.17 = (f32[512]{0:T(512)S(1)}, f32[512]{0:T(512)}, u32[]{:S(2)}) copy-start(f32[512]{0:T(512)} %param.14) | copy-start | bytes 6148
  108.6 2.8 %copy-start.21 = (bf16[1024,512]{1,0:T(8,128)(2,1)S(1)}, bf16[1024,512]{1,0:T(8,128)(2,1)}, u32[]{:S(2)}) copy-start(bf16[1024,512]{1,0:T(8,128)(2,1)} %copy-done.20) | copy-start | bytes 3145732
  108.6 7.3 %collective-permute-start.31 = (bf16[256,512]{1,0:T(8,128)(2,1)}, bf16[256,512]{1,0:T(8,128)(2,1)}, u32[]{:S(2)}, u32[]{:S(2)}) collective-permute-start(bf16[256,512]{1,0:T(8,128)(2,1)} %concat.1.own_ref), channel_id=1, source_target_pairs={{0,8},{4,12},{8,0},{12,4},{16,24},{20,28},{24,16},{28,20},{1,9},{5... | collective-permute-start | bytes 786440 | tf_op jit(solution)/shard_map/feed_weights/ppermute | solution.py:611
  108.6 13.6 %collective-permute-start.34 = (bf16[256,512]{1,0:T(8,128)(2,1)}, bf16[256,512]{1,0:T(8,128)(2,1)}, u32[]{:S(2)}, u32[]{:S(2)}) collective-permute-start(bf16[256,512]{1,0:T(8,128)(2,1)} %concat.1.own_ref), channel_id=1, source_target_pairs={{0,4},{4,0},{8,12},{12,8},{16,20},{20,16},{24,28},{28,24},{1,5},{5... | collective-permute-start | bytes 786440 | tf_op jit(solution)/shard_map/feed_weights/ppermute | solution.py:611
  108.7 2.7 %collective-permute-start.23 = (bf16[528,512]{1,0:T(8,128)(2,1)}, bf16[528,512]{1,0:T(8,128)(2,1)S(1)}, u32[]{:S(2)}, u32[]{:S(2)}) collective-permute-start(bf16[528,512]{1,0:T(8,128)(2,1)} %pair.1.near_ref.own_ref), channel_id=1, source_target_pairs={{0,1},{1,0},{2,3},{3,2},{4,5},{5,4},{6,7},{7,6},{8,9},{9,8},{10,11... | collective-permute-start | bytes 1622024 | tf_op jit(solution)/shard_map/sum_first/ppermute | solution.py:611
  109.4 9.1 %collective-permute-start.30 = (bf16[144,512]{1,0:T(8,128)(2,1)}, bf16[144,512]{1,0:T(8,128)(2,1)}, u32[]{:S(2)}, u32[]{:S(2)}) collective-permute-start(bf16[144,512]{1,0:T(8,128)(2,1)} %merge.2.a_ref), channel_id=1, source_target_pairs={{0,4},{4,0},{8,12},{12,8},{16,20},{20,16},{24,28},{28,24},{1,5},{5... | collective-permute-start | bytes 442376 | tf_op jit(solution)/shard_map/rest_weights/ppermute | solution.py:611
  115.9 8.8 %collective-permute-start.33 = (bf16[256,512]{1,0:T(8,128)(2,1)}, bf16[256,512]{1,0:T(8,128)(2,1)}, u32[]{:S(2)}, u32[]{:S(2)}) collective-permute-start(bf16[256,512]{1,0:T(8,128)(2,1)} %collective-permute-done.31.own_ref), channel_id=1, source_target_pairs={{0,4},{4,0},{8,12},{12,8},{16,20},{20,16},{24,28},{28,24},{1,5},{5... | collective-permute-start | bytes 786440 | tf_op jit(solution)/shard_map/feed_weights/ppermute | solution.py:611
  120.2 7.8 %collective-permute-start.32 = (bf16[272,512]{1,0:T(8,128)(2,1)}, bf16[272,512]{1,0:T(8,128)(2,1)}, u32[]{:S(2)}, u32[]{:S(2)}) collective-permute-start(bf16[272,512]{1,0:T(8,128)(2,1)} %merge.3.near_ref), channel_id=1, source_target_pairs={{0,8},{4,12},{8,0},{12,4},{16,24},{20,28},{24,16},{28,20},{1,9},{5... | collective-permute-start | bytes 835592 | tf_op jit(solution)/shard_map/rest_weights/ppermute | solution.py:611
  (12 other events, 16.6 us)

commit v7 on v6

--- a/solution.py
+++ b/solution.py
@@ -98,13 +98,20 @@
     return jnp.concatenate([v[i * 8 : (i + 1) * 8] for i in range(count)], axis=1)
 
 
+def sums_of(sums_ref, which):
+    pair = sums_ref[:, which // 2].astype(f32)
+    blocks = pair.shape[1] // 2
+    start = which % 2 * blocks
+    return pair[:, start : start + blocks].reshape(-1, pair.shape[2])
+
+
 def columns_of(sums_ref, start, count):
-    slots, _, blocks, width = sums_ref.shape
-    parts = [sums_ref[:, start + j].reshape(slots * blocks, width) for j in range(count)]
-    return jnp.concatenate(parts, axis=1)
-
-
-def project_kernel(tile, tok_ref, gain_ref, bias_ref, w_ref, first_ref, qkv_ref, sum_ref, wcat):
+    return jnp.concatenate([sums_of(sums_ref, start + j) for j in range(count)], axis=1)
+
+
+def project_kernel(
+    tile, tok_ref, gain_ref, bias_ref, w_ref, first_ref, qkv_ref, out_ref, wcat, sum_ref
+):
     width = w_ref.shape[2]
     for s in range(3):
         wcat[:, s * width : (s + 1) * width] = w_ref[s]
@@ -120,11 +127,13 @@
             qkv_ref[s, at] = part
             if s:
                 mean = jnp.mean(part.astype(f32).reshape(per, SPAN, width), axis=1)
-                sum_ref[s - 1, i * per : (i + 1) * per] = mean.astype(bf16).astype(f32)
+                sum_ref[s - 1, i * per : (i + 1) * per] = mean
         sums = [jnp.sum(x.reshape(per, SPAN, -1), axis=1) for x in (first.astype(f32), n)]
         total = jnp.concatenate(sums, axis=1)
         for j in range(sum_ref.shape[0] - 2):
             sum_ref[2 + j, i * per : (i + 1) * per] = total[:, j * width : (j + 1) * width]
+    for j in range(out_ref.shape[0]):
+        out_ref[j] = jnp.concatenate([sum_ref[2 * j], sum_ref[2 * j + 1]]).astype(bf16)
 
 
 def local_kernel(qkv_ref, exp_ref, stat_ref):
@@ -149,8 +158,8 @@
     lanes = exp_ref.shape[2]
     slots = sums_ref.shape[0]
     place = place_ref[0]
-    keys = sums_ref[:, 0].reshape(slots * blocks, -1).astype(bf16)
-    values = sums_ref[:, 1].reshape(slots * blocks, -1).astype(bf16)
+    keys = sums_of(sums_ref, 0).astype(bf16)
+    values = sums_of(sums_ref, 1).astype(bf16)
     row = lax.broadcasted_iota(i32, (slots * blocks, lanes), 0)
     at_block = ((row // blocks) ^ place) * blocks + row % blocks
     for b in range(blocks):
@@ -381,8 +390,8 @@
     vec_ref[24:32] += fold(cot)
 
     grad_att = nt(low, wo_ref[...]).astype(bf16)
-    far_keys = sums_ref[:, 0].reshape(-1, width).astype(bf16)
-    far_values = sums_ref[:, 1].reshape(-1, width).astype(bf16)
+    far_keys = sums_of(sums_ref, 0).astype(bf16)
+    far_values = sums_of(sums_ref, 1).astype(bf16)
     far_gk = jnp.zeros(far_keys.shape, f32)
     far_gv = jnp.zeros(far_keys.shape, f32)
     for b in range(prob_ref.shape[0]):
@@ -526,6 +535,10 @@
 
 def spacer_kernel(x_ref, out_ref):
     out_ref[...] = x_ref[...] * 0.5
+
+
+def keep_kernel(x_ref, out_ref):
+    out_ref[...] = x_ref[...]
 
 
 def concat_kernel(a_ref, b_ref, out_ref):
@@ -798,9 +811,12 @@
             (
                 sds((rows, dim), bf16),
                 sds((3, rows, width), bf16),
-                sds((2 + 2 * (dim // width), blocks, width), f32),
+                sds((1 + dim // width, 2 * blocks, width), bf16),
             ),
-            [pltpu.VMEM((dim, 3 * width), bf16)],
+            [
+                pltpu.VMEM((dim, 3 * width), bf16),
+                pltpu.VMEM((2 + 2 * (dim // width), blocks, width), f32),
+            ],
             60,
         )
         local = plain(
@@ -873,7 +889,7 @@
             mib=60,
         )
         slot_shape = (group, 2, blocks, width)
-        sums_shape = (group, 2 + 2 * (dim // width), blocks, width)
+        sums_shape = (group, 1 + dim // width, 2 * blocks, width)
         back = gridded(
             back_kernel,
             "back",
@@ -975,6 +991,9 @@
         def concat(a, b):
             return like(concat_kernel, "concat", (2 * a.shape[0], a.shape[1]), bf16, a, b)
 
+        def keep(x):
+            return like(keep_kernel, "keep", x.shape, bf16, x)
+
         def pl_add(a, b):
             return like(slot_kernel, "plus", a.shape, f32, a, b)
 
@@ -1070,7 +1089,9 @@
             cotangent,
         )
 
-        total = near_sum(line(add_low, mine, swap(theirs, "mp", 1, "sum_second")), "sum_second")
+        got = swap(theirs, "mp", 1, "sum_second")
+        mine = line(keep, mine)
+        total = near_sum(line(add_low, mine, got), "sum_second")
         far = swap(total, "mp", last_far, "sum_second")
         other = swap(total, "mp", 1, "sum_second")
         out_theirs, out_mine, theirs, mine = line(

time: 131 us -> 129 us (0.985)
    pallas_call x6 -> x7, Pallas kernels: 6.9 us -> 6.94 us  [like(): return plain(kernel, name, specs, (sds(shape, dtype),))(*operands)[0]]
where the time goes in v7:
time: 129 us
  Pallas kernels  60.1 us (47%)
  waiting for transfers between devices  32.9 us (26%)
  starting transfers between devices  30.9 us (24%)
  local copies, waits for them, and re-layouts  3.08 us (2%)
    pallas_call x12, Pallas kernels, __call__(): result = work(*inputs)  36.4 us
    ppermute x35, waiting for transfers between devices, swap(): return lax.ppermute(x, axis, [(i, i ^ mask) for i in range(n)])  32.9 us
    ppermute x35, starting transfers between devices, swap(): return lax.ppermute(x, axis, [(i, i ^ mask) for i in range(n)])  30.9 us
    pallas_call x7, Pallas kernels, like(): return plain(kernel, name, specs, (sds(shape, dtype),))(*operands)[0]  6.94 us
    pallas_call x1, Pallas kernels, per_device(): back(*a)  6.81 us
    pallas_call x2, Pallas kernels, feed_unpack(): pl.pallas_call(functools.partial(feed_unpack_kernel, n_dp // 4, 1 if held...  4.14 us
    pallas_call x3, Pallas kernels, add_parts(): pl.pallas_call(functools.partial(add_kernel, parts), out_shape=(part,) *...  3.42 us
    unnamed x84, local copies, waits for them, and re-layouts  3.06 us
  transfers between devices with their start and end apart: 35, of which 16 were waited for; matrix products, arithmetic and copies ran while one was open for 0% of the time, Pallas kernels for 36%

profile of v7, /device:TPU:0, one launch (start us, length us, event | category | flops | bytes accessed | tf_op | source)
XLA Modules:
  0.0 128.7 jit_solution(12817625572607689715)
XLA Ops:
  0.6 3.0 %collective-permute-start = (bf16[128,512]{1,0:T(8,128)(2,1)}, bf16[128,512]{1,0:T(8,128)(2,1)S(1)}, u32[]{:S(2)}, u32[]{:S(2)}) collective-permute-start(bf16[128,512]{1,0:T(8,128)(2,1)} %wo_ref), channel_id=1, source_target_pairs={{0,2},{1,3},{2,0},{3,1},{4,6},{5,7},{6,4},{7,5},{8,10},{9,11},{10,... | collective-permute-start | bytes 393224 | tf_op jit(solution)/shard_map/gather_w_out/ppermute | solution.py:624
  3.7 3.9 %project.1 = (bf16[1024,512]{1,0:T(8,128)(2,1)}, bf16[3,1024,128]{2,1,0:T(8,128)(2,1)}, bf16[5,16,128]{2,1,0:T(8,128)(2,1)}) custom-call(bf16[1024,512]{1,0:T(8,128)(2,1)} %tok_ref.3, f32[1,512]{1,0:T(1,128)} %bitcast.24, f32[1,512]{1,0:T(1,128)} %bitcast.29, bf16[3,512,128]{2,1,0:T(8,128)(2,1)} %w_ref.2), custom_call_target="tpu_custom_call" | custom-call | flops 115000000512 | bytes 1 | tf_op jit(solution)/shard_map/project/pallas_call | solution.py:648
  7.6 1.6 %collective-permute-start.1 = (bf16[1,5,16,128]{3,2,1,0:T(8,128)(2,1)}, bf16[1,5,16,128]{3,2,1,0:T(8,128)(2,1)S(1)}, u32[]{:S(2)}, u32[]{:S(2)}) collective-permute-start(bf16[1,5,16,128]{3,2,1,0:T(8,128)(2,1)} %bitcast.27), channel_id=1, source_target_pairs={{0,4},{4,0},{8,12},{12,8},{16,20},{20,16},{24,28},{28,24},{1,5},{5... | collective-permute-start | bytes 61448 | tf_op jit(solution)/shard_map/summaries/ppermute | solution.py:624
  9.1 1.1 copy-done.25
  10.3 0.5 local.1
  10.8 0.9 collective-permute-done.1
  11.7 1.6 %collective-permute-start.2 = (bf16[2,5,16,128]{3,2,1,0:T(8,128)(2,1)S(1)}, bf16[2,5,16,128]{3,2,1,0:T(8,128)(2,1)S(1)}, u32[]{:S(2)}, u32[]{:S(2)}) collective-permute-start(bf16[2,5,16,128]{3,2,1,0:T(8,128)(2,1)S(1)} %constant_dynamic-update-slice_fusion), channel_id=1, source_target_pairs={{0,8},{4,12},{8,0},{12,4},{16,24},{20,28},{24,16},{28,20},{1,9},{5... | collective-permute-start | bytes 122888 | tf_op jit(solution)/shard_map/summaries/ppermute | solution.py:624
  13.3 0.5 collective-permute-start.4
  13.8 1.9 %collective-permute-done.2 = bf16[2,5,16,128]{3,2,1,0:T(8,128)(2,1)S(1)} collective-permute-done((bf16[2,5,16,128]{3,2,1,0:T(8,128)(2,1)S(1)}, bf16[2,5,16,128]{3,2,1,0:T(8,128)(2,1)S(1)}, u32[]{:S(2)}, u32[]{:S(2)}) %collective-permute-start.2) | collective-permute-done | bytes 40992 | tf_op jit(solution)/shard_map/summaries/ppermute | solution.py:624
  15.8 1.5 %attend.1 = (bf16[8,160,256]{2,1,0:T(8,128)(2,1)S(1)}, bf16[1024,128]{1,0:T(8,128)(2,1)S(1)}) custom-call(s32[1]{0:T(128)} %bitcast.2.place_ref, bf16[3,1024,128]{2,1,0:T(8,128)(2,1)S(1)} %copy-done.25, f32[8,128,256]{2,1,0:T(8,128)S(1)} %get-tuple-element.222.exp_ref, f32[8,2,256]{2,1,0:T(2,128)S(1)} %get-tuple-element.223.stat_ref, ...), custom_call_target="tpu_custom_call" | custom-call | flops 115000000512 | bytes 1 | tf_op jit(solution)/shard_map/attend/pallas_call | solution.py:648
  17.4 1.5 %collective-permute-start.6 = (bf16[1024,128]{1,0:T(8,128)(2,1)S(1)}, bf16[1024,128]{1,0:T(8,128)(2,1)S(1)}, u32[]{:S(2)}, u32[]{:S(2)}) collective-permute-start(bf16[1024,128]{1,0:T(8,128)(2,1)S(1)} %get-tuple-element.296.refs_0_.att_ref), channel_id=1, source_target_pairs={{0,2},{1,3},{2,0},{3,1},{4,6},{5,7},{6,4},{7,5},{8,10},{9,11},{10,... | collective-permute-start | bytes 786440 | tf_op jit(solution)/shard_map/gather_attended/ppermute | solution.py:624
  18.9 6.1 %collective-permute-done.6.refs_2_ = bf16[1024,128]{1,0:T(8,128)(2,1)S(1)} collective-permute-done((bf16[1024,128]{1,0:T(8,128)(2,1)S(1)}, bf16[1024,128]{1,0:T(8,128)(2,1)S(1)}, u32[]{:S(2)}, u32[]{:S(2)}) %collective-permute-start.6) | collective-permute-done | bytes 262176 | tf_op jit(solution)/shard_map/gather_attended/ppermute | solution.py:624
  25.0 0.6 pad_add_fusion.pos_ref
  25.6 0.9 collective-permute-done.7.refs_3_
  26.5 0.7 copy-done.37
  27.2 8.9 %feed.1 = (f32[1024,512]{1,0:T(8,128)}, bf16[1024,512]{1,0:T(8,128)(2,1)}, bf16[1024,512]{1,0:T(8,128)(2,1)}, bf16[1024,512]{1,0:T(8,128)(2,1)}, bf16[512,512]{1...) custom-call(s32[4]{0:T(128)} %pad_add_fusion.pos_ref, bf16[1024,512]{1,0:T(8,128)(2,1)} %tok_ref.3, ...), custom_call_target="tpu_custom_call" | custom-call | flops 115000000512 | bytes 1 | tf_op jit(solution)/shard_map/feed/pallas_call | solution.py:648
  36.4 1.0 copy-done.29
  37.5 0.8 collective-permute-done.8.b_ref
  38.4 0.9 add.26.own_ref
  39.3 1.5 %collective-permute-start.10 = (bf16[512,512]{1,0:T(8,128)(2,1)}, bf16[512,512]{1,0:T(8,128)(2,1)}, u32[]{:S(2)}, u32[]{:S(2)}) collective-permute-start(bf16[512,512]{1,0:T(8,128)(2,1)} %add.26.own_ref), channel_id=1, source_target_pairs={{0,2},{1,3},{2,0},{3,1},{4,6},{5,7},{6,4},{7,5},{8,10},{9,11},{10,... | collective-permute-start | bytes 1572872 | tf_op jit(solution)/shard_map/sum_second/ppermute | solution.py:624
  40.9 3.8 %weights.1 = (bf16[512,512]{1,0:T(8,128)(2,1)S(1)}, bf16[512,512]{1,0:T(8,128)(2,1)S(1)}, bf16[512,512]{1,0:T(8,128)(2,1)}, bf16[512,512]{1,0:T(8,128)(2,1)S(1)}) custom-call(s32[4]{0:T(128)S(1)} %copy-done.3, bf16[1024,512]{1,0:T(8,128)(2,1)S(1)} %copy-done.23, bf16[1024,512]{1,0:T(8,128)(2,1)S(1)} %copy-done.22, bf16[1024,512]{1,0:T(8,128)(2,1)S(1)} %copy-done.24, ...), custom_call_target="tpu_custom_call" | custom-call | flops 115000000512 | bytes 1 | tf_op jit(solution)/shard_map/weights/pallas_call | solution.py:648
  44.7 0.5 collective-permute-start.9
  45.6 1.1 collective-permute-done.9.b_ref
  46.7 0.9 add.27.own_ref
  47.7 5.9 %collective-permute-done.10.far_ref = bf16[512,512]{1,0:T(8,128)(2,1)} collective-permute-done((bf16[512,512]{1,0:T(8,128)(2,1)}, bf16[512,512]{1,0:T(8,128)(2,1)}, u32[]{:S(2)}, u32[]{:S(2)}) %collective-permute-start.10) | collective-permute-done | bytes 524320 | tf_op jit(solution)/shard_map/sum_second/ppermute | solution.py:624
  53.6 0.5 collective-permute-start.14
  54.1 1.5 %collective-permute-start.11 = (bf16[512,512]{1,0:T(8,128)(2,1)}, bf16[512,512]{1,0:T(8,128)(2,1)}, u32[]{:S(2)}, u32[]{:S(2)}) collective-permute-start(bf16[512,512]{1,0:T(8,128)(2,1)} %add.27.own_ref), channel_id=1, source_target_pairs={{0,2},{1,3},{2,0},{3,1},{4,6},{5,7},{6,4},{7,5},{8,10},{9,11},{10,... | collective-permute-start | bytes 1572872 | tf_op jit(solution)/shard_map/sum_output/ppermute | solution.py:624
  55.6 0.8 collective-permute-done.13.other_far_ref
  56.5 6.8 %back.1 = (bf16[1024,512]{1,0:T(8,128)(2,1)S(1)}, bf16[1024,384]{1,0:T(8,128)(2,1)S(1)}, f32[4,2,8,128]{3,2,1,0:T(8,128)S(1)}, f32[32,512]{1,0:T(8,128)S(1)}) custom-call(s32[4]{0:T(128)S(1)} %copy-done.4, bf16[512,512]{1,0:T(8,128)(2,1)} %add.26.own_ref, bf16[512,512]{1,0:T(8,128)(2,1)} %collective-permute-done.10.far_ref, ...), custom_call_target="tpu_custom_call" | custom-call | flops 115000000512 | bytes 1 | tf_op jit(solution)/shard_map/back/pallas_call | solution.py:1111
  63.3 1.6 %split.2 = (bf16[256,512]{1,0:T(8,128)(2,1)S(1)}, bf16[256,512]{1,0:T(8,128)(2,1)S(1)}) custom-call(s32[1]{0:T(128)} %bitcast.11.bit_ref, bf16[512,512]{1,0:T(8,128)(2,1)S(1)} %get-tuple-element.288.a_ref, bf16[512,512]{1,0:T(8,128)(2,1)} %collective-permute-done.15.b_ref), custom_call_target="tpu_custom_call" | custom-call | flops 115000000512 | bytes 1 | tf_op jit(solution)/shard_map/split/pallas_call | solution.py:687
  65.1 3.9 %rest_weights.1 = (bf16[272,512]{1,0:T(8,128)(2,1)}, bf16[272,512]{1,0:T(8,128)(2,1)}) custom-call(s32[1]{0:T(128)} %bitcast.3.bit_ref, bf16[1024,512]{1,0:T(8,128)(2,1)} %get-tuple-element.293.first_ref, bf16[1024,384]{1,0:T(8,128)(2,1)} %copy-done.27, bf16[1024,512]{1,0:T(8,128)(2,1)} %copy-done.20, bf16[1024,128]{1,0:T(8,128)(2,1)} %copy-done.11, ...), custom_call_target="tpu_custom_call" | custom-call | flops 115000000512 | bytes 1 | tf_op jit(solution)/shard_map/rest_weights/pallas_call | solution.py:648
  69.1 1.5 %collective-permute-start.19 = (bf16[256,512]{1,0:T(8,128)(2,1)S(1)}, bf16[256,512]{1,0:T(8,128)(2,1)S(1)}, u32[]{:S(2)}, u32[]{:S(2)}) collective-permute-start(bf16[256,512]{1,0:T(8,128)(2,1)S(1)} %get-tuple-element.310), channel_id=1, source_target_pairs={{0,4},{4,0},{8,12},{12,8},{16,20},{20,16},{24,28},{28,24},{1,5},{5... | collective-permute-start | bytes 786440 | tf_op jit(solution)/shard_map/feed_weights/ppermute | solution.py:624
  70.6 2.0 %first.1 = (bf16[528,512]{1,0:T(8,128)(2,1)S(1)}, bf16[528,512]{1,0:T(8,128)(2,1)S(1)}) custom-call(s32[4]{0:T(128)S(1)} %copy-done.5, bf16[1024,384]{1,0:T(8,128)(2,1)S(1)} %copy-done.28, f32[4,2,8,128]{3,2,1,0:T(8,128)S(1)} %copy-done.32, bf16[4,5,16,128]{3,2,1,0:T(8,128)(2,1)S(1)} %copy-done.2, bf16[3,512,128]{2,1,0:T(8,128)(2,1)S(1)} %copy-done.10, ...), custom_call_target="tpu_custom_call" | custom-call | flops 115000000512 | bytes 1 | tf_op jit(solution)/shard_map/first/pallas_call | solution.py:648
  73.3 4.4 %collective-permute-done.19.b_ref = bf16[256,512]{1,0:T(8,128)(2,1)S(1)} collective-permute-done((bf16[256,512]{1,0:T(8,128)(2,1)S(1)}, bf16[256,512]{1,0:T(8,128)(2,1)S(1)}, u32[]{:S(2)}, u32[]{:S(2)}) %collective-permute-start.19) | collective-permute-done | bytes 262176 | tf_op jit(solution)/shard_map/feed_weights/ppermute | solution.py:624
  77.7 0.7 split.3
  78.4 2.6 %collective-permute-start.21 = (bf16[128,512]{1,0:T(8,128)(2,1)}, bf16[128,512]{1,0:T(8,128)(2,1)}, u32[]{:S(2)}, u32[]{:S(2)}) collective-permute-start(bf16[128,512]{1,0:T(8,128)(2,1)} %get-tuple-element.328), channel_id=1, source_target_pairs={{0,16},{4,20},{8,24},{12,28},{16,0},{20,4},{24,8},{28,12},{1,17},{... | collective-permute-start | bytes 393224 | tf_op jit(solution)/shard_map/feed_weights/ppermute | solution.py:624
  81.0 0.9 pair.1.near_ref.own_ref
  82.0 1.5 %collective-permute-start.20 = (bf16[528,512]{1,0:T(8,128)(2,1)}, bf16[528,512]{1,0:T(8,128)(2,1)}, u32[]{:S(2)}, u32[]{:S(2)}) collective-permute-start(bf16[528,512]{1,0:T(8,128)(2,1)} %pair.1.near_ref.own_ref), channel_id=1, source_target_pairs={{0,2},{1,3},{2,0},{3,1},{4,6},{5,7},{6,4},{7,5},{8,10},{9,11},{10,... | collective-permute-start | bytes 1622024 | tf_op jit(solution)/shard_map/sum_first/ppermute | solution.py:624
  83.4 0.7 collective-permute-done.17.b_ref
  84.2 1.1 split_first.1
  85.2 0.8 collective-permute-start.22
  86.1 3.4 %output.1 = bf16[1024,512]{1,0:T(8,128)(2,1)} custom-call(s32[4]{0:T(128)S(1)} %copy-done.5, bf16[512,512]{1,0:T(8,128)(2,1)} %add.27.own_ref, bf16[512,512]{1,0:T(8,128)(2,1)} %collective-permute-done.11.far_ref, bf16[512,512]{1,0:T(8,128)(2,1)} %collective-permute-done.14.other_ref, bf16[512,512]{1,0:T(8,128)(2,1)} %collective-permute-done.16.other_far_ref, ...), custom_call_target="tpu_custom_call" | custom-call | flops 115000000512 | bytes 1 | tf_op jit(solution)/shard_map/output/pallas_call | solution.py:648
  89.5 0.9 collective-permute-done.22.b_ref
  90.4 0.7 split_second.1
  91.2 1.0 collective-permute-start.27
  92.2 1.6 %add.28.a_ref = bf16[128,512]{1,0:T(8,128)(2,1)} custom-call(bf16[128,512]{1,0:T(8,128)(2,1)S(1)} %get-tuple-element.335.a_ref, bf16[128,512]{1,0:T(8,128)(2,1)} %collective-permute-done.21.b_ref), custom_call_target="tpu_custom_call" | custom-call | flops 115000000512 | bytes 1 | tf_op jit(solution)/shard_map/add/pallas_call | solution.py:660
  93.8 1.9 %collective-permute-start.29 = (bf16[128,512]{1,0:T(8,128)(2,1)}, bf16[128,512]{1,0:T(8,128)(2,1)}, u32[]{:S(2)}, u32[]{:S(2)}) collective-permute-start(bf16[128,512]{1,0:T(8,128)(2,1)} %add.28.a_ref), channel_id=1, source_target_pairs={{0,16},{4,20},{8,24},{12,28},{16,0},{20,4},{24,8},{28,12},{1,17},{... | collective-permute-start | bytes 393224 | tf_op jit(solution)/shard_map/feed_weights/ppermute | solution.py:624
  95.8 0.6 plus.1.extra_ref
  96.4 1.5 %collective-permute-start.26 = (f32[8,512]{1,0:T(8,128)}, f32[8,512]{1,0:T(8,128)}, u32[]{:S(2)}, u32[]{:S(2)}) collective-permute-start(f32[8,512]{1,0:T(8,128)} %plus.1.extra_ref), channel_id=1, source_target_pairs={{0,2},{1,3},{2,0},{3,1},{4,6},{5,7},{6,4},{7,5},{8,10},{9,11},{10,... | collective-permute-start | bytes 49160 | tf_op jit(solution)/shard_map/sum_extra/ppermute | solution.py:624
  97.9 1.3 piece.1.a_ref
  99.2 1.0 collective-permute-start.28
  100.2 5.3 %collective-permute-done.29.b_ref = bf16[128,512]{1,0:T(8,128)(2,1)} collective-permute-done((bf16[128,512]{1,0:T(8,128)(2,1)}, bf16[128,512]{1,0:T(8,128)(2,1)}, u32[]{:S(2)}, u32[]{:S(2)}) %collective-permute-start.29) | collective-permute-done | bytes 131104 | tf_op jit(solution)/shard_map/feed_weights/ppermute | solution.py:624
  105.5 1.7 %concat.1.own_ref = bf16[256,512]{1,0:T(8,128)(2,1)} custom-call(bf16[128,512]{1,0:T(8,128)(2,1)} %add.28.a_ref, bf16[128,512]{1,0:T(8,128)(2,1)} %collective-permute-done.29.b_ref), custom_call_target="tpu_custom_call" | custom-call | flops 115000000512 | bytes 1 | tf_op jit(solution)/shard_map/concat/pallas_call | solution.py:986
  107.4 0.7 merge.2.a_ref
  108.1 1.9 %collective-permute-start.30 = (bf16[144,512]{1,0:T(8,128)(2,1)}, bf16[144,512]{1,0:T(8,128)(2,1)}, u32[]{:S(2)}, u32[]{:S(2)}) collective-permute-start(bf16[144,512]{1,0:T(8,128)(2,1)} %merge.2.a_ref), channel_id=1, source_target_pairs={{0,4},{4,0},{8,12},{12,8},{16,20},{20,16},{24,28},{28,24},{1,5},{5... | collective-permute-start | bytes 442376 | tf_op jit(solution)/shard_map/rest_weights/ppermute | solution.py:624
  110.1 4.5 %last.1 = bf16[1024,512]{1,0:T(8,128)(2,1)} custom-call(s32[4]{0:T(128)S(1)} %copy-done.5, bf16[528,512]{1,0:T(8,128)(2,1)} %pair.1.near_ref.own_ref, bf16[528,512]{1,0:T(8,128)(2,1)} %collective-permute-done.20.far_ref, bf16[528,512]{1,0:T(8,128)(2,1)S(1)} %collective-permute-done.23.other_ref, bf16[528,512]{1,0:T(8,128)(2,1)} %collective-permute-done.24.other_far_ref, ...), custom_call_target="tpu_custom_call" | custom-call | flops 115000000512 | bytes 1 | tf_op jit(solution)/shard_map/last/pallas_call | solution.py:648
  114.5 1.4 %collective-permute-start.33 = (bf16[256,512]{1,0:T(8,128)(2,1)}, bf16[256,512]{1,0:T(8,128)(2,1)}, u32[]{:S(2)}, u32[]{:S(2)}) collective-permute-start(bf16[256,512]{1,0:T(8,128)(2,1)} %collective-permute-done.31.own_ref), channel_id=1, source_target_pairs={{0,4},{4,0},{8,12},{12,8},{16,20},{20,16},{24,28},{28,24},{1,5},{5... | collective-permute-start | bytes 786440 | tf_op jit(solution)/shard_map/feed_weights/ppermute | solution.py:624
  116.0 1.2 collective-permute-done.30.b_ref
  117.2 1.7 %merge.3.near_ref = bf16[272,512]{1,0:T(8,128)(2,1)} custom-call(bf16[144,512]{1,0:T(8,128)(2,1)} %merge.2.a_ref, bf16[144,512]{1,0:T(8,128)(2,1)} %collective-permute-done.30.b_ref), custom_call_target="tpu_custom_call" | custom-call | flops 115000000512 | bytes 1 | tf_op jit(solution)/shard_map/merge/pallas_call | solution.py:986
  118.9 2.0 %collective-permute-start.32 = (bf16[272,512]{1,0:T(8,128)(2,1)}, bf16[272,512]{1,0:T(8,128)(2,1)}, u32[]{:S(2)}, u32[]{:S(2)}) collective-permute-start(bf16[272,512]{1,0:T(8,128)(2,1)} %merge.3.near_ref), channel_id=1, source_target_pairs={{0,8},{4,12},{8,0},{12,4},{16,24},{20,28},{24,16},{28,20},{1,9},{5... | collective-permute-start | bytes 835592 | tf_op jit(solution)/shard_map/rest_weights/ppermute | solution.py:624
  120.8 2.1 %feed_unpack.2 = (f32[512,512]{1,0:T(8,128)}, f32[512,512]{1,0:T(8,128)}) custom-call(s32[1]{0:T(128)S(6)} %add.19.at_ref, bf16[256,512]{1,0:T(8,128)(2,1)} %concat.1.own_ref, bf16[256,512]{1,0:T(8,128)(2,1)} %collective-permute-done.34.one_ref), custom_call_target="tpu_custom_call" | custom-call | flops 115000000512 | bytes 1 | tf_op jit(solution)/shard_map/feed_unpack/pallas_call | solution.py:962
  123.3 2.1 %feed_unpack.3 = (f32[512,512]{1,0:T(8,128)}, f32[512,512]{1,0:T(8,128)}) custom-call(s32[1]{0:T(128)S(6)} %add.19.at_ref, bf16[256,512]{1,0:T(8,128)(2,1)} %collective-permute-done.31.own_ref, bf16[256,512]{1,0:T(8,128)(2,1)} %collective-permute-done.33.one_ref, ...), custom_call_target="tpu_custom_call", output_to_operand_aliasing={{0}: (3, {}), {1}: (4, {})} | custom-call | flops 115000000512 | bytes 1 | tf_op jit(solution)/shard_map/feed_unpack/pallas_call | solution.py:962
  125.4 1.3 collective-permute-done.32.far_ref
  126.6 2.1 %rest_unpack.1 = (f32[3,512,128]{2,1,0:T(8,128)}, f32[128,512]{1,0:T(8,128)}, f32[1,512]{1,0:T(1,128)}, f32[1,512]{1,0:T(1,128)}, f32[1,512]{1,0:T(1,128)}, /*in...) custom-call(s32[1]{0:T(128)S(6)} %add.19.at_ref, bf16[272,512]{1,0:T(8,128)(2,1)} %merge.3.near_ref, ...), custom_call_target="tpu_custom_call" | custom-call | flops 115000000512 | bytes 1 | tf_op jit(solution)/shard_map/rest_unpack/pallas_call | solution.py:648
  (123 shorter events, 2.4 us)
Async XLA Ops:
  0.6 6.9 %collective-permute-start = (bf16[128,512]{1,0:T(8,128)(2,1)}, bf16[128,512]{1,0:T(8,128)(2,1)S(1)}, u32[]{:S(2)}, u32[]{:S(2)}) collective-permute-start(bf16[128,512]{1,0:T(8,128)(2,1)} %wo_ref), channel_id=1, source_target_pairs={{0,2},{1,3},{2,0},{3,1},{4,6},{5,7},{6,4},{7,5},{8,10},{9,11},{10,... | collective-permute-start | bytes 393224 | tf_op jit(solution)/shard_map/gather_w_out/ppermute | solution.py:624
  7.6 5.7 %copy-start.38 = (bf16[128,512]{1,0:T(8,128)(2,1)}, bf16[128,512]{1,0:T(8,128)(2,1)S(1)}, u32[]{:S(2)}) copy-start(bf16[128,512]{1,0:T(8,128)(2,1)S(1)} %collective-permute-done.refs_6_) | copy-start | bytes 393220
  7.6 5.7 %copy-start.12 = (bf16[128,512]{1,0:T(8,128)(2,1)S(1)}, bf16[128,512]{1,0:T(8,128)(2,1)}, u32[]{:S(2)}) copy-start(bf16[128,512]{1,0:T(8,128)(2,1)} %wo_ref) | copy-start | bytes 393220
  7.6 4.1 %collective-permute-start.1 = (bf16[1,5,16,128]{3,2,1,0:T(8,128)(2,1)}, bf16[1,5,16,128]{3,2,1,0:T(8,128)(2,1)S(1)}, u32[]{:S(2)}, u32[]{:S(2)}) collective-permute-start(bf16[1,5,16,128]{3,2,1,0:T(8,128)(2,1)} %bitcast.27), channel_id=1, source_target_pairs={{0,4},{4,0},{8,12},{12,8},{16,20},{20,16},{24,28},{28,24},{1,5},{5... | collective-permute-start | bytes 61448 | tf_op jit(solution)/shard_map/summaries/ppermute | solution.py:624
  11.7 4.1 %collective-permute-start.2 = (bf16[2,5,16,128]{3,2,1,0:T(8,128)(2,1)S(1)}, bf16[2,5,16,128]{3,2,1,0:T(8,128)(2,1)S(1)}, u32[]{:S(2)}, u32[]{:S(2)}) collective-permute-start(bf16[2,5,16,128]{3,2,1,0:T(8,128)(2,1)S(1)} %constant_dynamic-update-slice_fusion), channel_id=1, source_target_pairs={{0,8},{4,12},{8,0},{12,4},{16,24},{20,28},{24,16},{28,20},{1,9},{5... | collective-permute-start | bytes 122888 | tf_op jit(solution)/shard_map/summaries/ppermute | solution.py:624
  13.3 2.4 %collective-permute-start.3 = (bf16[128,512]{1,0:T(8,128)(2,1)S(1)}, bf16[128,512]{1,0:T(8,128)(2,1)S(1)}, u32[]{:S(2)}, u32[]{:S(2)}) collective-permute-start(bf16[128,512]{1,0:T(8,128)(2,1)S(1)} %copy-done.12), channel_id=1, source_target_pairs={{0,1},{1,0},{2,3},{3,2},{4,5},{5,4},{6,7},{7,6},{8,9},{9,8},{10,11... | collective-permute-start | bytes 393224 | tf_op jit(solution)/shard_map/gather_w_out/ppermute | solution.py:624
  13.3 2.5 %collective-permute-start.4 = (bf16[128,512]{1,0:T(8,128)(2,1)S(1)}, bf16[128,512]{1,0:T(8,128)(2,1)S(1)}, u32[]{:S(2)}, u32[]{:S(2)}) collective-permute-start(bf16[128,512]{1,0:T(8,128)(2,1)S(1)} %collective-permute-done.refs_6_), channel_id=1, source_target_pairs={{0,1},{1,0},{2,3},{3,2},{4,5},{5,4},{6,7},{7,6},{8,9},{9,8},{10,11... | collective-permute-start | bytes 393224 | tf_op jit(solution)/shard_map/gather_w_out/ppermute | solution.py:624
  17.3 9.2 %copy-start.11 = (bf16[1024,128]{1,0:T(8,128)(2,1)}, bf16[1024,128]{1,0:T(8,128)(2,1)S(1)}, u32[]{:S(2)}) copy-start(bf16[1024,128]{1,0:T(8,128)(2,1)S(1)} %get-tuple-element.296.refs_0_.att_ref) | copy-start | bytes 786436
  17.4 7.6 %collective-permute-start.6 = (bf16[1024,128]{1,0:T(8,128)(2,1)S(1)}, bf16[1024,128]{1,0:T(8,128)(2,1)S(1)}, u32[]{:S(2)}, u32[]{:S(2)}) collective-permute-start(bf16[1024,128]{1,0:T(8,128)(2,1)S(1)} %get-tuple-element.296.refs_0_.att_ref), channel_id=1, source_target_pairs={{0,2},{1,3},{2,0},{3,1},{4,6},{5,7},{6,4},{7,5},{8,10},{9,11},{10,... | collective-permute-start | bytes 786440 | tf_op jit(solution)/shard_map/gather_attended/ppermute | solution.py:624
  18.9 6.7 %collective-permute-start.5 = (bf16[1024,128]{1,0:T(8,128)(2,1)S(1)}, bf16[1024,128]{1,0:T(8,128)(2,1)S(1)}, u32[]{:S(2)}, u32[]{:S(2)}) collective-permute-start(bf16[1024,128]{1,0:T(8,128)(2,1)S(1)} %get-tuple-element.296.refs_0_.att_ref), channel_id=1, source_target_pairs={{0,1},{1,0},{2,3},{3,2},{4,5},{5,4},{6,7},{7,6},{8,9},{9,8},{10,11... | collective-permute-start | bytes 786440 | tf_op jit(solution)/shard_map/gather_attended/ppermute | solution.py:624
  25.0 1.5 %collective-permute-start.7 = (bf16[1024,128]{1,0:T(8,128)(2,1)S(1)}, bf16[1024,128]{1,0:T(8,128)(2,1)S(1)}, u32[]{:S(2)}, u32[]{:S(2)}) collective-permute-start(bf16[1024,128]{1,0:T(8,128)(2,1)S(1)} %collective-permute-done.6.refs_2_), channel_id=1, source_target_pairs={{0,1},{1,0},{2,3},{3,2},{4,5},{5,4},{6,7},{7,6},{8,9},{9,8},{10,11... | collective-permute-start | bytes 786440 | tf_op jit(solution)/shard_map/gather_attended/ppermute | solution.py:624
  36.2 2.2 %collective-permute-start.8 = (bf16[512,512]{1,0:T(8,128)(2,1)}, bf16[512,512]{1,0:T(8,128)(2,1)S(1)}, u32[]{:S(2)}, u32[]{:S(2)}) collective-permute-start(bf16[512,512]{1,0:T(8,128)(2,1)} %get-tuple-element.250), channel_id=1, source_target_pairs={{0,1},{1,0},{2,3},{3,2},{4,5},{5,4},{6,7},{7,6},{8,9},{9,8},{10,11... | collective-permute-start | bytes 1572872 | tf_op jit(solution)/shard_map/sum_second/ppermute | solution.py:624
  37.5 3.3 %copy-start.3 = (s32[4]{0:T(128)S(1)}, s32[4]{0:T(128)}, u32[]{:S(2)}) copy-start(s32[4]{0:T(128)} %pad_add_fusion.pos_ref) | copy-start | bytes 52
  37.5 3.3 %copy-start.6 = (bf16[1024,512]{1,0:T(8,128)(2,1)S(1)}, bf16[1024,512]{1,0:T(8,128)(2,1)}, u32[]{:S(2)}) copy-start(bf16[1024,512]{1,0:T(8,128)(2,1)} %cot_ref.1) | copy-start | bytes 3145732
  37.5 3.3 %copy-start.9 = (bf16[512,512]{1,0:T(8,128)(2,1)S(1)}, bf16[512,512]{1,0:T(8,128)(2,1)}, u32[]{:S(2)}) copy-start(bf16[512,512]{1,0:T(8,128)(2,1)} %down_ref) | copy-start | bytes 1572868
  37.5 3.3 %copy-start.22 = (bf16[1024,512]{1,0:T(8,128)(2,1)S(1)}, bf16[1024,512]{1,0:T(8,128)(2,1)}, u32[]{:S(2)}) copy-start(bf16[1024,512]{1,0:T(8,128)(2,1)} %get-tuple-element.255.second_ref) | copy-start | bytes 3145732
  37.5 3.3 %copy-start.23 = (bf16[1024,512]{1,0:T(8,128)(2,1)S(1)}, bf16[1024,512]{1,0:T(8,128)(2,1)}, u32[]{:S(2)}) copy-start(bf16[1024,512]{1,0:T(8,128)(2,1)} %get-tuple-element.254.active_ref) | copy-start | bytes 3145732
  37.5 3.3 %copy-start.24 = (bf16[1024,512]{1,0:T(8,128)(2,1)S(1)}, bf16[1024,512]{1,0:T(8,128)(2,1)}, u32[]{:S(2)}) copy-start(bf16[1024,512]{1,0:T(8,128)(2,1)} %get-tuple-element.256.grad_ref) | copy-start | bytes 3145732
  39.3 14.3 %collective-permute-start.10 = (bf16[512,512]{1,0:T(8,128)(2,1)}, bf16[512,512]{1,0:T(8,128)(2,1)}, u32[]{:S(2)}, u32[]{:S(2)}) collective-permute-start(bf16[512,512]{1,0:T(8,128)(2,1)} %add.26.own_ref), channel_id=1, source_target_pairs={{0,2},{1,3},{2,0},{3,1},{4,6},{5,7},{6,4},{7,5},{8,10},{9,11},{10,... | collective-permute-start | bytes 1572872 | tf_op jit(solution)/shard_map/sum_second/ppermute | solution.py:624
  40.8 14.8 %collective-permute-start.12 = (bf16[512,512]{1,0:T(8,128)(2,1)}, bf16[512,512]{1,0:T(8,128)(2,1)}, u32[]{:S(2)}, u32[]{:S(2)}) collective-permute-start(bf16[512,512]{1,0:T(8,128)(2,1)} %add.26.own_ref), channel_id=1, source_target_pairs={{0,1},{1,0},{2,3},{3,2},{4,5},{5,4},{6,7},{7,6},{8,9},{9,8},{10,11... | collective-permute-start | bytes 1572872 | tf_op jit(solution)/shard_map/sum_second/ppermute | solution.py:624
  40.8 4.3 %copy-start.16 = (f32[512]{0:T(512)S(1)}, f32[512]{0:T(512)}, u32[]{:S(2)}) copy-start(f32[512]{0:T(512)} %param.14) | copy-start | bytes 6148
  44.7 2.0 %collective-permute-start.9 = (bf16[512,512]{1,0:T(8,128)(2,1)S(1)}, bf16[512,512]{1,0:T(8,128)(2,1)S(1)}, u32[]{:S(2)}, u32[]{:S(2)}) collective-permute-start(bf16[512,512]{1,0:T(8,128)(2,1)S(1)} %get-tuple-element.260), channel_id=1, source_target_pairs={{0,1},{1,0},{2,3},{3,2},{4,5},{5,4},{6,7},{7,6},{8,9},{9,8},{10,11... | collective-permute-start | bytes 1572872 | tf_op jit(solution)/shard_map/sum_output/ppermute | solution.py:624
  45.2 18.1 %collective-permute-start.15 = (bf16[512,512]{1,0:T(8,128)(2,1)}, bf16[512,512]{1,0:T(8,128)(2,1)}, u32[]{:S(2)}, u32[]{:S(2)}) collective-permute-start(bf16[512,512]{1,0:T(8,128)(2,1)} %get-tuple-element.286), channel_id=1, source_target_pairs={{0,8},{4,12},{8,0},{12,4},{16,24},{20,28},{24,16},{28,20},{1,9},{5... | collective-permute-start | bytes 1572872 | tf_op jit(solution)/shard_map/feed_weights/ppermute | solution.py:624
  47.6 8.8 %copy-start.1 = (bf16[4,5,16,128]{3,2,1,0:T(8,128)(2,1)S(1)}, bf16[4,5,16,128]{3,2,1,0:T(8,128)(2,1)}, u32[]{:S(2)}) copy-start(bf16[4,5,16,128]{3,2,1,0:T(8,128)(2,1)} %copy-done) | copy-start | bytes 245764
  47.6 8.8 %copy-start.4 = (s32[4]{0:T(128)S(1)}, s32[4]{0:T(128)}, u32[]{:S(2)}) copy-start(s32[4]{0:T(128)} %pad_add_fusion.pos_ref) | copy-start | bytes 52
  47.6 8.8 %copy-start.7 = (bf16[1024,512]{1,0:T(8,128)(2,1)S(1)}, bf16[1024,512]{1,0:T(8,128)(2,1)}, u32[]{:S(2)}) copy-start(bf16[1024,512]{1,0:T(8,128)(2,1)} %cot_ref.1) | copy-start | bytes 3145732
  47.6 8.8 %copy-start.13 = (bf16[128,512]{1,0:T(8,128)(2,1)S(1)}, bf16[128,512]{1,0:T(8,128)(2,1)}, u32[]{:S(2)}) copy-start(bf16[128,512]{1,0:T(8,128)(2,1)} %wo_ref) | copy-start | bytes 393220
  47.6 8.8 %copy-start.14 = (f32[512]{0:T(512)S(1)}, f32[512]{0:T(512)}, u32[]{:S(2)}) copy-start(f32[512]{0:T(512)} %param.19) | copy-start | bytes 6148
  47.6 8.8 %copy-start.18 = (f32[1024,512]{1,0:T(8,128)S(1)}, f32[1024,512]{1,0:T(8,128)}, u32[]{:S(2)}) copy-start(f32[1024,512]{1,0:T(8,128)} %get-tuple-element.326.mid_ref) | copy-start | bytes 6291460
  47.6 8.8 %copy-start.26 = (bf16[3,1024,128]{2,1,0:T(8,128)(2,1)S(1)}, bf16[3,1024,128]{2,1,0:T(8,128)(2,1)}, u32[]{:S(2)}) copy-start(bf16[3,1024,128]{2,1,0:T(8,128)(2,1)} %get-tuple-element.280.qkv_ref) | copy-start | bytes 2359300
  53.6 2.8 %collective-permute-start.13 = (bf16[512,512]{1,0:T(8,128)(2,1)}, bf16[512,512]{1,0:T(8,128)(2,1)S(1)}, u32[]{:S(2)}, u32[]{:S(2)}) collective-permute-start(bf16[512,512]{1,0:T(8,128)(2,1)} %collective-permute-done.10.far_ref), channel_id=1, source_target_pairs={{0,1},{1,0},{2,3},{3,2},{4,5},{5,4},{6,7},{7,6},{8,9},{9,8},{10,11... | collective-permute-start | bytes 1572872 | tf_op jit(solution)/shard_map/sum_second/ppermute | solution.py:624
  53.6 11.4 %collective-permute-start.14 = (bf16[512,512]{1,0:T(8,128)(2,1)}, bf16[512,512]{1,0:T(8,128)(2,1)}, u32[]{:S(2)}, u32[]{:S(2)}) collective-permute-start(bf16[512,512]{1,0:T(8,128)(2,1)} %add.27.own_ref), channel_id=1, source_target_pairs={{0,1},{1,0},{2,3},{3,2},{4,5},{5,4},{6,7},{7,6},{8,9},{9,8},{10,11... | collective-permute-start | bytes 1572872 | tf_op jit(solution)/shard_map/sum_output/ppermute | solution.py:624
  54.1 14.9 %collective-permute-start.11 = (bf16[512,512]{1,0:T(8,128)(2,1)}, bf16[512,512]{1,0:T(8,128)(2,1)}, u32[]{:S(2)}, u32[]{:S(2)}) collective-permute-start(bf16[512,512]{1,0:T(8,128)(2,1)} %add.27.own_ref), channel_id=1, source_target_pairs={{0,2},{1,3},{2,0},{3,1},{4,6},{5,7},{6,4},{7,5},{8,10},{9,11},{10,... | collective-permute-start | bytes 1572872 | tf_op jit(solution)/shard_map/sum_output/ppermute | solution.py:624
  65.0 5.6 %copy-start.2 = (bf16[4,5,16,128]{3,2,1,0:T(8,128)(2,1)S(1)}, bf16[4,5,16,128]{3,2,1,0:T(8,128)(2,1)}, u32[]{:S(2)}) copy-start(bf16[4,5,16,128]{3,2,1,0:T(8,128)(2,1)} %copy-done) | copy-start | bytes 245764
  65.0 5.6 %copy-start.5 = (s32[4]{0:T(128)S(1)}, s32[4]{0:T(128)}, u32[]{:S(2)}) copy-start(s32[4]{0:T(128)} %pad_add_fusion.pos_ref) | copy-start | bytes 52
  65.0 5.6 %copy-start.8 = (bf16[1024,512]{1,0:T(8,128)(2,1)S(1)}, bf16[1024,512]{1,0:T(8,128)(2,1)}, u32[]{:S(2)}) copy-start(bf16[1024,512]{1,0:T(8,128)(2,1)} %tok_ref.3) | copy-start | bytes 3145732
  65.0 5.6 %copy-start.10 = (bf16[3,512,128]{2,1,0:T(8,128)(2,1)S(1)}, bf16[3,512,128]{2,1,0:T(8,128)(2,1)}, u32[]{:S(2)}) copy-start(bf16[3,512,128]{2,1,0:T(8,128)(2,1)} %w_ref.2) | copy-start | bytes 1179652
  65.0 5.6 %copy-start.28 = (bf16[1024,384]{1,0:T(8,128)(2,1)S(1)}, bf16[1024,384]{1,0:T(8,128)(2,1)}, u32[]{:S(2)}) copy-start(bf16[1024,384]{1,0:T(8,128)(2,1)} %copy-done.27) | copy-start | bytes 2359300
  65.0 5.6 %copy-start.32 = (f32[4,2,8,128]{3,2,1,0:T(8,128)S(1)}, f32[4,2,8,128]{3,2,1,0:T(8,128)}, u32[]{:S(2)}) copy-start(f32[4,2,8,128]{3,2,1,0:T(8,128)} %copy-done.31) | copy-start | bytes 98308
  69.0 16.2 %collective-permute-start.16 = (bf16[512,512]{1,0:T(8,128)(2,1)}, bf16[512,512]{1,0:T(8,128)(2,1)}, u32[]{:S(2)}, u32[]{:S(2)}) collective-permute-start(bf16[512,512]{1,0:T(8,128)(2,1)} %collective-permute-done.11.far_ref), channel_id=1, source_target_pairs={{0,1},{1,0},{2,3},{3,2},{4,5},{5,4},{6,7},{7,6},{8,9},{9,8},{10,11... | collective-permute-start | bytes 1572872 | tf_op jit(solution)/shard_map/sum_output/ppermute | solution.py:624
  69.1 8.6 %collective-permute-start.19 = (bf16[256,512]{1,0:T(8,128)(2,1)S(1)}, bf16[256,512]{1,0:T(8,128)(2,1)S(1)}, u32[]{:S(2)}, u32[]{:S(2)}) collective-permute-start(bf16[256,512]{1,0:T(8,128)(2,1)S(1)} %get-tuple-element.310), channel_id=1, source_target_pairs={{0,4},{4,0},{8,12},{12,8},{16,20},{20,16},{24,28},{28,24},{1,5},{5... | collective-permute-start | bytes 786440 | tf_op jit(solution)/shard_map/feed_weights/ppermute | solution.py:624
  72.7 8.3 %collective-permute-start.18 = (bf16[528,512]{1,0:T(8,128)(2,1)S(1)}, bf16[528,512]{1,0:T(8,128)(2,1)S(1)}, u32[]{:S(2)}, u32[]{:S(2)}) collective-permute-start(bf16[528,512]{1,0:T(8,128)(2,1)S(1)} %get-tuple-element.309), channel_id=1, source_target_pairs={{0,1},{1,0},{2,3},{3,2},{4,5},{5,4},{6,7},{7,6},{8,9},{9,8},{10,11... | collective-permute-start | bytes 1622024 | tf_op jit(solution)/shard_map/sum_first/ppermute | solution.py:624
  72.8 11.3 %collective-permute-start.17 = (bf16[272,512]{1,0:T(8,128)(2,1)}, bf16[272,512]{1,0:T(8,128)(2,1)}, u32[]{:S(2)}, u32[]{:S(2)}) collective-permute-start(bf16[272,512]{1,0:T(8,128)(2,1)} %get-tuple-element.301), channel_id=1, source_target_pairs={{0,8},{4,12},{8,0},{12,4},{16,24},{20,28},{24,16},{28,20},{1,9},{5... | collective-permute-start | bytes 835592 | tf_op jit(solution)/shard_map/rest_weights/ppermute | solution.py:624
  78.4 12.8 %collective-permute-start.21 = (bf16[128,512]{1,0:T(8,128)(2,1)}, bf16[128,512]{1,0:T(8,128)(2,1)}, u32[]{:S(2)}, u32[]{:S(2)}) collective-permute-start(bf16[128,512]{1,0:T(8,128)(2,1)} %get-tuple-element.328), channel_id=1, source_target_pairs={{0,16},{4,20},{8,24},{12,28},{16,0},{20,4},{24,8},{28,12},{1,17},{... | collective-permute-start | bytes 393224 | tf_op jit(solution)/shard_map/feed_weights/ppermute | solution.py:624
  81.0 3.1 %copy-start.30 = (bf16[272,512]{1,0:T(8,128)(2,1)S(1)}, bf16[272,512]{1,0:T(8,128)(2,1)}, u32[]{:S(2)}) copy-start(bf16[272,512]{1,0:T(8,128)(2,1)} %get-tuple-element.318.a_ref) | copy-start | bytes 835588
  81.9 4.1 %copy-start.15 = (f32[512]{0:T(512)S(1)}, f32[512]{0:T(512)}, u32[]{:S(2)}) copy-start(f32[512]{0:T(512)} %param.24) | copy-start | bytes 6148
  82.0 4.1 %copy-start.19 = (f32[1024,512]{1,0:T(8,128)S(1)}, f32[1024,512]{1,0:T(8,128)}, u32[]{:S(2)}) copy-start(f32[1024,512]{1,0:T(8,128)} %get-tuple-element.326.mid_ref) | copy-start | bytes 6291460
  82.0 13.9 %collective-permute-start.20 = (bf16[528,512]{1,0:T(8,128)(2,1)}, bf16[528,512]{1,0:T(8,128)(2,1)}, u32[]{:S(2)}, u32[]{:S(2)}) collective-permute-start(bf16[528,512]{1,0:T(8,128)(2,1)} %pair.1.near_ref.own_ref), channel_id=1, source_target_pairs={{0,2},{1,3},{2,0},{3,1},{4,6},{5,7},{6,4},{7,5},{8,10},{9,11},{10,... | collective-permute-start | bytes 1622024 | tf_op jit(solution)/shard_map/sum_first/ppermute | solution.py:624
  85.2 5.2 %collective-permute-start.22 = (bf16[144,512]{1,0:T(8,128)(2,1)S(1)}, bf16[144,512]{1,0:T(8,128)(2,1)S(1)}, u32[]{:S(2)}, u32[]{:S(2)}) collective-permute-start(bf16[144,512]{1,0:T(8,128)(2,1)S(1)} %get-tuple-element.329), channel_id=1, source_target_pairs={{0,4},{4,0},{8,12},{12,8},{16,20},{20,16},{24,28},{28,24},{1,5},{5... | collective-permute-start | bytes 442376 | tf_op jit(solution)/shard_map/rest_weights/ppermute | solution.py:624
  91.2 4.7 %collective-permute-start.25 = (f32[8,512]{1,0:T(8,128)S(1)}, f32[8,512]{1,0:T(8,128)S(1)}, u32[]{:S(2)}, u32[]{:S(2)}) collective-permute-start(f32[8,512]{1,0:T(8,128)S(1)} %get-tuple-element.339.a_ref), channel_id=1, source_target_pairs={{0,1},{1,0},{2,3},{3,2},{4,5},{5,4},{6,7},{7,6},{8,9},{9,8},{10,11... | collective-permute-start | bytes 49160 | tf_op jit(solution)/shard_map/sum_extra/ppermute | solution.py:624
  91.2 6.7 %collective-permute-start.27 = (bf16[64,512]{1,0:T(8,128)(2,1)}, bf16[64,512]{1,0:T(8,128)(2,1)}, u32[]{:S(2)}, u32[]{:S(2)}) collective-permute-start(bf16[64,512]{1,0:T(8,128)(2,1)} %get-tuple-element.342), channel_id=1, source_target_pairs={{0,16},{4,20},{8,24},{12,28},{16,0},{20,4},{24,8},{28,12},{1,17},{... | collective-permute-start | bytes 196616 | tf_op jit(solution)/shard_map/rest_weights/ppermute | solution.py:624
  93.8 4.1 %copy-start.33 = (f32[8,512]{1,0:T(8,128)S(1)}, f32[8,512]{1,0:T(8,128)}, u32[]{:S(2)}) copy-start(f32[8,512]{1,0:T(8,128)} %get-tuple-element.349.up_ref) | copy-start | bytes 49156
  93.8 11.7 %collective-permute-start.29 = (bf16[128,512]{1,0:T(8,128)(2,1)}, bf16[128,512]{1,0:T(8,128)(2,1)}, u32[]{:S(2)}, u32[]{:S(2)}) collective-permute-start(bf16[128,512]{1,0:T(8,128)(2,1)} %add.28.a_ref), channel_id=1, source_target_pairs={{0,16},{4,20},{8,24},{12,28},{16,0},{20,4},{24,8},{28,12},{1,17},{... | collective-permute-start | bytes 393224 | tf_op jit(solution)/shard_map/feed_weights/ppermute | solution.py:624
  95.8 14.2 %collective-permute-start.24 = (bf16[528,512]{1,0:T(8,128)(2,1)}, bf16[528,512]{1,0:T(8,128)(2,1)}, u32[]{:S(2)}, u32[]{:S(2)}) collective-permute-start(bf16[528,512]{1,0:T(8,128)(2,1)} %collective-permute-done.20.far_ref), channel_id=1, source_target_pairs={{0,1},{1,0},{2,3},{3,2},{4,5},{5,4},{6,7},{7,6},{8,9},{9,8},{10,11... | collective-permute-start | bytes 1622024 | tf_op jit(solution)/shard_map/sum_first/ppermute | solution.py:624
  96.4 11.7 %collective-permute-start.26 = (f32[8,512]{1,0:T(8,128)}, f32[8,512]{1,0:T(8,128)}, u32[]{:S(2)}, u32[]{:S(2)}) collective-permute-start(f32[8,512]{1,0:T(8,128)} %plus.1.extra_ref), channel_id=1, source_target_pairs={{0,2},{1,3},{2,0},{3,1},{4,6},{5,7},{6,4},{7,5},{8,10},{9,11},{10,... | collective-permute-start | bytes 49160 | tf_op jit(solution)/shard_map/sum_extra/ppermute | solution.py:624
  99.2 8.1 %collective-permute-start.28 = (bf16[80,512]{1,0:T(8,128)(2,1)S(1)}, bf16[80,512]{1,0:T(8,128)(2,1)S(1)}, u32[]{:S(2)}, u32[]{:S(2)}) collective-permute-start(bf16[80,512]{1,0:T(8,128)(2,1)S(1)} %piece.1.a_ref), channel_id=1, source_target_pairs={{0,16},{4,20},{8,24},{12,28},{16,0},{20,4},{24,8},{28,12},{1,17},{... | collective-permute-start | bytes 245768 | tf_op jit(solution)/shard_map/rest_weights/ppermute | solution.py:624
  107.2 2.8 %copy-start.17 = (f32[512]{0:T(512)S(1)}, f32[512]{0:T(512)}, u32[]{:S(2)}) copy-start(f32[512]{0:T(512)} %param.14) | copy-start | bytes 6148
  107.2 2.8 %copy-start.21 = (bf16[1024,512]{1,0:T(8,128)(2,1)S(1)}, bf16[1024,512]{1,0:T(8,128)(2,1)}, u32[]{:S(2)}) copy-start(bf16[1024,512]{1,0:T(8,128)(2,1)} %copy-done.20) | copy-start | bytes 3145732
  107.2 7.3 %collective-permute-start.31 = (bf16[256,512]{1,0:T(8,128)(2,1)}, bf16[256,512]{1,0:T(8,128)(2,1)}, u32[]{:S(2)}, u32[]{:S(2)}) collective-permute-start(bf16[256,512]{1,0:T(8,128)(2,1)} %concat.1.own_ref), channel_id=1, source_target_pairs={{0,8},{4,12},{8,0},{12,4},{16,24},{20,28},{24,16},{28,20},{1,9},{5... | collective-permute-start | bytes 786440 | tf_op jit(solution)/shard_map/feed_weights/ppermute | solution.py:624
  107.2 13.6 %collective-permute-start.34 = (bf16[256,512]{1,0:T(8,128)(2,1)}, bf16[256,512]{1,0:T(8,128)(2,1)}, u32[]{:S(2)}, u32[]{:S(2)}) collective-permute-start(bf16[256,512]{1,0:T(8,128)(2,1)} %concat.1.own_ref), channel_id=1, source_target_pairs={{0,4},{4,0},{8,12},{12,8},{16,20},{20,16},{24,28},{28,24},{1,5},{5... | collective-permute-start | bytes 786440 | tf_op jit(solution)/shard_map/feed_weights/ppermute | solution.py:624
  107.3 2.7 %collective-permute-start.23 = (bf16[528,512]{1,0:T(8,128)(2,1)}, bf16[528,512]{1,0:T(8,128)(2,1)S(1)}, u32[]{:S(2)}, u32[]{:S(2)}) collective-permute-start(bf16[528,512]{1,0:T(8,128)(2,1)} %pair.1.near_ref.own_ref), channel_id=1, source_target_pairs={{0,1},{1,0},{2,3},{3,2},{4,5},{5,4},{6,7},{7,6},{8,9},{9,8},{10,11... | collective-permute-start | bytes 1622024 | tf_op jit(solution)/shard_map/sum_first/ppermute | solution.py:624
  108.1 9.1 %collective-permute-start.30 = (bf16[144,512]{1,0:T(8,128)(2,1)}, bf16[144,512]{1,0:T(8,128)(2,1)}, u32[]{:S(2)}, u32[]{:S(2)}) collective-permute-start(bf16[144,512]{1,0:T(8,128)(2,1)} %merge.2.a_ref), channel_id=1, source_target_pairs={{0,4},{4,0},{8,12},{12,8},{16,20},{20,16},{24,28},{28,24},{1,5},{5... | collective-permute-start | bytes 442376 | tf_op jit(solution)/shard_map/rest_weights/ppermute | solution.py:624
  114.5 8.8 %collective-permute-start.33 = (bf16[256,512]{1,0:T(8,128)(2,1)}, bf16[256,512]{1,0:T(8,128)(2,1)}, u32[]{:S(2)}, u32[]{:S(2)}) collective-permute-start(bf16[256,512]{1,0:T(8,128)(2,1)} %collective-permute-done.31.own_ref), channel_id=1, source_target_pairs={{0,4},{4,0},{8,12},{12,8},{16,20},{20,16},{24,28},{28,24},{1,5},{5... | collective-permute-start | bytes 786440 | tf_op jit(solution)/shard_map/feed_weights/ppermute | solution.py:624
  118.9 7.8 %collective-permute-start.32 = (bf16[272,512]{1,0:T(8,128)(2,1)}, bf16[272,512]{1,0:T(8,128)(2,1)}, u32[]{:S(2)}, u32[]{:S(2)}) collective-permute-start(bf16[272,512]{1,0:T(8,128)(2,1)} %merge.3.near_ref), channel_id=1, source_target_pairs={{0,8},{4,12},{8,0},{12,4},{16,24},{20,28},{24,16},{28,20},{1,9},{5... | collective-permute-start | bytes 835592 | tf_op jit(solution)/shard_map/rest_weights/ppermute | solution.py:624
  (12 other events, 16.4 us)

commit v8 on v7

--- a/solution.py
+++ b/solution.py
@@ -31,7 +31,7 @@
 
 
 def cost():
-    return pl.CostEstimate(flops=115_000_000_000, bytes_accessed=1, transcendentals=0)
+    return pl.CostEstimate(flops=12_000_000_000, bytes_accessed=1, transcendentals=0)
 
 
 def nt(a, b):

time: 129 us -> 122 us (0.946)
  Pallas kernels: 60.1 us -> 38.4 us
  waiting for transfers between devices: 32.9 us -> 46 us
  local copies, waits for them, and re-layouts: 3.08 us -> 5.2 us
  starting transfers between devices: 30.9 us -> 29.4 us
    ppermute x35, waiting for transfers between devices: 32.9 us -> 46 us  [swap(): return lax.ppermute(x, axis, [(i, i ^ mask) for i in range(n)])]
    pallas_call x7, Pallas kernels: 6.94 us -> 0.29 us  [like(): return plain(kernel, name, specs, (sds(shape, dtype),))(*operands)[0]]
    pallas_call x12, Pallas kernels: 36.4 us -> 30.1 us  [__call__(): result = work(*inputs)]
    pallas_call x3, Pallas kernels: 3.42 us -> 0.28 us  [add_parts(): pl.pallas_call(functools.partial(add_kernel, parts), out_shape=(part,) *...]
    unnamed x84 -> x78, local copies, waits for them, and re-layouts: 3.06 us -> 5.18 us
    pallas_call x2, Pallas kernels: 2.34 us -> 0.24 us  [split_sum(): pl.pallas_call(split_kernel, out_shape=(half, half), in_specs=[SMEM, VMEM...]
    pallas_call x2, Pallas kernels: 4.14 us -> 2.08 us  [feed_unpack(): pl.pallas_call(functools.partial(feed_unpack_kernel, n_dp // 4, 1 if held...]
    ppermute x35, starting transfers between devices: 30.9 us -> 29.4 us  [swap(): return lax.ppermute(x, axis, [(i, i ^ mask) for i in range(n)])]
  transfers between devices with their start and end apart: 35 -> 35, of which waited for: 16 -> 19; matrix products, arithmetic and copies ran while one was open for 0% -> 0% of each run, Pallas kernels for 36% -> 22%
where the time goes in v8:
time: 122 us; the launch traced here: 121 us
  waiting for transfers between devices  46 us (38%)
  Pallas kernels  38.4 us (31%)
  starting transfers between devices  29.4 us (24%)
  local copies, waits for them, and re-layouts  5.2 us (4%)
    ppermute x35, waiting for transfers between devices, swap(): return lax.ppermute(x, axis, [(i, i ^ mask) for i in range(n)])  46 us
    pallas_call x12, Pallas kernels, __call__(): result = work(*inputs)  30.1 us
    ppermute x35, starting transfers between devices, swap(): return lax.ppermute(x, axis, [(i, i ^ mask) for i in range(n)])  29.4 us
    pallas_call x1, Pallas kernels, per_device(): back(*a)  5.48 us
    unnamed x78, local copies, waits for them, and re-layouts  5.18 us
  transfers between devices with their start and end apart: 35, of which 19 were waited for; matrix products, arithmetic and copies ran while one was open for 0% of the time, Pallas kernels for 22%

profile of v8, /device:TPU:0, one launch (start us, length us, event | category | flops | bytes accessed | tf_op | source)
XLA Modules:
  0.0 120.9 jit_solution(911930314742563675)
XLA Ops:
  0.6 3.0 %collective-permute-start = (bf16[128,512]{1,0:T(8,128)(2,1)}, bf16[128,512]{1,0:T(8,128)(2,1)S(1)}, u32[]{:S(2)}, u32[]{:S(2)}) collective-permute-start(bf16[128,512]{1,0:T(8,128)(2,1)} %wo_ref), channel_id=1, source_target_pairs={{0,2},{1,3},{2,0},{3,1},{4,6},{5,7},{6,4},{7,5},{8,10},{9,11},{10,... | collective-permute-start | bytes 393224 | tf_op jit(solution)/shard_map/gather_w_out/ppermute | solution.py:624
  3.7 3.9 %project.1 = (bf16[1024,512]{1,0:T(8,128)(2,1)}, bf16[3,1024,128]{2,1,0:T(8,128)(2,1)}, bf16[5,16,128]{2,1,0:T(8,128)(2,1)}) custom-call(bf16[1024,512]{1,0:T(8,128)(2,1)} %tok_ref.3, f32[1,512]{1,0:T(1,128)} %bitcast.24, f32[1,512]{1,0:T(1,128)} %bitcast.29, bf16[3,512,128]{2,1,0:T(8,128)(2,1)} %w_ref.2), custom_call_target="tpu_custom_call" | custom-call | flops 12000000000 | bytes 1 | tf_op jit(solution)/shard_map/project/pallas_call | solution.py:648
  7.6 1.6 %collective-permute-start.1 = (bf16[1,5,16,128]{3,2,1,0:T(8,128)(2,1)}, bf16[1,5,16,128]{3,2,1,0:T(8,128)(2,1)S(1)}, u32[]{:S(2)}, u32[]{:S(2)}) collective-permute-start(bf16[1,5,16,128]{3,2,1,0:T(8,128)(2,1)} %bitcast.27), channel_id=1, source_target_pairs={{0,4},{4,0},{8,12},{12,8},{16,20},{20,16},{24,28},{28,24},{1,5},{5... | collective-permute-start | bytes 61448 | tf_op jit(solution)/shard_map/summaries/ppermute | solution.py:624
  9.1 1.1 copy-done.21
  10.3 0.5 local.1
  10.8 0.9 collective-permute-done.1
  11.7 1.6 %collective-permute-start.2 = (bf16[2,5,16,128]{3,2,1,0:T(8,128)(2,1)S(1)}, bf16[2,5,16,128]{3,2,1,0:T(8,128)(2,1)S(1)}, u32[]{:S(2)}, u32[]{:S(2)}) collective-permute-start(bf16[2,5,16,128]{3,2,1,0:T(8,128)(2,1)S(1)} %constant_dynamic-update-slice_fusion), channel_id=1, source_target_pairs={{0,8},{4,12},{8,0},{12,4},{16,24},{20,28},{24,16},{28,20},{1,9},{5... | collective-permute-start | bytes 122888 | tf_op jit(solution)/shard_map/summaries/ppermute | solution.py:624
  13.3 0.5 collective-permute-start.4
  13.8 1.9 %collective-permute-done.2 = bf16[2,5,16,128]{3,2,1,0:T(8,128)(2,1)S(1)} collective-permute-done((bf16[2,5,16,128]{3,2,1,0:T(8,128)(2,1)S(1)}, bf16[2,5,16,128]{3,2,1,0:T(8,128)(2,1)S(1)}, u32[]{:S(2)}, u32[]{:S(2)}) %collective-permute-start.2) | collective-permute-done | bytes 40992 | tf_op jit(solution)/shard_map/summaries/ppermute | solution.py:624
  15.8 1.5 %attend.1 = (bf16[8,160,256]{2,1,0:T(8,128)(2,1)S(1)}, bf16[1024,128]{1,0:T(8,128)(2,1)S(1)}) custom-call(s32[1]{0:T(128)} %bitcast.2.place_ref, bf16[3,1024,128]{2,1,0:T(8,128)(2,1)S(1)} %copy-done.21, f32[8,128,256]{2,1,0:T(8,128)S(1)} %get-tuple-element.222.exp_ref, f32[8,2,256]{2,1,0:T(2,128)S(1)} %get-tuple-element.223.stat_ref, ...), custom_call_target="tpu_custom_call" | custom-call | flops 12000000000 | bytes 1 | tf_op jit(solution)/shard_map/attend/pallas_call | solution.py:648
  17.3 1.5 %collective-permute-start.6 = (bf16[1024,128]{1,0:T(8,128)(2,1)S(1)}, bf16[1024,128]{1,0:T(8,128)(2,1)S(1)}, u32[]{:S(2)}, u32[]{:S(2)}) collective-permute-start(bf16[1024,128]{1,0:T(8,128)(2,1)S(1)} %get-tuple-element.296.refs_0_.att_ref), channel_id=1, source_target_pairs={{0,2},{1,3},{2,0},{3,1},{4,6},{5,7},{6,4},{7,5},{8,10},{9,11},{10,... | collective-permute-start | bytes 786440 | tf_op jit(solution)/shard_map/gather_attended/ppermute | solution.py:624
  18.9 6.1 %collective-permute-done.6.refs_2_ = bf16[1024,128]{1,0:T(8,128)(2,1)S(1)} collective-permute-done((bf16[1024,128]{1,0:T(8,128)(2,1)S(1)}, bf16[1024,128]{1,0:T(8,128)(2,1)S(1)}, u32[]{:S(2)}, u32[]{:S(2)}) %collective-permute-start.6) | collective-permute-done | bytes 262176 | tf_op jit(solution)/shard_map/gather_attended/ppermute | solution.py:624
  25.0 0.6 pad_add_fusion.pos_ref
  25.6 0.9 collective-permute-done.7.refs_3_
  26.5 0.7 copy-done.34
  27.2 8.9 %feed.1 = (f32[1024,512]{1,0:T(8,128)}, bf16[1024,512]{1,0:T(8,128)(2,1)}, bf16[1024,512]{1,0:T(8,128)(2,1)}, bf16[1024,512]{1,0:T(8,128)(2,1)}, bf16[512,512]{1...) custom-call(s32[4]{0:T(128)} %pad_add_fusion.pos_ref, bf16[1024,512]{1,0:T(8,128)(2,1)} %tok_ref.3, ...), custom_call_target="tpu_custom_call" | custom-call | flops 12000000000 | bytes 1 | tf_op jit(solution)/shard_map/feed/pallas_call | solution.py:648
  36.1 0.2 collective-permute-start.8
  36.4 1.0 copy-done.25
  37.5 0.8 collective-permute-done.8.b_ref
  38.5 1.5 %collective-permute-start.10 = (bf16[512,512]{1,0:T(8,128)(2,1)S(1)}, bf16[512,512]{1,0:T(8,128)(2,1)S(1)}, u32[]{:S(2)}, u32[]{:S(2)}) collective-permute-start(bf16[512,512]{1,0:T(8,128)(2,1)S(1)} %add.26.own_ref), channel_id=1, source_target_pairs={{0,2},{1,3},{2,0},{3,1},{4,6},{5,7},{6,4},{7,5},{8,10},{9,11},{10,... | collective-permute-start | bytes 1572872 | tf_op jit(solution)/shard_map/sum_second/ppermute | solution.py:624
  40.1 3.0 %weights.1 = (bf16[512,512]{1,0:T(8,128)(2,1)S(1)}, bf16[512,512]{1,0:T(8,128)(2,1)S(1)}, bf16[512,512]{1,0:T(8,128)(2,1)S(1)}, bf16[512,512]{1,0:T(8,128)(2,1)S(1)}) custom-call(s32[4]{0:T(128)S(1)} %copy-done.2, bf16[1024,512]{1,0:T(8,128)(2,1)S(1)} %copy-done.19, bf16[1024,512]{1,0:T(8,128)(2,1)S(1)} %copy-done.18, bf16[1024,512]{1,0:T(8,128)(2,1)S(1)} %copy-done.20, ...), custom_call_target="tpu_custom_call" | custom-call | flops 12000000000 | bytes 1 | tf_op jit(solution)/shard_map/weights/pallas_call | solution.py:648
  43.1 0.6 collective-permute-start.9
  43.7 0.4 collective-permute-start.15
  44.1 1.1 collective-permute-done.9.b_ref
  45.4 7.1 %collective-permute-done.10.far_ref = bf16[512,512]{1,0:T(8,128)(2,1)S(1)} collective-permute-done((bf16[512,512]{1,0:T(8,128)(2,1)S(1)}, bf16[512,512]{1,0:T(8,128)(2,1)S(1)}, u32[]{:S(2)}, u32[]{:S(2)}) %collective-permute-start.10) | collective-permute-done | bytes 524320 | tf_op jit(solution)/shard_map/sum_second/ppermute | solution.py:624
  52.5 0.5 collective-permute-start.14
  53.0 1.5 %collective-permute-start.11 = (bf16[512,512]{1,0:T(8,128)(2,1)S(1)}, bf16[512,512]{1,0:T(8,128)(2,1)S(1)}, u32[]{:S(2)}, u32[]{:S(2)}) collective-permute-start(bf16[512,512]{1,0:T(8,128)(2,1)S(1)} %add.27.own_ref), channel_id=1, source_target_pairs={{0,2},{1,3},{2,0},{3,1},{4,6},{5,7},{6,4},{7,5},{8,10},{9,11},{10,... | collective-permute-start | bytes 1572872 | tf_op jit(solution)/shard_map/sum_output/ppermute | solution.py:624
  54.5 5.5 %back.1 = (bf16[1024,512]{1,0:T(8,128)(2,1)S(1)}, bf16[1024,384]{1,0:T(8,128)(2,1)S(1)}, f32[4,2,8,128]{3,2,1,0:T(8,128)S(1)}, f32[32,512]{1,0:T(8,128)S(1)}) custom-call(s32[4]{0:T(128)S(1)} %copy-done.2, bf16[512,512]{1,0:T(8,128)(2,1)S(1)} %add.26.own_ref, bf16[512,512]{1,0:T(8,128)(2,1)S(1)} %collective-permute-done.10.far_ref, ...), custom_call_target="tpu_custom_call" | custom-call | flops 12000000000 | bytes 1 | tf_op jit(solution)/shard_map/back/pallas_call | solution.py:1111
  60.1 0.2 split.2
  60.2 0.8 copy-done.16
  61.0 0.3 copy-done.23
  61.3 3.9 %rest_weights.1 = (bf16[272,512]{1,0:T(8,128)(2,1)}, bf16[272,512]{1,0:T(8,128)(2,1)}) custom-call(s32[1]{0:T(128)} %bitcast.3.bit_ref, bf16[1024,512]{1,0:T(8,128)(2,1)} %get-tuple-element.293.first_ref, bf16[1024,384]{1,0:T(8,128)(2,1)} %copy-done.23, bf16[1024,512]{1,0:T(8,128)(2,1)} %copy-done.16, bf16[1024,128]{1,0:T(8,128)(2,1)} %copy-done.7, ...), custom_call_target="tpu_custom_call" | custom-call | flops 12000000000 | bytes 1 | tf_op jit(solution)/shard_map/rest_weights/pallas_call | solution.py:648
  65.2 1.7 %collective-permute-done.11.far_ref = bf16[512,512]{1,0:T(8,128)(2,1)S(1)} collective-permute-done((bf16[512,512]{1,0:T(8,128)(2,1)S(1)}, bf16[512,512]{1,0:T(8,128)(2,1)S(1)}, u32[]{:S(2)}, u32[]{:S(2)}) %collective-permute-start.11) | collective-permute-done | bytes 524320 | tf_op jit(solution)/shard_map/sum_output/ppermute | solution.py:624
  66.8 1.5 %collective-permute-start.19 = (bf16[256,512]{1,0:T(8,128)(2,1)S(1)}, bf16[256,512]{1,0:T(8,128)(2,1)S(1)}, u32[]{:S(2)}, u32[]{:S(2)}) collective-permute-start(bf16[256,512]{1,0:T(8,128)(2,1)S(1)} %get-tuple-element.310), channel_id=1, source_target_pairs={{0,4},{4,0},{8,12},{12,8},{16,20},{20,16},{24,28},{28,24},{1,5},{5... | collective-permute-start | bytes 786440 | tf_op jit(solution)/shard_map/feed_weights/ppermute | solution.py:624
  68.4 1.1 copy-done.24
  69.5 2.0 %first.1 = (bf16[528,512]{1,0:T(8,128)(2,1)S(1)}, bf16[528,512]{1,0:T(8,128)(2,1)S(1)}) custom-call(s32[4]{0:T(128)S(1)} %copy-done.2, bf16[1024,384]{1,0:T(8,128)(2,1)S(1)} %copy-done.24, f32[4,2,8,128]{3,2,1,0:T(8,128)S(1)} %copy-done.28, bf16[4,5,16,128]{3,2,1,0:T(8,128)(2,1)S(1)} %copy-done.1, bf16[3,512,128]{2,1,0:T(8,128)(2,1)S(1)} %copy-done.6, ...), custom_call_target="tpu_custom_call" | custom-call | flops 12000000000 | bytes 1 | tf_op jit(solution)/shard_map/first/pallas_call | solution.py:648
  71.6 0.3 collective-permute-start.18
  71.9 0.4 collective-permute-start.17
  72.3 3.3 %collective-permute-done.19.b_ref = bf16[256,512]{1,0:T(8,128)(2,1)S(1)} collective-permute-done((bf16[256,512]{1,0:T(8,128)(2,1)S(1)}, bf16[256,512]{1,0:T(8,128)(2,1)S(1)}, u32[]{:S(2)}, u32[]{:S(2)}) %collective-permute-start.19) | collective-permute-done | bytes 262176 | tf_op jit(solution)/shard_map/feed_weights/ppermute | solution.py:624
  75.6 2.7 %collective-permute-start.21 = (bf16[128,512]{1,0:T(8,128)(2,1)S(1)}, bf16[128,512]{1,0:T(8,128)(2,1)S(1)}, u32[]{:S(2)}, u32[]{:S(2)}) collective-permute-start(bf16[128,512]{1,0:T(8,128)(2,1)S(1)} %get-tuple-element.328), channel_id=1, source_target_pairs={{0,16},{4,20},{8,24},{12,28},{16,0},{20,4},{24,8},{28,12},{1,17},{... | collective-permute-start | bytes 393224 | tf_op jit(solution)/shard_map/feed_weights/ppermute | solution.py:624
  78.5 1.6 %collective-permute-start.20 = (bf16[528,512]{1,0:T(8,128)(2,1)S(1)}, bf16[528,512]{1,0:T(8,128)(2,1)S(1)}, u32[]{:S(2)}, u32[]{:S(2)}) collective-permute-start(bf16[528,512]{1,0:T(8,128)(2,1)S(1)} %pair.1.near_ref.own_ref), channel_id=1, source_target_pairs={{0,2},{1,3},{2,0},{3,1},{4,6},{5,7},{6,4},{7,5},{8,10},{9,11},{10,... | collective-permute-start | bytes 1622024 | tf_op jit(solution)/shard_map/sum_first/ppermute | solution.py:624
  80.0 3.5 %collective-permute-done.17.b_ref = bf16[272,512]{1,0:T(8,128)(2,1)S(1)} collective-permute-done((bf16[272,512]{1,0:T(8,128)(2,1)S(1)}, bf16[272,512]{1,0:T(8,128)(2,1)S(1)}, u32[]{:S(2)}, u32[]{:S(2)}) %collective-permute-start.17) | collective-permute-done | bytes 278560 | tf_op jit(solution)/shard_map/rest_weights/ppermute | solution.py:624
  83.6 0.6 collective-permute-start.22
  84.2 1.9 %output.1 = bf16[1024,512]{1,0:T(8,128)(2,1)} custom-call(s32[4]{0:T(128)S(1)} %copy-done.2, bf16[512,512]{1,0:T(8,128)(2,1)S(1)} %add.27.own_ref, bf16[512,512]{1,0:T(8,128)(2,1)S(1)} %collective-permute-done.11.far_ref, bf16[512,512]{1,0:T(8,128)(2,1)S(1)} %collective-permute-done.14.other_ref, bf16[512,512]{1,0:T(8,128)(2,1)S(1)} %collective-permute-done.16.other_far_ref, ...), custom_call_target="tpu_custom_call" | custom-call | flops 12000000000 | bytes 1 | tf_op jit(solution)/shard_map/output/pallas_call | solution.py:648
  86.1 2.8 %collective-permute-done.22.b_ref = bf16[144,512]{1,0:T(8,128)(2,1)S(1)} collective-permute-done((bf16[144,512]{1,0:T(8,128)(2,1)S(1)}, bf16[144,512]{1,0:T(8,128)(2,1)S(1)}, u32[]{:S(2)}, u32[]{:S(2)}) %collective-permute-start.22) | collective-permute-done | bytes 147488 | tf_op jit(solution)/shard_map/rest_weights/ppermute | solution.py:624
  88.9 0.2 split_second.1
  89.1 0.4 collective-permute-start.27
  89.5 2.7 %collective-permute-start.29 = (bf16[128,512]{1,0:T(8,128)(2,1)S(1)}, bf16[128,512]{1,0:T(8,128)(2,1)S(1)}, u32[]{:S(2)}, u32[]{:S(2)}) collective-permute-start(bf16[128,512]{1,0:T(8,128)(2,1)S(1)} %add.28.a_ref), channel_id=1, source_target_pairs={{0,16},{4,20},{8,24},{12,28},{16,0},{20,4},{24,8},{28,12},{1,17},{... | collective-permute-start | bytes 393224 | tf_op jit(solution)/shard_map/feed_weights/ppermute | solution.py:624
  92.2 1.5 %collective-permute-start.26 = (f32[8,512]{1,0:T(8,128)S(1)}, f32[8,512]{1,0:T(8,128)S(1)}, u32[]{:S(2)}, u32[]{:S(2)}) collective-permute-start(f32[8,512]{1,0:T(8,128)S(1)} %plus.1.extra_ref), channel_id=1, source_target_pairs={{0,2},{1,3},{2,0},{3,1},{4,6},{5,7},{6,4},{7,5},{8,10},{9,11},{10,... | collective-permute-start | bytes 49160 | tf_op jit(solution)/shard_map/sum_extra/ppermute | solution.py:624
  93.7 4.1 %collective-permute-done.27.got_ref = bf16[64,512]{1,0:T(8,128)(2,1)S(1)} collective-permute-done((bf16[64,512]{1,0:T(8,128)(2,1)S(1)}, bf16[64,512]{1,0:T(8,128)(2,1)S(1)}, u32[]{:S(2)}, u32[]{:S(2)}) %collective-permute-start.27) | collective-permute-done | bytes 65568 | tf_op jit(solution)/shard_map/rest_weights/ppermute | solution.py:624
  98.0 2.6 %collective-permute-done.29.b_ref = bf16[128,512]{1,0:T(8,128)(2,1)S(1)} collective-permute-done((bf16[128,512]{1,0:T(8,128)(2,1)S(1)}, bf16[128,512]{1,0:T(8,128)(2,1)S(1)}, u32[]{:S(2)}, u32[]{:S(2)}) %collective-permute-start.29) | collective-permute-done | bytes 131104 | tf_op jit(solution)/shard_map/feed_weights/ppermute | solution.py:624
  100.6 0.2 collective-permute-start.31
  100.8 1.4 %collective-permute-start.34 = (bf16[256,512]{1,0:T(8,128)(2,1)S(1)}, bf16[256,512]{1,0:T(8,128)(2,1)S(1)}, u32[]{:S(2)}, u32[]{:S(2)}) collective-permute-start(bf16[256,512]{1,0:T(8,128)(2,1)S(1)} %concat.1.own_ref), channel_id=1, source_target_pairs={{0,4},{4,0},{8,12},{12,8},{16,20},{20,16},{24,28},{28,24},{1,5},{5... | collective-permute-start | bytes 786440 | tf_op jit(solution)/shard_map/feed_weights/ppermute | solution.py:624
  102.2 2.4 %collective-permute-done.28.b_ref = bf16[80,512]{1,0:T(8,128)(2,1)S(1)} collective-permute-done((bf16[80,512]{1,0:T(8,128)(2,1)S(1)}, bf16[80,512]{1,0:T(8,128)(2,1)S(1)}, u32[]{:S(2)}, u32[]{:S(2)}) %collective-permute-start.28) | collective-permute-done | bytes 81952 | tf_op jit(solution)/shard_map/rest_weights/ppermute | solution.py:624
  104.7 1.8 %collective-permute-done.23.other_ref = bf16[528,512]{1,0:T(8,128)(2,1)S(1)} collective-permute-done((bf16[528,512]{1,0:T(8,128)(2,1)S(1)}, bf16[528,512]{1,0:T(8,128)(2,1)S(1)}, u32[]{:S(2)}, u32[]{:S(2)}) %collective-permute-start.23) | collective-permute-done | bytes 540704 | tf_op jit(solution)/shard_map/sum_first/ppermute | solution.py:624
  106.6 3.1 %last.1 = bf16[1024,512]{1,0:T(8,128)(2,1)} custom-call(s32[4]{0:T(128)S(1)} %copy-done.2, bf16[528,512]{1,0:T(8,128)(2,1)S(1)} %pair.1.near_ref.own_ref, bf16[528,512]{1,0:T(8,128)(2,1)S(1)} %collective-permute-done.20.far_ref, bf16[528,512]{1,0:T(8,128)(2,1)S(1)} %collective-permute-done.23.other_ref, ...), custom_call_target="tpu_custom_call" | custom-call | flops 12000000000 | bytes 1 | tf_op jit(solution)/shard_map/last/pallas_call | solution.py:648
  109.6 0.5 collective-permute-done.31.own_ref
  110.1 2.0 %collective-permute-done.30.b_ref = bf16[144,512]{1,0:T(8,128)(2,1)S(1)} collective-permute-done((bf16[144,512]{1,0:T(8,128)(2,1)S(1)}, bf16[144,512]{1,0:T(8,128)(2,1)S(1)}, u32[]{:S(2)}, u32[]{:S(2)}) %collective-permute-start.30) | collective-permute-done | bytes 147488 | tf_op jit(solution)/shard_map/rest_weights/ppermute | solution.py:624
  112.1 3.0 %collective-permute-start.32 = (bf16[272,512]{1,0:T(8,128)(2,1)S(1)}, bf16[272,512]{1,0:T(8,128)(2,1)S(1)}, u32[]{:S(2)}, u32[]{:S(2)}) collective-permute-start(bf16[272,512]{1,0:T(8,128)(2,1)S(1)} %merge.3.near_ref), channel_id=1, source_target_pairs={{0,8},{4,12},{8,0},{12,4},{16,24},{20,28},{24,16},{28,20},{1,9},{5... | collective-permute-start | bytes 835592 | tf_op jit(solution)/shard_map/rest_weights/ppermute | solution.py:624
  115.2 1.0 feed_unpack.2
  116.2 2.2 %collective-permute-done.33.one_ref = bf16[256,512]{1,0:T(8,128)(2,1)S(1)} collective-permute-done((bf16[256,512]{1,0:T(8,128)(2,1)S(1)}, bf16[256,512]{1,0:T(8,128)(2,1)S(1)}, u32[]{:S(2)}, u32[]{:S(2)}) %collective-permute-start.33) | collective-permute-done | bytes 262176 | tf_op jit(solution)/shard_map/feed_weights/ppermute | solution.py:624
  118.4 1.0 feed_unpack.3
  119.4 0.4 collective-permute-done.32.far_ref
  119.8 1.1 rest_unpack.1
  (117 shorter events, 1.2 us)
Async XLA Ops:
  0.6 6.9 %collective-permute-start = (bf16[128,512]{1,0:T(8,128)(2,1)}, bf16[128,512]{1,0:T(8,128)(2,1)S(1)}, u32[]{:S(2)}, u32[]{:S(2)}) collective-permute-start(bf16[128,512]{1,0:T(8,128)(2,1)} %wo_ref), channel_id=1, source_target_pairs={{0,2},{1,3},{2,0},{3,1},{4,6},{5,7},{6,4},{7,5},{8,10},{9,11},{10,... | collective-permute-start | bytes 393224 | tf_op jit(solution)/shard_map/gather_w_out/ppermute | solution.py:624
  7.6 5.7 %copy-start.35 = (bf16[128,512]{1,0:T(8,128)(2,1)}, bf16[128,512]{1,0:T(8,128)(2,1)S(1)}, u32[]{:S(2)}) copy-start(bf16[128,512]{1,0:T(8,128)(2,1)S(1)} %collective-permute-done.refs_6_) | copy-start | bytes 393220
  7.6 5.7 %copy-start.8 = (bf16[128,512]{1,0:T(8,128)(2,1)S(1)}, bf16[128,512]{1,0:T(8,128)(2,1)}, u32[]{:S(2)}) copy-start(bf16[128,512]{1,0:T(8,128)(2,1)} %wo_ref) | copy-start | bytes 393220
  7.6 4.1 %collective-permute-start.1 = (bf16[1,5,16,128]{3,2,1,0:T(8,128)(2,1)}, bf16[1,5,16,128]{3,2,1,0:T(8,128)(2,1)S(1)}, u32[]{:S(2)}, u32[]{:S(2)}) collective-permute-start(bf16[1,5,16,128]{3,2,1,0:T(8,128)(2,1)} %bitcast.27), channel_id=1, source_target_pairs={{0,4},{4,0},{8,12},{12,8},{16,20},{20,16},{24,28},{28,24},{1,5},{5... | collective-permute-start | bytes 61448 | tf_op jit(solution)/shard_map/summaries/ppermute | solution.py:624
  11.7 4.1 %collective-permute-start.2 = (bf16[2,5,16,128]{3,2,1,0:T(8,128)(2,1)S(1)}, bf16[2,5,16,128]{3,2,1,0:T(8,128)(2,1)S(1)}, u32[]{:S(2)}, u32[]{:S(2)}) collective-permute-start(bf16[2,5,16,128]{3,2,1,0:T(8,128)(2,1)S(1)} %constant_dynamic-update-slice_fusion), channel_id=1, source_target_pairs={{0,8},{4,12},{8,0},{12,4},{16,24},{20,28},{24,16},{28,20},{1,9},{5... | collective-permute-start | bytes 122888 | tf_op jit(solution)/shard_map/summaries/ppermute | solution.py:624
  13.3 2.4 %collective-permute-start.3 = (bf16[128,512]{1,0:T(8,128)(2,1)S(1)}, bf16[128,512]{1,0:T(8,128)(2,1)S(1)}, u32[]{:S(2)}, u32[]{:S(2)}) collective-permute-start(bf16[128,512]{1,0:T(8,128)(2,1)S(1)} %copy-done.8), channel_id=1, source_target_pairs={{0,1},{1,0},{2,3},{3,2},{4,5},{5,4},{6,7},{7,6},{8,9},{9,8},{10,11... | collective-permute-start | bytes 393224 | tf_op jit(solution)/shard_map/gather_w_out/ppermute | solution.py:624
  13.3 2.5 %collective-permute-start.4 = (bf16[128,512]{1,0:T(8,128)(2,1)S(1)}, bf16[128,512]{1,0:T(8,128)(2,1)S(1)}, u32[]{:S(2)}, u32[]{:S(2)}) collective-permute-start(bf16[128,512]{1,0:T(8,128)(2,1)S(1)} %collective-permute-done.refs_6_), channel_id=1, source_target_pairs={{0,1},{1,0},{2,3},{3,2},{4,5},{5,4},{6,7},{7,6},{8,9},{9,8},{10,11... | collective-permute-start | bytes 393224 | tf_op jit(solution)/shard_map/gather_w_out/ppermute | solution.py:624
  15.7 38.8 %copy-start = (bf16[4,5,16,128]{3,2,1,0:T(8,128)(2,1)}, bf16[4,5,16,128]{3,2,1,0:T(8,128)(2,1)S(1)}, u32[]{:S(2)}) copy-start(bf16[4,5,16,128]{3,2,1,0:T(8,128)(2,1)S(1)} %constant_dynamic-update-slice_fusion.2.sums_ref) | copy-start | bytes 245764
  15.8 1.5 %copy-start.36 = (bf16[128,512]{1,0:T(8,128)(2,1)}, bf16[128,512]{1,0:T(8,128)(2,1)S(1)}, u32[]{:S(2)}) copy-start(bf16[128,512]{1,0:T(8,128)(2,1)S(1)} %collective-permute-done.3.refs_5_) | copy-start | bytes 393220
  15.8 1.5 %copy-start.37 = (bf16[128,512]{1,0:T(8,128)(2,1)}, bf16[128,512]{1,0:T(8,128)(2,1)S(1)}, u32[]{:S(2)}) copy-start(bf16[128,512]{1,0:T(8,128)(2,1)S(1)} %collective-permute-done.4.refs_7_) | copy-start | bytes 393220
  17.3 9.2 %copy-start.7 = (bf16[1024,128]{1,0:T(8,128)(2,1)}, bf16[1024,128]{1,0:T(8,128)(2,1)S(1)}, u32[]{:S(2)}) copy-start(bf16[1024,128]{1,0:T(8,128)(2,1)S(1)} %get-tuple-element.296.refs_0_.att_ref) | copy-start | bytes 786436
  17.3 7.6 %collective-permute-start.6 = (bf16[1024,128]{1,0:T(8,128)(2,1)S(1)}, bf16[1024,128]{1,0:T(8,128)(2,1)S(1)}, u32[]{:S(2)}, u32[]{:S(2)}) collective-permute-start(bf16[1024,128]{1,0:T(8,128)(2,1)S(1)} %get-tuple-element.296.refs_0_.att_ref), channel_id=1, source_target_pairs={{0,2},{1,3},{2,0},{3,1},{4,6},{5,7},{6,4},{7,5},{8,10},{9,11},{10,... | collective-permute-start | bytes 786440 | tf_op jit(solution)/shard_map/gather_attended/ppermute | solution.py:624
  18.9 6.7 %collective-permute-start.5 = (bf16[1024,128]{1,0:T(8,128)(2,1)S(1)}, bf16[1024,128]{1,0:T(8,128)(2,1)S(1)}, u32[]{:S(2)}, u32[]{:S(2)}) collective-permute-start(bf16[1024,128]{1,0:T(8,128)(2,1)S(1)} %get-tuple-element.296.refs_0_.att_ref), channel_id=1, source_target_pairs={{0,1},{1,0},{2,3},{3,2},{4,5},{5,4},{6,7},{7,6},{8,9},{9,8},{10,11... | collective-permute-start | bytes 786440 | tf_op jit(solution)/shard_map/gather_attended/ppermute | solution.py:624
  25.0 1.5 %copy-start.32 = (bf16[1024,128]{1,0:T(8,128)(2,1)}, bf16[1024,128]{1,0:T(8,128)(2,1)S(1)}, u32[]{:S(2)}) copy-start(bf16[1024,128]{1,0:T(8,128)(2,1)S(1)} %collective-permute-done.6.refs_2_) | copy-start | bytes 786436
  25.0 1.5 %collective-permute-start.7 = (bf16[1024,128]{1,0:T(8,128)(2,1)S(1)}, bf16[1024,128]{1,0:T(8,128)(2,1)S(1)}, u32[]{:S(2)}, u32[]{:S(2)}) collective-permute-start(bf16[1024,128]{1,0:T(8,128)(2,1)S(1)} %collective-permute-done.6.refs_2_), channel_id=1, source_target_pairs={{0,1},{1,0},{2,3},{3,2},{4,5},{5,4},{6,7},{7,6},{8,9},{9,8},{10,11... | collective-permute-start | bytes 786440 | tf_op jit(solution)/shard_map/gather_attended/ppermute | solution.py:624
  36.1 2.2 %collective-permute-start.8 = (bf16[512,512]{1,0:T(8,128)(2,1)}, bf16[512,512]{1,0:T(8,128)(2,1)S(1)}, u32[]{:S(2)}, u32[]{:S(2)}) collective-permute-start(bf16[512,512]{1,0:T(8,128)(2,1)} %get-tuple-element.250), channel_id=1, source_target_pairs={{0,1},{1,0},{2,3},{3,2},{4,5},{5,4},{6,7},{7,6},{8,9},{9,8},{10,11... | collective-permute-start | bytes 1572872 | tf_op jit(solution)/shard_map/sum_second/ppermute | solution.py:624
  37.4 2.6 %copy-start.2 = (s32[4]{0:T(128)S(1)}, s32[4]{0:T(128)}, u32[]{:S(2)}) copy-start(s32[4]{0:T(128)} %pad_add_fusion.pos_ref) | copy-start | bytes 52
  37.4 2.6 %copy-start.3 = (bf16[1024,512]{1,0:T(8,128)(2,1)S(1)}, bf16[1024,512]{1,0:T(8,128)(2,1)}, u32[]{:S(2)}) copy-start(bf16[1024,512]{1,0:T(8,128)(2,1)} %cot_ref.1) | copy-start | bytes 3145732
  37.5 2.6 %copy-start.5 = (bf16[512,512]{1,0:T(8,128)(2,1)S(1)}, bf16[512,512]{1,0:T(8,128)(2,1)}, u32[]{:S(2)}) copy-start(bf16[512,512]{1,0:T(8,128)(2,1)} %down_ref) | copy-start | bytes 1572868
  37.5 2.6 %copy-start.18 = (bf16[1024,512]{1,0:T(8,128)(2,1)S(1)}, bf16[1024,512]{1,0:T(8,128)(2,1)}, u32[]{:S(2)}) copy-start(bf16[1024,512]{1,0:T(8,128)(2,1)} %get-tuple-element.255.second_ref) | copy-start | bytes 3145732
  37.5 2.6 %copy-start.19 = (bf16[1024,512]{1,0:T(8,128)(2,1)S(1)}, bf16[1024,512]{1,0:T(8,128)(2,1)}, u32[]{:S(2)}) copy-start(bf16[1024,512]{1,0:T(8,128)(2,1)} %get-tuple-element.254.active_ref) | copy-start | bytes 3145732
  37.5 2.6 %copy-start.20 = (bf16[1024,512]{1,0:T(8,128)(2,1)S(1)}, bf16[1024,512]{1,0:T(8,128)(2,1)}, u32[]{:S(2)}) copy-start(bf16[1024,512]{1,0:T(8,128)(2,1)} %get-tuple-element.256.grad_ref) | copy-start | bytes 3145732
  38.5 14.0 %collective-permute-start.10 = (bf16[512,512]{1,0:T(8,128)(2,1)S(1)}, bf16[512,512]{1,0:T(8,128)(2,1)S(1)}, u32[]{:S(2)}, u32[]{:S(2)}) collective-permute-start(bf16[512,512]{1,0:T(8,128)(2,1)S(1)} %add.26.own_ref), channel_id=1, source_target_pairs={{0,2},{1,3},{2,0},{3,1},{4,6},{5,7},{6,4},{7,5},{8,10},{9,11},{10,... | collective-permute-start | bytes 1572872 | tf_op jit(solution)/shard_map/sum_second/ppermute | solution.py:624
  40.0 14.5 %collective-permute-start.12 = (bf16[512,512]{1,0:T(8,128)(2,1)S(1)}, bf16[512,512]{1,0:T(8,128)(2,1)S(1)}, u32[]{:S(2)}, u32[]{:S(2)}) collective-permute-start(bf16[512,512]{1,0:T(8,128)(2,1)S(1)} %add.26.own_ref), channel_id=1, source_target_pairs={{0,1},{1,0},{2,3},{3,2},{4,5},{5,4},{6,7},{7,6},{8,9},{9,8},{10,11... | collective-permute-start | bytes 1572872 | tf_op jit(solution)/shard_map/sum_second/ppermute | solution.py:624
  40.1 3.6 %copy-start.12 = (f32[512]{0:T(512)S(1)}, f32[512]{0:T(512)}, u32[]{:S(2)}) copy-start(f32[512]{0:T(512)} %param.14) | copy-start | bytes 6148
  43.1 2.1 %collective-permute-start.9 = (bf16[512,512]{1,0:T(8,128)(2,1)S(1)}, bf16[512,512]{1,0:T(8,128)(2,1)S(1)}, u32[]{:S(2)}, u32[]{:S(2)}) collective-permute-start(bf16[512,512]{1,0:T(8,128)(2,1)S(1)} %get-tuple-element.260), channel_id=1, source_target_pairs={{0,1},{1,0},{2,3},{3,2},{4,5},{5,4},{6,7},{7,6},{8,9},{9,8},{10,11... | collective-permute-start | bytes 1572872 | tf_op jit(solution)/shard_map/sum_output/ppermute | solution.py:624
  43.7 16.4 %collective-permute-start.15 = (bf16[512,512]{1,0:T(8,128)(2,1)S(1)}, bf16[512,512]{1,0:T(8,128)(2,1)S(1)}, u32[]{:S(2)}, u32[]{:S(2)}) collective-permute-start(bf16[512,512]{1,0:T(8,128)(2,1)S(1)} %get-tuple-element.286), channel_id=1, source_target_pairs={{0,8},{4,12},{8,0},{12,4},{16,24},{20,28},{24,16},{28,20},{1,9},{5... | collective-permute-start | bytes 1572872 | tf_op jit(solution)/shard_map/feed_weights/ppermute | solution.py:624
  45.3 9.2 %copy-start.9 = (bf16[128,512]{1,0:T(8,128)(2,1)S(1)}, bf16[128,512]{1,0:T(8,128)(2,1)}, u32[]{:S(2)}) copy-start(bf16[128,512]{1,0:T(8,128)(2,1)} %wo_ref) | copy-start | bytes 393220
  45.3 9.2 %copy-start.10 = (f32[512]{0:T(512)S(1)}, f32[512]{0:T(512)}, u32[]{:S(2)}) copy-start(f32[512]{0:T(512)} %param.19) | copy-start | bytes 6148
  45.4 9.2 %copy-start.14 = (f32[1024,512]{1,0:T(8,128)S(1)}, f32[1024,512]{1,0:T(8,128)}, u32[]{:S(2)}) copy-start(f32[1024,512]{1,0:T(8,128)} %get-tuple-element.326.mid_ref) | copy-start | bytes 6291460
  45.4 9.2 %copy-start.22 = (bf16[3,1024,128]{2,1,0:T(8,128)(2,1)S(1)}, bf16[3,1024,128]{2,1,0:T(8,128)(2,1)}, u32[]{:S(2)}) copy-start(bf16[3,1024,128]{2,1,0:T(8,128)(2,1)} %get-tuple-element.280.qkv_ref) | copy-start | bytes 2359300
  52.5 2.0 %collective-permute-start.13 = (bf16[512,512]{1,0:T(8,128)(2,1)S(1)}, bf16[512,512]{1,0:T(8,128)(2,1)S(1)}, u32[]{:S(2)}, u32[]{:S(2)}) collective-permute-start(bf16[512,512]{1,0:T(8,128)(2,1)S(1)} %collective-permute-done.10.far_ref), channel_id=1, source_target_pairs={{0,1},{1,0},{2,3},{3,2},{4,5},{5,4},{6,7},{7,6},{8,9},{9,8},{10,11... | collective-permute-start | bytes 1572872 | tf_op jit(solution)/shard_map/sum_second/ppermute | solution.py:624
  52.5 8.8 %collective-permute-start.14 = (bf16[512,512]{1,0:T(8,128)(2,1)S(1)}, bf16[512,512]{1,0:T(8,128)(2,1)S(1)}, u32[]{:S(2)}, u32[]{:S(2)}) collective-permute-start(bf16[512,512]{1,0:T(8,128)(2,1)S(1)} %add.27.own_ref), channel_id=1, source_target_pairs={{0,1},{1,0},{2,3},{3,2},{4,5},{5,4},{6,7},{7,6},{8,9},{9,8},{10,11... | collective-permute-start | bytes 1572872 | tf_op jit(solution)/shard_map/sum_output/ppermute | solution.py:624
  53.0 13.8 %collective-permute-start.11 = (bf16[512,512]{1,0:T(8,128)(2,1)S(1)}, bf16[512,512]{1,0:T(8,128)(2,1)S(1)}, u32[]{:S(2)}, u32[]{:S(2)}) collective-permute-start(bf16[512,512]{1,0:T(8,128)(2,1)S(1)} %add.27.own_ref), channel_id=1, source_target_pairs={{0,2},{1,3},{2,0},{3,1},{4,6},{5,7},{6,4},{7,5},{8,10},{9,11},{10,... | collective-permute-start | bytes 1572872 | tf_op jit(solution)/shard_map/sum_output/ppermute | solution.py:624
  61.3 7.1 %copy-start.1 = (bf16[4,5,16,128]{3,2,1,0:T(8,128)(2,1)S(1)}, bf16[4,5,16,128]{3,2,1,0:T(8,128)(2,1)}, u32[]{:S(2)}) copy-start(bf16[4,5,16,128]{3,2,1,0:T(8,128)(2,1)} %copy-done) | copy-start | bytes 245764
  61.3 7.1 %copy-start.4 = (bf16[1024,512]{1,0:T(8,128)(2,1)S(1)}, bf16[1024,512]{1,0:T(8,128)(2,1)}, u32[]{:S(2)}) copy-start(bf16[1024,512]{1,0:T(8,128)(2,1)} %tok_ref.3) | copy-start | bytes 3145732
  61.3 7.1 %copy-start.6 = (bf16[3,512,128]{2,1,0:T(8,128)(2,1)S(1)}, bf16[3,512,128]{2,1,0:T(8,128)(2,1)}, u32[]{:S(2)}) copy-start(bf16[3,512,128]{2,1,0:T(8,128)(2,1)} %w_ref.2) | copy-start | bytes 1179652
  61.3 7.1 %copy-start.28 = (f32[4,2,8,128]{3,2,1,0:T(8,128)S(1)}, f32[4,2,8,128]{3,2,1,0:T(8,128)}, u32[]{:S(2)}) copy-start(f32[4,2,8,128]{3,2,1,0:T(8,128)} %copy-done.27) | copy-start | bytes 98308
  66.8 16.8 %collective-permute-start.16 = (bf16[512,512]{1,0:T(8,128)(2,1)S(1)}, bf16[512,512]{1,0:T(8,128)(2,1)S(1)}, u32[]{:S(2)}, u32[]{:S(2)}) collective-permute-start(bf16[512,512]{1,0:T(8,128)(2,1)S(1)} %collective-permute-done.11.far_ref), channel_id=1, source_target_pairs={{0,1},{1,0},{2,3},{3,2},{4,5},{5,4},{6,7},{7,6},{8,9},{9,8},{10,11... | collective-permute-start | bytes 1572872 | tf_op jit(solution)/shard_map/sum_output/ppermute | solution.py:624
  66.8 8.7 %collective-permute-start.19 = (bf16[256,512]{1,0:T(8,128)(2,1)S(1)}, bf16[256,512]{1,0:T(8,128)(2,1)S(1)}, u32[]{:S(2)}, u32[]{:S(2)}) collective-permute-start(bf16[256,512]{1,0:T(8,128)(2,1)S(1)} %get-tuple-element.310), channel_id=1, source_target_pairs={{0,4},{4,0},{8,12},{12,8},{16,20},{20,16},{24,28},{28,24},{1,5},{5... | collective-permute-start | bytes 786440 | tf_op jit(solution)/shard_map/feed_weights/ppermute | solution.py:624
  69.5 2.3 %copy-start.31 = (bf16[272,512]{1,0:T(8,128)(2,1)S(1)}, bf16[272,512]{1,0:T(8,128)(2,1)}, u32[]{:S(2)}) copy-start(bf16[272,512]{1,0:T(8,128)(2,1)} %get-tuple-element.301) | copy-start | bytes 835588
  71.6 6.7 %collective-permute-start.18 = (bf16[528,512]{1,0:T(8,128)(2,1)S(1)}, bf16[528,512]{1,0:T(8,128)(2,1)S(1)}, u32[]{:S(2)}, u32[]{:S(2)}) collective-permute-start(bf16[528,512]{1,0:T(8,128)(2,1)S(1)} %get-tuple-element.309), channel_id=1, source_target_pairs={{0,1},{1,0},{2,3},{3,2},{4,5},{5,4},{6,7},{7,6},{8,9},{9,8},{10,11... | collective-permute-start | bytes 1622024 | tf_op jit(solution)/shard_map/sum_first/ppermute | solution.py:624
  71.9 11.7 %collective-permute-start.17 = (bf16[272,512]{1,0:T(8,128)(2,1)S(1)}, bf16[272,512]{1,0:T(8,128)(2,1)S(1)}, u32[]{:S(2)}, u32[]{:S(2)}) collective-permute-start(bf16[272,512]{1,0:T(8,128)(2,1)S(1)} %copy-done.31), channel_id=1, source_target_pairs={{0,8},{4,12},{8,0},{12,4},{16,24},{20,28},{24,16},{28,20},{1,9},{5... | collective-permute-start | bytes 835592 | tf_op jit(solution)/shard_map/rest_weights/ppermute | solution.py:624
  75.6 13.5 %collective-permute-start.21 = (bf16[128,512]{1,0:T(8,128)(2,1)S(1)}, bf16[128,512]{1,0:T(8,128)(2,1)S(1)}, u32[]{:S(2)}, u32[]{:S(2)}) collective-permute-start(bf16[128,512]{1,0:T(8,128)(2,1)S(1)} %get-tuple-element.328), channel_id=1, source_target_pairs={{0,16},{4,20},{8,24},{12,28},{16,0},{20,4},{24,8},{28,12},{1,17},{... | collective-permute-start | bytes 393224 | tf_op jit(solution)/shard_map/feed_weights/ppermute | solution.py:624
  78.3 5.2 %copy-start.26 = (bf16[272,512]{1,0:T(8,128)(2,1)S(1)}, bf16[272,512]{1,0:T(8,128)(2,1)}, u32[]{:S(2)}) copy-start(bf16[272,512]{1,0:T(8,128)(2,1)} %get-tuple-element.318.a_ref) | copy-start | bytes 835588
  78.4 5.8 %copy-start.11 = (f32[512]{0:T(512)S(1)}, f32[512]{0:T(512)}, u32[]{:S(2)}) copy-start(f32[512]{0:T(512)} %param.24) | copy-start | bytes 6148
  78.5 5.7 %copy-start.15 = (f32[1024,512]{1,0:T(8,128)S(1)}, f32[1024,512]{1,0:T(8,128)}, u32[]{:S(2)}) copy-start(f32[1024,512]{1,0:T(8,128)} %get-tuple-element.326.mid_ref) | copy-start | bytes 6291460
  78.5 13.8 %collective-permute-start.20 = (bf16[528,512]{1,0:T(8,128)(2,1)S(1)}, bf16[528,512]{1,0:T(8,128)(2,1)S(1)}, u32[]{:S(2)}, u32[]{:S(2)}) collective-permute-start(bf16[528,512]{1,0:T(8,128)(2,1)S(1)} %pair.1.near_ref.own_ref), channel_id=1, source_target_pairs={{0,2},{1,3},{2,0},{3,1},{4,6},{5,7},{6,4},{7,5},{8,10},{9,11},{10,... | collective-permute-start | bytes 1622024 | tf_op jit(solution)/shard_map/sum_first/ppermute | solution.py:624
  83.6 5.3 %collective-permute-start.22 = (bf16[144,512]{1,0:T(8,128)(2,1)S(1)}, bf16[144,512]{1,0:T(8,128)(2,1)S(1)}, u32[]{:S(2)}, u32[]{:S(2)}) collective-permute-start(bf16[144,512]{1,0:T(8,128)(2,1)S(1)} %get-tuple-element.329), channel_id=1, source_target_pairs={{0,4},{4,0},{8,12},{12,8},{16,20},{20,16},{24,28},{28,24},{1,5},{5... | collective-permute-start | bytes 442376 | tf_op jit(solution)/shard_map/rest_weights/ppermute | solution.py:624
  89.1 3.1 %collective-permute-start.25 = (f32[8,512]{1,0:T(8,128)S(1)}, f32[8,512]{1,0:T(8,128)S(1)}, u32[]{:S(2)}, u32[]{:S(2)}) collective-permute-start(f32[8,512]{1,0:T(8,128)S(1)} %get-tuple-element.339.a_ref), channel_id=1, source_target_pairs={{0,1},{1,0},{2,3},{3,2},{4,5},{5,4},{6,7},{7,6},{8,9},{9,8},{10,11... | collective-permute-start | bytes 49160 | tf_op jit(solution)/shard_map/sum_extra/ppermute | solution.py:624
  89.1 8.7 %collective-permute-start.27 = (bf16[64,512]{1,0:T(8,128)(2,1)S(1)}, bf16[64,512]{1,0:T(8,128)(2,1)S(1)}, u32[]{:S(2)}, u32[]{:S(2)}) collective-permute-start(bf16[64,512]{1,0:T(8,128)(2,1)S(1)} %get-tuple-element.342), channel_id=1, source_target_pairs={{0,16},{4,20},{8,24},{12,28},{16,0},{20,4},{24,8},{28,12},{1,17},{... | collective-permute-start | bytes 196616 | tf_op jit(solution)/shard_map/rest_weights/ppermute | solution.py:624
  89.5 8.3 %copy-start.29 = (f32[8,512]{1,0:T(8,128)S(1)}, f32[8,512]{1,0:T(8,128)}, u32[]{:S(2)}) copy-start(f32[8,512]{1,0:T(8,128)} %get-tuple-element.349.up_ref) | copy-start | bytes 49156
  89.5 11.0 %collective-permute-start.29 = (bf16[128,512]{1,0:T(8,128)(2,1)S(1)}, bf16[128,512]{1,0:T(8,128)(2,1)S(1)}, u32[]{:S(2)}, u32[]{:S(2)}) collective-permute-start(bf16[128,512]{1,0:T(8,128)(2,1)S(1)} %add.28.a_ref), channel_id=1, source_target_pairs={{0,16},{4,20},{8,24},{12,28},{16,0},{20,4},{24,8},{28,12},{1,17},{... | collective-permute-start | bytes 393224 | tf_op jit(solution)/shard_map/feed_weights/ppermute | solution.py:624
  92.2 14.3 %collective-permute-start.24 = (bf16[528,512]{1,0:T(8,128)(2,1)S(1)}, bf16[528,512]{1,0:T(8,128)(2,1)S(1)}, u32[]{:S(2)}, u32[]{:S(2)}) collective-permute-start(bf16[528,512]{1,0:T(8,128)(2,1)S(1)} %collective-permute-done.20.far_ref), channel_id=1, source_target_pairs={{0,1},{1,0},{2,3},{3,2},{4,5},{5,4},{6,7},{7,6},{8,9},{9,8},{10,11... | collective-permute-start | bytes 1622024 | tf_op jit(solution)/shard_map/sum_first/ppermute | solution.py:624
  92.2 12.4 %collective-permute-start.26 = (f32[8,512]{1,0:T(8,128)S(1)}, f32[8,512]{1,0:T(8,128)S(1)}, u32[]{:S(2)}, u32[]{:S(2)}) collective-permute-start(f32[8,512]{1,0:T(8,128)S(1)} %plus.1.extra_ref), channel_id=1, source_target_pairs={{0,2},{1,3},{2,0},{3,1},{4,6},{5,7},{6,4},{7,5},{8,10},{9,11},{10,... | collective-permute-start | bytes 49160 | tf_op jit(solution)/shard_map/sum_extra/ppermute | solution.py:624
  97.9 6.7 %collective-permute-start.28 = (bf16[80,512]{1,0:T(8,128)(2,1)S(1)}, bf16[80,512]{1,0:T(8,128)(2,1)S(1)}, u32[]{:S(2)}, u32[]{:S(2)}) collective-permute-start(bf16[80,512]{1,0:T(8,128)(2,1)S(1)} %piece.1.a_ref), channel_id=1, source_target_pairs={{0,16},{4,20},{8,24},{12,28},{16,0},{20,4},{24,8},{28,12},{1,17},{... | collective-permute-start | bytes 245768 | tf_op jit(solution)/shard_map/rest_weights/ppermute | solution.py:624
  100.6 6.0 %copy-start.13 = (f32[512]{0:T(512)S(1)}, f32[512]{0:T(512)}, u32[]{:S(2)}) copy-start(f32[512]{0:T(512)} %param.14) | copy-start | bytes 6148
  100.6 6.0 %copy-start.17 = (bf16[1024,512]{1,0:T(8,128)(2,1)S(1)}, bf16[1024,512]{1,0:T(8,128)(2,1)}, u32[]{:S(2)}) copy-start(bf16[1024,512]{1,0:T(8,128)(2,1)} %copy-done.16) | copy-start | bytes 3145732
  100.6 9.5 %collective-permute-start.31 = (bf16[256,512]{1,0:T(8,128)(2,1)S(1)}, bf16[256,512]{1,0:T(8,128)(2,1)S(1)}, u32[]{:S(2)}, u32[]{:S(2)}) collective-permute-start(bf16[256,512]{1,0:T(8,128)(2,1)S(1)} %concat.1.own_ref), channel_id=1, source_target_pairs={{0,8},{4,12},{8,0},{12,4},{16,24},{20,28},{24,16},{28,20},{1,9},{5... | collective-permute-start | bytes 786440 | tf_op jit(solution)/shard_map/feed_weights/ppermute | solution.py:624
  100.8 14.3 %collective-permute-start.34 = (bf16[256,512]{1,0:T(8,128)(2,1)S(1)}, bf16[256,512]{1,0:T(8,128)(2,1)S(1)}, u32[]{:S(2)}, u32[]{:S(2)}) collective-permute-start(bf16[256,512]{1,0:T(8,128)(2,1)S(1)} %concat.1.own_ref), channel_id=1, source_target_pairs={{0,4},{4,0},{8,12},{12,8},{16,20},{20,16},{24,28},{28,24},{1,5},{5... | collective-permute-start | bytes 786440 | tf_op jit(solution)/shard_map/feed_weights/ppermute | solution.py:624
  104.6 1.9 %collective-permute-start.23 = (bf16[528,512]{1,0:T(8,128)(2,1)S(1)}, bf16[528,512]{1,0:T(8,128)(2,1)S(1)}, u32[]{:S(2)}, u32[]{:S(2)}) collective-permute-start(bf16[528,512]{1,0:T(8,128)(2,1)S(1)} %pair.1.near_ref.own_ref), channel_id=1, source_target_pairs={{0,1},{1,0},{2,3},{3,2},{4,5},{5,4},{6,7},{7,6},{8,9},{9,8},{10,11... | collective-permute-start | bytes 1622024 | tf_op jit(solution)/shard_map/sum_first/ppermute | solution.py:624
  104.7 7.4 %collective-permute-start.30 = (bf16[144,512]{1,0:T(8,128)(2,1)S(1)}, bf16[144,512]{1,0:T(8,128)(2,1)S(1)}, u32[]{:S(2)}, u32[]{:S(2)}) collective-permute-start(bf16[144,512]{1,0:T(8,128)(2,1)S(1)} %merge.2.a_ref), channel_id=1, source_target_pairs={{0,4},{4,0},{8,12},{12,8},{16,20},{20,16},{24,28},{28,24},{1,5},{5... | collective-permute-start | bytes 442376 | tf_op jit(solution)/shard_map/rest_weights/ppermute | solution.py:624
  110.1 8.2 %collective-permute-start.33 = (bf16[256,512]{1,0:T(8,128)(2,1)S(1)}, bf16[256,512]{1,0:T(8,128)(2,1)S(1)}, u32[]{:S(2)}, u32[]{:S(2)}) collective-permute-start(bf16[256,512]{1,0:T(8,128)(2,1)S(1)} %collective-permute-done.31.own_ref), channel_id=1, source_target_pairs={{0,4},{4,0},{8,12},{12,8},{16,20},{20,16},{24,28},{28,24},{1,5},{5... | collective-permute-start | bytes 786440 | tf_op jit(solution)/shard_map/feed_weights/ppermute | solution.py:624
  112.1 7.7 %collective-permute-start.32 = (bf16[272,512]{1,0:T(8,128)(2,1)S(1)}, bf16[272,512]{1,0:T(8,128)(2,1)S(1)}, u32[]{:S(2)}, u32[]{:S(2)}) collective-permute-start(bf16[272,512]{1,0:T(8,128)(2,1)S(1)} %merge.3.near_ref), channel_id=1, source_target_pairs={{0,8},{4,12},{8,0},{12,4},{16,24},{20,28},{24,16},{28,20},{1,9},{5... | collective-permute-start | bytes 835592 | tf_op jit(solution)/shard_map/rest_weights/ppermute | solution.py:624
  (9 other events, 9.7 us)

commit v9 on v8

--- a/solution.py
+++ b/solution.py
@@ -1134,12 +1134,12 @@
         theirs, mine = line(first_grad, pos, gqkv, slot_grad, sums, w_qkv, tokens)
         got = swap(theirs, "mp", 1, "sum_first")
         feed_sum.step()
+        theirs_w, rest = line(split_first, bit_of(feed_masks[1]), rest, rest_got)
+        rest_got = swap(theirs_w, "dp", feed_masks[1], "rest_weights")
         total = line(pair, mine, got)
         for m in far_masks[:-1]:
             total = line(pair, total, swap(total, "mp", m, "sum_first"))
         far = swap(total, "mp", last_far, "sum_first")
-        theirs_w, rest = line(split_first, bit_of(feed_masks[1]), rest, rest_got)
-        rest_got = swap(theirs_w, "dp", feed_masks[1], "rest_weights")
         output = line(
             output_sum, pos, out_total, out_far, out_other, out_other_far, mid, b_down[None]
         )

time: 122 us -> 119 us (0.975)
  waiting for transfers between devices: 46 us -> 42.6 us
    ppermute x35, waiting for transfers between devices: 46 us -> 42.6 us  [swap(): return lax.ppermute(x, axis, [(i, i ^ mask) for i in range(n)])]
    unnamed x78 -> x76, local copies, waits for them, and re-layouts: 5.18 us -> 5.19 us
  transfers between devices with their start and end apart: 35 -> 35, of which waited for: 19 -> 17; matrix products, arithmetic and copies ran while one was open for 0% -> 1% of each run, Pallas kernels for 22% -> 23%
where the time goes in v9:
time: 119 us; the launch traced here: 118 us
  waiting for transfers between devices  42.6 us (36%)
  Pallas kernels  38.4 us (32%)
  starting transfers between devices  30.3 us (25%)
  local copies, waits for them, and re-layouts  5.21 us (4%)
    ppermute x35, waiting for transfers between devices, swap(): return lax.ppermute(x, axis, [(i, i ^ mask) for i in range(n)])  42.6 us
    ppermute x35, starting transfers between devices, swap(): return lax.ppermute(x, axis, [(i, i ^ mask) for i in range(n)])  30.3 us
    pallas_call x12, Pallas kernels, __call__(): result = work(*inputs)  30.1 us
    pallas_call x1, Pallas kernels, per_device(): back(*a)  5.47 us
    unnamed x76, local copies, waits for them, and re-layouts  5.19 us
  transfers between devices with their start and end apart: 35, of which 17 were waited for; matrix products, arithmetic and copies ran while one was open for 1% of the time, Pallas kernels for 23%

profile of v9, /device:TPU:0, one launch (start us, length us, event | category | flops | bytes accessed | tf_op | source)
XLA Modules:
  0.0 118.3 jit_solution(6241023866573209812)
XLA Ops:
  0.6 3.0 %collective-permute-start = (bf16[128,512]{1,0:T(8,128)(2,1)}, bf16[128,512]{1,0:T(8,128)(2,1)S(1)}, u32[]{:S(2)}, u32[]{:S(2)}) collective-permute-start(bf16[128,512]{1,0:T(8,128)(2,1)} %wo_ref), channel_id=1, source_target_pairs={{0,2},{1,3},{2,0},{3,1},{4,6},{5,7},{6,4},{7,5},{8,10},{9,11},{10,... | collective-permute-start | bytes 393224 | tf_op jit(solution)/shard_map/gather_w_out/ppermute | solution.py:624
  3.7 3.9 %project.1 = (bf16[1024,512]{1,0:T(8,128)(2,1)}, bf16[3,1024,128]{2,1,0:T(8,128)(2,1)}, bf16[5,16,128]{2,1,0:T(8,128)(2,1)}) custom-call(bf16[1024,512]{1,0:T(8,128)(2,1)} %tok_ref.3, f32[1,512]{1,0:T(1,128)} %bitcast.24, f32[1,512]{1,0:T(1,128)} %bitcast.29, bf16[3,512,128]{2,1,0:T(8,128)(2,1)} %w_ref.2), custom_call_target="tpu_custom_call" | custom-call | flops 12000000000 | bytes 1 | tf_op jit(solution)/shard_map/project/pallas_call | solution.py:648
  7.6 1.6 %collective-permute-start.1 = (bf16[1,5,16,128]{3,2,1,0:T(8,128)(2,1)}, bf16[1,5,16,128]{3,2,1,0:T(8,128)(2,1)S(1)}, u32[]{:S(2)}, u32[]{:S(2)}) collective-permute-start(bf16[1,5,16,128]{3,2,1,0:T(8,128)(2,1)} %bitcast.27), channel_id=1, source_target_pairs={{0,4},{4,0},{8,12},{12,8},{16,20},{20,16},{24,28},{28,24},{1,5},{5... | collective-permute-start | bytes 61448 | tf_op jit(solution)/shard_map/summaries/ppermute | solution.py:624
  9.1 1.1 copy-done.21
  10.3 0.5 local.1
  10.8 0.9 collective-permute-done.1
  11.7 1.6 %collective-permute-start.2 = (bf16[2,5,16,128]{3,2,1,0:T(8,128)(2,1)S(1)}, bf16[2,5,16,128]{3,2,1,0:T(8,128)(2,1)S(1)}, u32[]{:S(2)}, u32[]{:S(2)}) collective-permute-start(bf16[2,5,16,128]{3,2,1,0:T(8,128)(2,1)S(1)} %constant_dynamic-update-slice_fusion), channel_id=1, source_target_pairs={{0,8},{4,12},{8,0},{12,4},{16,24},{20,28},{24,16},{28,20},{1,9},{5... | collective-permute-start | bytes 122888 | tf_op jit(solution)/shard_map/summaries/ppermute | solution.py:624
  13.3 0.5 collective-permute-start.4
  13.8 1.9 %collective-permute-done.2 = bf16[2,5,16,128]{3,2,1,0:T(8,128)(2,1)S(1)} collective-permute-done((bf16[2,5,16,128]{3,2,1,0:T(8,128)(2,1)S(1)}, bf16[2,5,16,128]{3,2,1,0:T(8,128)(2,1)S(1)}, u32[]{:S(2)}, u32[]{:S(2)}) %collective-permute-start.2) | collective-permute-done | bytes 40992 | tf_op jit(solution)/shard_map/summaries/ppermute | solution.py:624
  15.8 1.5 %attend.1 = (bf16[8,160,256]{2,1,0:T(8,128)(2,1)S(1)}, bf16[1024,128]{1,0:T(8,128)(2,1)S(1)}) custom-call(s32[1]{0:T(128)} %bitcast.2.place_ref, bf16[3,1024,128]{2,1,0:T(8,128)(2,1)S(1)} %copy-done.21, f32[8,128,256]{2,1,0:T(8,128)S(1)} %get-tuple-element.222.exp_ref, f32[8,2,256]{2,1,0:T(2,128)S(1)} %get-tuple-element.223.stat_ref, ...), custom_call_target="tpu_custom_call" | custom-call | flops 12000000000 | bytes 1 | tf_op jit(solution)/shard_map/attend/pallas_call | solution.py:648
  17.3 1.5 %collective-permute-start.6 = (bf16[1024,128]{1,0:T(8,128)(2,1)S(1)}, bf16[1024,128]{1,0:T(8,128)(2,1)S(1)}, u32[]{:S(2)}, u32[]{:S(2)}) collective-permute-start(bf16[1024,128]{1,0:T(8,128)(2,1)S(1)} %get-tuple-element.296.refs_0_.att_ref), channel_id=1, source_target_pairs={{0,2},{1,3},{2,0},{3,1},{4,6},{5,7},{6,4},{7,5},{8,10},{9,11},{10,... | collective-permute-start | bytes 786440 | tf_op jit(solution)/shard_map/gather_attended/ppermute | solution.py:624
  18.9 6.1 %collective-permute-done.6.refs_2_ = bf16[1024,128]{1,0:T(8,128)(2,1)S(1)} collective-permute-done((bf16[1024,128]{1,0:T(8,128)(2,1)S(1)}, bf16[1024,128]{1,0:T(8,128)(2,1)S(1)}, u32[]{:S(2)}, u32[]{:S(2)}) %collective-permute-start.6) | collective-permute-done | bytes 262176 | tf_op jit(solution)/shard_map/gather_attended/ppermute | solution.py:624
  25.0 0.6 pad_add_fusion.pos_ref
  25.6 0.9 collective-permute-done.7.refs_3_
  26.5 0.7 copy-done.33
  27.2 8.9 %feed.1 = (f32[1024,512]{1,0:T(8,128)}, bf16[1024,512]{1,0:T(8,128)(2,1)}, bf16[1024,512]{1,0:T(8,128)(2,1)}, bf16[1024,512]{1,0:T(8,128)(2,1)}, bf16[512,512]{1...) custom-call(s32[4]{0:T(128)} %pad_add_fusion.pos_ref, bf16[1024,512]{1,0:T(8,128)(2,1)} %tok_ref.3, ...), custom_call_target="tpu_custom_call" | custom-call | flops 12000000000 | bytes 1 | tf_op jit(solution)/shard_map/feed/pallas_call | solution.py:648
  36.2 0.2 collective-permute-start.8
  36.4 1.0 copy-done.25
  37.5 0.8 collective-permute-done.8.b_ref
  38.5 1.6 %collective-permute-start.10 = (bf16[512,512]{1,0:T(8,128)(2,1)S(1)}, bf16[512,512]{1,0:T(8,128)(2,1)S(1)}, u32[]{:S(2)}, u32[]{:S(2)}) collective-permute-start(bf16[512,512]{1,0:T(8,128)(2,1)S(1)} %add.26.own_ref), channel_id=1, source_target_pairs={{0,2},{1,3},{2,0},{3,1},{4,6},{5,7},{6,4},{7,5},{8,10},{9,11},{10,... | collective-permute-start | bytes 1572872 | tf_op jit(solution)/shard_map/sum_second/ppermute | solution.py:624
  40.1 3.0 %weights.1 = (bf16[512,512]{1,0:T(8,128)(2,1)S(1)}, bf16[512,512]{1,0:T(8,128)(2,1)S(1)}, bf16[512,512]{1,0:T(8,128)(2,1)S(1)}, bf16[512,512]{1,0:T(8,128)(2,1)S(1)}) custom-call(s32[4]{0:T(128)S(1)} %copy-done.2, bf16[1024,512]{1,0:T(8,128)(2,1)S(1)} %copy-done.19, bf16[1024,512]{1,0:T(8,128)(2,1)S(1)} %copy-done.18, bf16[1024,512]{1,0:T(8,128)(2,1)S(1)} %copy-done.20, ...), custom_call_target="tpu_custom_call" | custom-call | flops 12000000000 | bytes 1 | tf_op jit(solution)/shard_map/weights/pallas_call | solution.py:648
  43.1 0.6 collective-permute-start.9
  43.7 0.4 collective-permute-start.15
  44.2 1.1 collective-permute-done.9.b_ref
  45.4 7.1 %collective-permute-done.10.far_ref = bf16[512,512]{1,0:T(8,128)(2,1)S(1)} collective-permute-done((bf16[512,512]{1,0:T(8,128)(2,1)S(1)}, bf16[512,512]{1,0:T(8,128)(2,1)S(1)}, u32[]{:S(2)}, u32[]{:S(2)}) %collective-permute-start.10) | collective-permute-done | bytes 524320 | tf_op jit(solution)/shard_map/sum_second/ppermute | solution.py:624
  52.5 0.5 collective-permute-start.14
  53.0 1.5 %collective-permute-start.11 = (bf16[512,512]{1,0:T(8,128)(2,1)S(1)}, bf16[512,512]{1,0:T(8,128)(2,1)S(1)}, u32[]{:S(2)}, u32[]{:S(2)}) collective-permute-start(bf16[512,512]{1,0:T(8,128)(2,1)S(1)} %add.27.own_ref), channel_id=1, source_target_pairs={{0,2},{1,3},{2,0},{3,1},{4,6},{5,7},{6,4},{7,5},{8,10},{9,11},{10,... | collective-permute-start | bytes 1572872 | tf_op jit(solution)/shard_map/sum_output/ppermute | solution.py:624
  54.6 5.5 %back.1 = (bf16[1024,512]{1,0:T(8,128)(2,1)S(1)}, bf16[1024,384]{1,0:T(8,128)(2,1)S(1)}, f32[4,2,8,128]{3,2,1,0:T(8,128)S(1)}, f32[32,512]{1,0:T(8,128)S(1)}) custom-call(s32[4]{0:T(128)S(1)} %copy-done.2, bf16[512,512]{1,0:T(8,128)(2,1)S(1)} %add.26.own_ref, bf16[512,512]{1,0:T(8,128)(2,1)S(1)} %collective-permute-done.10.far_ref, ...), custom_call_target="tpu_custom_call" | custom-call | flops 12000000000 | bytes 1 | tf_op jit(solution)/shard_map/back/pallas_call | solution.py:1111
  60.1 0.2 split.2
  60.3 0.8 copy-done.16
  61.0 0.3 copy-done.23
  61.3 3.9 %rest_weights.1 = (bf16[272,512]{1,0:T(8,128)(2,1)}, bf16[272,512]{1,0:T(8,128)(2,1)}) custom-call(s32[1]{0:T(128)} %bitcast.3.bit_ref, bf16[1024,512]{1,0:T(8,128)(2,1)} %get-tuple-element.293.first_ref, bf16[1024,384]{1,0:T(8,128)(2,1)} %copy-done.23, bf16[1024,512]{1,0:T(8,128)(2,1)} %copy-done.16, bf16[1024,128]{1,0:T(8,128)(2,1)} %copy-done.7, ...), custom_call_target="tpu_custom_call" | custom-call | flops 12000000000 | bytes 1 | tf_op jit(solution)/shard_map/rest_weights/pallas_call | solution.py:648
  65.2 1.7 %collective-permute-done.11.far_ref = bf16[512,512]{1,0:T(8,128)(2,1)S(1)} collective-permute-done((bf16[512,512]{1,0:T(8,128)(2,1)S(1)}, bf16[512,512]{1,0:T(8,128)(2,1)S(1)}, u32[]{:S(2)}, u32[]{:S(2)}) %collective-permute-start.11) | collective-permute-done | bytes 524320 | tf_op jit(solution)/shard_map/sum_output/ppermute | solution.py:624
  66.9 1.5 %collective-permute-start.19 = (bf16[256,512]{1,0:T(8,128)(2,1)S(1)}, bf16[256,512]{1,0:T(8,128)(2,1)S(1)}, u32[]{:S(2)}, u32[]{:S(2)}) collective-permute-start(bf16[256,512]{1,0:T(8,128)(2,1)S(1)} %get-tuple-element.310), channel_id=1, source_target_pairs={{0,4},{4,0},{8,12},{12,8},{16,20},{20,16},{24,28},{28,24},{1,5},{5... | collective-permute-start | bytes 786440 | tf_op jit(solution)/shard_map/feed_weights/ppermute | solution.py:624
  68.4 0.4 collective-permute-start.18
  68.8 1.1 copy-done.24
  70.0 2.0 %first.1 = (bf16[528,512]{1,0:T(8,128)(2,1)S(1)}, bf16[528,512]{1,0:T(8,128)(2,1)S(1)}) custom-call(s32[4]{0:T(128)S(1)} %copy-done.2, bf16[1024,384]{1,0:T(8,128)(2,1)S(1)} %copy-done.24, f32[4,2,8,128]{3,2,1,0:T(8,128)S(1)} %copy-done.28, bf16[4,5,16,128]{3,2,1,0:T(8,128)(2,1)S(1)} %copy-done.1, bf16[3,512,128]{2,1,0:T(8,128)(2,1)S(1)} %copy-done.6, ...), custom_call_target="tpu_custom_call" | custom-call | flops 12000000000 | bytes 1 | tf_op jit(solution)/shard_map/first/pallas_call | solution.py:648
  72.1 3.5 %collective-permute-done.19.b_ref = bf16[256,512]{1,0:T(8,128)(2,1)S(1)} collective-permute-done((bf16[256,512]{1,0:T(8,128)(2,1)S(1)}, bf16[256,512]{1,0:T(8,128)(2,1)S(1)}, u32[]{:S(2)}, u32[]{:S(2)}) %collective-permute-start.19) | collective-permute-done | bytes 262176 | tf_op jit(solution)/shard_map/feed_weights/ppermute | solution.py:624
  75.7 2.7 %collective-permute-start.21 = (bf16[128,512]{1,0:T(8,128)(2,1)S(1)}, bf16[128,512]{1,0:T(8,128)(2,1)S(1)}, u32[]{:S(2)}, u32[]{:S(2)}) collective-permute-start(bf16[128,512]{1,0:T(8,128)(2,1)S(1)} %get-tuple-element.328), channel_id=1, source_target_pairs={{0,16},{4,20},{8,24},{12,28},{16,0},{20,4},{24,8},{28,12},{1,17},{... | collective-permute-start | bytes 393224 | tf_op jit(solution)/shard_map/feed_weights/ppermute | solution.py:624
  78.4 1.6 %collective-permute-start.22 = (bf16[144,512]{1,0:T(8,128)(2,1)S(1)}, bf16[144,512]{1,0:T(8,128)(2,1)S(1)}, u32[]{:S(2)}, u32[]{:S(2)}) collective-permute-start(bf16[144,512]{1,0:T(8,128)(2,1)S(1)} %get-tuple-element.329), channel_id=1, source_target_pairs={{0,4},{4,0},{8,12},{12,8},{16,20},{20,16},{24,28},{28,24},{1,5},{5... | collective-permute-start | bytes 442376 | tf_op jit(solution)/shard_map/rest_weights/ppermute | solution.py:624
  80.0 0.1 pair.1.near_ref.own_ref
  80.1 1.5 %collective-permute-start.20 = (bf16[528,512]{1,0:T(8,128)(2,1)S(1)}, bf16[528,512]{1,0:T(8,128)(2,1)S(1)}, u32[]{:S(2)}, u32[]{:S(2)}) collective-permute-start(bf16[528,512]{1,0:T(8,128)(2,1)S(1)} %pair.1.near_ref.own_ref), channel_id=1, source_target_pairs={{0,2},{1,3},{2,0},{3,1},{4,6},{5,7},{6,4},{7,5},{8,10},{9,11},{10,... | collective-permute-start | bytes 1622024 | tf_op jit(solution)/shard_map/sum_first/ppermute | solution.py:624
  81.7 1.9 %output.1 = bf16[1024,512]{1,0:T(8,128)(2,1)} custom-call(s32[4]{0:T(128)S(1)} %copy-done.2, bf16[512,512]{1,0:T(8,128)(2,1)S(1)} %add.27.own_ref, bf16[512,512]{1,0:T(8,128)(2,1)S(1)} %collective-permute-done.11.far_ref, bf16[512,512]{1,0:T(8,128)(2,1)S(1)} %collective-permute-done.14.other_ref, bf16[512,512]{1,0:T(8,128)(2,1)S(1)} %collective-permute-done.16.other_far_ref, ...), custom_call_target="tpu_custom_call" | custom-call | flops 12000000000 | bytes 1 | tf_op jit(solution)/shard_map/output/pallas_call | solution.py:648
  83.7 0.2 split_second.1
  83.9 0.6 collective-permute-done.21.b_ref
  84.6 1.5 %collective-permute-start.27 = (bf16[64,512]{1,0:T(8,128)(2,1)S(1)}, bf16[64,512]{1,0:T(8,128)(2,1)S(1)}, u32[]{:S(2)}, u32[]{:S(2)}) collective-permute-start(bf16[64,512]{1,0:T(8,128)(2,1)S(1)} %get-tuple-element.342), channel_id=1, source_target_pairs={{0,16},{4,20},{8,24},{12,28},{16,0},{20,4},{24,8},{28,12},{1,17},{... | collective-permute-start | bytes 196616 | tf_op jit(solution)/shard_map/rest_weights/ppermute | solution.py:624
  86.1 1.5 %collective-permute-start.29 = (bf16[128,512]{1,0:T(8,128)(2,1)S(1)}, bf16[128,512]{1,0:T(8,128)(2,1)S(1)}, u32[]{:S(2)}, u32[]{:S(2)}) collective-permute-start(bf16[128,512]{1,0:T(8,128)(2,1)S(1)} %add.28.a_ref), channel_id=1, source_target_pairs={{0,16},{4,20},{8,24},{12,28},{16,0},{20,4},{24,8},{28,12},{1,17},{... | collective-permute-start | bytes 393224 | tf_op jit(solution)/shard_map/feed_weights/ppermute | solution.py:624
  87.6 6.0 %collective-permute-done.20.far_ref = bf16[528,512]{1,0:T(8,128)(2,1)S(1)} collective-permute-done((bf16[528,512]{1,0:T(8,128)(2,1)S(1)}, bf16[528,512]{1,0:T(8,128)(2,1)S(1)}, u32[]{:S(2)}, u32[]{:S(2)}) %collective-permute-start.20) | collective-permute-done | bytes 540704 | tf_op jit(solution)/shard_map/sum_first/ppermute | solution.py:624
  93.6 1.5 %collective-permute-start.26 = (f32[8,512]{1,0:T(8,128)S(1)}, f32[8,512]{1,0:T(8,128)S(1)}, u32[]{:S(2)}, u32[]{:S(2)}) collective-permute-start(f32[8,512]{1,0:T(8,128)S(1)} %plus.1.extra_ref), channel_id=1, source_target_pairs={{0,2},{1,3},{2,0},{3,1},{4,6},{5,7},{6,4},{7,5},{8,10},{9,11},{10,... | collective-permute-start | bytes 49160 | tf_op jit(solution)/shard_map/sum_extra/ppermute | solution.py:624
  95.2 1.1 collective-permute-start.28
  96.4 1.0 collective-permute-start.31
  97.4 0.7 collective-permute-start.34
  98.1 4.4 %collective-permute-done.28.b_ref = bf16[80,512]{1,0:T(8,128)(2,1)S(1)} collective-permute-done((bf16[80,512]{1,0:T(8,128)(2,1)S(1)}, bf16[80,512]{1,0:T(8,128)(2,1)S(1)}, u32[]{:S(2)}, u32[]{:S(2)}) %collective-permute-start.28) | collective-permute-done | bytes 81952 | tf_op jit(solution)/shard_map/rest_weights/ppermute | solution.py:624
  102.5 0.6 collective-permute-start.30
  103.1 1.3 %collective-permute-done.23.other_ref = bf16[528,512]{1,0:T(8,128)(2,1)S(1)} collective-permute-done((bf16[528,512]{1,0:T(8,128)(2,1)S(1)}, bf16[528,512]{1,0:T(8,128)(2,1)S(1)}, u32[]{:S(2)}, u32[]{:S(2)}) %collective-permute-start.23) | collective-permute-done | bytes 540704 | tf_op jit(solution)/shard_map/sum_first/ppermute | solution.py:624
  104.4 3.1 %last.1 = bf16[1024,512]{1,0:T(8,128)(2,1)} custom-call(s32[4]{0:T(128)S(1)} %copy-done.2, bf16[528,512]{1,0:T(8,128)(2,1)S(1)} %pair.1.near_ref.own_ref, bf16[528,512]{1,0:T(8,128)(2,1)S(1)} %collective-permute-done.20.far_ref, bf16[528,512]{1,0:T(8,128)(2,1)S(1)} %collective-permute-done.23.other_ref, ...), custom_call_target="tpu_custom_call" | custom-call | flops 12000000000 | bytes 1 | tf_op jit(solution)/shard_map/last/pallas_call | solution.py:648
  107.5 0.6 collective-permute-start.33
  108.0 0.8 collective-permute-done.30.b_ref
  108.8 0.9 collective-permute-start.32
  109.7 1.0 feed_unpack.2
  110.8 5.0 %collective-permute-done.33.one_ref = bf16[256,512]{1,0:T(8,128)(2,1)S(1)} collective-permute-done((bf16[256,512]{1,0:T(8,128)(2,1)S(1)}, bf16[256,512]{1,0:T(8,128)(2,1)S(1)}, u32[]{:S(2)}, u32[]{:S(2)}) %collective-permute-start.33) | collective-permute-done | bytes 262176 | tf_op jit(solution)/shard_map/feed_weights/ppermute | solution.py:624
  115.8 1.0 feed_unpack.3
  116.9 0.3 collective-permute-done.32.far_ref
  117.2 1.1 rest_unpack.1
  (115 shorter events, 1.1 us)
Async XLA Ops:
  0.6 6.9 %collective-permute-start = (bf16[128,512]{1,0:T(8,128)(2,1)}, bf16[128,512]{1,0:T(8,128)(2,1)S(1)}, u32[]{:S(2)}, u32[]{:S(2)}) collective-permute-start(bf16[128,512]{1,0:T(8,128)(2,1)} %wo_ref), channel_id=1, source_target_pairs={{0,2},{1,3},{2,0},{3,1},{4,6},{5,7},{6,4},{7,5},{8,10},{9,11},{10,... | collective-permute-start | bytes 393224 | tf_op jit(solution)/shard_map/gather_w_out/ppermute | solution.py:624
  7.6 5.7 %copy-start.34 = (bf16[128,512]{1,0:T(8,128)(2,1)}, bf16[128,512]{1,0:T(8,128)(2,1)S(1)}, u32[]{:S(2)}) copy-start(bf16[128,512]{1,0:T(8,128)(2,1)S(1)} %collective-permute-done.refs_6_) | copy-start | bytes 393220
  7.6 5.7 %copy-start.8 = (bf16[128,512]{1,0:T(8,128)(2,1)S(1)}, bf16[128,512]{1,0:T(8,128)(2,1)}, u32[]{:S(2)}) copy-start(bf16[128,512]{1,0:T(8,128)(2,1)} %wo_ref) | copy-start | bytes 393220
  7.6 4.1 %collective-permute-start.1 = (bf16[1,5,16,128]{3,2,1,0:T(8,128)(2,1)}, bf16[1,5,16,128]{3,2,1,0:T(8,128)(2,1)S(1)}, u32[]{:S(2)}, u32[]{:S(2)}) collective-permute-start(bf16[1,5,16,128]{3,2,1,0:T(8,128)(2,1)} %bitcast.27), channel_id=1, source_target_pairs={{0,4},{4,0},{8,12},{12,8},{16,20},{20,16},{24,28},{28,24},{1,5},{5... | collective-permute-start | bytes 61448 | tf_op jit(solution)/shard_map/summaries/ppermute | solution.py:624
  10.3 1.4 %copy-start.30 = (bf16[5,16,128]{2,1,0:T(8,128)(2,1)S(1)}, bf16[5,16,128]{2,1,0:T(8,128)(2,1)}, u32[]{:S(2)}) copy-start(bf16[5,16,128]{2,1,0:T(8,128)(2,1)} %get-tuple-element.212) | copy-start | bytes 61444
  11.7 4.1 %collective-permute-start.2 = (bf16[2,5,16,128]{3,2,1,0:T(8,128)(2,1)S(1)}, bf16[2,5,16,128]{3,2,1,0:T(8,128)(2,1)S(1)}, u32[]{:S(2)}, u32[]{:S(2)}) collective-permute-start(bf16[2,5,16,128]{3,2,1,0:T(8,128)(2,1)S(1)} %constant_dynamic-update-slice_fusion), channel_id=1, source_target_pairs={{0,8},{4,12},{8,0},{12,4},{16,24},{20,28},{24,16},{28,20},{1,9},{5... | collective-permute-start | bytes 122888 | tf_op jit(solution)/shard_map/summaries/ppermute | solution.py:624
  13.3 2.4 %collective-permute-start.3 = (bf16[128,512]{1,0:T(8,128)(2,1)S(1)}, bf16[128,512]{1,0:T(8,128)(2,1)S(1)}, u32[]{:S(2)}, u32[]{:S(2)}) collective-permute-start(bf16[128,512]{1,0:T(8,128)(2,1)S(1)} %copy-done.8), channel_id=1, source_target_pairs={{0,1},{1,0},{2,3},{3,2},{4,5},{5,4},{6,7},{7,6},{8,9},{9,8},{10,11... | collective-permute-start | bytes 393224 | tf_op jit(solution)/shard_map/gather_w_out/ppermute | solution.py:624
  13.3 2.5 %collective-permute-start.4 = (bf16[128,512]{1,0:T(8,128)(2,1)S(1)}, bf16[128,512]{1,0:T(8,128)(2,1)S(1)}, u32[]{:S(2)}, u32[]{:S(2)}) collective-permute-start(bf16[128,512]{1,0:T(8,128)(2,1)S(1)} %collective-permute-done.refs_6_), channel_id=1, source_target_pairs={{0,1},{1,0},{2,3},{3,2},{4,5},{5,4},{6,7},{7,6},{8,9},{9,8},{10,11... | collective-permute-start | bytes 393224 | tf_op jit(solution)/shard_map/gather_w_out/ppermute | solution.py:624
  15.7 38.8 %copy-start = (bf16[4,5,16,128]{3,2,1,0:T(8,128)(2,1)}, bf16[4,5,16,128]{3,2,1,0:T(8,128)(2,1)S(1)}, u32[]{:S(2)}) copy-start(bf16[4,5,16,128]{3,2,1,0:T(8,128)(2,1)S(1)} %constant_dynamic-update-slice_fusion.2.sums_ref) | copy-start | bytes 245764
  15.8 1.5 %copy-start.35 = (bf16[128,512]{1,0:T(8,128)(2,1)}, bf16[128,512]{1,0:T(8,128)(2,1)S(1)}, u32[]{:S(2)}) copy-start(bf16[128,512]{1,0:T(8,128)(2,1)S(1)} %collective-permute-done.3.refs_5_) | copy-start | bytes 393220
  15.8 1.5 %copy-start.36 = (bf16[128,512]{1,0:T(8,128)(2,1)}, bf16[128,512]{1,0:T(8,128)(2,1)S(1)}, u32[]{:S(2)}) copy-start(bf16[128,512]{1,0:T(8,128)(2,1)S(1)} %collective-permute-done.4.refs_7_) | copy-start | bytes 393220
  17.3 9.2 %copy-start.7 = (bf16[1024,128]{1,0:T(8,128)(2,1)}, bf16[1024,128]{1,0:T(8,128)(2,1)S(1)}, u32[]{:S(2)}) copy-start(bf16[1024,128]{1,0:T(8,128)(2,1)S(1)} %get-tuple-element.296.refs_0_.att_ref) | copy-start | bytes 786436
  17.3 7.6 %collective-permute-start.6 = (bf16[1024,128]{1,0:T(8,128)(2,1)S(1)}, bf16[1024,128]{1,0:T(8,128)(2,1)S(1)}, u32[]{:S(2)}, u32[]{:S(2)}) collective-permute-start(bf16[1024,128]{1,0:T(8,128)(2,1)S(1)} %get-tuple-element.296.refs_0_.att_ref), channel_id=1, source_target_pairs={{0,2},{1,3},{2,0},{3,1},{4,6},{5,7},{6,4},{7,5},{8,10},{9,11},{10,... | collective-permute-start | bytes 786440 | tf_op jit(solution)/shard_map/gather_attended/ppermute | solution.py:624
  18.9 6.7 %collective-permute-start.5 = (bf16[1024,128]{1,0:T(8,128)(2,1)S(1)}, bf16[1024,128]{1,0:T(8,128)(2,1)S(1)}, u32[]{:S(2)}, u32[]{:S(2)}) collective-permute-start(bf16[1024,128]{1,0:T(8,128)(2,1)S(1)} %get-tuple-element.296.refs_0_.att_ref), channel_id=1, source_target_pairs={{0,1},{1,0},{2,3},{3,2},{4,5},{5,4},{6,7},{7,6},{8,9},{9,8},{10,11... | collective-permute-start | bytes 786440 | tf_op jit(solution)/shard_map/gather_attended/ppermute | solution.py:624
  25.0 1.5 %copy-start.31 = (bf16[1024,128]{1,0:T(8,128)(2,1)}, bf16[1024,128]{1,0:T(8,128)(2,1)S(1)}, u32[]{:S(2)}) copy-start(bf16[1024,128]{1,0:T(8,128)(2,1)S(1)} %collective-permute-done.6.refs_2_) | copy-start | bytes 786436
  25.0 1.5 %collective-permute-start.7 = (bf16[1024,128]{1,0:T(8,128)(2,1)S(1)}, bf16[1024,128]{1,0:T(8,128)(2,1)S(1)}, u32[]{:S(2)}, u32[]{:S(2)}) collective-permute-start(bf16[1024,128]{1,0:T(8,128)(2,1)S(1)} %collective-permute-done.6.refs_2_), channel_id=1, source_target_pairs={{0,1},{1,0},{2,3},{3,2},{4,5},{5,4},{6,7},{7,6},{8,9},{9,8},{10,11... | collective-permute-start | bytes 786440 | tf_op jit(solution)/shard_map/gather_attended/ppermute | solution.py:624
  36.2 2.2 %collective-permute-start.8 = (bf16[512,512]{1,0:T(8,128)(2,1)}, bf16[512,512]{1,0:T(8,128)(2,1)S(1)}, u32[]{:S(2)}, u32[]{:S(2)}) collective-permute-start(bf16[512,512]{1,0:T(8,128)(2,1)} %get-tuple-element.250), channel_id=1, source_target_pairs={{0,1},{1,0},{2,3},{3,2},{4,5},{5,4},{6,7},{7,6},{8,9},{9,8},{10,11... | collective-permute-start | bytes 1572872 | tf_op jit(solution)/shard_map/sum_second/ppermute | solution.py:624
  37.5 2.6 %copy-start.2 = (s32[4]{0:T(128)S(1)}, s32[4]{0:T(128)}, u32[]{:S(2)}) copy-start(s32[4]{0:T(128)} %pad_add_fusion.pos_ref) | copy-start | bytes 52
  37.5 2.6 %copy-start.3 = (bf16[1024,512]{1,0:T(8,128)(2,1)S(1)}, bf16[1024,512]{1,0:T(8,128)(2,1)}, u32[]{:S(2)}) copy-start(bf16[1024,512]{1,0:T(8,128)(2,1)} %cot_ref.1) | copy-start | bytes 3145732
  37.5 2.6 %copy-start.5 = (bf16[512,512]{1,0:T(8,128)(2,1)S(1)}, bf16[512,512]{1,0:T(8,128)(2,1)}, u32[]{:S(2)}) copy-start(bf16[512,512]{1,0:T(8,128)(2,1)} %down_ref) | copy-start | bytes 1572868
  37.5 2.6 %copy-start.18 = (bf16[1024,512]{1,0:T(8,128)(2,1)S(1)}, bf16[1024,512]{1,0:T(8,128)(2,1)}, u32[]{:S(2)}) copy-start(bf16[1024,512]{1,0:T(8,128)(2,1)} %get-tuple-element.255.second_ref) | copy-start | bytes 3145732
  37.5 2.5 %copy-start.19 = (bf16[1024,512]{1,0:T(8,128)(2,1)S(1)}, bf16[1024,512]{1,0:T(8,128)(2,1)}, u32[]{:S(2)}) copy-start(bf16[1024,512]{1,0:T(8,128)(2,1)} %get-tuple-element.254.active_ref) | copy-start | bytes 3145732
  37.5 2.5 %copy-start.20 = (bf16[1024,512]{1,0:T(8,128)(2,1)S(1)}, bf16[1024,512]{1,0:T(8,128)(2,1)}, u32[]{:S(2)}) copy-start(bf16[1024,512]{1,0:T(8,128)(2,1)} %get-tuple-element.256.grad_ref) | copy-start | bytes 3145732
  38.5 14.1 %collective-permute-start.10 = (bf16[512,512]{1,0:T(8,128)(2,1)S(1)}, bf16[512,512]{1,0:T(8,128)(2,1)S(1)}, u32[]{:S(2)}, u32[]{:S(2)}) collective-permute-start(bf16[512,512]{1,0:T(8,128)(2,1)S(1)} %add.26.own_ref), channel_id=1, source_target_pairs={{0,2},{1,3},{2,0},{3,1},{4,6},{5,7},{6,4},{7,5},{8,10},{9,11},{10,... | collective-permute-start | bytes 1572872 | tf_op jit(solution)/shard_map/sum_second/ppermute | solution.py:624
  40.0 14.5 %collective-permute-start.12 = (bf16[512,512]{1,0:T(8,128)(2,1)S(1)}, bf16[512,512]{1,0:T(8,128)(2,1)S(1)}, u32[]{:S(2)}, u32[]{:S(2)}) collective-permute-start(bf16[512,512]{1,0:T(8,128)(2,1)S(1)} %add.26.own_ref), channel_id=1, source_target_pairs={{0,1},{1,0},{2,3},{3,2},{4,5},{5,4},{6,7},{7,6},{8,9},{9,8},{10,11... | collective-permute-start | bytes 1572872 | tf_op jit(solution)/shard_map/sum_second/ppermute | solution.py:624
  40.1 3.6 %copy-start.12 = (f32[512]{0:T(512)S(1)}, f32[512]{0:T(512)}, u32[]{:S(2)}) copy-start(f32[512]{0:T(512)} %param.14) | copy-start | bytes 6148
  43.1 2.1 %collective-permute-start.9 = (bf16[512,512]{1,0:T(8,128)(2,1)S(1)}, bf16[512,512]{1,0:T(8,128)(2,1)S(1)}, u32[]{:S(2)}, u32[]{:S(2)}) collective-permute-start(bf16[512,512]{1,0:T(8,128)(2,1)S(1)} %get-tuple-element.260), channel_id=1, source_target_pairs={{0,1},{1,0},{2,3},{3,2},{4,5},{5,4},{6,7},{7,6},{8,9},{9,8},{10,11... | collective-permute-start | bytes 1572872 | tf_op jit(solution)/shard_map/sum_output/ppermute | solution.py:624
  43.7 16.4 %collective-permute-start.15 = (bf16[512,512]{1,0:T(8,128)(2,1)S(1)}, bf16[512,512]{1,0:T(8,128)(2,1)S(1)}, u32[]{:S(2)}, u32[]{:S(2)}) collective-permute-start(bf16[512,512]{1,0:T(8,128)(2,1)S(1)} %get-tuple-element.286), channel_id=1, source_target_pairs={{0,8},{4,12},{8,0},{12,4},{16,24},{20,28},{24,16},{28,20},{1,9},{5... | collective-permute-start | bytes 1572872 | tf_op jit(solution)/shard_map/feed_weights/ppermute | solution.py:624
  45.4 9.2 %copy-start.9 = (bf16[128,512]{1,0:T(8,128)(2,1)S(1)}, bf16[128,512]{1,0:T(8,128)(2,1)}, u32[]{:S(2)}) copy-start(bf16[128,512]{1,0:T(8,128)(2,1)} %wo_ref) | copy-start | bytes 393220
  45.4 9.2 %copy-start.10 = (f32[512]{0:T(512)S(1)}, f32[512]{0:T(512)}, u32[]{:S(2)}) copy-start(f32[512]{0:T(512)} %param.19) | copy-start | bytes 6148
  45.4 9.2 %copy-start.14 = (f32[1024,512]{1,0:T(8,128)S(1)}, f32[1024,512]{1,0:T(8,128)}, u32[]{:S(2)}) copy-start(f32[1024,512]{1,0:T(8,128)} %get-tuple-element.326.mid_ref) | copy-start | bytes 6291460
  45.4 9.2 %copy-start.22 = (bf16[3,1024,128]{2,1,0:T(8,128)(2,1)S(1)}, bf16[3,1024,128]{2,1,0:T(8,128)(2,1)}, u32[]{:S(2)}) copy-start(bf16[3,1024,128]{2,1,0:T(8,128)(2,1)} %get-tuple-element.280.qkv_ref) | copy-start | bytes 2359300
  52.5 2.0 %collective-permute-start.13 = (bf16[512,512]{1,0:T(8,128)(2,1)S(1)}, bf16[512,512]{1,0:T(8,128)(2,1)S(1)}, u32[]{:S(2)}, u32[]{:S(2)}) collective-permute-start(bf16[512,512]{1,0:T(8,128)(2,1)S(1)} %collective-permute-done.10.far_ref), channel_id=1, source_target_pairs={{0,1},{1,0},{2,3},{3,2},{4,5},{5,4},{6,7},{7,6},{8,9},{9,8},{10,11... | collective-permute-start | bytes 1572872 | tf_op jit(solution)/shard_map/sum_second/ppermute | solution.py:624
  52.5 8.8 %collective-permute-start.14 = (bf16[512,512]{1,0:T(8,128)(2,1)S(1)}, bf16[512,512]{1,0:T(8,128)(2,1)S(1)}, u32[]{:S(2)}, u32[]{:S(2)}) collective-permute-start(bf16[512,512]{1,0:T(8,128)(2,1)S(1)} %add.27.own_ref), channel_id=1, source_target_pairs={{0,1},{1,0},{2,3},{3,2},{4,5},{5,4},{6,7},{7,6},{8,9},{9,8},{10,11... | collective-permute-start | bytes 1572872 | tf_op jit(solution)/shard_map/sum_output/ppermute | solution.py:624
  53.0 13.8 %collective-permute-start.11 = (bf16[512,512]{1,0:T(8,128)(2,1)S(1)}, bf16[512,512]{1,0:T(8,128)(2,1)S(1)}, u32[]{:S(2)}, u32[]{:S(2)}) collective-permute-start(bf16[512,512]{1,0:T(8,128)(2,1)S(1)} %add.27.own_ref), channel_id=1, source_target_pairs={{0,2},{1,3},{2,0},{3,1},{4,6},{5,7},{6,4},{7,5},{8,10},{9,11},{10,... | collective-permute-start | bytes 1572872 | tf_op jit(solution)/shard_map/sum_output/ppermute | solution.py:624
  61.3 7.5 %copy-start.1 = (bf16[4,5,16,128]{3,2,1,0:T(8,128)(2,1)S(1)}, bf16[4,5,16,128]{3,2,1,0:T(8,128)(2,1)}, u32[]{:S(2)}) copy-start(bf16[4,5,16,128]{3,2,1,0:T(8,128)(2,1)} %copy-done) | copy-start | bytes 245764
  61.3 7.5 %copy-start.4 = (bf16[1024,512]{1,0:T(8,128)(2,1)S(1)}, bf16[1024,512]{1,0:T(8,128)(2,1)}, u32[]{:S(2)}) copy-start(bf16[1024,512]{1,0:T(8,128)(2,1)} %tok_ref.3) | copy-start | bytes 3145732
  61.3 7.5 %copy-start.6 = (bf16[3,512,128]{2,1,0:T(8,128)(2,1)S(1)}, bf16[3,512,128]{2,1,0:T(8,128)(2,1)}, u32[]{:S(2)}) copy-start(bf16[3,512,128]{2,1,0:T(8,128)(2,1)} %w_ref.2) | copy-start | bytes 1179652
  61.3 7.5 %copy-start.28 = (f32[4,2,8,128]{3,2,1,0:T(8,128)S(1)}, f32[4,2,8,128]{3,2,1,0:T(8,128)}, u32[]{:S(2)}) copy-start(f32[4,2,8,128]{3,2,1,0:T(8,128)} %copy-done.27) | copy-start | bytes 98308
  66.9 14.8 %collective-permute-start.16 = (bf16[512,512]{1,0:T(8,128)(2,1)S(1)}, bf16[512,512]{1,0:T(8,128)(2,1)S(1)}, u32[]{:S(2)}, u32[]{:S(2)}) collective-permute-start(bf16[512,512]{1,0:T(8,128)(2,1)S(1)} %collective-permute-done.11.far_ref), channel_id=1, source_target_pairs={{0,1},{1,0},{2,3},{3,2},{4,5},{5,4},{6,7},{7,6},{8,9},{9,8},{10,11... | collective-permute-start | bytes 1572872 | tf_op jit(solution)/shard_map/sum_output/ppermute | solution.py:624
  66.9 8.7 %collective-permute-start.19 = (bf16[256,512]{1,0:T(8,128)(2,1)S(1)}, bf16[256,512]{1,0:T(8,128)(2,1)S(1)}, u32[]{:S(2)}, u32[]{:S(2)}) collective-permute-start(bf16[256,512]{1,0:T(8,128)(2,1)S(1)} %get-tuple-element.310), channel_id=1, source_target_pairs={{0,4},{4,0},{8,12},{12,8},{16,20},{20,16},{24,28},{28,24},{1,5},{5... | collective-permute-start | bytes 786440 | tf_op jit(solution)/shard_map/feed_weights/ppermute | solution.py:624
  68.4 10.0 %collective-permute-start.18 = (bf16[272,512]{1,0:T(8,128)(2,1)}, bf16[272,512]{1,0:T(8,128)(2,1)S(1)}, u32[]{:S(2)}, u32[]{:S(2)}) collective-permute-start(bf16[272,512]{1,0:T(8,128)(2,1)} %get-tuple-element.309), channel_id=1, source_target_pairs={{0,8},{4,12},{8,0},{12,4},{16,24},{20,28},{24,16},{28,20},{1,9},{5... | collective-permute-start | bytes 835592 | tf_op jit(solution)/shard_map/rest_weights/ppermute | solution.py:624
  72.0 8.0 %collective-permute-start.17 = (bf16[528,512]{1,0:T(8,128)(2,1)S(1)}, bf16[528,512]{1,0:T(8,128)(2,1)S(1)}, u32[]{:S(2)}, u32[]{:S(2)}) collective-permute-start(bf16[528,512]{1,0:T(8,128)(2,1)S(1)} %get-tuple-element.308), channel_id=1, source_target_pairs={{0,1},{1,0},{2,3},{3,2},{4,5},{5,4},{6,7},{7,6},{8,9},{9,8},{10,11... | collective-permute-start | bytes 1622024 | tf_op jit(solution)/shard_map/sum_first/ppermute | solution.py:624
  75.6 2.7 %copy-start.26 = (bf16[272,512]{1,0:T(8,128)(2,1)S(1)}, bf16[272,512]{1,0:T(8,128)(2,1)}, u32[]{:S(2)}) copy-start(bf16[272,512]{1,0:T(8,128)(2,1)} %get-tuple-element.316.a_ref) | copy-start | bytes 835588
  75.7 8.9 %collective-permute-start.21 = (bf16[128,512]{1,0:T(8,128)(2,1)S(1)}, bf16[128,512]{1,0:T(8,128)(2,1)S(1)}, u32[]{:S(2)}, u32[]{:S(2)}) collective-permute-start(bf16[128,512]{1,0:T(8,128)(2,1)S(1)} %get-tuple-element.328), channel_id=1, source_target_pairs={{0,16},{4,20},{8,24},{12,28},{16,0},{20,4},{24,8},{28,12},{1,17},{... | collective-permute-start | bytes 393224 | tf_op jit(solution)/shard_map/feed_weights/ppermute | solution.py:624
  78.4 5.3 %collective-permute-start.22 = (bf16[144,512]{1,0:T(8,128)(2,1)S(1)}, bf16[144,512]{1,0:T(8,128)(2,1)S(1)}, u32[]{:S(2)}, u32[]{:S(2)}) collective-permute-start(bf16[144,512]{1,0:T(8,128)(2,1)S(1)} %get-tuple-element.329), channel_id=1, source_target_pairs={{0,4},{4,0},{8,12},{12,8},{16,20},{20,16},{24,28},{28,24},{1,5},{5... | collective-permute-start | bytes 442376 | tf_op jit(solution)/shard_map/rest_weights/ppermute | solution.py:624
  80.0 1.7 %copy-start.11 = (f32[512]{0:T(512)S(1)}, f32[512]{0:T(512)}, u32[]{:S(2)}) copy-start(f32[512]{0:T(512)} %param.24) | copy-start | bytes 6148
  80.0 1.7 %copy-start.15 = (f32[1024,512]{1,0:T(8,128)S(1)}, f32[1024,512]{1,0:T(8,128)}, u32[]{:S(2)}) copy-start(f32[1024,512]{1,0:T(8,128)} %get-tuple-element.326.mid_ref) | copy-start | bytes 6291460
  80.1 13.4 %collective-permute-start.20 = (bf16[528,512]{1,0:T(8,128)(2,1)S(1)}, bf16[528,512]{1,0:T(8,128)(2,1)S(1)}, u32[]{:S(2)}, u32[]{:S(2)}) collective-permute-start(bf16[528,512]{1,0:T(8,128)(2,1)S(1)} %pair.1.near_ref.own_ref), channel_id=1, source_target_pairs={{0,2},{1,3},{2,0},{3,1},{4,6},{5,7},{6,4},{7,5},{8,10},{9,11},{10,... | collective-permute-start | bytes 1622024 | tf_op jit(solution)/shard_map/sum_first/ppermute | solution.py:624
  83.9 9.6 %collective-permute-start.25 = (f32[8,512]{1,0:T(8,128)S(1)}, f32[8,512]{1,0:T(8,128)S(1)}, u32[]{:S(2)}, u32[]{:S(2)}) collective-permute-start(f32[8,512]{1,0:T(8,128)S(1)} %get-tuple-element.339.a_ref), channel_id=1, source_target_pairs={{0,1},{1,0},{2,3},{3,2},{4,5},{5,4},{6,7},{7,6},{8,9},{9,8},{10,11... | collective-permute-start | bytes 49160 | tf_op jit(solution)/shard_map/sum_extra/ppermute | solution.py:624
  84.6 10.6 %collective-permute-start.27 = (bf16[64,512]{1,0:T(8,128)(2,1)S(1)}, bf16[64,512]{1,0:T(8,128)(2,1)S(1)}, u32[]{:S(2)}, u32[]{:S(2)}) collective-permute-start(bf16[64,512]{1,0:T(8,128)(2,1)S(1)} %get-tuple-element.342), channel_id=1, source_target_pairs={{0,16},{4,20},{8,24},{12,28},{16,0},{20,4},{24,8},{28,12},{1,17},{... | collective-permute-start | bytes 196616 | tf_op jit(solution)/shard_map/rest_weights/ppermute | solution.py:624
  86.1 9.0 %copy-start.29 = (f32[8,512]{1,0:T(8,128)S(1)}, f32[8,512]{1,0:T(8,128)}, u32[]{:S(2)}) copy-start(f32[8,512]{1,0:T(8,128)} %get-tuple-element.349.up_ref) | copy-start | bytes 49156
  86.1 10.2 %collective-permute-start.29 = (bf16[128,512]{1,0:T(8,128)(2,1)S(1)}, bf16[128,512]{1,0:T(8,128)(2,1)S(1)}, u32[]{:S(2)}, u32[]{:S(2)}) collective-permute-start(bf16[128,512]{1,0:T(8,128)(2,1)S(1)} %add.28.a_ref), channel_id=1, source_target_pairs={{0,16},{4,20},{8,24},{12,28},{16,0},{20,4},{24,8},{28,12},{1,17},{... | collective-permute-start | bytes 393224 | tf_op jit(solution)/shard_map/feed_weights/ppermute | solution.py:624
  93.6 10.8 %collective-permute-start.24 = (bf16[528,512]{1,0:T(8,128)(2,1)S(1)}, bf16[528,512]{1,0:T(8,128)(2,1)S(1)}, u32[]{:S(2)}, u32[]{:S(2)}) collective-permute-start(bf16[528,512]{1,0:T(8,128)(2,1)S(1)} %collective-permute-done.20.far_ref), channel_id=1, source_target_pairs={{0,1},{1,0},{2,3},{3,2},{4,5},{5,4},{6,7},{7,6},{8,9},{9,8},{10,11... | collective-permute-start | bytes 1622024 | tf_op jit(solution)/shard_map/sum_first/ppermute | solution.py:624
  93.6 8.9 %collective-permute-start.26 = (f32[8,512]{1,0:T(8,128)S(1)}, f32[8,512]{1,0:T(8,128)S(1)}, u32[]{:S(2)}, u32[]{:S(2)}) collective-permute-start(f32[8,512]{1,0:T(8,128)S(1)} %plus.1.extra_ref), channel_id=1, source_target_pairs={{0,2},{1,3},{2,0},{3,1},{4,6},{5,7},{6,4},{7,5},{8,10},{9,11},{10,... | collective-permute-start | bytes 49160 | tf_op jit(solution)/shard_map/sum_extra/ppermute | solution.py:624
  95.2 7.3 %collective-permute-start.28 = (bf16[80,512]{1,0:T(8,128)(2,1)S(1)}, bf16[80,512]{1,0:T(8,128)(2,1)S(1)}, u32[]{:S(2)}, u32[]{:S(2)}) collective-permute-start(bf16[80,512]{1,0:T(8,128)(2,1)S(1)} %piece.1.a_ref), channel_id=1, source_target_pairs={{0,16},{4,20},{8,24},{12,28},{16,0},{20,4},{24,8},{28,12},{1,17},{... | collective-permute-start | bytes 245768 | tf_op jit(solution)/shard_map/rest_weights/ppermute | solution.py:624
  96.3 8.1 %copy-start.13 = (f32[512]{0:T(512)S(1)}, f32[512]{0:T(512)}, u32[]{:S(2)}) copy-start(f32[512]{0:T(512)} %param.14) | copy-start | bytes 6148
  96.3 8.0 %copy-start.17 = (bf16[1024,512]{1,0:T(8,128)(2,1)S(1)}, bf16[1024,512]{1,0:T(8,128)(2,1)}, u32[]{:S(2)}) copy-start(bf16[1024,512]{1,0:T(8,128)(2,1)} %copy-done.16) | copy-start | bytes 3145732
  96.4 11.1 %collective-permute-start.31 = (bf16[256,512]{1,0:T(8,128)(2,1)S(1)}, bf16[256,512]{1,0:T(8,128)(2,1)S(1)}, u32[]{:S(2)}, u32[]{:S(2)}) collective-permute-start(bf16[256,512]{1,0:T(8,128)(2,1)S(1)} %concat.1.own_ref), channel_id=1, source_target_pairs={{0,8},{4,12},{8,0},{12,4},{16,24},{20,28},{24,16},{28,20},{1,9},{5... | collective-permute-start | bytes 786440 | tf_op jit(solution)/shard_map/feed_weights/ppermute | solution.py:624
  97.4 12.4 %collective-permute-start.34 = (bf16[256,512]{1,0:T(8,128)(2,1)S(1)}, bf16[256,512]{1,0:T(8,128)(2,1)S(1)}, u32[]{:S(2)}, u32[]{:S(2)}) collective-permute-start(bf16[256,512]{1,0:T(8,128)(2,1)S(1)} %concat.1.own_ref), channel_id=1, source_target_pairs={{0,4},{4,0},{8,12},{12,8},{16,20},{20,16},{24,28},{28,24},{1,5},{5... | collective-permute-start | bytes 786440 | tf_op jit(solution)/shard_map/feed_weights/ppermute | solution.py:624
  102.4 1.9 %collective-permute-start.23 = (bf16[528,512]{1,0:T(8,128)(2,1)S(1)}, bf16[528,512]{1,0:T(8,128)(2,1)S(1)}, u32[]{:S(2)}, u32[]{:S(2)}) collective-permute-start(bf16[528,512]{1,0:T(8,128)(2,1)S(1)} %pair.1.near_ref.own_ref), channel_id=1, source_target_pairs={{0,1},{1,0},{2,3},{3,2},{4,5},{5,4},{6,7},{7,6},{8,9},{9,8},{10,11... | collective-permute-start | bytes 1622024 | tf_op jit(solution)/shard_map/sum_first/ppermute | solution.py:624
  102.5 6.3 %collective-permute-start.30 = (bf16[144,512]{1,0:T(8,128)(2,1)S(1)}, bf16[144,512]{1,0:T(8,128)(2,1)S(1)}, u32[]{:S(2)}, u32[]{:S(2)}) collective-permute-start(bf16[144,512]{1,0:T(8,128)(2,1)S(1)} %merge.2.a_ref), channel_id=1, source_target_pairs={{0,4},{4,0},{8,12},{12,8},{16,20},{20,16},{24,28},{28,24},{1,5},{5... | collective-permute-start | bytes 442376 | tf_op jit(solution)/shard_map/rest_weights/ppermute | solution.py:624
  107.5 8.3 %collective-permute-start.33 = (bf16[256,512]{1,0:T(8,128)(2,1)S(1)}, bf16[256,512]{1,0:T(8,128)(2,1)S(1)}, u32[]{:S(2)}, u32[]{:S(2)}) collective-permute-start(bf16[256,512]{1,0:T(8,128)(2,1)S(1)} %collective-permute-done.31.own_ref), channel_id=1, source_target_pairs={{0,4},{4,0},{8,12},{12,8},{16,20},{20,16},{24,28},{28,24},{1,5},{5... | collective-permute-start | bytes 786440 | tf_op jit(solution)/shard_map/feed_weights/ppermute | solution.py:624
  108.8 8.4 %collective-permute-start.32 = (bf16[272,512]{1,0:T(8,128)(2,1)S(1)}, bf16[272,512]{1,0:T(8,128)(2,1)S(1)}, u32[]{:S(2)}, u32[]{:S(2)}) collective-permute-start(bf16[272,512]{1,0:T(8,128)(2,1)S(1)} %merge.3.near_ref), channel_id=1, source_target_pairs={{0,8},{4,12},{8,0},{12,4},{16,24},{20,28},{24,16},{28,20},{1,9},{5... | collective-permute-start | bytes 835592 | tf_op jit(solution)/shard_map/rest_weights/ppermute | solution.py:624
  (8 other events, 8.4 us)

commit v10 on v9

--- a/solution.py
+++ b/solution.py
@@ -1123,19 +1123,19 @@
             sums,
         )
 
+        theirs_w, rest = line(
+            rest_weights, first_bit, first, gqkv, grad_low, attended, slot_grad, sums
+        )
+        rest_got = swap(theirs_w, "dp", feed_masks[0], "rest_weights")
         feed_sum.step()
         (out_other,) = wait(out_other)
-        theirs_w, rest = line(
-            rest_weights, first_bit, first, gqkv, grad_low, attended, slot_grad, sums
-        )
-        rest_got = swap(theirs_w, "dp", feed_masks[0], "rest_weights")
         (out_far,) = wait(out_far)
         out_other_far = swap(out_far, "mp", 1, "sum_output")
         theirs, mine = line(first_grad, pos, gqkv, slot_grad, sums, w_qkv, tokens)
         got = swap(theirs, "mp", 1, "sum_first")
-        feed_sum.step()
         theirs_w, rest = line(split_first, bit_of(feed_masks[1]), rest, rest_got)
         rest_got = swap(theirs_w, "dp", feed_masks[1], "rest_weights")
+        feed_sum.step()
         total = line(pair, mine, got)
         for m in far_masks[:-1]:
             total = line(pair, total, swap(total, "mp", m, "sum_first"))

time: 119 us -> 119 us (level)
  starting transfers between devices: 30.3 us -> 28.5 us
    ppermute x35, starting transfers between devices: 30.3 us -> 28.5 us  [swap(): return lax.ppermute(x, axis, [(i, i ^ mask) for i in range(n)])]
    unnamed x76 -> x80, local copies, waits for them, and re-layouts: 5.19 us -> 6.15 us
  transfers between devices with their start and end apart: 35 -> 35, of which waited for: 17 -> 18; matrix products, arithmetic and copies ran while one was open for 1% -> 1% of each run, Pallas kernels for 23% -> 23%
where the time goes in v10:
time: 119 us; the launch traced here: 118 us
  waiting for transfers between devices  43.6 us (37%)
  Pallas kernels  38.3 us (32%)
  starting transfers between devices  28.5 us (24%)
  local copies, waits for them, and re-layouts  6.17 us (5%)
    ppermute x35, waiting for transfers between devices, swap(): return lax.ppermute(x, axis, [(i, i ^ mask) for i in range(n)])  43.6 us
    pallas_call x12, Pallas kernels, __call__(): result = work(*inputs)  30 us
    ppermute x35, starting transfers between devices, swap(): return lax.ppermute(x, axis, [(i, i ^ mask) for i in range(n)])  28.5 us
    unnamed x80, local copies, waits for them, and re-layouts  6.15 us
    pallas_call x1, Pallas kernels, per_device(): back(*a)  5.47 us
  transfers between devices with their start and end apart: 35, of which 18 were waited for; matrix products, arithmetic and copies ran while one was open for 1% of the time, Pallas kernels for 23%

profile of v10, /device:TPU:0, one launch (start us, length us, event | category | flops | bytes accessed | tf_op | source)
XLA Modules:
  0.0 118.4 jit_solution(8937080495078690895)
XLA Ops:
  0.6 3.0 %collective-permute-start = (bf16[128,512]{1,0:T(8,128)(2,1)}, bf16[128,512]{1,0:T(8,128)(2,1)S(1)}, u32[]{:S(2)}, u32[]{:S(2)}) collective-permute-start(bf16[128,512]{1,0:T(8,128)(2,1)} %wo_ref), channel_id=1, source_target_pairs={{0,2},{1,3},{2,0},{3,1},{4,6},{5,7},{6,4},{7,5},{8,10},{9,11},{10,... | collective-permute-start | bytes 393224 | tf_op jit(solution)/shard_map/gather_w_out/ppermute | solution.py:624
  3.7 3.9 %project.1 = (bf16[1024,512]{1,0:T(8,128)(2,1)}, bf16[3,1024,128]{2,1,0:T(8,128)(2,1)}, bf16[5,16,128]{2,1,0:T(8,128)(2,1)}) custom-call(bf16[1024,512]{1,0:T(8,128)(2,1)} %tok_ref.3, f32[1,512]{1,0:T(1,128)} %bitcast.24, f32[1,512]{1,0:T(1,128)} %bitcast.29, bf16[3,512,128]{2,1,0:T(8,128)(2,1)} %w_ref.2), custom_call_target="tpu_custom_call" | custom-call | flops 12000000000 | bytes 1 | tf_op jit(solution)/shard_map/project/pallas_call | solution.py:648
  7.6 1.6 %collective-permute-start.1 = (bf16[1,5,16,128]{3,2,1,0:T(8,128)(2,1)}, bf16[1,5,16,128]{3,2,1,0:T(8,128)(2,1)S(1)}, u32[]{:S(2)}, u32[]{:S(2)}) collective-permute-start(bf16[1,5,16,128]{3,2,1,0:T(8,128)(2,1)} %bitcast.27), channel_id=1, source_target_pairs={{0,4},{4,0},{8,12},{12,8},{16,20},{20,16},{24,28},{28,24},{1,5},{5... | collective-permute-start | bytes 61448 | tf_op jit(solution)/shard_map/summaries/ppermute | solution.py:624
  9.1 1.1 copy-done.20
  10.3 0.5 local.1
  10.8 0.9 collective-permute-done.1
  11.7 1.6 %collective-permute-start.2 = (bf16[2,5,16,128]{3,2,1,0:T(8,128)(2,1)S(1)}, bf16[2,5,16,128]{3,2,1,0:T(8,128)(2,1)S(1)}, u32[]{:S(2)}, u32[]{:S(2)}) collective-permute-start(bf16[2,5,16,128]{3,2,1,0:T(8,128)(2,1)S(1)} %constant_dynamic-update-slice_fusion), channel_id=1, source_target_pairs={{0,8},{4,12},{8,0},{12,4},{16,24},{20,28},{24,16},{28,20},{1,9},{5... | collective-permute-start | bytes 122888 | tf_op jit(solution)/shard_map/summaries/ppermute | solution.py:624
  13.3 0.5 collective-permute-start.4
  13.8 1.9 %collective-permute-done.2 = bf16[2,5,16,128]{3,2,1,0:T(8,128)(2,1)S(1)} collective-permute-done((bf16[2,5,16,128]{3,2,1,0:T(8,128)(2,1)S(1)}, bf16[2,5,16,128]{3,2,1,0:T(8,128)(2,1)S(1)}, u32[]{:S(2)}, u32[]{:S(2)}) %collective-permute-start.2) | collective-permute-done | bytes 40992 | tf_op jit(solution)/shard_map/summaries/ppermute | solution.py:624
  15.8 1.5 %attend.1 = (bf16[8,160,256]{2,1,0:T(8,128)(2,1)S(1)}, bf16[1024,128]{1,0:T(8,128)(2,1)S(1)}) custom-call(s32[1]{0:T(128)} %bitcast.2.place_ref, bf16[3,1024,128]{2,1,0:T(8,128)(2,1)S(1)} %copy-done.20, f32[8,128,256]{2,1,0:T(8,128)S(1)} %get-tuple-element.222.exp_ref, f32[8,2,256]{2,1,0:T(2,128)S(1)} %get-tuple-element.223.stat_ref, ...), custom_call_target="tpu_custom_call" | custom-call | flops 12000000000 | bytes 1 | tf_op jit(solution)/shard_map/attend/pallas_call | solution.py:648
  17.3 1.5 %collective-permute-start.6 = (bf16[1024,128]{1,0:T(8,128)(2,1)S(1)}, bf16[1024,128]{1,0:T(8,128)(2,1)S(1)}, u32[]{:S(2)}, u32[]{:S(2)}) collective-permute-start(bf16[1024,128]{1,0:T(8,128)(2,1)S(1)} %get-tuple-element.291.refs_0_.att_ref), channel_id=1, source_target_pairs={{0,2},{1,3},{2,0},{3,1},{4,6},{5,7},{6,4},{7,5},{8,10},{9,11},{10,... | collective-permute-start | bytes 786440 | tf_op jit(solution)/shard_map/gather_attended/ppermute | solution.py:624
  18.9 6.1 %collective-permute-done.6.refs_2_ = bf16[1024,128]{1,0:T(8,128)(2,1)S(1)} collective-permute-done((bf16[1024,128]{1,0:T(8,128)(2,1)S(1)}, bf16[1024,128]{1,0:T(8,128)(2,1)S(1)}, u32[]{:S(2)}, u32[]{:S(2)}) %collective-permute-start.6) | collective-permute-done | bytes 262176 | tf_op jit(solution)/shard_map/gather_attended/ppermute | solution.py:624
  25.0 0.6 pad_add_fusion.pos_ref
  25.6 0.9 collective-permute-done.7.refs_3_
  26.5 0.7 copy-done.35
  27.2 8.9 %feed.1 = (f32[1024,512]{1,0:T(8,128)}, bf16[1024,512]{1,0:T(8,128)(2,1)}, bf16[1024,512]{1,0:T(8,128)(2,1)}, bf16[1024,512]{1,0:T(8,128)(2,1)}, bf16[512,512]{1...) custom-call(s32[4]{0:T(128)} %pad_add_fusion.pos_ref, bf16[1024,512]{1,0:T(8,128)(2,1)} %tok_ref.3, ...), custom_call_target="tpu_custom_call" | custom-call | flops 12000000000 | bytes 1 | tf_op jit(solution)/shard_map/feed/pallas_call | solution.py:648
  36.2 0.2 collective-permute-start.8
  36.4 1.0 copy-done.24
  37.5 0.8 collective-permute-done.8.b_ref
  38.5 1.6 %collective-permute-start.10 = (bf16[512,512]{1,0:T(8,128)(2,1)S(1)}, bf16[512,512]{1,0:T(8,128)(2,1)S(1)}, u32[]{:S(2)}, u32[]{:S(2)}) collective-permute-start(bf16[512,512]{1,0:T(8,128)(2,1)S(1)} %add.26.own_ref), channel_id=1, source_target_pairs={{0,2},{1,3},{2,0},{3,1},{4,6},{5,7},{6,4},{7,5},{8,10},{9,11},{10,... | collective-permute-start | bytes 1572872 | tf_op jit(solution)/shard_map/sum_second/ppermute | solution.py:624
  40.1 3.0 %weights.1 = (bf16[512,512]{1,0:T(8,128)(2,1)S(1)}, bf16[512,512]{1,0:T(8,128)(2,1)S(1)}, bf16[512,512]{1,0:T(8,128)(2,1)S(1)}, bf16[512,512]{1,0:T(8,128)(2,1)S(1)}) custom-call(s32[4]{0:T(128)S(1)} %copy-done.2, bf16[1024,512]{1,0:T(8,128)(2,1)S(1)} %copy-done.18, bf16[1024,512]{1,0:T(8,128)(2,1)S(1)} %copy-done.17, bf16[1024,512]{1,0:T(8,128)(2,1)S(1)} %copy-done.19, ...), custom_call_target="tpu_custom_call" | custom-call | flops 12000000000 | bytes 1 | tf_op jit(solution)/shard_map/weights/pallas_call | solution.py:648
  43.1 0.6 collective-permute-start.9
  43.7 0.2 copy-done.25
  43.9 0.4 collective-permute-start.13
  44.4 0.9 collective-permute-done.9.b_ref
  45.4 7.1 %collective-permute-done.10.far_ref = bf16[512,512]{1,0:T(8,128)(2,1)S(1)} collective-permute-done((bf16[512,512]{1,0:T(8,128)(2,1)S(1)}, bf16[512,512]{1,0:T(8,128)(2,1)S(1)}, u32[]{:S(2)}, u32[]{:S(2)}) %collective-permute-start.10) | collective-permute-done | bytes 524320 | tf_op jit(solution)/shard_map/sum_second/ppermute | solution.py:624
  52.5 0.5 collective-permute-start.12
  53.0 1.5 %collective-permute-start.11 = (bf16[512,512]{1,0:T(8,128)(2,1)S(1)}, bf16[512,512]{1,0:T(8,128)(2,1)S(1)}, u32[]{:S(2)}, u32[]{:S(2)}) collective-permute-start(bf16[512,512]{1,0:T(8,128)(2,1)S(1)} %add.27.own_ref), channel_id=1, source_target_pairs={{0,2},{1,3},{2,0},{3,1},{4,6},{5,7},{6,4},{7,5},{8,10},{9,11},{10,... | collective-permute-start | bytes 1572872 | tf_op jit(solution)/shard_map/sum_output/ppermute | solution.py:624
  54.6 5.5 %back.1 = (bf16[1024,512]{1,0:T(8,128)(2,1)S(1)}, bf16[1024,384]{1,0:T(8,128)(2,1)S(1)}, f32[4,2,8,128]{3,2,1,0:T(8,128)S(1)}, f32[32,512]{1,0:T(8,128)S(1)}) custom-call(s32[4]{0:T(128)S(1)} %copy-done.2, bf16[512,512]{1,0:T(8,128)(2,1)S(1)} %add.26.own_ref, bf16[512,512]{1,0:T(8,128)(2,1)S(1)} %collective-permute-done.10.far_ref, ...), custom_call_target="tpu_custom_call" | custom-call | flops 12000000000 | bytes 1 | tf_op jit(solution)/shard_map/back/pallas_call | solution.py:1111
  60.1 1.0 copy-done.15
  61.0 0.9 copy-done.22
  61.9 0.6 copy-done.28
  62.5 3.8 %rest_weights.1 = (bf16[272,512]{1,0:T(8,128)(2,1)}, bf16[272,512]{1,0:T(8,128)(2,1)}) custom-call(s32[1]{0:T(128)} %bitcast.3.bit_ref, bf16[1024,512]{1,0:T(8,128)(2,1)} %get-tuple-element.288.first_ref, bf16[1024,384]{1,0:T(8,128)(2,1)} %copy-done.22, bf16[1024,512]{1,0:T(8,128)(2,1)} %copy-done.15, bf16[1024,128]{1,0:T(8,128)(2,1)} %copy-done.7, ...), custom_call_target="tpu_custom_call" | custom-call | flops 12000000000 | bytes 1 | tf_op jit(solution)/shard_map/rest_weights/pallas_call | solution.py:648
  66.6 0.3 collective-permute-done.11.far_ref
  66.9 0.4 copy-done.32
  67.3 0.4 collective-permute-start.19
  67.7 1.5 %collective-permute-start.18 = (bf16[256,512]{1,0:T(8,128)(2,1)S(1)}, bf16[256,512]{1,0:T(8,128)(2,1)S(1)}, u32[]{:S(2)}, u32[]{:S(2)}) collective-permute-start(bf16[256,512]{1,0:T(8,128)(2,1)S(1)} %get-tuple-element.309), channel_id=1, source_target_pairs={{0,4},{4,0},{8,12},{12,8},{16,20},{20,16},{24,28},{28,24},{1,5},{5... | collective-permute-start | bytes 786440 | tf_op jit(solution)/shard_map/feed_weights/ppermute | solution.py:624
  69.3 2.0 %first.1 = (bf16[528,512]{1,0:T(8,128)(2,1)S(1)}, bf16[528,512]{1,0:T(8,128)(2,1)S(1)}) custom-call(s32[4]{0:T(128)S(1)} %copy-done.2, bf16[1024,384]{1,0:T(8,128)(2,1)S(1)} %copy-done.23, f32[4,2,8,128]{3,2,1,0:T(8,128)S(1)} %copy-done.29, bf16[4,5,16,128]{3,2,1,0:T(8,128)(2,1)S(1)} %copy-done.1, bf16[3,512,128]{2,1,0:T(8,128)(2,1)S(1)} %copy-done.6, ...), custom_call_target="tpu_custom_call" | custom-call | flops 12000000000 | bytes 1 | tf_op jit(solution)/shard_map/first/pallas_call | solution.py:648
  71.4 4.5 %collective-permute-done.19.b_ref = bf16[272,512]{1,0:T(8,128)(2,1)S(1)} collective-permute-done((bf16[272,512]{1,0:T(8,128)(2,1)S(1)}, bf16[272,512]{1,0:T(8,128)(2,1)S(1)}, u32[]{:S(2)}, u32[]{:S(2)}) %collective-permute-start.19) | collective-permute-done | bytes 278560 | tf_op jit(solution)/shard_map/rest_weights/ppermute | solution.py:624
  76.0 1.6 %collective-permute-start.22 = (bf16[144,512]{1,0:T(8,128)(2,1)S(1)}, bf16[144,512]{1,0:T(8,128)(2,1)S(1)}, u32[]{:S(2)}, u32[]{:S(2)}) collective-permute-start(bf16[144,512]{1,0:T(8,128)(2,1)S(1)} %get-tuple-element.329), channel_id=1, source_target_pairs={{0,4},{4,0},{8,12},{12,8},{16,20},{20,16},{24,28},{28,24},{1,5},{5... | collective-permute-start | bytes 442376 | tf_op jit(solution)/shard_map/rest_weights/ppermute | solution.py:624
  77.7 2.6 %collective-permute-start.21 = (bf16[128,512]{1,0:T(8,128)(2,1)S(1)}, bf16[128,512]{1,0:T(8,128)(2,1)S(1)}, u32[]{:S(2)}, u32[]{:S(2)}) collective-permute-start(bf16[128,512]{1,0:T(8,128)(2,1)S(1)} %get-tuple-element.328), channel_id=1, source_target_pairs={{0,16},{4,20},{8,24},{12,28},{16,0},{20,4},{24,8},{28,12},{1,17},{... | collective-permute-start | bytes 393224 | tf_op jit(solution)/shard_map/feed_weights/ppermute | solution.py:624
  80.5 1.6 %collective-permute-start.20 = (bf16[528,512]{1,0:T(8,128)(2,1)S(1)}, bf16[528,512]{1,0:T(8,128)(2,1)S(1)}, u32[]{:S(2)}, u32[]{:S(2)}) collective-permute-start(bf16[528,512]{1,0:T(8,128)(2,1)S(1)} %pair.1.near_ref.own_ref), channel_id=1, source_target_pairs={{0,2},{1,3},{2,0},{3,1},{4,6},{5,7},{6,4},{7,5},{8,10},{9,11},{10,... | collective-permute-start | bytes 1622024 | tf_op jit(solution)/shard_map/sum_first/ppermute | solution.py:624
  82.0 1.8 %output.1 = bf16[1024,512]{1,0:T(8,128)(2,1)} custom-call(s32[4]{0:T(128)S(1)} %copy-done.2, bf16[512,512]{1,0:T(8,128)(2,1)S(1)} %add.27.own_ref, bf16[512,512]{1,0:T(8,128)(2,1)S(1)} %collective-permute-done.11.far_ref, bf16[512,512]{1,0:T(8,128)(2,1)S(1)} %collective-permute-done.12.other_ref, bf16[512,512]{1,0:T(8,128)(2,1)S(1)} %collective-permute-done.16.other_far_ref, ...), custom_call_target="tpu_custom_call" | custom-call | flops 12000000000 | bytes 1 | tf_op jit(solution)/shard_map/output/pallas_call | solution.py:648
  83.9 0.2 split_second.1
  84.1 1.8 %collective-permute-done.21.b_ref = bf16[128,512]{1,0:T(8,128)(2,1)S(1)} collective-permute-done((bf16[128,512]{1,0:T(8,128)(2,1)S(1)}, bf16[128,512]{1,0:T(8,128)(2,1)S(1)}, u32[]{:S(2)}, u32[]{:S(2)}) %collective-permute-start.21) | collective-permute-done | bytes 131104 | tf_op jit(solution)/shard_map/feed_weights/ppermute | solution.py:624
  85.9 0.4 collective-permute-start.27
  86.3 2.5 %collective-permute-start.29 = (bf16[128,512]{1,0:T(8,128)(2,1)S(1)}, bf16[128,512]{1,0:T(8,128)(2,1)S(1)}, u32[]{:S(2)}, u32[]{:S(2)}) collective-permute-start(bf16[128,512]{1,0:T(8,128)(2,1)S(1)} %add.28.a_ref), channel_id=1, source_target_pairs={{0,16},{4,20},{8,24},{12,28},{16,0},{20,4},{24,8},{28,12},{1,17},{... | collective-permute-start | bytes 393224 | tf_op jit(solution)/shard_map/feed_weights/ppermute | solution.py:624
  88.9 4.5 %collective-permute-done.20.far_ref = bf16[528,512]{1,0:T(8,128)(2,1)S(1)} collective-permute-done((bf16[528,512]{1,0:T(8,128)(2,1)S(1)}, bf16[528,512]{1,0:T(8,128)(2,1)S(1)}, u32[]{:S(2)}, u32[]{:S(2)}) %collective-permute-start.20) | collective-permute-done | bytes 540704 | tf_op jit(solution)/shard_map/sum_first/ppermute | solution.py:624
  93.4 1.7 %collective-permute-start.26 = (f32[8,512]{1,0:T(8,128)S(1)}, f32[8,512]{1,0:T(8,128)S(1)}, u32[]{:S(2)}, u32[]{:S(2)}) collective-permute-start(f32[8,512]{1,0:T(8,128)S(1)} %plus.1.extra_ref), channel_id=1, source_target_pairs={{0,2},{1,3},{2,0},{3,1},{4,6},{5,7},{6,4},{7,5},{8,10},{9,11},{10,... | collective-permute-start | bytes 49160 | tf_op jit(solution)/shard_map/sum_extra/ppermute | solution.py:624
  95.5 1.7 %collective-permute-done.29.b_ref = bf16[128,512]{1,0:T(8,128)(2,1)S(1)} collective-permute-done((bf16[128,512]{1,0:T(8,128)(2,1)S(1)}, bf16[128,512]{1,0:T(8,128)(2,1)S(1)}, u32[]{:S(2)}, u32[]{:S(2)}) %collective-permute-start.29) | collective-permute-done | bytes 131104 | tf_op jit(solution)/shard_map/feed_weights/ppermute | solution.py:624
  97.2 0.3 collective-permute-start.31
  97.5 0.5 collective-permute-start.34
  98.1 4.5 %collective-permute-done.28.b_ref = bf16[80,512]{1,0:T(8,128)(2,1)S(1)} collective-permute-done((bf16[80,512]{1,0:T(8,128)(2,1)S(1)}, bf16[80,512]{1,0:T(8,128)(2,1)S(1)}, u32[]{:S(2)}, u32[]{:S(2)}) %collective-permute-start.28) | collective-permute-done | bytes 81952 | tf_op jit(solution)/shard_map/rest_weights/ppermute | solution.py:624
  102.6 0.6 collective-permute-start.30
  103.2 1.3 %collective-permute-done.23.other_ref = bf16[528,512]{1,0:T(8,128)(2,1)S(1)} collective-permute-done((bf16[528,512]{1,0:T(8,128)(2,1)S(1)}, bf16[528,512]{1,0:T(8,128)(2,1)S(1)}, u32[]{:S(2)}, u32[]{:S(2)}) %collective-permute-start.23) | collective-permute-done | bytes 540704 | tf_op jit(solution)/shard_map/sum_first/ppermute | solution.py:624
  104.5 3.1 %last.1 = bf16[1024,512]{1,0:T(8,128)(2,1)} custom-call(s32[4]{0:T(128)S(1)} %copy-done.2, bf16[528,512]{1,0:T(8,128)(2,1)S(1)} %pair.1.near_ref.own_ref, bf16[528,512]{1,0:T(8,128)(2,1)S(1)} %collective-permute-done.20.far_ref, bf16[528,512]{1,0:T(8,128)(2,1)S(1)} %collective-permute-done.23.other_ref, ...), custom_call_target="tpu_custom_call" | custom-call | flops 12000000000 | bytes 1 | tf_op jit(solution)/shard_map/last/pallas_call | solution.py:648
  107.6 0.5 collective-permute-start.33
  108.1 0.8 collective-permute-done.30.b_ref
  108.9 0.8 collective-permute-start.32
  109.7 1.0 feed_unpack.2
  110.8 5.1 %collective-permute-done.33.one_ref = bf16[256,512]{1,0:T(8,128)(2,1)S(1)} collective-permute-done((bf16[256,512]{1,0:T(8,128)(2,1)S(1)}, bf16[256,512]{1,0:T(8,128)(2,1)S(1)}, u32[]{:S(2)}, u32[]{:S(2)}) %collective-permute-start.33) | collective-permute-done | bytes 262176 | tf_op jit(solution)/shard_map/feed_weights/ppermute | solution.py:624
  115.9 1.0 feed_unpack.3
  117.0 0.3 collective-permute-done.32.far_ref
  117.3 1.1 rest_unpack.1
  (119 shorter events, 1.7 us)
Async XLA Ops:
  0.6 6.9 %collective-permute-start = (bf16[128,512]{1,0:T(8,128)(2,1)}, bf16[128,512]{1,0:T(8,128)(2,1)S(1)}, u32[]{:S(2)}, u32[]{:S(2)}) collective-permute-start(bf16[128,512]{1,0:T(8,128)(2,1)} %wo_ref), channel_id=1, source_target_pairs={{0,2},{1,3},{2,0},{3,1},{4,6},{5,7},{6,4},{7,5},{8,10},{9,11},{10,... | collective-permute-start | bytes 393224 | tf_op jit(solution)/shard_map/gather_w_out/ppermute | solution.py:624
  7.6 5.7 %copy-start.36 = (bf16[128,512]{1,0:T(8,128)(2,1)}, bf16[128,512]{1,0:T(8,128)(2,1)S(1)}, u32[]{:S(2)}) copy-start(bf16[128,512]{1,0:T(8,128)(2,1)S(1)} %collective-permute-done.refs_6_) | copy-start | bytes 393220
  7.6 5.7 %copy-start.8 = (bf16[128,512]{1,0:T(8,128)(2,1)S(1)}, bf16[128,512]{1,0:T(8,128)(2,1)}, u32[]{:S(2)}) copy-start(bf16[128,512]{1,0:T(8,128)(2,1)} %wo_ref) | copy-start | bytes 393220
  7.6 4.1 %collective-permute-start.1 = (bf16[1,5,16,128]{3,2,1,0:T(8,128)(2,1)}, bf16[1,5,16,128]{3,2,1,0:T(8,128)(2,1)S(1)}, u32[]{:S(2)}, u32[]{:S(2)}) collective-permute-start(bf16[1,5,16,128]{3,2,1,0:T(8,128)(2,1)} %bitcast.27), channel_id=1, source_target_pairs={{0,4},{4,0},{8,12},{12,8},{16,20},{20,16},{24,28},{28,24},{1,5},{5... | collective-permute-start | bytes 61448 | tf_op jit(solution)/shard_map/summaries/ppermute | solution.py:624
  11.7 4.1 %collective-permute-start.2 = (bf16[2,5,16,128]{3,2,1,0:T(8,128)(2,1)S(1)}, bf16[2,5,16,128]{3,2,1,0:T(8,128)(2,1)S(1)}, u32[]{:S(2)}, u32[]{:S(2)}) collective-permute-start(bf16[2,5,16,128]{3,2,1,0:T(8,128)(2,1)S(1)} %constant_dynamic-update-slice_fusion), channel_id=1, source_target_pairs={{0,8},{4,12},{8,0},{12,4},{16,24},{20,28},{24,16},{28,20},{1,9},{5... | collective-permute-start | bytes 122888 | tf_op jit(solution)/shard_map/summaries/ppermute | solution.py:624
  13.3 2.4 %collective-permute-start.3 = (bf16[128,512]{1,0:T(8,128)(2,1)S(1)}, bf16[128,512]{1,0:T(8,128)(2,1)S(1)}, u32[]{:S(2)}, u32[]{:S(2)}) collective-permute-start(bf16[128,512]{1,0:T(8,128)(2,1)S(1)} %copy-done.8), channel_id=1, source_target_pairs={{0,1},{1,0},{2,3},{3,2},{4,5},{5,4},{6,7},{7,6},{8,9},{9,8},{10,11... | collective-permute-start | bytes 393224 | tf_op jit(solution)/shard_map/gather_w_out/ppermute | solution.py:624
  13.3 2.5 %collective-permute-start.4 = (bf16[128,512]{1,0:T(8,128)(2,1)S(1)}, bf16[128,512]{1,0:T(8,128)(2,1)S(1)}, u32[]{:S(2)}, u32[]{:S(2)}) collective-permute-start(bf16[128,512]{1,0:T(8,128)(2,1)S(1)} %collective-permute-done.refs_6_), channel_id=1, source_target_pairs={{0,1},{1,0},{2,3},{3,2},{4,5},{5,4},{6,7},{7,6},{8,9},{9,8},{10,11... | collective-permute-start | bytes 393224 | tf_op jit(solution)/shard_map/gather_w_out/ppermute | solution.py:624
  15.7 38.8 %copy-start = (bf16[4,5,16,128]{3,2,1,0:T(8,128)(2,1)}, bf16[4,5,16,128]{3,2,1,0:T(8,128)(2,1)S(1)}, u32[]{:S(2)}) copy-start(bf16[4,5,16,128]{3,2,1,0:T(8,128)(2,1)S(1)} %constant_dynamic-update-slice_fusion.2.sums_ref) | copy-start | bytes 245764
  15.8 1.5 %copy-start.37 = (bf16[128,512]{1,0:T(8,128)(2,1)}, bf16[128,512]{1,0:T(8,128)(2,1)S(1)}, u32[]{:S(2)}) copy-start(bf16[128,512]{1,0:T(8,128)(2,1)S(1)} %collective-permute-done.3.refs_5_) | copy-start | bytes 393220
  15.8 1.5 %copy-start.38 = (bf16[128,512]{1,0:T(8,128)(2,1)}, bf16[128,512]{1,0:T(8,128)(2,1)S(1)}, u32[]{:S(2)}) copy-start(bf16[128,512]{1,0:T(8,128)(2,1)S(1)} %collective-permute-done.4.refs_7_) | copy-start | bytes 393220
  17.3 9.2 %copy-start.7 = (bf16[1024,128]{1,0:T(8,128)(2,1)}, bf16[1024,128]{1,0:T(8,128)(2,1)S(1)}, u32[]{:S(2)}) copy-start(bf16[1024,128]{1,0:T(8,128)(2,1)S(1)} %get-tuple-element.291.refs_0_.att_ref) | copy-start | bytes 786436
  17.3 7.6 %collective-permute-start.6 = (bf16[1024,128]{1,0:T(8,128)(2,1)S(1)}, bf16[1024,128]{1,0:T(8,128)(2,1)S(1)}, u32[]{:S(2)}, u32[]{:S(2)}) collective-permute-start(bf16[1024,128]{1,0:T(8,128)(2,1)S(1)} %get-tuple-element.291.refs_0_.att_ref), channel_id=1, source_target_pairs={{0,2},{1,3},{2,0},{3,1},{4,6},{5,7},{6,4},{7,5},{8,10},{9,11},{10,... | collective-permute-start | bytes 786440 | tf_op jit(solution)/shard_map/gather_attended/ppermute | solution.py:624
  18.9 6.7 %collective-permute-start.5 = (bf16[1024,128]{1,0:T(8,128)(2,1)S(1)}, bf16[1024,128]{1,0:T(8,128)(2,1)S(1)}, u32[]{:S(2)}, u32[]{:S(2)}) collective-permute-start(bf16[1024,128]{1,0:T(8,128)(2,1)S(1)} %get-tuple-element.291.refs_0_.att_ref), channel_id=1, source_target_pairs={{0,1},{1,0},{2,3},{3,2},{4,5},{5,4},{6,7},{7,6},{8,9},{9,8},{10,11... | collective-permute-start | bytes 786440 | tf_op jit(solution)/shard_map/gather_attended/ppermute | solution.py:624
  25.0 1.5 %copy-start.33 = (bf16[1024,128]{1,0:T(8,128)(2,1)}, bf16[1024,128]{1,0:T(8,128)(2,1)S(1)}, u32[]{:S(2)}) copy-start(bf16[1024,128]{1,0:T(8,128)(2,1)S(1)} %collective-permute-done.6.refs_2_) | copy-start | bytes 786436
  25.0 1.5 %collective-permute-start.7 = (bf16[1024,128]{1,0:T(8,128)(2,1)S(1)}, bf16[1024,128]{1,0:T(8,128)(2,1)S(1)}, u32[]{:S(2)}, u32[]{:S(2)}) collective-permute-start(bf16[1024,128]{1,0:T(8,128)(2,1)S(1)} %collective-permute-done.6.refs_2_), channel_id=1, source_target_pairs={{0,1},{1,0},{2,3},{3,2},{4,5},{5,4},{6,7},{7,6},{8,9},{9,8},{10,11... | collective-permute-start | bytes 786440 | tf_op jit(solution)/shard_map/gather_attended/ppermute | solution.py:624
  36.2 2.2 %collective-permute-start.8 = (bf16[512,512]{1,0:T(8,128)(2,1)}, bf16[512,512]{1,0:T(8,128)(2,1)S(1)}, u32[]{:S(2)}, u32[]{:S(2)}) collective-permute-start(bf16[512,512]{1,0:T(8,128)(2,1)} %get-tuple-element.250), channel_id=1, source_target_pairs={{0,1},{1,0},{2,3},{3,2},{4,5},{5,4},{6,7},{7,6},{8,9},{9,8},{10,11... | collective-permute-start | bytes 1572872 | tf_op jit(solution)/shard_map/sum_second/ppermute | solution.py:624
  37.4 2.6 %copy-start.2 = (s32[4]{0:T(128)S(1)}, s32[4]{0:T(128)}, u32[]{:S(2)}) copy-start(s32[4]{0:T(128)} %pad_add_fusion.pos_ref) | copy-start | bytes 52
  37.5 2.6 %copy-start.3 = (bf16[1024,512]{1,0:T(8,128)(2,1)S(1)}, bf16[1024,512]{1,0:T(8,128)(2,1)}, u32[]{:S(2)}) copy-start(bf16[1024,512]{1,0:T(8,128)(2,1)} %cot_ref.1) | copy-start | bytes 3145732
  37.5 2.6 %copy-start.5 = (bf16[512,512]{1,0:T(8,128)(2,1)S(1)}, bf16[512,512]{1,0:T(8,128)(2,1)}, u32[]{:S(2)}) copy-start(bf16[512,512]{1,0:T(8,128)(2,1)} %down_ref) | copy-start | bytes 1572868
  37.5 2.6 %copy-start.17 = (bf16[1024,512]{1,0:T(8,128)(2,1)S(1)}, bf16[1024,512]{1,0:T(8,128)(2,1)}, u32[]{:S(2)}) copy-start(bf16[1024,512]{1,0:T(8,128)(2,1)} %get-tuple-element.255.second_ref) | copy-start | bytes 3145732
  37.5 2.6 %copy-start.18 = (bf16[1024,512]{1,0:T(8,128)(2,1)S(1)}, bf16[1024,512]{1,0:T(8,128)(2,1)}, u32[]{:S(2)}) copy-start(bf16[1024,512]{1,0:T(8,128)(2,1)} %get-tuple-element.254.active_ref) | copy-start | bytes 3145732
  37.5 2.6 %copy-start.19 = (bf16[1024,512]{1,0:T(8,128)(2,1)S(1)}, bf16[1024,512]{1,0:T(8,128)(2,1)}, u32[]{:S(2)}) copy-start(bf16[1024,512]{1,0:T(8,128)(2,1)} %get-tuple-element.256.grad_ref) | copy-start | bytes 3145732
  38.5 14.0 %collective-permute-start.10 = (bf16[512,512]{1,0:T(8,128)(2,1)S(1)}, bf16[512,512]{1,0:T(8,128)(2,1)S(1)}, u32[]{:S(2)}, u32[]{:S(2)}) collective-permute-start(bf16[512,512]{1,0:T(8,128)(2,1)S(1)} %add.26.own_ref), channel_id=1, source_target_pairs={{0,2},{1,3},{2,0},{3,1},{4,6},{5,7},{6,4},{7,5},{8,10},{9,11},{10,... | collective-permute-start | bytes 1572872 | tf_op jit(solution)/shard_map/sum_second/ppermute | solution.py:624
  40.0 14.5 %collective-permute-start.14 = (bf16[512,512]{1,0:T(8,128)(2,1)S(1)}, bf16[512,512]{1,0:T(8,128)(2,1)S(1)}, u32[]{:S(2)}, u32[]{:S(2)}) collective-permute-start(bf16[512,512]{1,0:T(8,128)(2,1)S(1)} %add.26.own_ref), channel_id=1, source_target_pairs={{0,1},{1,0},{2,3},{3,2},{4,5},{5,4},{6,7},{7,6},{8,9},{9,8},{10,11... | collective-permute-start | bytes 1572872 | tf_op jit(solution)/shard_map/sum_second/ppermute | solution.py:624
  40.1 3.6 %copy-start.12 = (f32[512]{0:T(512)S(1)}, f32[512]{0:T(512)}, u32[]{:S(2)}) copy-start(f32[512]{0:T(512)} %param.14) | copy-start | bytes 6148
  43.1 2.1 %collective-permute-start.9 = (bf16[512,512]{1,0:T(8,128)(2,1)S(1)}, bf16[512,512]{1,0:T(8,128)(2,1)S(1)}, u32[]{:S(2)}, u32[]{:S(2)}) collective-permute-start(bf16[512,512]{1,0:T(8,128)(2,1)S(1)} %get-tuple-element.260), channel_id=1, source_target_pairs={{0,1},{1,0},{2,3},{3,2},{4,5},{5,4},{6,7},{7,6},{8,9},{9,8},{10,11... | collective-permute-start | bytes 1572872 | tf_op jit(solution)/shard_map/sum_output/ppermute | solution.py:624
  43.9 22.4 %collective-permute-start.13 = (bf16[512,512]{1,0:T(8,128)(2,1)S(1)}, bf16[512,512]{1,0:T(8,128)(2,1)S(1)}, u32[]{:S(2)}, u32[]{:S(2)}) collective-permute-start(bf16[512,512]{1,0:T(8,128)(2,1)S(1)} %get-tuple-element.267), channel_id=1, source_target_pairs={{0,8},{4,12},{8,0},{12,4},{16,24},{20,28},{24,16},{28,20},{1,9},{5... | collective-permute-start | bytes 1572872 | tf_op jit(solution)/shard_map/feed_weights/ppermute | solution.py:624
  45.4 9.2 %copy-start.9 = (bf16[128,512]{1,0:T(8,128)(2,1)S(1)}, bf16[128,512]{1,0:T(8,128)(2,1)}, u32[]{:S(2)}) copy-start(bf16[128,512]{1,0:T(8,128)(2,1)} %wo_ref) | copy-start | bytes 393220
  45.4 9.2 %copy-start.10 = (f32[512]{0:T(512)S(1)}, f32[512]{0:T(512)}, u32[]{:S(2)}) copy-start(f32[512]{0:T(512)} %param.19) | copy-start | bytes 6148
  45.4 9.2 %copy-start.13 = (f32[1024,512]{1,0:T(8,128)S(1)}, f32[1024,512]{1,0:T(8,128)}, u32[]{:S(2)}) copy-start(f32[1024,512]{1,0:T(8,128)} %get-tuple-element.326.mid_ref) | copy-start | bytes 6291460
  45.4 9.2 %copy-start.21 = (bf16[3,1024,128]{2,1,0:T(8,128)(2,1)S(1)}, bf16[3,1024,128]{2,1,0:T(8,128)(2,1)}, u32[]{:S(2)}) copy-start(bf16[3,1024,128]{2,1,0:T(8,128)(2,1)} %get-tuple-element.281.qkv_ref) | copy-start | bytes 2359300
  52.5 2.0 %collective-permute-start.15 = (bf16[512,512]{1,0:T(8,128)(2,1)S(1)}, bf16[512,512]{1,0:T(8,128)(2,1)S(1)}, u32[]{:S(2)}, u32[]{:S(2)}) collective-permute-start(bf16[512,512]{1,0:T(8,128)(2,1)S(1)} %collective-permute-done.10.far_ref), channel_id=1, source_target_pairs={{0,1},{1,0},{2,3},{3,2},{4,5},{5,4},{6,7},{7,6},{8,9},{9,8},{10,11... | collective-permute-start | bytes 1572872 | tf_op jit(solution)/shard_map/sum_second/ppermute | solution.py:624
  52.5 14.1 %collective-permute-start.12 = (bf16[512,512]{1,0:T(8,128)(2,1)S(1)}, bf16[512,512]{1,0:T(8,128)(2,1)S(1)}, u32[]{:S(2)}, u32[]{:S(2)}) collective-permute-start(bf16[512,512]{1,0:T(8,128)(2,1)S(1)} %add.27.own_ref), channel_id=1, source_target_pairs={{0,1},{1,0},{2,3},{3,2},{4,5},{5,4},{6,7},{7,6},{8,9},{9,8},{10,11... | collective-permute-start | bytes 1572872 | tf_op jit(solution)/shard_map/sum_output/ppermute | solution.py:624
  53.0 13.8 %collective-permute-start.11 = (bf16[512,512]{1,0:T(8,128)(2,1)S(1)}, bf16[512,512]{1,0:T(8,128)(2,1)S(1)}, u32[]{:S(2)}, u32[]{:S(2)}) collective-permute-start(bf16[512,512]{1,0:T(8,128)(2,1)S(1)} %add.27.own_ref), channel_id=1, source_target_pairs={{0,2},{1,3},{2,0},{3,1},{4,6},{5,7},{6,4},{7,5},{8,10},{9,11},{10,... | collective-permute-start | bytes 1572872 | tf_op jit(solution)/shard_map/sum_output/ppermute | solution.py:624
  62.5 3.8 %copy-start.26 = (bf16[512,512]{1,0:T(8,128)(2,1)S(1)}, bf16[512,512]{1,0:T(8,128)(2,1)}, u32[]{:S(2)}) copy-start(bf16[512,512]{1,0:T(8,128)(2,1)} %copy-done.25) | copy-start | bytes 1572868
  66.3 2.9 %copy-start.1 = (bf16[4,5,16,128]{3,2,1,0:T(8,128)(2,1)S(1)}, bf16[4,5,16,128]{3,2,1,0:T(8,128)(2,1)}, u32[]{:S(2)}) copy-start(bf16[4,5,16,128]{3,2,1,0:T(8,128)(2,1)} %copy-done) | copy-start | bytes 245764
  66.4 2.9 %copy-start.4 = (bf16[1024,512]{1,0:T(8,128)(2,1)S(1)}, bf16[1024,512]{1,0:T(8,128)(2,1)}, u32[]{:S(2)}) copy-start(bf16[1024,512]{1,0:T(8,128)(2,1)} %tok_ref.3) | copy-start | bytes 3145732
  66.4 2.9 %copy-start.6 = (bf16[3,512,128]{2,1,0:T(8,128)(2,1)S(1)}, bf16[3,512,128]{2,1,0:T(8,128)(2,1)}, u32[]{:S(2)}) copy-start(bf16[3,512,128]{2,1,0:T(8,128)(2,1)} %w_ref.2) | copy-start | bytes 1179652
  66.4 2.9 %copy-start.23 = (bf16[1024,384]{1,0:T(8,128)(2,1)S(1)}, bf16[1024,384]{1,0:T(8,128)(2,1)}, u32[]{:S(2)}) copy-start(bf16[1024,384]{1,0:T(8,128)(2,1)} %copy-done.22) | copy-start | bytes 2359300
  66.4 2.9 %copy-start.29 = (f32[4,2,8,128]{3,2,1,0:T(8,128)S(1)}, f32[4,2,8,128]{3,2,1,0:T(8,128)}, u32[]{:S(2)}) copy-start(f32[4,2,8,128]{3,2,1,0:T(8,128)} %copy-done.28) | copy-start | bytes 98308
  66.8 15.2 %collective-permute-start.16 = (bf16[512,512]{1,0:T(8,128)(2,1)S(1)}, bf16[512,512]{1,0:T(8,128)(2,1)S(1)}, u32[]{:S(2)}, u32[]{:S(2)}) collective-permute-start(bf16[512,512]{1,0:T(8,128)(2,1)S(1)} %collective-permute-done.11.far_ref), channel_id=1, source_target_pairs={{0,1},{1,0},{2,3},{3,2},{4,5},{5,4},{6,7},{7,6},{8,9},{9,8},{10,11... | collective-permute-start | bytes 1572872 | tf_op jit(solution)/shard_map/sum_output/ppermute | solution.py:624
  67.3 8.6 %collective-permute-start.19 = (bf16[272,512]{1,0:T(8,128)(2,1)S(1)}, bf16[272,512]{1,0:T(8,128)(2,1)S(1)}, u32[]{:S(2)}, u32[]{:S(2)}) collective-permute-start(bf16[272,512]{1,0:T(8,128)(2,1)S(1)} %copy-done.32), channel_id=1, source_target_pairs={{0,8},{4,12},{8,0},{12,4},{16,24},{20,28},{24,16},{28,20},{1,9},{5... | collective-permute-start | bytes 835592 | tf_op jit(solution)/shard_map/rest_weights/ppermute | solution.py:624
  67.7 8.2 %copy-start.27 = (bf16[272,512]{1,0:T(8,128)(2,1)S(1)}, bf16[272,512]{1,0:T(8,128)(2,1)}, u32[]{:S(2)}) copy-start(bf16[272,512]{1,0:T(8,128)(2,1)} %get-tuple-element.312.a_ref) | copy-start | bytes 835588
  67.7 8.3 %collective-permute-start.18 = (bf16[256,512]{1,0:T(8,128)(2,1)S(1)}, bf16[256,512]{1,0:T(8,128)(2,1)S(1)}, u32[]{:S(2)}, u32[]{:S(2)}) collective-permute-start(bf16[256,512]{1,0:T(8,128)(2,1)S(1)} %get-tuple-element.309), channel_id=1, source_target_pairs={{0,4},{4,0},{8,12},{12,8},{16,20},{20,16},{24,28},{28,24},{1,5},{5... | collective-permute-start | bytes 786440 | tf_op jit(solution)/shard_map/feed_weights/ppermute | solution.py:624
  71.3 9.0 %collective-permute-start.17 = (bf16[528,512]{1,0:T(8,128)(2,1)S(1)}, bf16[528,512]{1,0:T(8,128)(2,1)S(1)}, u32[]{:S(2)}, u32[]{:S(2)}) collective-permute-start(bf16[528,512]{1,0:T(8,128)(2,1)S(1)} %get-tuple-element.308), channel_id=1, source_target_pairs={{0,1},{1,0},{2,3},{3,2},{4,5},{5,4},{6,7},{7,6},{8,9},{9,8},{10,11... | collective-permute-start | bytes 1622024 | tf_op jit(solution)/shard_map/sum_first/ppermute | solution.py:624
  76.0 7.8 %collective-permute-start.22 = (bf16[144,512]{1,0:T(8,128)(2,1)S(1)}, bf16[144,512]{1,0:T(8,128)(2,1)S(1)}, u32[]{:S(2)}, u32[]{:S(2)}) collective-permute-start(bf16[144,512]{1,0:T(8,128)(2,1)S(1)} %get-tuple-element.329), channel_id=1, source_target_pairs={{0,4},{4,0},{8,12},{12,8},{16,20},{20,16},{24,28},{28,24},{1,5},{5... | collective-permute-start | bytes 442376 | tf_op jit(solution)/shard_map/rest_weights/ppermute | solution.py:624
  77.7 8.2 %collective-permute-start.21 = (bf16[128,512]{1,0:T(8,128)(2,1)S(1)}, bf16[128,512]{1,0:T(8,128)(2,1)S(1)}, u32[]{:S(2)}, u32[]{:S(2)}) collective-permute-start(bf16[128,512]{1,0:T(8,128)(2,1)S(1)} %get-tuple-element.328), channel_id=1, source_target_pairs={{0,16},{4,20},{8,24},{12,28},{16,0},{20,4},{24,8},{28,12},{1,17},{... | collective-permute-start | bytes 393224 | tf_op jit(solution)/shard_map/feed_weights/ppermute | solution.py:624
  80.3 1.7 %copy-start.11 = (f32[512]{0:T(512)S(1)}, f32[512]{0:T(512)}, u32[]{:S(2)}) copy-start(f32[512]{0:T(512)} %param.24) | copy-start | bytes 6148
  80.3 1.7 %copy-start.14 = (f32[1024,512]{1,0:T(8,128)S(1)}, f32[1024,512]{1,0:T(8,128)}, u32[]{:S(2)}) copy-start(f32[1024,512]{1,0:T(8,128)} %get-tuple-element.326.mid_ref) | copy-start | bytes 6291460
  80.5 12.9 %collective-permute-start.20 = (bf16[528,512]{1,0:T(8,128)(2,1)S(1)}, bf16[528,512]{1,0:T(8,128)(2,1)S(1)}, u32[]{:S(2)}, u32[]{:S(2)}) collective-permute-start(bf16[528,512]{1,0:T(8,128)(2,1)S(1)} %pair.1.near_ref.own_ref), channel_id=1, source_target_pairs={{0,2},{1,3},{2,0},{3,1},{4,6},{5,7},{6,4},{7,5},{8,10},{9,11},{10,... | collective-permute-start | bytes 1622024 | tf_op jit(solution)/shard_map/sum_first/ppermute | solution.py:624
  84.1 9.3 %collective-permute-start.25 = (f32[8,512]{1,0:T(8,128)S(1)}, f32[8,512]{1,0:T(8,128)S(1)}, u32[]{:S(2)}, u32[]{:S(2)}) collective-permute-start(f32[8,512]{1,0:T(8,128)S(1)} %get-tuple-element.339.a_ref), channel_id=1, source_target_pairs={{0,1},{1,0},{2,3},{3,2},{4,5},{5,4},{6,7},{7,6},{8,9},{9,8},{10,11... | collective-permute-start | bytes 49160 | tf_op jit(solution)/shard_map/sum_extra/ppermute | solution.py:624
  85.9 9.4 %collective-permute-start.27 = (bf16[64,512]{1,0:T(8,128)(2,1)S(1)}, bf16[64,512]{1,0:T(8,128)(2,1)S(1)}, u32[]{:S(2)}, u32[]{:S(2)}) collective-permute-start(bf16[64,512]{1,0:T(8,128)(2,1)S(1)} %get-tuple-element.342), channel_id=1, source_target_pairs={{0,16},{4,20},{8,24},{12,28},{16,0},{20,4},{24,8},{28,12},{1,17},{... | collective-permute-start | bytes 196616 | tf_op jit(solution)/shard_map/rest_weights/ppermute | solution.py:624
  86.3 9.0 %copy-start.30 = (f32[8,512]{1,0:T(8,128)S(1)}, f32[8,512]{1,0:T(8,128)}, u32[]{:S(2)}) copy-start(f32[8,512]{1,0:T(8,128)} %get-tuple-element.349.up_ref) | copy-start | bytes 49156
  86.3 10.9 %collective-permute-start.29 = (bf16[128,512]{1,0:T(8,128)(2,1)S(1)}, bf16[128,512]{1,0:T(8,128)(2,1)S(1)}, u32[]{:S(2)}, u32[]{:S(2)}) collective-permute-start(bf16[128,512]{1,0:T(8,128)(2,1)S(1)} %add.28.a_ref), channel_id=1, source_target_pairs={{0,16},{4,20},{8,24},{12,28},{16,0},{20,4},{24,8},{28,12},{1,17},{... | collective-permute-start | bytes 393224 | tf_op jit(solution)/shard_map/feed_weights/ppermute | solution.py:624
  93.4 11.1 %collective-permute-start.24 = (bf16[528,512]{1,0:T(8,128)(2,1)S(1)}, bf16[528,512]{1,0:T(8,128)(2,1)S(1)}, u32[]{:S(2)}, u32[]{:S(2)}) collective-permute-start(bf16[528,512]{1,0:T(8,128)(2,1)S(1)} %collective-permute-done.20.far_ref), channel_id=1, source_target_pairs={{0,1},{1,0},{2,3},{3,2},{4,5},{5,4},{6,7},{7,6},{8,9},{9,8},{10,11... | collective-permute-start | bytes 1622024 | tf_op jit(solution)/shard_map/sum_first/ppermute | solution.py:624
  93.4 9.2 %collective-permute-start.26 = (f32[8,512]{1,0:T(8,128)S(1)}, f32[8,512]{1,0:T(8,128)S(1)}, u32[]{:S(2)}, u32[]{:S(2)}) collective-permute-start(f32[8,512]{1,0:T(8,128)S(1)} %plus.1.extra_ref), channel_id=1, source_target_pairs={{0,2},{1,3},{2,0},{3,1},{4,6},{5,7},{6,4},{7,5},{8,10},{9,11},{10,... | collective-permute-start | bytes 49160 | tf_op jit(solution)/shard_map/sum_extra/ppermute | solution.py:624
  95.3 7.2 %collective-permute-start.28 = (bf16[80,512]{1,0:T(8,128)(2,1)S(1)}, bf16[80,512]{1,0:T(8,128)(2,1)S(1)}, u32[]{:S(2)}, u32[]{:S(2)}) collective-permute-start(bf16[80,512]{1,0:T(8,128)(2,1)S(1)} %piece.1.a_ref), channel_id=1, source_target_pairs={{0,16},{4,20},{8,24},{12,28},{16,0},{20,4},{24,8},{28,12},{1,17},{... | collective-permute-start | bytes 245768 | tf_op jit(solution)/shard_map/rest_weights/ppermute | solution.py:624
  97.2 7.3 %copy-start.16 = (bf16[1024,512]{1,0:T(8,128)(2,1)S(1)}, bf16[1024,512]{1,0:T(8,128)(2,1)}, u32[]{:S(2)}) copy-start(bf16[1024,512]{1,0:T(8,128)(2,1)} %copy-done.15) | copy-start | bytes 3145732
  97.2 10.3 %collective-permute-start.31 = (bf16[256,512]{1,0:T(8,128)(2,1)S(1)}, bf16[256,512]{1,0:T(8,128)(2,1)S(1)}, u32[]{:S(2)}, u32[]{:S(2)}) collective-permute-start(bf16[256,512]{1,0:T(8,128)(2,1)S(1)} %concat.1.own_ref), channel_id=1, source_target_pairs={{0,8},{4,12},{8,0},{12,4},{16,24},{20,28},{24,16},{28,20},{1,9},{5... | collective-permute-start | bytes 786440 | tf_op jit(solution)/shard_map/feed_weights/ppermute | solution.py:624
  97.5 12.2 %collective-permute-start.34 = (bf16[256,512]{1,0:T(8,128)(2,1)S(1)}, bf16[256,512]{1,0:T(8,128)(2,1)S(1)}, u32[]{:S(2)}, u32[]{:S(2)}) collective-permute-start(bf16[256,512]{1,0:T(8,128)(2,1)S(1)} %concat.1.own_ref), channel_id=1, source_target_pairs={{0,4},{4,0},{8,12},{12,8},{16,20},{20,16},{24,28},{28,24},{1,5},{5... | collective-permute-start | bytes 786440 | tf_op jit(solution)/shard_map/feed_weights/ppermute | solution.py:624
  102.5 1.9 %collective-permute-start.23 = (bf16[528,512]{1,0:T(8,128)(2,1)S(1)}, bf16[528,512]{1,0:T(8,128)(2,1)S(1)}, u32[]{:S(2)}, u32[]{:S(2)}) collective-permute-start(bf16[528,512]{1,0:T(8,128)(2,1)S(1)} %pair.1.near_ref.own_ref), channel_id=1, source_target_pairs={{0,1},{1,0},{2,3},{3,2},{4,5},{5,4},{6,7},{7,6},{8,9},{9,8},{10,11... | collective-permute-start | bytes 1622024 | tf_op jit(solution)/shard_map/sum_first/ppermute | solution.py:624
  102.6 6.3 %collective-permute-start.30 = (bf16[144,512]{1,0:T(8,128)(2,1)S(1)}, bf16[144,512]{1,0:T(8,128)(2,1)S(1)}, u32[]{:S(2)}, u32[]{:S(2)}) collective-permute-start(bf16[144,512]{1,0:T(8,128)(2,1)S(1)} %merge.2.a_ref), channel_id=1, source_target_pairs={{0,4},{4,0},{8,12},{12,8},{16,20},{20,16},{24,28},{28,24},{1,5},{5... | collective-permute-start | bytes 442376 | tf_op jit(solution)/shard_map/rest_weights/ppermute | solution.py:624
  107.6 8.3 %collective-permute-start.33 = (bf16[256,512]{1,0:T(8,128)(2,1)S(1)}, bf16[256,512]{1,0:T(8,128)(2,1)S(1)}, u32[]{:S(2)}, u32[]{:S(2)}) collective-permute-start(bf16[256,512]{1,0:T(8,128)(2,1)S(1)} %collective-permute-done.31.own_ref), channel_id=1, source_target_pairs={{0,4},{4,0},{8,12},{12,8},{16,20},{20,16},{24,28},{28,24},{1,5},{5... | collective-permute-start | bytes 786440 | tf_op jit(solution)/shard_map/feed_weights/ppermute | solution.py:624
  108.9 8.4 %collective-permute-start.32 = (bf16[272,512]{1,0:T(8,128)(2,1)S(1)}, bf16[272,512]{1,0:T(8,128)(2,1)S(1)}, u32[]{:S(2)}, u32[]{:S(2)}) collective-permute-start(bf16[272,512]{1,0:T(8,128)(2,1)S(1)} %merge.3.near_ref), channel_id=1, source_target_pairs={{0,8},{4,12},{8,0},{12,4},{16,24},{20,28},{24,16},{28,20},{1,9},{5... | collective-permute-start | bytes 835592 | tf_op jit(solution)/shard_map/rest_weights/ppermute | solution.py:624
  (10 other events, 9.4 us)
